TPU v7x, 32 devices: a whole 2x2x4 slice. The times are simulated.
32 devices in a mesh: parts: 2 (over y), wide: 8 (over z, x), narrow: 2 (over core).
Axes of the slice: x: 2, y: 2, z: 4, core: 2. Of those that a mesh axis runs over, the one named last changes fastest.
Arguments:
- queries: bfloat16 [2, 16, 4096], P(None, ('parts', 'wide'), 'narrow'), parts along dimension 1, may hold values from -96 to 96
- new_kv: bfloat16 [2, 16, 2, 1024], P(None, ('parts', 'wide'), None, 'narrow'), parts along dimension 1, may hold values from -5 to 5
- cache_keys: bfloat16 [16, 8, 128, 128], P(('parts', 'wide'), 'narrow'), parts along dimension 0, may hold values from -6 to 6
- stored_values: bfloat16 [16, 8, 128, 128], P(('parts', 'wide'), 'narrow'), parts along dimension 0, may hold values from -6 to 6
- lengths: int32 [16], P(('parts', 'wide')), parts along dimension 0, may hold values from 2 to 126
- residual: bfloat16 [2, 16, 4096], P(None, ('parts', 'wide'), 'narrow'), parts along dimension 1, may hold values from -32 to 32
- norm_gain: float32 [4096], P('narrow'), may hold values from 0.1 to 1.9
- gate_weight: bfloat16 [4096, 2, 28672], P(None, 'narrow', 'wide'), may hold values from -0.09375 to 0.09375
- up_weight: bfloat16 [4096, 2, 28672], P(None, 'narrow', 'wide'), may hold values from -0.09375 to 0.09375
Outputs:
- attended: bfloat16 [2, 16, 4096], P(None, ('parts', 'wide'), 'narrow'), parts along dimension 1
- activated: bfloat16 [2, 16, 14336], P(None, ('parts', 'wide'), 'narrow'), parts along dimension 1
There are 2 independent parts, one for each index of `parts`. A program takes and returns all parts, laid end to end along the dimension named above; an argument that names none is the same for every part. Nothing has to cross between parts.
All inputs are finite; a program needn't handle non-finite values.
Results may differ from a plain program's by a relative error of at most 0.0062.
Values may be sent and summed in bfloat16 or wider, within the bound.
No kernel may reach another device: no remote copies, remote signals or barrier semaphores. Data moves between devices by JAX's collectives and lax.ppermute only.
A program may use at most 128 MiB of HBM per device.

v0:
```python
import jax
import jax.numpy as jnp
from jax import lax
from jax.sharding import PartitionSpec as P

D = 4096
HEAD_SIZE = 128
QUERY_HEADS = 32
KEY_VALUE_HEADS = 8
DECODE_STEPS = 2


def attend(queries, new_kv, cache_keys, stored_values, lengths):
    steps, rollouts, width = queries.shape
    kv_heads = cache_keys.shape[1]
    hist = cache_keys.shape[2]
    query_group = QUERY_HEADS // KEY_VALUE_HEADS
    scale = 1.0 / HEAD_SIZE**0.5
    query_vector = queries.reshape(steps, rollouts, kv_heads, query_group, HEAD_SIZE)
    newest_keys = new_kv[:, :, 0].reshape(steps, rollouts, kv_heads, HEAD_SIZE)
    newest_values = new_kv[:, :, 1].reshape(steps, rollouts, kv_heads, HEAD_SIZE)
    cached = (
        jnp.einsum(
            "srhgd,rhpd->srhgp", query_vector, cache_keys, preferred_element_type=jnp.float32
        )
        * scale
    )
    recent = (
        jnp.einsum(
            "srhgd,trhd->srhgt", query_vector, newest_keys, preferred_element_type=jnp.float32
        )
        * scale
    )
    valid = (jnp.arange(hist)[None, :] < lengths[:, None])[None, :, None, None, :]
    causal = (jnp.arange(steps)[None, :] <= jnp.arange(steps)[:, None])[:, None, None, None, :]
    cached = jnp.where(valid, cached, -1e30)
    recent = jnp.where(causal, recent, -1e30)
    top = jnp.maximum(jnp.max(cached, -1), jnp.max(recent, -1))
    e_cached = jnp.where(valid, jnp.exp(cached - top[..., None]), 0.0)
    e_recent = jnp.where(causal, jnp.exp(recent - top[..., None]), 0.0)
    total = jnp.sum(e_cached, -1) + jnp.sum(e_recent, -1)
    w_cached = (e_cached / total[..., None]).astype(jnp.bfloat16)
    w_recent = (e_recent / total[..., None]).astype(jnp.bfloat16)
    out = jnp.einsum(
        "srhgp,rhpd->srhgd", w_cached, stored_values, preferred_element_type=jnp.float32
    )
    out = out + jnp.einsum(
        "srhgt,trhd->srhgd", w_recent, newest_values, preferred_element_type=jnp.float32
    )
    return out.reshape(steps, rollouts, width).astype(jnp.bfloat16)


def normalize(mixed, norm_gain):
    squares = jnp.sum(mixed * mixed, -1)
    total = lax.psum(squares, "narrow")
    return (mixed * lax.rsqrt(total / D + 1e-05)[..., None] * norm_gain).astype(jnp.bfloat16)


def feed_forward(normed, gate_weight, up_weight):
    steps, rollouts, half = normed.shape
    width = lax.axis_size("wide")
    serving = width * 3 // 4
    worker = lax.axis_index("wide") >= serving
    features = gate_weight.shape[0]
    columns = gate_weight.shape[2]
    whole = lax.all_gather(normed, "narrow", axis=2, tiled=True)
    target = (jnp.arange(width) >= serving)[None, :, None, None]
    outgoing = jnp.where(target, whole[:, None], jnp.zeros((), jnp.bfloat16))
    arrived = lax.all_to_all(outgoing, "wide", split_axis=1, concat_axis=1, tiled=True).reshape(
        steps, width * rollouts, features
    )
    live_rows = arrived[:, : serving * rollouts].reshape(steps * serving * rollouts, features)

    def produce():
        gate = jnp.dot(
            live_rows, gate_weight.reshape(features, columns), preferred_element_type=jnp.float32
        )
        up = jnp.dot(
            live_rows, up_weight.reshape(features, columns), preferred_element_type=jnp.float32
        )
        return (
            (jax.nn.silu(gate) * up)
            .astype(jnp.bfloat16)
            .reshape(steps, serving * rollouts, columns)
        )

    def feed_nothing():
        return jnp.zeros((steps, serving * rollouts, columns), jnp.bfloat16)

    hidden = lax.cond(worker, produce, feed_nothing)
    padding = jnp.zeros((steps, (width - serving) * rollouts, columns), jnp.bfloat16)
    outgoing_rows = jnp.concatenate([hidden, padding], 1)
    back = lax.all_to_all(outgoing_rows, "wide", split_axis=1, concat_axis=2, tiled=True)
    return back[:, :, serving * columns :]


def shards(
    queries, new_kv, cache_keys, stored_values, lengths, residual, norm_gain, gate_weight, up_weight
):
    width = lax.axis_size("wide")
    serving = width * 3 // 4
    owner = lax.axis_index("wide") < serving

    def compute():
        return attend(queries, new_kv, cache_keys, stored_values, lengths)

    def body_nothing():
        return jnp.zeros(queries.shape, jnp.bfloat16)

    attended = lax.cond(owner, compute, body_nothing)
    mixed = residual.astype(jnp.float32) + attended.astype(jnp.float32)
    pieces = []
    for step in range(DECODE_STEPS):
        normed = normalize(mixed[step : step + 1], norm_gain)
        pieces.append(feed_forward(normed, gate_weight, up_weight))
    activated = jnp.concatenate(pieces, 0)
    return (attended, activated)


def solution(mesh):
    placed = (
        P(None, ("parts", "wide"), "narrow"),
        P(None, ("parts", "wide"), None, "narrow"),
        P(("parts", "wide"), "narrow", None, None),
        P(("parts", "wide"), "narrow", None, None),
        P(("parts", "wide")),
        P(None, ("parts", "wide"), "narrow"),
        P("narrow"),
        P(None, "narrow", "wide"),
        P(None, "narrow", "wide"),
    )
    return jax.shard_map(
        shards,
        mesh=mesh,
        in_specs=placed,
        out_specs=(P(None, ("parts", "wide"), "narrow"), P(None, ("parts", "wide"), "narrow")),
        check_vma=False,
    )
```

profile of v0, /device:TPU:0, one launch (start us, length us, event | category | flops | bytes accessed | tf_op | source)
XLA Modules:
  0.0 105.1 jit_solution(8735320190457465777)
XLA Ops:
  0.7 6.6 %conditional.3 = (bf16[2,1,2048]{2,0,1:T(2,128)(2,1)}, f32[2,1,2048]{2,0,1:T(2,128)S(1)}) conditional(s32[]{:T(128)} %convert_element_type.66, () %tuple.30, (s32[1]{0:T(128)}, bf16[1,4,128,128]{3,2,1,0:T(8,128)(2,1)}, bf16[2,1,2048]{2,0,1:T(2,128)(2,1)}, bf16[2,1,2,512]{3,2,1,0:T(2,128)(2,1)}, bf16[1,4,128,128]{3,2,1,0:T(8,128)(2,1)}) %tuple.31), branch_computations={%region_0.0_spmd, %region_1.6_spmd} | conditional | flops 2184004 | bytes 462500 | solution.py:110
  0.7 0.7 iota_compare_fusion.1
  1.3 0.7 copy.45
  2.0 0.7 reshape.267
  2.7 0.2 convolution_multiply_fusion.1
  2.9 0.1 fusion.15
  3.0 1.2 %fusion.46 = (f32[2,4,4]{2,0,1:T(2,128)S(1)}, f32[2,1,4,4,128]{4,3,0,2,1:T(4,128)S(1)}) fusion(bf16[2,4,4,128]{3,2,1,0:T(4,128)(2,1)S(1)} %reshape.267, bf16[1,4,128,128]{3,2,1,0:T(8,128)(2,1)} %get-tuple-element.53, pred[128]{0:T(512)(128)(4,1)S(1)} %iota_compare_fusion.1), kind=kOutput, calls=%fused_computation.59 | convolution fusion | flops 1060832 | bytes 155904 | tf_op jit(solution)/shard_map/cond/branch_1_fun/srhgd,rhpd->srhgp/dot_general | solution.py:23
  4.2 0.1 fusion.19
  4.3 0.2 fusion.8
  4.5 0.1 fusion.17
  4.6 1.1 %fusion.5 = f32[4,2,4,128]{3,2,1,0:T(4,128)S(1)} fusion(bf16[1,4,128,128]{3,2,1,0:T(8,128)(2,1)} %get-tuple-element.56, f32[2,1,4,4,128]{4,3,0,2,1:T(4,128)S(1)} %get-tuple-element.97, f32[2,4,4]{2,0,1:T(2,128)S(1)} %add.28, f32[2,4,4]{2,0,1:T(2,128)S(1)} %max.8, pred[128]{0:T(512)(128)(4,1)S(1)} %iota_compare_fusion.1), kind=kOutput, calls=%fused_computation.8 | convolution fusion | flops 1064960 | bytes 164224 | tf_op jit(solution)/shard_map/cond/branch_1_fun/srhgp,rhpd->srhgd/dot_general | solution.py:44
  5.7 0.2 fusion.2
  5.9 0.6 convert_element_type.57
  6.5 0.7 convert_element_type.58
  7.2 0.7 convert_add_fusion
  7.9 0.7 multiply_reduce_fusion.1
  8.6 3.2 %all-reduce.2 = (f32[1,1]{1,0:T(1,128)}, f32[1,1]{1,0:T(1,128)}) all-reduce(f32[1,1]{1,0:T(1,128)} %bitcast.37, f32[1,1]{1,0:T(1,128)} %bitcast.32), channel_id=1, replica_groups=mesh['parts'=2,'wide'=8,'narrow'=2] {'narrow'}, use_global_device_ids=true, to_apply=%region_11.12 | all-reduce | flops 2 | bytes 16 | tf_op jit(solution)/shard_map/psum | solution.py:55
  13.1 0.7 multiply_convert_fusion.1
  13.8 1.8 %all_gather.6 = bf16[1,1,4096]{2,0,1:T(2,128)(2,1)S(1)} all-gather(bf16[1,1,2048]{2,0,1:T(2,128)(2,1)S(1)} %get-tuple-element.98), channel_id=1, replica_groups=mesh['parts'=2,'wide'=8,'narrow'=2] {'narrow'}, dimensions={2}, use_global_device_ids=true | all-gather | bytes 12288 | tf_op jit(solution)/shard_map/all_gather | solution.py:66
  15.7 1.8 %all_gather.7 = bf16[1,1,4096]{2,0,1:T(2,128)(2,1)S(1)} all-gather(bf16[1,1,2048]{2,0,1:T(2,128)(2,1)S(1)} %get-tuple-element.99), channel_id=1, replica_groups=mesh['parts'=2,'wide'=8,'narrow'=2] {'narrow'}, dimensions={2}, use_global_device_ids=true | all-gather | bytes 12288 | tf_op jit(solution)/shard_map/all_gather | solution.py:66
  17.5 0.1 reduce.6
  17.5 0.1 reduce.7
  17.6 0.2 broadcast_select_fusion.1
  17.8 0.5 broadcast.169
  18.3 0.9 reduce.10
  19.3 0.6 reshape.301
  19.9 6.1 %all-to-all-start = ((bf16[8,2,2048]{2,1,0:T(2,128)(2,1)}), bf16[8,2,2048]{2,1,0:T(2,128)(2,1)S(1)}, u32[]{:S(2)}, u32[]{:S(2)}) async-start(bf16[8,2,2048]{2,1,0:T(2,128)(2,1)} %reshape.301), calls=%async_computation | async-start | bytes 131072 | tf_op jit(solution)/shard_map/all_to_all | solution.py:69
  26.0 0.9 reduce.8
  27.0 0.7 reshape.297
  27.6 5.3 %all-to-all-done = bf16[8,2,2048]{2,1,0:T(2,128)(2,1)S(1)} async-done(((bf16[8,2,2048]{2,1,0:T(2,128)(2,1)}), bf16[8,2,2048]{2,1,0:T(2,128)(2,1)S(1)}, u32[]{:S(2)}, u32[]{:S(2)}) %all-to-all-start) | async-done | bytes 65568 | tf_op jit(solution)/shard_map/all_to_all | solution.py:69
  32.9 3.3 %all-to-all-start.2 = ((bf16[8,2,2048]{2,1,0:T(2,128)(2,1)}), bf16[8,2,2048]{2,1,0:T(2,128)(2,1)S(1)}, u32[]{:S(2)}, u32[]{:S(2)}) async-start(bf16[8,2,2048]{2,1,0:T(2,128)(2,1)} %reshape.297), calls=%async_computation.2 | async-start | bytes 131072 | tf_op jit(solution)/shard_map/all_to_all | solution.py:69
  36.3 0.1 reshape.302
  36.4 0.1 copy.47
  36.5 0.1 pad_bitcast_fusion.1
  36.6 0.9 reduce.11
  37.5 0.6 reshape.303
  38.1 5.0 %all-to-all-done.2 = bf16[8,2,2048]{2,1,0:T(2,128)(2,1)S(1)} async-done(((bf16[8,2,2048]{2,1,0:T(2,128)(2,1)}), bf16[8,2,2048]{2,1,0:T(2,128)(2,1)S(1)}, u32[]{:S(2)}, u32[]{:S(2)}) %all-to-all-start.2) | async-done | bytes 65568 | tf_op jit(solution)/shard_map/all_to_all | solution.py:69
  43.1 23.7 %all-to-all-start.1 = ((bf16[8,2,1792]{2,1,0:T(2,128)(2,1)}), bf16[8,2,1792]{2,1,0:T(2,128)(2,1)S(1)}, u32[]{:S(2)}, u32[]{:S(2)}) async-start(bf16[8,2,1792]{2,1,0:T(2,128)(2,1)} %reshape.303), calls=%async_computation.1 | async-start | bytes 114688 | tf_op jit(solution)/shard_map/all_to_all | solution.py:93
  66.9 0.1 reshape.298
  67.0 0.1 copy.50
  67.0 0.1 pad_bitcast_fusion
  67.2 0.9 reduce.9
  68.0 0.6 reshape.299
  68.7 5.0 %all-to-all-done.1 = bf16[8,2,1792]{2,1,0:T(2,128)(2,1)S(1)} async-done(((bf16[8,2,1792]{2,1,0:T(2,128)(2,1)}), bf16[8,2,1792]{2,1,0:T(2,128)(2,1)S(1)}, u32[]{:S(2)}, u32[]{:S(2)}) %all-to-all-start.1) | async-done | bytes 57376 | tf_op jit(solution)/shard_map/all_to_all | solution.py:93
  73.7 23.8 %all-to-all-start.3 = ((bf16[8,2,1792]{2,1,0:T(2,128)(2,1)}), bf16[8,2,1792]{2,1,0:T(2,128)(2,1)S(1)}, u32[]{:S(2)}, u32[]{:S(2)}) async-start(bf16[8,2,1792]{2,1,0:T(2,128)(2,1)} %reshape.299), calls=%async_computation.3 | async-start | bytes 114688 | tf_op jit(solution)/shard_map/all_to_all | solution.py:93
  97.6 6.8 %all-to-all-done.3 = bf16[8,2,1792]{2,1,0:T(2,128)(2,1)S(1)} async-done(((bf16[8,2,1792]{2,1,0:T(2,128)(2,1)}), bf16[8,2,1792]{2,1,0:T(2,128)(2,1)S(1)}, u32[]{:S(2)}, u32[]{:S(2)}) %all-to-all-start.3) | async-done | bytes 57376 | tf_op jit(solution)/shard_map/all_to_all | solution.py:93
  104.5 0.7 pad_maximum_fusion
  (13 shorter events, 0.3 us)
Async XLA Ops:
  19.9 13.0 %all-to-all-start = ((bf16[8,2,2048]{2,1,0:T(2,128)(2,1)}), bf16[8,2,2048]{2,1,0:T(2,128)(2,1)S(1)}, u32[]{:S(2)}, u32[]{:S(2)}) async-start(bf16[8,2,2048]{2,1,0:T(2,128)(2,1)} %reshape.301), calls=%async_computation | async-start | bytes 131072 | tf_op jit(solution)/shard_map/all_to_all | solution.py:69
  32.9 10.2 %all-to-all-start.2 = ((bf16[8,2,2048]{2,1,0:T(2,128)(2,1)}), bf16[8,2,2048]{2,1,0:T(2,128)(2,1)S(1)}, u32[]{:S(2)}, u32[]{:S(2)}) async-start(bf16[8,2,2048]{2,1,0:T(2,128)(2,1)} %reshape.297), calls=%async_computation.2 | async-start | bytes 131072 | tf_op jit(solution)/shard_map/all_to_all | solution.py:69
  43.1 30.6 %all-to-all-start.1 = ((bf16[8,2,1792]{2,1,0:T(2,128)(2,1)}), bf16[8,2,1792]{2,1,0:T(2,128)(2,1)S(1)}, u32[]{:S(2)}, u32[]{:S(2)}) async-start(bf16[8,2,1792]{2,1,0:T(2,128)(2,1)} %reshape.303), calls=%async_computation.1 | async-start | bytes 114688 | tf_op jit(solution)/shard_map/all_to_all | solution.py:93
  73.7 30.7 %all-to-all-start.3 = ((bf16[8,2,1792]{2,1,0:T(2,128)(2,1)}), bf16[8,2,1792]{2,1,0:T(2,128)(2,1)S(1)}, u32[]{:S(2)}, u32[]{:S(2)}) async-start(bf16[8,2,1792]{2,1,0:T(2,128)(2,1)} %reshape.299), calls=%async_computation.3 | async-start | bytes 114688 | tf_op jit(solution)/shard_map/all_to_all | solution.py:93
where the time goes:
time: 106 us; the launch traced here: 105 us
  starting transfers between devices  57 us (54%)
  waiting for transfers between devices  22.2 us (21%)
  other arithmetic  8.58 us (8%)
  blocking collectives  6.83 us (6%)
  local copies, waits for them, and re-layouts  5.75 us (5%)
  matrix products  2.66 us (3%)
  between operations  2.06 us (2%)
    all_to_all x2, starting transfers between devices, feed_forward(): lax.all_to_all(outgoing_rows, 'wide', split_axis=1, concat_axis=2, tiled=...  47.5 us
    all_to_all x2, waiting for transfers between devices, feed_forward(): lax.all_to_all(outgoing_rows, 'wide', split_axis=1, concat_axis=2, tiled=...  11.8 us
    all_to_all x2, waiting for transfers between devices, feed_forward(): lax.all_to_all(outgoing, 'wide', split_axis=1, concat_axis=1, tiled=True)  10.4 us
    all_to_all x2, starting transfers between devices, feed_forward(): lax.all_to_all(outgoing, 'wide', split_axis=1, concat_axis=1, tiled=True)  9.45 us
    all_gather x2, blocking collectives, feed_forward(): whole = lax.all_gather(normed, 'narrow', axis=2, tiled=True)  3.64 us
    unnamed x4, other arithmetic  3.6 us
    unnamed x11, local copies, waits for them, and re-layouts  3.52 us
    psum x1, blocking collectives, normalize(): total = lax.psum(squares, 'narrow')  3.2 us
  transfers between devices with their start and end apart: 4, of which 4 were waited for; matrix products, arithmetic and copies ran while one was open for 5% of the time, Pallas kernels for 0%

commit v1 on v0

v1 whole, which is shorter than its diff:
```python
import functools

import jax
import jax.numpy as jnp
from jax import lax
from jax.experimental import pallas as pl
from jax.experimental.pallas import tpu as pltpu
from jax.sharding import PartitionSpec as P

D = 4096
HEAD_SIZE = 128
STEPS = 2
TAIL = 128
EPS = 1e-05


def attend_kernel(serving, lengths, q, kv, keys, values, residual, gain, attended, sent):
    owner = lax.axis_index("wide") < serving
    heads, hist, _ = keys.shape
    width = q.shape[1]
    group = width // (heads * HEAD_SIZE)

    @pl.when(jnp.logical_not(owner))
    def _():
        attended[...] = jnp.zeros_like(attended)
        sent[...] = jnp.zeros_like(sent)

    @pl.when(owner)
    def _():
        length = lengths[0]
        slot = lax.broadcasted_iota(jnp.int32, (hist, HEAD_SIZE), 0)
        rows = group * STEPS
        place = lax.broadcasted_iota(jnp.int32, (rows, hist), 1)
        step = lax.broadcasted_iota(jnp.int32, (rows, hist), 0) % STEPS
        first = hist - STEPS
        seen = (place < length) | ((place >= first) & (place - first <= step))
        squares = jnp.zeros((STEPS, 1), jnp.float32)
        for h in range(heads):
            lanes = slice(h * HEAD_SIZE, (h + 1) * HEAD_SIZE)
            k, v = keys[h], values[h]
            for t in range(STEPS):
                k = jnp.where(slot == first + t, kv[t, 0:1, lanes], k)
                v = jnp.where(slot == first + t, kv[t, 1:2, lanes], v)
            cols = [(h * group + g) * HEAD_SIZE for g in range(group)]
            query = jnp.concatenate(
                [q[:, c : c + HEAD_SIZE].astype(jnp.float32) for c in cols], 0
            ).astype(jnp.bfloat16)
            scores = lax.dot_general(
                query, k, (((1,), (1,)), ((), ())), preferred_element_type=jnp.float32
            ) * (1.0 / HEAD_SIZE**0.5)
            scores = jnp.where(seen, scores, -1e30)
            top = jnp.max(scores, -1, keepdims=True)
            e = jnp.where(seen, jnp.exp(scores - top), 0.0)
            weights = (e / jnp.sum(e, -1, keepdims=True)).astype(jnp.bfloat16)
            out = jnp.dot(weights, v, preferred_element_type=jnp.float32)
            for g, c in enumerate(cols):
                here = slice(c, c + HEAD_SIZE)
                got = out[g * STEPS : (g + 1) * STEPS].astype(jnp.bfloat16)
                attended[:, here] = got
                mixed = residual[:, here].astype(jnp.float32) + got.astype(jnp.float32)
                squares += jnp.sum(mixed * mixed, -1, keepdims=True)
                sent[:, here] = (mixed * gain[:, here]).astype(jnp.bfloat16)
        high = squares.astype(jnp.bfloat16)
        low = (squares - high.astype(jnp.float32)).astype(jnp.bfloat16)
        lane = lax.broadcasted_iota(jnp.int32, (STEPS, TAIL), 1)
        sent[:, width:] = jnp.where(
            lane == 0,
            high.astype(jnp.float32),
            jnp.where(lane == 1, low.astype(jnp.float32), 0.0),
        ).astype(jnp.bfloat16)


def forward_kernel(serving, narrow, tile, gathered, gate, up, *rest):
    outs = rest[:serving]
    x, scale, gates, ups, sems = rest[serving:]
    wide = lax.axis_index("wide")
    features, columns = gate.shape
    tiles = columns // tile
    half = features // narrow
    depth = gates.shape[0]

    def copies(j):
        here = pl.ds(j * tile, tile)
        s = j % depth
        return (
            pltpu.make_async_copy(gate.at[:, here], gates.at[s], sems.at[0, s]),
            pltpu.make_async_copy(up.at[:, here], ups.at[s], sems.at[1, s]),
        )

    @pl.when(wide < serving)
    def _():
        for out in outs:
            out[...] = jnp.zeros_like(out)

    @pl.when(wide >= serving)
    def _():
        for j in range(min(depth, tiles)):
            for c in copies(j):
                c.start()
        rows, tails = [], []
        for i in range(serving):
            owner = lax.rem(i + wide - serving, serving)
            parts = [gathered[owner * narrow + n] for n in range(narrow)]
            rows.append(jnp.concatenate([p[:, :half] for p in parts], 1).astype(jnp.float32))
            tails.append(sum(p[:, half:].astype(jnp.float32) for p in parts))
        pad = x.shape[0] - STEPS * serving
        if pad:
            rows.append(jnp.zeros((pad, features), jnp.float32))
            tails.append(jnp.zeros((pad, TAIL), jnp.float32))
        x[...] = jnp.concatenate(rows, 0).astype(jnp.bfloat16)
        squares = jnp.sum(jnp.concatenate(tails, 0), -1, keepdims=True)
        scale[...] = jnp.broadcast_to(lax.rsqrt(squares / D + EPS), scale.shape)
        for j in range(tiles):
            for c in copies(j):
                c.wait()
            s = j % depth
            r = scale[:, 0:1]
            g = jnp.dot(x[...], gates[s], preferred_element_type=jnp.float32) * r
            u = jnp.dot(x[...], ups[s], preferred_element_type=jnp.float32) * r
            hidden = (g / (1.0 + jnp.exp(-g)) * u).astype(jnp.bfloat16)
            for i, out in enumerate(outs):
                out[:, j * tile : (j + 1) * tile] = hidden[i * STEPS : (i + 1) * STEPS]
            if j + depth < tiles:
                for c in copies(j + depth):
                    c.start()


def shards(queries, new_kv, keys, values, lengths, residual, gain, gate, up):
    wide = lax.axis_size("wide")
    narrow = lax.axis_size("narrow")
    serving = wide * 3 // 4
    workers = wide - serving
    half = queries.shape[2]
    features, _, columns = gate.shape
    vmem = pl.BlockSpec(memory_space=pltpu.VMEM)
    attended, sent = pl.pallas_call(
        functools.partial(attend_kernel, serving),
        out_shape=(
            jax.ShapeDtypeStruct((STEPS, half), jnp.bfloat16),
            jax.ShapeDtypeStruct((STEPS, half + TAIL), jnp.bfloat16),
        ),
        in_specs=[pl.BlockSpec(memory_space=pltpu.SMEM)] + [vmem] * 6,
        out_specs=(vmem, vmem),
        compiler_params=pltpu.CompilerParams(vmem_limit_bytes=8 << 20),
    )(
        lengths,
        queries.reshape(STEPS, half),
        new_kv.reshape(STEPS, 2, -1),
        keys.reshape(keys.shape[1:]),
        values.reshape(values.shape[1:]),
        residual.reshape(STEPS, half),
        gain.reshape(1, half),
    )
    gathered = lax.all_gather(sent, ("wide", "narrow"), axis=0)
    tile = next((t for t in (512, 256, 128) if columns % t == 0), columns)
    depth = min(3, columns // tile)
    padded = -(-STEPS * serving // 16) * 16
    hidden = pl.pallas_call(
        functools.partial(forward_kernel, serving, narrow, tile),
        out_shape=[jax.ShapeDtypeStruct((STEPS, columns), jnp.bfloat16)] * serving,
        in_specs=[vmem, pl.BlockSpec(memory_space=pl.ANY), pl.BlockSpec(memory_space=pl.ANY)],
        out_specs=[vmem] * serving,
        scratch_shapes=[
            pltpu.VMEM((padded, features), jnp.bfloat16),
            pltpu.VMEM((padded, 128), jnp.float32),
            pltpu.VMEM((depth, features, tile), jnp.bfloat16),
            pltpu.VMEM((depth, features, tile), jnp.bfloat16),
            pltpu.SemaphoreType.DMA((2, depth)),
        ],
        compiler_params=pltpu.CompilerParams(vmem_limit_bytes=48 << 20),
    )(gathered, gate.reshape(features, columns), up.reshape(features, columns))
    back = [
        lax.ppermute(h, "wide", [(serving + k, (i + k) % serving) for k in range(workers)])
        for i, h in enumerate(hidden)
    ]
    me = lax.axis_index("wide")
    pieces = []
    for k in range(workers):
        mine = lax.rem(me + serving - k, serving)
        piece = back[0]
        for i in range(1, serving):
            piece = jnp.where(mine == i, back[i], piece)
        pieces.append(jnp.where(me < serving, piece, jnp.zeros((), jnp.bfloat16)))
    activated = jnp.concatenate(pieces, 1)
    return attended.reshape(STEPS, 1, half), activated.reshape(STEPS, 1, -1)


def solution(mesh):
    rows = P(None, ("parts", "wide"), "narrow")
    placed = (
        rows,
        P(None, ("parts", "wide"), None, "narrow"),
        P(("parts", "wide"), "narrow", None, None),
        P(("parts", "wide"), "narrow", None, None),
        P(("parts", "wide")),
        rows,
        P("narrow"),
        P(None, "narrow", "wide"),
        P(None, "narrow", "wide"),
    )
    return jax.shard_map(
        shards, mesh=mesh, in_specs=placed, out_specs=(rows, rows), check_vma=False
    )
```

time: 106 us -> 60.3 us (0.57)
  starting transfers between devices: 57 us -> 5.22 us
  blocking collectives: 6.83 us -> 22 us
  other arithmetic: 8.58 us -> 0.7 us
  matrix products: 2.66 us -> 0 us
  Pallas kernels: 0 us -> 2.12 us
  waiting for transfers between devices: 22.2 us -> 23.9 us
  local copies, waits for them, and re-layouts: 5.75 us -> 4.58 us
    all_to_all x4 -> x0, starting transfers between devices: 57 us -> none  [the longest x2 47.5 us: feed_forward(): lax.all_to_all(outgoing_rows, 'wide', split_axis=1, concat_axis=2, tiled=...]
    ppermute x0 -> x6, waiting for transfers between devices: none -> 23.9 us  [shards(): lax.ppermute(h, 'wide', [(serving + k, (i + k) % serving) for k in range(...]
    all_to_all x4 -> x0, waiting for transfers between devices: 22.2 us -> none  [the longest x2 11.8 us: feed_forward(): lax.all_to_all(outgoing_rows, 'wide', split_axis=1, concat_axis=2, tiled=...]
    all_gather x2 -> x1, blocking collectives: 3.64 us -> 22 us  [shards(): gathered = lax.all_gather(sent, ('wide', 'narrow'), axis=0)]
    ppermute x0 -> x6, starting transfers between devices: none -> 5.22 us  [shards(): lax.ppermute(h, 'wide', [(serving + k, (i + k) % serving) for k in range(...]
    unnamed x4 -> x0, other arithmetic: 3.6 us -> none
    psum x1 -> x0, blocking collectives: 3.2 us -> none  [normalize(): total = lax.psum(squares, 'narrow')]
    dot_general x4 -> x0, matrix products: 2.66 us -> none  [the longest x1 1.18 us: attend(): jnp.einsum('srhgd,rhpd->srhgp', query_vector, cache_keys, preferred_eleme...]
  transfers between devices with their start and end apart: 4 -> 6, of which waited for: 4 -> 2; matrix products, arithmetic and copies ran while one was open for 5% -> 0% of each run, Pallas kernels for 0% -> 0%
where the time goes in v1:
time: 60.3 us; the launch traced here: 59.9 us
  waiting for transfers between devices  23.9 us (40%)
  blocking collectives  22 us (36%)
  starting transfers between devices  5.22 us (9%)
  local copies, waits for them, and re-layouts  4.58 us (8%)
  Pallas kernels  2.12 us (4%)
  between operations  1.42 us (2%)
  other arithmetic  0.7 us (1%)
    ppermute x6, waiting for transfers between devices, shards(): lax.ppermute(h, 'wide', [(serving + k, (i + k) % serving) for k in range(...  23.9 us
    all_gather x1, blocking collectives, shards(): gathered = lax.all_gather(sent, ('wide', 'narrow'), axis=0)  22 us
    ppermute x6, starting transfers between devices, shards(): lax.ppermute(h, 'wide', [(serving + k, (i + k) % serving) for k in range(...  5.22 us
    unnamed x12, local copies, waits for them, and re-layouts  4.58 us
    pallas_call x1, Pallas kernels, shards(): pl.pallas_call(functools.partial(attend_kernel, serving), out_shape=(jax....  2.06 us
  transfers between devices with their start and end apart: 6, of which 2 were waited for; matrix products, arithmetic and copies ran while one was open for 0% of the time, Pallas kernels for 0%

profile of v1, /device:TPU:0, one launch (start us, length us, event | category | flops | bytes accessed | tf_op | source)
XLA Modules:
  0.0 59.9 jit_solution(13587645243024669308)
XLA Ops:
  1.3 0.0 copy-start
  1.3 0.9 %copy-done = bf16[1,4,128,128]{3,2,1,0:T(8,128)(2,1)S(1)} copy-done((bf16[1,4,128,128]{3,2,1,0:T(8,128)(2,1)S(1)}, bf16[1,4,128,128]{3,2,1,0:T(8,128)(2,1)}, u32[]{:S(2)}) %copy-start) | copy-done | bytes 131096
  2.2 0.0 copy-start.1
  2.2 0.9 %copy-done.1 = bf16[1,4,128,128]{3,2,1,0:T(8,128)(2,1)S(1)} copy-done((bf16[1,4,128,128]{3,2,1,0:T(8,128)(2,1)S(1)}, bf16[1,4,128,128]{3,2,1,0:T(8,128)(2,1)}, u32[]{:S(2)}) %copy-start.1) | copy-done | bytes 131096
  3.1 0.0 copy-start.2
  3.1 0.7 %copy-done.2 = bf16[2,1,2048]{2,0,1:T(2,128)(2,1)S(1)} copy-done((bf16[2,1,2048]{2,0,1:T(2,128)(2,1)S(1)}, bf16[2,1,2048]{2,0,1:T(2,128)(2,1)}, u32[]{:S(2)}) %copy-start.2) | copy-done | bytes 8216
  3.8 0.0 copy-start.3
  3.8 0.7 %copy-done.3 = bf16[2,1,2048]{2,0,1:T(2,128)(2,1)S(1)} copy-done((bf16[2,1,2048]{2,0,1:T(2,128)(2,1)S(1)}, bf16[2,1,2048]{2,0,1:T(2,128)(2,1)}, u32[]{:S(2)}) %copy-start.3) | copy-done | bytes 8216
  4.5 0.0 copy-start.4
  4.5 0.7 %copy-done.4 = f32[2048]{0:T(1024)S(1)} copy-done((f32[2048]{0:T(1024)S(1)}, f32[2048]{0:T(1024)}, u32[]{:S(2)}) %copy-start.4) | copy-done | bytes 8216
  5.2 0.0 copy-start.5
  5.2 0.7 %copy-done.5 = bf16[2,1,2,512]{3,2,1,0:T(2,128)(2,1)S(1)} copy-done((bf16[2,1,2,512]{3,2,1,0:T(2,128)(2,1)S(1)}, bf16[2,1,2,512]{3,2,1,0:T(2,128)(2,1)}, u32[]{:S(2)}) %copy-start.5) | copy-done | bytes 4120
  5.9 2.1 %shard_map.104 = (bf16[2,2048]{1,0:T(2,128)(2,1)}, bf16[2,2176]{1,0:T(2,128)(2,1)S(1)}) custom-call(s32[1]{0:T(128)S(6)} %copy.11.lengths, bf16[2,2048]{1,0:T(2,128)(2,1)S(1)} %bitcast.15, bf16[2,2,512]{2,1,0:T(2,128)(2,1)S(1)} %bitcast.18, bf16[4,128,128]{2,1,0:T(8,128)(2,1)S(1)} %bitcast.12, bf16[4,128,128]{2,1,0:T(8,128)(2,1)S(1)} %bitcast.13, ...), custom_call_target="tpu_custom_call" | custom-call | tf_op jit(solution)/shard_map/pallas_call | solution.py:136
  7.9 22.0 %all-gather.1.gathered = bf16[16,2,2176]{2,1,0:T(2,128)(2,1)S(1)} all-gather(bf16[1,2,2176]{2,1,0:T(2,128)(2,1)S(1)} %bitcast.14), channel_id=2, replica_groups=mesh['parts'=2,'wide'=8,'narrow'=2] {'wide','narrow'}, dimensions={0}, use_global_device_ids=true | all-gather | bytes 147968 | tf_op jit(solution)/shard_map/all_gather | solution.py:154
  29.9 0.1 shard_map.105
  30.0 1.3 %collective-permute-start = (bf16[2,3584]{1,0:T(2,128)(2,1)S(1)}, bf16[2,3584]{1,0:T(2,128)(2,1)S(1)}, u32[]{:S(2)}, u32[]{:S(2)}) collective-permute-start(bf16[2,3584]{1,0:T(2,128)(2,1)S(1)} %get-tuple-element.12), channel_id=1, source_target_pairs={{12,10},{14,0},{13,11},{15,1},{28,26},{30,16},{29,27},{31,17}} | collective-permute-start | bytes 43016 | tf_op jit(solution)/shard_map/ppermute | solution.py:173
  31.3 0.7 %collective-permute-start.1 = (bf16[2,3584]{1,0:T(2,128)(2,1)S(1)}, bf16[2,3584]{1,0:T(2,128)(2,1)S(1)}, u32[]{:S(2)}, u32[]{:S(2)}) collective-permute-start(bf16[2,3584]{1,0:T(2,128)(2,1)S(1)} %get-tuple-element.13), channel_id=1, source_target_pairs={{12,8},{14,10},{13,9},{15,11},{28,24},{30,26},{29,25},{31,27}} | collective-permute-start | bytes 43016 | tf_op jit(solution)/shard_map/ppermute | solution.py:173
  31.9 0.7 %collective-permute-start.2 = (bf16[2,3584]{1,0:T(2,128)(2,1)S(1)}, bf16[2,3584]{1,0:T(2,128)(2,1)S(1)}, u32[]{:S(2)}, u32[]{:S(2)}) collective-permute-start(bf16[2,3584]{1,0:T(2,128)(2,1)S(1)} %get-tuple-element.14), channel_id=1, source_target_pairs={{12,6},{14,8},{13,7},{15,9},{28,22},{30,24},{29,23},{31,25}} | collective-permute-start | bytes 43016 | tf_op jit(solution)/shard_map/ppermute | solution.py:173
  32.6 0.7 %collective-permute-start.3 = (bf16[2,3584]{1,0:T(2,128)(2,1)S(1)}, bf16[2,3584]{1,0:T(2,128)(2,1)S(1)}, u32[]{:S(2)}, u32[]{:S(2)}) collective-permute-start(bf16[2,3584]{1,0:T(2,128)(2,1)S(1)} %get-tuple-element.15), channel_id=1, source_target_pairs={{12,4},{14,6},{13,5},{15,7},{28,20},{30,22},{29,21},{31,23}} | collective-permute-start | bytes 43016 | tf_op jit(solution)/shard_map/ppermute | solution.py:173
  33.3 0.7 %collective-permute-start.4 = (bf16[2,3584]{1,0:T(2,128)(2,1)S(1)}, bf16[2,3584]{1,0:T(2,128)(2,1)S(1)}, u32[]{:S(2)}, u32[]{:S(2)}) collective-permute-start(bf16[2,3584]{1,0:T(2,128)(2,1)S(1)} %get-tuple-element.16), channel_id=1, source_target_pairs={{12,2},{14,4},{13,3},{15,5},{28,18},{30,20},{29,19},{31,21}} | collective-permute-start | bytes 43016 | tf_op jit(solution)/shard_map/ppermute | solution.py:173
  34.0 17.8 %collective-permute-done = bf16[2,3584]{1,0:T(2,128)(2,1)S(1)} collective-permute-done((bf16[2,3584]{1,0:T(2,128)(2,1)S(1)}, bf16[2,3584]{1,0:T(2,128)(2,1)S(1)}, u32[]{:S(2)}, u32[]{:S(2)}) %collective-permute-start) | collective-permute-done | bytes 14368 | tf_op jit(solution)/shard_map/ppermute | solution.py:173
  51.8 1.3 %collective-permute-start.5 = (bf16[2,3584]{1,0:T(2,128)(2,1)S(1)}, bf16[2,3584]{1,0:T(2,128)(2,1)S(1)}, u32[]{:S(2)}, u32[]{:S(2)}) collective-permute-start(bf16[2,3584]{1,0:T(2,128)(2,1)S(1)} %get-tuple-element.17), channel_id=1, source_target_pairs={{12,0},{14,2},{13,1},{15,3},{28,16},{30,18},{29,17},{31,19}} | collective-permute-start | bytes 43016 | tf_op jit(solution)/shard_map/ppermute | solution.py:173
  53.1 0.0 collective-permute-done.1
  53.1 0.0 collective-permute-done.2
  53.1 0.0 collective-permute-done.3
  53.1 0.0 collective-permute-done.4
  53.1 6.0 %collective-permute-done.5 = bf16[2,3584]{1,0:T(2,128)(2,1)S(1)} collective-permute-done((bf16[2,3584]{1,0:T(2,128)(2,1)S(1)}, bf16[2,3584]{1,0:T(2,128)(2,1)S(1)}, u32[]{:S(2)}, u32[]{:S(2)}) %collective-permute-start.5) | collective-permute-done | bytes 14368 | tf_op jit(solution)/shard_map/ppermute | solution.py:173
  59.2 0.1 broadcast_select_fusion.11
  59.2 0.6 %maximum_bitcast_fusion = bf16[2,1,7168]{2,0,1:T(2,128)(2,1)} fusion(bf16[2,3584]{1,0:T(2,128)(2,1)S(1)} %get-tuple-element.19, bf16[2,3584]{1,0:T(2,128)(2,1)S(1)} %get-tuple-element.18), kind=kLoop, calls=%fused_computation | loop fusion | flops 57344 | bytes 57344 | tf_op jit(solution)/shard_map/reshape | solution.py:185
Async XLA Ops:
  1.3 0.9 %copy-start = (bf16[1,4,128,128]{3,2,1,0:T(8,128)(2,1)S(1)}, bf16[1,4,128,128]{3,2,1,0:T(8,128)(2,1)}, u32[]{:S(2)}) copy-start(bf16[1,4,128,128]{3,2,1,0:T(8,128)(2,1)} %param.11) | copy-start | bytes 393220
  2.2 0.9 %copy-start.1 = (bf16[1,4,128,128]{3,2,1,0:T(8,128)(2,1)S(1)}, bf16[1,4,128,128]{3,2,1,0:T(8,128)(2,1)}, u32[]{:S(2)}) copy-start(bf16[1,4,128,128]{3,2,1,0:T(8,128)(2,1)} %param.12) | copy-start | bytes 393220
  3.1 0.7 %copy-start.2 = (bf16[2,1,2048]{2,0,1:T(2,128)(2,1)S(1)}, bf16[2,1,2048]{2,0,1:T(2,128)(2,1)}, u32[]{:S(2)}) copy-start(bf16[2,1,2048]{2,0,1:T(2,128)(2,1)} %param.9) | copy-start | bytes 24580
  3.8 0.7 %copy-start.3 = (bf16[2,1,2048]{2,0,1:T(2,128)(2,1)S(1)}, bf16[2,1,2048]{2,0,1:T(2,128)(2,1)}, u32[]{:S(2)}) copy-start(bf16[2,1,2048]{2,0,1:T(2,128)(2,1)} %param.14) | copy-start | bytes 24580
  4.5 0.7 %copy-start.4 = (f32[2048]{0:T(1024)S(1)}, f32[2048]{0:T(1024)}, u32[]{:S(2)}) copy-start(f32[2048]{0:T(1024)} %param.15) | copy-start | bytes 24580
  5.2 0.7 %copy-start.5 = (bf16[2,1,2,512]{3,2,1,0:T(2,128)(2,1)S(1)}, bf16[2,1,2,512]{3,2,1,0:T(2,128)(2,1)}, u32[]{:S(2)}) copy-start(bf16[2,1,2,512]{3,2,1,0:T(2,128)(2,1)} %param.10) | copy-start | bytes 12292
  30.0 21.8 %collective-permute-start = (bf16[2,3584]{1,0:T(2,128)(2,1)S(1)}, bf16[2,3584]{1,0:T(2,128)(2,1)S(1)}, u32[]{:S(2)}, u32[]{:S(2)}) collective-permute-start(bf16[2,3584]{1,0:T(2,128)(2,1)S(1)} %get-tuple-element.12), channel_id=1, source_target_pairs={{12,10},{14,0},{13,11},{15,1},{28,26},{30,16},{29,27},{31,17}} | collective-permute-start | bytes 43016 | tf_op jit(solution)/shard_map/ppermute | solution.py:173
  31.3 21.8 %collective-permute-start.1 = (bf16[2,3584]{1,0:T(2,128)(2,1)S(1)}, bf16[2,3584]{1,0:T(2,128)(2,1)S(1)}, u32[]{:S(2)}, u32[]{:S(2)}) collective-permute-start(bf16[2,3584]{1,0:T(2,128)(2,1)S(1)} %get-tuple-element.13), channel_id=1, source_target_pairs={{12,8},{14,10},{13,9},{15,11},{28,24},{30,26},{29,25},{31,27}} | collective-permute-start | bytes 43016 | tf_op jit(solution)/shard_map/ppermute | solution.py:173
  31.9 21.2 %collective-permute-start.2 = (bf16[2,3584]{1,0:T(2,128)(2,1)S(1)}, bf16[2,3584]{1,0:T(2,128)(2,1)S(1)}, u32[]{:S(2)}, u32[]{:S(2)}) collective-permute-start(bf16[2,3584]{1,0:T(2,128)(2,1)S(1)} %get-tuple-element.14), channel_id=1, source_target_pairs={{12,6},{14,8},{13,7},{15,9},{28,22},{30,24},{29,23},{31,25}} | collective-permute-start | bytes 43016 | tf_op jit(solution)/shard_map/ppermute | solution.py:173
  32.6 20.5 %collective-permute-start.3 = (bf16[2,3584]{1,0:T(2,128)(2,1)S(1)}, bf16[2,3584]{1,0:T(2,128)(2,1)S(1)}, u32[]{:S(2)}, u32[]{:S(2)}) collective-permute-start(bf16[2,3584]{1,0:T(2,128)(2,1)S(1)} %get-tuple-element.15), channel_id=1, source_target_pairs={{12,4},{14,6},{13,5},{15,7},{28,20},{30,22},{29,21},{31,23}} | collective-permute-start | bytes 43016 | tf_op jit(solution)/shard_map/ppermute | solution.py:173
  33.3 19.8 %collective-permute-start.4 = (bf16[2,3584]{1,0:T(2,128)(2,1)S(1)}, bf16[2,3584]{1,0:T(2,128)(2,1)S(1)}, u32[]{:S(2)}, u32[]{:S(2)}) collective-permute-start(bf16[2,3584]{1,0:T(2,128)(2,1)S(1)} %get-tuple-element.16), channel_id=1, source_target_pairs={{12,2},{14,4},{13,3},{15,5},{28,18},{30,20},{29,19},{31,21}} | collective-permute-start | bytes 43016 | tf_op jit(solution)/shard_map/ppermute | solution.py:173
  51.8 7.4 %collective-permute-start.5 = (bf16[2,3584]{1,0:T(2,128)(2,1)S(1)}, bf16[2,3584]{1,0:T(2,128)(2,1)S(1)}, u32[]{:S(2)}, u32[]{:S(2)}) collective-permute-start(bf16[2,3584]{1,0:T(2,128)(2,1)S(1)} %get-tuple-element.17), channel_id=1, source_target_pairs={{12,0},{14,2},{13,1},{15,3},{28,16},{30,18},{29,17},{31,19}} | collective-permute-start | bytes 43016 | tf_op jit(solution)/shard_map/ppermute | solution.py:173

commit v2 on v1

v2 whole, which is shorter than its diff:
```python
import functools

import jax
import jax.numpy as jnp
from jax import lax
from jax.experimental import pallas as pl
from jax.experimental.pallas import tpu as pltpu
from jax.sharding import PartitionSpec as P

D = 4096
HEAD_SIZE = 128
STEPS = 2
TAIL = 128
EPS = 1e-05
FETCH = (2, 2, 1, 2)


def pair(squares):
    high = squares.astype(jnp.bfloat16).astype(jnp.float32)
    lane = lax.broadcasted_iota(jnp.int32, (squares.shape[0], TAIL), 1)
    both = jnp.where(lane == 0, high, jnp.where(lane == 1, squares - high, 0.0))
    return both.astype(jnp.bfloat16)


def fetches(share, spans, gate, up, held, sems):
    tile = held.shape[3]
    base = lax.axis_index("parts") * (gate.shape[1] // share) if share > 1 else 0
    copies = []
    for c, j in enumerate(spans):
        here = pl.ds(pl.multiple_of(base + j * tile, 128) if share > 1 else j * tile, tile)
        for m, matrix in enumerate((gate, up)):
            copies.append(pltpu.make_async_copy(matrix.at[:, here], held.at[c, m], sems.at[c, m]))
    return copies


def fetch_kernel(serving, share, spans, _, gate, up, held, sems):
    @pl.when(lax.axis_index("wide") >= serving)
    def _():
        copies = fetches(share, spans, gate, up, held, sems)
        for c in copies:
            c.start()
        for c in copies:
            c.wait()


def attend_kernel(serving, share, spans, lengths, *refs):
    sources, gate, up, attended, sent, weights_held = refs[:6], *refs[6:11]
    held, sems, weight_sems = refs[11:17], refs[17], refs[18]
    q, kv, keys, values, residual, gain = held
    owner = lax.axis_index("wide") < serving
    heads, hist, _ = keys.shape
    width = q.shape[1]
    group = width // (heads * HEAD_SIZE)

    @pl.when(jnp.logical_not(owner))
    def _():
        copies = fetches(share, spans, gate, up, weights_held, weight_sems)
        for c in copies:
            c.start()
        attended[...] = jnp.zeros_like(attended)
        sent[...] = jnp.zeros_like(sent)
        for c in copies:
            c.wait()

    @pl.when(owner)
    def _():
        copies = [
            pltpu.make_async_copy(source, place, sems.at[i])
            for i, (source, place) in enumerate(zip(sources, held))
        ]
        for c in copies:
            c.start()
        for c in copies:
            c.wait()
        length = lengths[0]
        slot = lax.broadcasted_iota(jnp.int32, (hist, HEAD_SIZE), 0)
        rows = group * STEPS
        place = lax.broadcasted_iota(jnp.int32, (rows, hist), 1)
        step = lax.broadcasted_iota(jnp.int32, (rows, hist), 0) % STEPS
        first = hist - STEPS
        seen = (place < length) | ((place >= first) & (place - first <= step))
        squares = jnp.zeros((STEPS, 1), jnp.float32)
        for h in range(heads):
            lanes = slice(h * HEAD_SIZE, (h + 1) * HEAD_SIZE)
            k, v = keys[h], values[h]
            for t in range(STEPS):
                k = jnp.where(slot == first + t, kv[t, 0:1, lanes], k)
                v = jnp.where(slot == first + t, kv[t, 1:2, lanes], v)
            cols = [(h * group + g) * HEAD_SIZE for g in range(group)]
            query = jnp.concatenate(
                [q[:, c : c + HEAD_SIZE].astype(jnp.float32) for c in cols], 0
            ).astype(jnp.bfloat16)
            scores = lax.dot_general(
                query, k, (((1,), (1,)), ((), ())), preferred_element_type=jnp.float32
            ) * (1.0 / HEAD_SIZE**0.5)
            scores = jnp.where(seen, scores, -1e30)
            top = jnp.max(scores, -1, keepdims=True)
            e = jnp.where(seen, jnp.exp(scores - top), 0.0)
            weights = (e / jnp.sum(e, -1, keepdims=True)).astype(jnp.bfloat16)
            out = jnp.dot(weights, v, preferred_element_type=jnp.float32)
            for g, c in enumerate(cols):
                here = slice(c, c + HEAD_SIZE)
                got = out[g * STEPS : (g + 1) * STEPS].astype(jnp.bfloat16)
                attended[:, here] = got
                mixed = residual[:, here].astype(jnp.float32) + got.astype(jnp.float32)
                squares += jnp.sum(mixed * mixed, -1, keepdims=True)
                sent[:, here] = (mixed * gain[:, here]).astype(jnp.bfloat16)
        sent[:, width:] = pair(squares)


def collect_kernel(blocks, workers, narrow, share, spans, *refs):
    arrived, (gate, up, _, rows, held, sems) = refs[:blocks], refs[blocks:]
    me = lax.axis_index("wide") - blocks * workers
    features = gate.shape[0]
    half = features // narrow

    @pl.when(me >= 0)
    def _():
        copies = fetches(share, spans, gate, up, held, sems)
        for c in copies:
            c.start()
        lines, tails = [], []
        for block in arrived:
            for shift in range(workers):
                owner = lax.rem(me + shift, workers)
                parts = [block[owner * narrow + n] for n in range(narrow)]
                lines.append(jnp.concatenate([p[:, :half] for p in parts], 1).astype(jnp.float32))
                tails.append(sum(p[:, half:].astype(jnp.float32) for p in parts))
        pad = rows.shape[0] - STEPS * blocks * workers
        if pad:
            lines.append(jnp.zeros((pad, features), jnp.float32))
            tails.append(jnp.zeros((pad, TAIL), jnp.float32))
        rows[:, :features] = jnp.concatenate(lines, 0).astype(jnp.bfloat16)
        rows[:, features:] = pair(jnp.sum(jnp.concatenate(tails, 0), -1, keepdims=True))
        for c in copies:
            c.wait()


def forward_kernel(serving, counts, *refs):
    held = refs[: len(counts)]
    rest = refs[len(counts) :]
    batches = len(rest) // 2
    rows, outs = rest[:batches], rest[batches:]
    features, tile = held[0].shape[2:]

    @pl.when(lax.axis_index("wide") >= serving)
    def _():
        x = jnp.concatenate([r[:, :features] for r in rows], 0)
        tails = jnp.concatenate([r[:, features:].astype(jnp.float32) for r in rows], 0)
        r = lax.rsqrt(jnp.sum(tails, -1, keepdims=True) / D + EPS)
        j = 0
        for piece, count in zip(held, counts):
            for c in range(count):
                g = jnp.dot(x, piece[c, 0], preferred_element_type=jnp.float32) * r
                u = jnp.dot(x, piece[c, 1], preferred_element_type=jnp.float32) * r
                hidden = g / (1.0 + jnp.exp(-g)) * u
                for b, out in enumerate(outs):
                    first = b * rows[0].shape[0]
                    for i in range(serving):
                        here = slice(first + i * STEPS, first + (i + 1) * STEPS)
                        out[i, :, j * tile : (j + 1) * tile] = hidden[here].astype(jnp.bfloat16)
                j += 1


def split_kernel(serving, *refs):
    batches, outs = refs[:-serving], refs[-serving:]
    local = batches[0].shape[2]

    @pl.when(lax.axis_index("wide") >= serving)
    def _():
        for p in range(len(batches)):

            @pl.when(lax.axis_index("parts") == p if len(batches) > 1 else True)
            def _():
                for d, batch in enumerate(batches):
                    q = (p + d) % len(batches)
                    for i, out in enumerate(outs):
                        out[:, q * local : (q + 1) * local] = batch[i]


def divide(count, shares):
    total, edges, run = sum(shares), [0], 0
    for s in shares:
        run += s
        edges.append(round(count * run / total))
    return [list(range(a, b)) for a, b in zip(edges, edges[1:])]


def swap(x, pairs):
    return lax.ppermute(x, "wide", pairs + [(b, a) for a, b in pairs])


def shards(queries, new_kv, keys, values, lengths, residual, gain, gate, up):
    wide = lax.axis_size("wide")
    narrow = lax.axis_size("narrow")
    parts = lax.axis_size("parts")
    serving = wide * 3 // 4
    workers = wide - serving
    blocks = serving // workers
    half = queries.shape[2]
    features, _, columns = gate.shape
    share = parts if columns % (parts * 128) == 0 else 1
    local = columns // share
    tile = next((t for t in (256, 128) if local % t == 0), local)
    spans = divide(local // tile, FETCH)
    vmem = pl.BlockSpec(memory_space=pltpu.VMEM)
    hbm = pl.BlockSpec(memory_space=pltpu.HBM)

    def in_hbm(a):
        return pltpu.with_memory_space_constraint(a, pltpu.HBM)

    def held(span):
        return pltpu.VMEM((max(len(span), 1), 2, features, tile), jnp.bfloat16)

    def fetch_sems(span):
        return pltpu.SemaphoreType.DMA((max(len(span), 1), 2))

    def fetch_time(span):
        moved = len(span) * 4 * features * tile
        return pl.CostEstimate(flops=0, bytes_accessed=moved, transcendentals=0)

    gate = in_hbm(gate.reshape(features, columns))
    up = in_hbm(up.reshape(features, columns))
    operands = (
        queries.reshape(STEPS, half),
        new_kv.reshape(STEPS, 2, -1),
        keys.reshape(keys.shape[1:]),
        values.reshape(values.shape[1:]),
        residual.reshape(STEPS, half),
        gain.reshape(1, half),
    )
    attended, sent, first = pl.pallas_call(
        functools.partial(attend_kernel, serving, share, spans[0]),
        out_shape=(
            jax.ShapeDtypeStruct((STEPS, half), jnp.bfloat16),
            jax.ShapeDtypeStruct((STEPS, half + TAIL), jnp.bfloat16),
            held(spans[0]),
        ),
        in_specs=[pl.BlockSpec(memory_space=pltpu.SMEM)] + [hbm] * 8,
        out_specs=(vmem, vmem, vmem),
        scratch_shapes=[pltpu.VMEM(o.shape, o.dtype) for o in operands]
        + [pltpu.SemaphoreType.DMA((6,)), fetch_sems(spans[0])],
        compiler_params=pltpu.CompilerParams(vmem_limit_bytes=16 << 20),
        cost_estimate=fetch_time(spans[0]),
    )(lengths, *map(in_hbm, operands), gate, up)
    weights = [first]

    def fetch(span, after):
        weights.append(
            pl.pallas_call(
                functools.partial(fetch_kernel, serving, share, span),
                out_shape=held(span),
                in_specs=[pl.BlockSpec(memory_space=pl.ANY), hbm, hbm],
                out_specs=vmem,
                scratch_shapes=[fetch_sems(span)],
                compiler_params=pltpu.CompilerParams(vmem_limit_bytes=16 << 20),
                cost_estimate=fetch_time(span),
            )(after, gate, up)
        )

    order = range(blocks)[::-1]
    groups = [
        [w * narrow + n for w in range(at, at + workers) for n in range(narrow)]
        for at in range(0, wide, workers)
    ]
    block = lax.all_gather(sent, ("wide", "narrow"), axis=0, axis_index_groups=groups)
    arrived = [
        lax.ppermute(block, "wide", [(b * workers + j, serving + j) for j in range(workers)])
        for b in order
    ]
    fetch(spans[1], block)
    padded = -(-STEPS * serving // 16) * 16
    rows, third = pl.pallas_call(
        functools.partial(collect_kernel, blocks, workers, narrow, share, spans[2]),
        out_shape=(jax.ShapeDtypeStruct((padded, features + TAIL), jnp.bfloat16), held(spans[2])),
        in_specs=[vmem] * blocks + [hbm, hbm, pl.BlockSpec(memory_space=pl.ANY)],
        out_specs=(vmem, vmem),
        scratch_shapes=[fetch_sems(spans[2])],
        compiler_params=pltpu.CompilerParams(vmem_limit_bytes=16 << 20),
        cost_estimate=fetch_time(spans[2]),
    )(*arrived, gate, up, weights[-1])
    weights.append(third)
    batch = [rows]
    for d in range(1, share):
        batch.append(lax.ppermute(rows, "parts", [((p + d) % parts, p) for p in range(parts)]))
    fetch(spans[3], rows)
    hidden = pl.pallas_call(
        functools.partial(forward_kernel, serving, [len(span) for span in spans]),
        out_shape=[jax.ShapeDtypeStruct((serving, STEPS, local), jnp.bfloat16)] * share,
        in_specs=[vmem] * (len(weights) + share),
        out_specs=[vmem] * share,
        compiler_params=pltpu.CompilerParams(vmem_limit_bytes=16 << 20),
    )(*weights, *batch)
    finished = [hidden[0]]
    for d in range(1, share):
        finished.append(
            lax.ppermute(hidden[share - d], "parts", [((p + d) % parts, p) for p in range(parts)])
        )
    messages = pl.pallas_call(
        functools.partial(split_kernel, serving),
        out_shape=[jax.ShapeDtypeStruct((STEPS, columns), jnp.bfloat16)] * serving,
        in_specs=[vmem] * share,
        out_specs=[vmem] * serving,
        compiler_params=pltpu.CompilerParams(vmem_limit_bytes=16 << 20),
    )(*finished)
    back = [
        [
            swap(
                messages[i * workers + s],
                [(serving + k, b * workers + (k + s) % workers) for k in range(workers)],
            )
            for s in range(workers)
        ]
        for i, b in enumerate(order)
    ]
    me = lax.axis_index("wide")
    pieces = []
    for k in range(workers):
        piece = jnp.zeros((), jnp.bfloat16)
        for i, b in enumerate(order):
            for s in range(workers):
                mine = me == b * workers + (k + s) % workers
                piece = jnp.where(mine, back[i][s], piece)
        pieces.append(piece)
    activated = jnp.concatenate(pieces, 1)
    return attended.reshape(STEPS, 1, half), activated.reshape(STEPS, 1, -1)


def solution(mesh):
    rows = P(None, ("parts", "wide"), "narrow")
    placed = (
        rows,
        P(None, ("parts", "wide"), None, "narrow"),
        P(("parts", "wide"), "narrow", None, None),
        P(("parts", "wide"), "narrow", None, None),
        P(("parts", "wide")),
        rows,
        P("narrow"),
        P(None, "narrow", "wide"),
        P(None, "narrow", "wide"),
    )
    return jax.shard_map(
        shards, mesh=mesh, in_specs=placed, out_specs=(rows, rows), check_vma=False
    )
```

time: 60.3 us -> 64 us (1.061)
  the two profiles are of different devices: /device:TPU:0 before, /device:TPU:16 now
where the time goes in v2:
time: 64 us; the launch traced here: 63.7 us
  starting transfers between devices  42.9 us (67%)
  waiting for transfers between devices  10.2 us (16%)
  blocking collectives  5.2 us (8%)
  Pallas kernels  3.29 us (5%)
  between operations  1.44 us (2%)
  other arithmetic  0.7 us (1%)
    ppermute x6, starting transfers between devices, swap(): return lax.ppermute(x, 'wide', pairs + [(b, a) for a, b in pairs])  34 us
    ppermute x3, starting transfers between devices, shards(): lax.ppermute(block, 'wide', [(b * workers + j, serving + j) for j in rang...  5.85 us
    all_gather x1, blocking collectives, shards(): lax.all_gather(sent, ('wide', 'narrow'), axis=0, axis_index_groups=groups)  5.2 us
    ppermute x1, waiting for transfers between devices, shards(): lax.ppermute(rows, 'parts', [((p + d) % parts, p) for p in range(parts)])  3.82 us
    ppermute x6, waiting for transfers between devices, swap(): return lax.ppermute(x, 'wide', pairs + [(b, a) for a, b in pairs])  3.64 us
    pallas_call x1, Pallas kernels, shards(): pl.pallas_call(functools.partial(attend_kernel, serving, share, spans[0])...  3.17 us
    ppermute x1, waiting for transfers between devices, shards(): lax.ppermute(hidden[share - d], 'parts', [((p + d) % parts, p) for p in r...  2.5 us
    ppermute x1, starting transfers between devices, shards(): lax.ppermute(rows, 'parts', [((p + d) % parts, p) for p in range(parts)])  1.58 us
  transfers between devices with their start and end apart: 11, of which 4 were waited for; matrix products, arithmetic and copies ran while one was open for 0% of the time, Pallas kernels for 0%

profile of v2, /device:TPU:16, one launch (start us, length us, event | category | flops | bytes accessed | tf_op | source)
XLA Modules:
  0.0 63.7 jit_solution(10952211855343931376)
XLA Ops:
  1.3 3.2 %shard_map.104 = (bf16[2,2048]{1,0:T(2,128)(2,1)}, bf16[2,2176]{1,0:T(2,128)(2,1)S(1)}, bf16[2,2,4096,256]{3,2,1,0:T(8,128)(2,1)S(1)}) custom-call(s32[1]{0:T(128)S(6)} %copy.11.lengths, bf16[2,2048]{1,0:T(2,128)(2,1)} %bitcast.23, bf16[2,2,512]{2,1,0:T(2,128)(2,1)} %bitcast.26, bf16[4,128,128]{2,1,0:T(8,128)(2,1)} %bitcast.21, ...), custom_call_target="tpu_custom_call" | custom-call | bytes 8388608 | tf_op jit(solution)/shard_map/pallas_call | solution.py:232
  4.5 5.2 %all-gather.1._ = bf16[4,2,2176]{2,1,0:T(2,128)(2,1)S(1)} all-gather(bf16[1,2,2176]{2,1,0:T(2,128)(2,1)S(1)} %bitcast.12), channel_id=2, replica_groups={{0,1,2,3},{4,5,6,7},{8,9,10,11},{12,13,14,15},{16,17,18,19},{20,21,22,2..., dimensions={0}, use_global_device_ids=true | all-gather | bytes 43520 | tf_op jit(solution)/shard_map/all_gather | solution.py:266
  9.7 4.5 %collective-permute-start = (bf16[4,2,2176]{2,1,0:T(2,128)(2,1)S(1)}, bf16[4,2,2176]{2,1,0:T(2,128)(2,1)S(1)}, u32[]{:S(2)}, u32[]{:S(2)}) collective-permute-start(bf16[4,2,2176]{2,1,0:T(2,128)(2,1)S(1)} %all-gather.1._), channel_id=1, source_target_pairs={{8,12},{10,14},{9,13},{11,15},{24,28},{26,30},{25,29},{27,31}} | collective-permute-start | bytes 104456 | tf_op jit(solution)/shard_map/ppermute | solution.py:268
  14.2 0.7 %collective-permute-start.1 = (bf16[4,2,2176]{2,1,0:T(2,128)(2,1)S(1)}, bf16[4,2,2176]{2,1,0:T(2,128)(2,1)S(1)}, u32[]{:S(2)}, u32[]{:S(2)}) collective-permute-start(bf16[4,2,2176]{2,1,0:T(2,128)(2,1)S(1)} %all-gather.1._), channel_id=1, source_target_pairs={{4,12},{6,14},{5,13},{7,15},{20,28},{22,30},{21,29},{23,31}} | collective-permute-start | bytes 104456 | tf_op jit(solution)/shard_map/ppermute | solution.py:268
  14.9 0.7 %collective-permute-start.2 = (bf16[4,2,2176]{2,1,0:T(2,128)(2,1)S(1)}, bf16[4,2,2176]{2,1,0:T(2,128)(2,1)S(1)}, u32[]{:S(2)}, u32[]{:S(2)}) collective-permute-start(bf16[4,2,2176]{2,1,0:T(2,128)(2,1)S(1)} %all-gather.1._), channel_id=1, source_target_pairs={{0,12},{2,14},{1,13},{3,15},{16,28},{18,30},{17,29},{19,31}} | collective-permute-start | bytes 104456 | tf_op jit(solution)/shard_map/ppermute | solution.py:268
  15.5 0.1 shard_map.105.refs_5_.refs_1_
  15.6 0.2 collective-permute-done.refs_0_
  15.8 0.0 collective-permute-done.1.refs_1_
  15.8 0.0 collective-permute-done.2.refs_2_
  15.8 1.6 %collective-permute-start.3 = (bf16[16,4224]{1,0:T(8,128)(2,1)S(1)}, bf16[16,4224]{1,0:T(8,128)(2,1)S(1)}, u32[]{:S(2)}, u32[]{:S(2)}) collective-permute-start(bf16[16,4224]{1,0:T(8,128)(2,1)S(1)} %get-tuple-element.19._.refs_4_), channel_id=1, source_target_pairs={{16,0},{0,16},{17,1},{1,17},{18,2},{2,18},{19,3},{3,19},{20,4},{4,... | collective-permute-start | bytes 405512 | tf_op jit(solution)/shard_map/ppermute | solution.py:285
  17.4 3.8 %collective-permute-done.3.refs_5_ = bf16[16,4224]{1,0:T(8,128)(2,1)S(1)} collective-permute-done((bf16[16,4224]{1,0:T(8,128)(2,1)S(1)}, bf16[16,4224]{1,0:T(8,128)(2,1)S(1)}, u32[]{:S(2)}, u32[]{:S(2)}) %collective-permute-start.3) | collective-permute-done | bytes 135200 | tf_op jit(solution)/shard_map/ppermute | solution.py:285
  21.3 1.5 %collective-permute-start.4 = (bf16[6,2,1792]{2,1,0:T(2,128)(2,1)S(1)}, bf16[6,2,1792]{2,1,0:T(2,128)(2,1)S(1)}, u32[]{:S(2)}, u32[]{:S(2)}) collective-permute-start(bf16[6,2,1792]{2,1,0:T(2,128)(2,1)S(1)} %get-tuple-element.21), channel_id=1, source_target_pairs={{16,0},{0,16},{17,1},{1,17},{18,2},{2,18},{19,3},{3,19},{20,4},{4,... | collective-permute-start | bytes 129032 | tf_op jit(solution)/shard_map/ppermute | solution.py:297
  22.8 2.5 %collective-permute-done.4.refs_1_ = bf16[6,2,1792]{2,1,0:T(2,128)(2,1)S(1)} collective-permute-done((bf16[6,2,1792]{2,1,0:T(2,128)(2,1)S(1)}, bf16[6,2,1792]{2,1,0:T(2,128)(2,1)S(1)}, u32[]{:S(2)}, u32[]{:S(2)}) %collective-permute-start.4) | collective-permute-done | bytes 43040 | tf_op jit(solution)/shard_map/ppermute | solution.py:297
  25.3 0.7 %collective-permute-start.5 = (bf16[2,3584]{1,0:T(2,128)(2,1)S(1)}, bf16[2,3584]{1,0:T(2,128)(2,1)S(1)}, u32[]{:S(2)}, u32[]{:S(2)}) collective-permute-start(bf16[2,3584]{1,0:T(2,128)(2,1)S(1)} %get-tuple-element.22), channel_id=1, source_target_pairs={{12,2},{14,0},{2,12},{0,14},{13,3},{15,1},{3,13},{1,15},{28,18},{3... | collective-permute-start | bytes 43016 | tf_op jit(solution)/shard_map/ppermute | solution.py:190
  25.9 0.7 %collective-permute-start.6 = (bf16[2,3584]{1,0:T(2,128)(2,1)S(1)}, bf16[2,3584]{1,0:T(2,128)(2,1)S(1)}, u32[]{:S(2)}, u32[]{:S(2)}) collective-permute-start(bf16[2,3584]{1,0:T(2,128)(2,1)S(1)} %get-tuple-element.23), channel_id=1, source_target_pairs={{12,0},{14,2},{0,12},{2,14},{13,1},{15,3},{1,13},{3,15},{28,16},{3... | collective-permute-start | bytes 43016 | tf_op jit(solution)/shard_map/ppermute | solution.py:190
  26.6 0.7 %collective-permute-start.7 = (bf16[2,3584]{1,0:T(2,128)(2,1)S(1)}, bf16[2,3584]{1,0:T(2,128)(2,1)S(1)}, u32[]{:S(2)}, u32[]{:S(2)}) collective-permute-start(bf16[2,3584]{1,0:T(2,128)(2,1)S(1)} %get-tuple-element.24), channel_id=1, source_target_pairs={{12,6},{14,4},{6,12},{4,14},{13,7},{15,5},{7,13},{5,15},{28,22},{3... | collective-permute-start | bytes 43016 | tf_op jit(solution)/shard_map/ppermute | solution.py:190
  27.3 0.7 %collective-permute-start.8 = (bf16[2,3584]{1,0:T(2,128)(2,1)S(1)}, bf16[2,3584]{1,0:T(2,128)(2,1)S(1)}, u32[]{:S(2)}, u32[]{:S(2)}) collective-permute-start(bf16[2,3584]{1,0:T(2,128)(2,1)S(1)} %get-tuple-element.25), channel_id=1, source_target_pairs={{12,4},{14,6},{4,12},{6,14},{13,5},{15,7},{5,13},{7,15},{28,20},{3... | collective-permute-start | bytes 43016 | tf_op jit(solution)/shard_map/ppermute | solution.py:190
  28.0 29.4 %collective-permute-start.9 = (bf16[2,3584]{1,0:T(2,128)(2,1)S(1)}, bf16[2,3584]{1,0:T(2,128)(2,1)S(1)}, u32[]{:S(2)}, u32[]{:S(2)}) collective-permute-start(bf16[2,3584]{1,0:T(2,128)(2,1)S(1)} %get-tuple-element.26), channel_id=1, source_target_pairs={{12,10},{14,8},{10,12},{8,14},{13,11},{15,9},{11,13},{9,15},{28,26... | collective-permute-start | bytes 43016 | tf_op jit(solution)/shard_map/ppermute | solution.py:190
  57.4 0.0 collective-permute-done.5
  57.4 1.9 %collective-permute-start.10 = (bf16[2,3584]{1,0:T(2,128)(2,1)S(1)}, bf16[2,3584]{1,0:T(2,128)(2,1)S(1)}, u32[]{:S(2)}, u32[]{:S(2)}) collective-permute-start(bf16[2,3584]{1,0:T(2,128)(2,1)S(1)} %get-tuple-element.27), channel_id=1, source_target_pairs={{12,8},{14,10},{8,12},{10,14},{13,9},{15,11},{9,13},{11,15},{28,24... | collective-permute-start | bytes 43016 | tf_op jit(solution)/shard_map/ppermute | solution.py:190
  59.3 0.0 collective-permute-done.6
  59.3 0.0 collective-permute-done.7
  59.3 0.0 collective-permute-done.8
  59.3 0.0 collective-permute-done.9
  59.4 3.6 %collective-permute-done.10 = bf16[2,3584]{1,0:T(2,128)(2,1)S(1)} collective-permute-done((bf16[2,3584]{1,0:T(2,128)(2,1)S(1)}, bf16[2,3584]{1,0:T(2,128)(2,1)S(1)}, u32[]{:S(2)}, u32[]{:S(2)}) %collective-permute-start.10) | collective-permute-done | bytes 14368 | tf_op jit(solution)/shard_map/ppermute | solution.py:190
  63.0 0.1 broadcast_select_fusion.11
  63.0 0.6 %maximum_bitcast_fusion = bf16[2,1,7168]{2,0,1:T(2,128)(2,1)} fusion(bf16[2,3584]{1,0:T(2,128)(2,1)S(1)} %get-tuple-element.29, bf16[2,3584]{1,0:T(2,128)(2,1)S(1)} %get-tuple-element.28), kind=kLoop, calls=%fused_computation | loop fusion | flops 57344 | bytes 57344 | tf_op jit(solution)/shard_map/reshape | solution.py:326
  (4 shorter events, 0.1 us)
Async XLA Ops:
  9.7 6.1 %collective-permute-start = (bf16[4,2,2176]{2,1,0:T(2,128)(2,1)S(1)}, bf16[4,2,2176]{2,1,0:T(2,128)(2,1)S(1)}, u32[]{:S(2)}, u32[]{:S(2)}) collective-permute-start(bf16[4,2,2176]{2,1,0:T(2,128)(2,1)S(1)} %all-gather.1._), channel_id=1, source_target_pairs={{8,12},{10,14},{9,13},{11,15},{24,28},{26,30},{25,29},{27,31}} | collective-permute-start | bytes 104456 | tf_op jit(solution)/shard_map/ppermute | solution.py:268
  14.2 1.6 %collective-permute-start.1 = (bf16[4,2,2176]{2,1,0:T(2,128)(2,1)S(1)}, bf16[4,2,2176]{2,1,0:T(2,128)(2,1)S(1)}, u32[]{:S(2)}, u32[]{:S(2)}) collective-permute-start(bf16[4,2,2176]{2,1,0:T(2,128)(2,1)S(1)} %all-gather.1._), channel_id=1, source_target_pairs={{4,12},{6,14},{5,13},{7,15},{20,28},{22,30},{21,29},{23,31}} | collective-permute-start | bytes 104456 | tf_op jit(solution)/shard_map/ppermute | solution.py:268
  14.9 0.9 %collective-permute-start.2 = (bf16[4,2,2176]{2,1,0:T(2,128)(2,1)S(1)}, bf16[4,2,2176]{2,1,0:T(2,128)(2,1)S(1)}, u32[]{:S(2)}, u32[]{:S(2)}) collective-permute-start(bf16[4,2,2176]{2,1,0:T(2,128)(2,1)S(1)} %all-gather.1._), channel_id=1, source_target_pairs={{0,12},{2,14},{1,13},{3,15},{16,28},{18,30},{17,29},{19,31}} | collective-permute-start | bytes 104456 | tf_op jit(solution)/shard_map/ppermute | solution.py:268
  15.8 5.4 %collective-permute-start.3 = (bf16[16,4224]{1,0:T(8,128)(2,1)S(1)}, bf16[16,4224]{1,0:T(8,128)(2,1)S(1)}, u32[]{:S(2)}, u32[]{:S(2)}) collective-permute-start(bf16[16,4224]{1,0:T(8,128)(2,1)S(1)} %get-tuple-element.19._.refs_4_), channel_id=1, source_target_pairs={{16,0},{0,16},{17,1},{1,17},{18,2},{2,18},{19,3},{3,19},{20,4},{4,... | collective-permute-start | bytes 405512 | tf_op jit(solution)/shard_map/ppermute | solution.py:285
  21.3 4.0 %collective-permute-start.4 = (bf16[6,2,1792]{2,1,0:T(2,128)(2,1)S(1)}, bf16[6,2,1792]{2,1,0:T(2,128)(2,1)S(1)}, u32[]{:S(2)}, u32[]{:S(2)}) collective-permute-start(bf16[6,2,1792]{2,1,0:T(2,128)(2,1)S(1)} %get-tuple-element.21), channel_id=1, source_target_pairs={{16,0},{0,16},{17,1},{1,17},{18,2},{2,18},{19,3},{3,19},{20,4},{4,... | collective-permute-start | bytes 129032 | tf_op jit(solution)/shard_map/ppermute | solution.py:297
  25.3 32.1 %collective-permute-start.5 = (bf16[2,3584]{1,0:T(2,128)(2,1)S(1)}, bf16[2,3584]{1,0:T(2,128)(2,1)S(1)}, u32[]{:S(2)}, u32[]{:S(2)}) collective-permute-start(bf16[2,3584]{1,0:T(2,128)(2,1)S(1)} %get-tuple-element.22), channel_id=1, source_target_pairs={{12,2},{14,0},{2,12},{0,14},{13,3},{15,1},{3,13},{1,15},{28,18},{3... | collective-permute-start | bytes 43016 | tf_op jit(solution)/shard_map/ppermute | solution.py:190
  25.9 33.4 %collective-permute-start.6 = (bf16[2,3584]{1,0:T(2,128)(2,1)S(1)}, bf16[2,3584]{1,0:T(2,128)(2,1)S(1)}, u32[]{:S(2)}, u32[]{:S(2)}) collective-permute-start(bf16[2,3584]{1,0:T(2,128)(2,1)S(1)} %get-tuple-element.23), channel_id=1, source_target_pairs={{12,0},{14,2},{0,12},{2,14},{13,1},{15,3},{1,13},{3,15},{28,16},{3... | collective-permute-start | bytes 43016 | tf_op jit(solution)/shard_map/ppermute | solution.py:190
  26.6 32.7 %collective-permute-start.7 = (bf16[2,3584]{1,0:T(2,128)(2,1)S(1)}, bf16[2,3584]{1,0:T(2,128)(2,1)S(1)}, u32[]{:S(2)}, u32[]{:S(2)}) collective-permute-start(bf16[2,3584]{1,0:T(2,128)(2,1)S(1)} %get-tuple-element.24), channel_id=1, source_target_pairs={{12,6},{14,4},{6,12},{4,14},{13,7},{15,5},{7,13},{5,15},{28,22},{3... | collective-permute-start | bytes 43016 | tf_op jit(solution)/shard_map/ppermute | solution.py:190
  27.3 32.1 %collective-permute-start.8 = (bf16[2,3584]{1,0:T(2,128)(2,1)S(1)}, bf16[2,3584]{1,0:T(2,128)(2,1)S(1)}, u32[]{:S(2)}, u32[]{:S(2)}) collective-permute-start(bf16[2,3584]{1,0:T(2,128)(2,1)S(1)} %get-tuple-element.25), channel_id=1, source_target_pairs={{12,4},{14,6},{4,12},{6,14},{13,5},{15,7},{5,13},{7,15},{28,20},{3... | collective-permute-start | bytes 43016 | tf_op jit(solution)/shard_map/ppermute | solution.py:190
  28.0 31.4 %collective-permute-start.9 = (bf16[2,3584]{1,0:T(2,128)(2,1)S(1)}, bf16[2,3584]{1,0:T(2,128)(2,1)S(1)}, u32[]{:S(2)}, u32[]{:S(2)}) collective-permute-start(bf16[2,3584]{1,0:T(2,128)(2,1)S(1)} %get-tuple-element.26), channel_id=1, source_target_pairs={{12,10},{14,8},{10,12},{8,14},{13,11},{15,9},{11,13},{9,15},{28,26... | collective-permute-start | bytes 43016 | tf_op jit(solution)/shard_map/ppermute | solution.py:190
  57.4 5.6 %collective-permute-start.10 = (bf16[2,3584]{1,0:T(2,128)(2,1)S(1)}, bf16[2,3584]{1,0:T(2,128)(2,1)S(1)}, u32[]{:S(2)}, u32[]{:S(2)}) collective-permute-start(bf16[2,3584]{1,0:T(2,128)(2,1)S(1)} %get-tuple-element.27), channel_id=1, source_target_pairs={{12,8},{14,10},{8,12},{10,14},{13,9},{15,11},{9,13},{11,15},{28,24... | collective-permute-start | bytes 43016 | tf_op jit(solution)/shard_map/ppermute | solution.py:190

commit v3 on v1

v3 whole, which is shorter than its diff:
```python
import functools

import jax
import jax.numpy as jnp
from jax import lax
from jax.experimental import pallas as pl
from jax.experimental.pallas import tpu as pltpu
from jax.sharding import PartitionSpec as P

D = 4096
HEAD_SIZE = 128
STEPS = 2
TAIL = 128
EPS = 1e-05
DEPTH = 256
EARLY = 5
SLOTS = 6


def pair(squares):
    high = squares.astype(jnp.bfloat16).astype(jnp.float32)
    lane = lax.broadcasted_iota(jnp.int32, (squares.shape[0], TAIL), 1)
    both = jnp.where(lane == 0, high, jnp.where(lane == 1, squares - high, 0.0))
    return both.astype(jnp.bfloat16)


def fetches(share, c, slot, gate, up, held, sems):
    depth, local = held.shape[2:]
    here = pl.ds(c * depth, depth)
    copies = []
    for m, matrix in enumerate((gate, up)):
        source = matrix.at[here]
        if share > 1:
            base = pl.multiple_of(lax.axis_index("parts") * local, 128)
            source = matrix.at[here, pl.ds(base, local)]
        copies.append(pltpu.make_async_copy(source, held.at[slot, m], sems.at[slot, m]))
    return copies


def fetch_kernel(serving, share, _, gate, up, held, sems):
    @pl.when(lax.axis_index("wide") >= serving)
    def _():
        copies = [fetches(share, c, c, gate, up, held, sems) for c in range(held.shape[0])]
        for some in copies:
            for c in some:
                c.start()
        for some in copies:
            for c in some:
                c.wait()


def blank_kernel(out):
    out[...] = jnp.zeros_like(out)


def attend_kernel(serving, lengths, *refs):
    sources, (attended, sent), held, sems = refs[:6], refs[6:8], refs[8:14], refs[14]
    q, kv, keys, values, residual, gain = held
    owner = lax.axis_index("wide") < serving
    heads, hist, _ = keys.shape
    width = q.shape[1]
    group = width // (heads * HEAD_SIZE)

    @pl.when(jnp.logical_not(owner))
    def _():
        attended[...] = jnp.zeros_like(attended)
        sent[...] = jnp.zeros_like(sent)

    @pl.when(owner)
    def _():
        copies = [
            pltpu.make_async_copy(source, place, sems.at[i])
            for i, (source, place) in enumerate(zip(sources, held))
        ]
        for c in copies:
            c.start()
        for c in copies:
            c.wait()
        length = lengths[0]
        slot = lax.broadcasted_iota(jnp.int32, (hist, HEAD_SIZE), 0)
        rows = group * STEPS
        place = lax.broadcasted_iota(jnp.int32, (rows, hist), 1)
        step = lax.broadcasted_iota(jnp.int32, (rows, hist), 0) % STEPS
        first = hist - STEPS
        seen = (place < length) | ((place >= first) & (place - first <= step))
        squares = jnp.zeros((STEPS, 1), jnp.float32)
        for h in range(heads):
            lanes = slice(h * HEAD_SIZE, (h + 1) * HEAD_SIZE)
            k, v = keys[h], values[h]
            for t in range(STEPS):
                k = jnp.where(slot == first + t, kv[t, 0:1, lanes], k)
                v = jnp.where(slot == first + t, kv[t, 1:2, lanes], v)
            cols = [(h * group + g) * HEAD_SIZE for g in range(group)]
            query = jnp.concatenate(
                [q[:, c : c + HEAD_SIZE].astype(jnp.float32) for c in cols], 0
            ).astype(jnp.bfloat16)
            scores = lax.dot_general(
                query, k, (((1,), (1,)), ((), ())), preferred_element_type=jnp.float32
            ) * (1.0 / HEAD_SIZE**0.5)
            scores = jnp.where(seen, scores, -1e30)
            top = jnp.max(scores, -1, keepdims=True)
            e = jnp.where(seen, jnp.exp(scores - top), 0.0)
            weights = (e / jnp.sum(e, -1, keepdims=True)).astype(jnp.bfloat16)
            out = jnp.dot(weights, v, preferred_element_type=jnp.float32)
            for g, c in enumerate(cols):
                here = slice(c, c + HEAD_SIZE)
                got = out[g * STEPS : (g + 1) * STEPS].astype(jnp.bfloat16)
                attended[:, here] = got
                mixed = residual[:, here].astype(jnp.float32) + got.astype(jnp.float32)
                squares += jnp.sum(mixed * mixed, -1, keepdims=True)
                sent[:, here] = (mixed * gain[:, here]).astype(jnp.bfloat16)
        sent[:, width:] = pair(squares)


def forward_kernel(blocks, workers, narrow, share, *refs):
    count = blocks * workers
    arrived, (held, gate, up), rest = refs[:blocks], refs[blocks : blocks + 3], refs[blocks + 3 :]
    outs, (x, sums, slots, sems) = rest[: -4], rest[-4:]
    me = lax.axis_index("wide") - count
    features = gate.shape[0]
    depth = held.shape[2]
    early, room = held.shape[0], slots.shape[0]
    total = features // depth
    half = features // narrow

    def stream(c):
        return fetches(share, c, (c - early) % room, gate, up, slots, sems)

    @pl.when(me >= 0)
    def _():
        for c in range(early, min(early + room, total)):
            for copy in stream(c):
                copy.start()
        lines, tails = [], []
        for d in range(share):
            part = lax.rem(lax.axis_index("parts") + d, share) if share > 1 else 0
            for block in arrived:
                for shift in range(workers):
                    owner = part * workers + lax.rem(me + shift, workers)
                    halves = [block[owner * narrow + n] for n in range(narrow)]
                    lines.append(
                        jnp.concatenate([h[:, :half] for h in halves], 1).astype(jnp.float32)
                    )
                    tails.append(sum(h[:, half:].astype(jnp.float32) for h in halves))
        pad = x.shape[0] - STEPS * count * share
        if pad:
            lines.append(jnp.zeros((pad, features), jnp.float32))
            tails.append(jnp.zeros((pad, TAIL), jnp.float32))
        x[...] = jnp.concatenate(lines, 0).astype(jnp.bfloat16)
        squares = jnp.sum(jnp.concatenate(tails, 0), -1, keepdims=True)
        r = lax.rsqrt(squares / D + EPS)
        for c in range(total):
            if c >= early:
                for copy in stream(c):
                    copy.wait()
            rows = x[:, c * depth : (c + 1) * depth]
            for m in range(2):
                block = held[c, m] if c < early else slots[(c - early) % room, m]
                product = jnp.dot(rows, block, preferred_element_type=jnp.float32)
                sums[m] = product if c == 0 else sums[m] + product
            if c >= early and c + room < total:
                for copy in stream(c + room):
                    copy.start()
        g, u = sums[0] * r, sums[1] * r
        hidden = (g / (1.0 + jnp.exp(-g)) * u).astype(jnp.bfloat16)
        for i, out in enumerate(outs):
            out[...] = hidden[i * STEPS : (i + 1) * STEPS]


def shards(queries, new_kv, keys, values, lengths, residual, gain, gate, up):
    wide = lax.axis_size("wide")
    narrow = lax.axis_size("narrow")
    serving = wide * 3 // 4
    workers = wide - serving
    blocks = serving // workers
    half = queries.shape[2]
    features, _, columns = gate.shape
    share = 1
    local = columns // share
    vmem = pl.BlockSpec(memory_space=pltpu.VMEM)
    hbm = pl.BlockSpec(memory_space=pltpu.HBM)
    owner = lax.axis_index("wide") < serving

    def in_hbm(a):
        return pltpu.with_memory_space_constraint(a, pltpu.HBM)

    gate = in_hbm(gate.reshape(features, columns))
    up = in_hbm(up.reshape(features, columns))
    operands = (
        queries.reshape(STEPS, half),
        new_kv.reshape(STEPS, 2, -1),
        keys.reshape(keys.shape[1:]),
        values.reshape(values.shape[1:]),
        residual.reshape(STEPS, half),
        gain.reshape(1, half),
    )
    attended, sent = pl.pallas_call(
        functools.partial(attend_kernel, serving),
        out_shape=(
            jax.ShapeDtypeStruct((STEPS, half), jnp.bfloat16),
            jax.ShapeDtypeStruct((STEPS, half + TAIL), jnp.bfloat16),
        ),
        in_specs=[pl.BlockSpec(memory_space=pltpu.SMEM)] + [hbm] * 6,
        out_specs=(vmem, vmem),
        scratch_shapes=[pltpu.VMEM(o.shape, o.dtype) for o in operands]
        + [pltpu.SemaphoreType.DMA((6,))],
        compiler_params=pltpu.CompilerParams(vmem_limit_bytes=8 << 20),
    )(lengths, *map(in_hbm, operands))

    groups = [
        [w * narrow + n for w in range(at, at + workers) for n in range(narrow)]
        for at in range(0, wide, workers)
    ]
    blank = pl.pallas_call(
        blank_kernel,
        out_shape=jax.ShapeDtypeStruct((workers * narrow, *sent.shape), jnp.bfloat16),
        out_specs=vmem,
        compiler_params=pltpu.CompilerParams(vmem_limit_bytes=8 << 20),
    )
    block = lax.cond(
        owner,
        lambda s: lax.all_gather(s, ("wide", "narrow"), axis=0, axis_index_groups=groups),
        lambda s: blank(),
        sent,
    )
    arrived = [
        lax.ppermute(block, "wide", [(b * workers + j, serving + j) for j in range(workers)])
        for b in range(blocks)
    ]
    early = min(EARLY, features // DEPTH - 1)
    held = pl.pallas_call(
        functools.partial(fetch_kernel, serving, share),
        out_shape=pltpu.VMEM((early, 2, DEPTH, local), jnp.bfloat16),
        in_specs=[pl.BlockSpec(memory_space=pl.ANY), hbm, hbm],
        out_specs=vmem,
        scratch_shapes=[pltpu.SemaphoreType.DMA((early, 2))],
        compiler_params=pltpu.CompilerParams(vmem_limit_bytes=4 << 20),
        cost_estimate=pl.CostEstimate(
            flops=0, bytes_accessed=early * 4 * DEPTH * local, transcendentals=0
        ),
    )(block, gate, up)
    padded = -(-STEPS * serving * share // 16) * 16
    hidden = pl.pallas_call(
        functools.partial(forward_kernel, blocks, workers, narrow, share),
        out_shape=[jax.ShapeDtypeStruct((STEPS, local), jnp.bfloat16)] * (serving * share),
        in_specs=[vmem] * (blocks + 1) + [hbm, hbm],
        out_specs=[vmem] * (serving * share),
        scratch_shapes=[
            pltpu.VMEM((padded, features), jnp.bfloat16),
            pltpu.VMEM((2, padded, local), jnp.float32),
            pltpu.VMEM((SLOTS, 2, DEPTH, local), jnp.bfloat16),
            pltpu.SemaphoreType.DMA((SLOTS, 2)),
        ],
        compiler_params=pltpu.CompilerParams(vmem_limit_bytes=32 << 20),
    )(*arrived, held, gate, up)
    back = [[None] * workers for _ in range(blocks)]
    for b in reversed(range(blocks)):
        for s in range(workers):
            pairs = [(serving + k, b * workers + (k + s) % workers) for k in range(workers)]
            back[b][s] = lax.ppermute(hidden[b * workers + s], "wide", pairs)
    me = lax.axis_index("wide")
    pieces = []
    for k in range(workers):
        piece = jnp.zeros((), jnp.bfloat16)
        for b in range(blocks):
            for s in range(workers):
                mine = me == b * workers + (k + s) % workers
                piece = jnp.where(mine, back[b][s], piece)
        pieces.append(piece)
    activated = jnp.concatenate(pieces, 1)
    return attended.reshape(STEPS, 1, half), activated.reshape(STEPS, 1, -1)


def solution(mesh):
    rows = P(None, ("parts", "wide"), "narrow")
    placed = (
        rows,
        P(None, ("parts", "wide"), None, "narrow"),
        P(("parts", "wide"), "narrow", None, None),
        P(("parts", "wide"), "narrow", None, None),
        P(("parts", "wide")),
        rows,
        P("narrow"),
        P(None, "narrow", "wide"),
        P(None, "narrow", "wide"),
    )
    return jax.shard_map(
        shards, mesh=mesh, in_specs=placed, out_specs=(rows, rows), check_vma=False
    )
```

time: 60.3 us -> 44.8 us (0.74)
  blocking collectives: 22 us -> 6.18 us
  local copies, waits for them, and re-layouts: 4.58 us -> 0 us
  starting transfers between devices: 5.22 us -> 7.84 us
  Pallas kernels: 2.12 us -> 3.36 us
  waiting for transfers between devices: 23.9 us -> 25 us
    all_gather x1, blocking collectives: 22 us -> 6.18 us  [shards(): lax.all_gather(s, ('wide', 'narrow'), axis=0, axis_index_groups=groups)]
    unnamed x12 -> x0, local copies, waits for them, and re-layouts: 4.58 us -> none
    ppermute x6 -> x9, starting transfers between devices: 5.22 us -> 7.84 us  [the longest x6 5.23 us: shards(): back[b][s] = lax.ppermute(hidden[b * workers + s], 'wide', pairs)]
    ppermute x6 -> x9, waiting for transfers between devices: 23.9 us -> 25 us  [the longest x6 24.8 us: shards(): back[b][s] = lax.ppermute(hidden[b * workers + s], 'wide', pairs)]
    pallas_call x1, Pallas kernels: 2.06 us -> 3.13 us  [shards(): pl.pallas_call(functools.partial(attend_kernel, serving), out_shape=(jax....]
  transfers between devices with their start and end apart: 6 -> 9, of which waited for: 2 -> 3; matrix products, arithmetic and copies ran while one was open for 0% -> 0% of each run, Pallas kernels for 0% -> 0%
where the time goes in v3:
time: 44.8 us; the launch traced here: 44.5 us
  waiting for transfers between devices  25 us (56%)
  starting transfers between devices  7.84 us (18%)
  blocking collectives  6.18 us (14%)
  Pallas kernels  3.36 us (8%)
  between operations  1.43 us (3%)
  other arithmetic  0.7 us (2%)
    ppermute x6, waiting for transfers between devices, shards(): back[b][s] = lax.ppermute(hidden[b * workers + s], 'wide', pairs)  24.8 us
    all_gather x1, blocking collectives, shards(): lax.all_gather(s, ('wide', 'narrow'), axis=0, axis_index_groups=groups)  6.18 us
    ppermute x6, starting transfers between devices, shards(): back[b][s] = lax.ppermute(hidden[b * workers + s], 'wide', pairs)  5.23 us
    pallas_call x1, Pallas kernels, shards(): pl.pallas_call(functools.partial(attend_kernel, serving), out_shape=(jax....  3.13 us
    ppermute x3, starting transfers between devices, shards(): lax.ppermute(block, 'wide', [(b * workers + j, serving + j) for j in rang...  2.61 us
  transfers between devices with their start and end apart: 9, of which 3 were waited for; matrix products, arithmetic and copies ran while one was open for 0% of the time, Pallas kernels for 0%

profile of v3, /device:TPU:0, one launch (start us, length us, event | category | flops | bytes accessed | tf_op | source)
XLA Modules:
  0.0 44.5 jit_solution(8500374987690770194)
XLA Ops:
  1.3 3.1 %shard_map.104 = (bf16[2,2048]{1,0:T(2,128)(2,1)}, bf16[2,2176]{1,0:T(2,128)(2,1)S(1)}) custom-call(s32[1]{0:T(128)S(6)} %copy.13.lengths, bf16[2,2048]{1,0:T(2,128)(2,1)} %bitcast.19, bf16[2,2,512]{2,1,0:T(2,128)(2,1)} %bitcast.22, bf16[4,128,128]{2,1,0:T(8,128)(2,1)} %bitcast.16, bf16[4,128,128]{2,1,0:T(8,128)(2,1)} %bitcast.17, bf16[2,2048]{1,0:T(2,128)(2,1)} %bitcast.20, ...), custom_call_target="tpu_custom_call" | custom-call | tf_op jit(solution)/shard_map/pallas_call | solution.py:197
  4.4 6.2 %conditional.1 = (bf16[4,2,2176]{2,1,0:T(2,128)(2,1)S(1)}) conditional(s32[]{:T(128)} %convert_element_type.3, () %tuple.14, bf16[2,2176]{1,0:T(2,128)(2,1)S(1)} %get-tuple-element.15), branch_computations={%region_0.0_spmd, %region_1.0_spmd} | conditional | bytes 43528 | solution.py:220
  4.4 6.2 %all-gather.1 = bf16[4,2,2176]{2,1,0:T(2,128)(2,1)S(1)} all-gather(bf16[1,2,2176]{2,1,0:T(2,128)(2,1)S(1)} %bitcast.18), channel_id=2, replica_groups={{0,1,2,3},{4,5,6,7},{8,9,10,11},{12,13,14,15},{16,17,18,19},{20,21,22,2..., dimensions={0}, use_global_device_ids=true | all-gather | bytes 43520 | tf_op jit(solution)/shard_map/cond/branch_1_fun/all_gather | solution.py:222
  10.6 1.3 %collective-permute-start = (bf16[4,2,2176]{2,1,0:T(2,128)(2,1)S(1)}, bf16[4,2,2176]{2,1,0:T(2,128)(2,1)S(1)}, u32[]{:S(2)}, u32[]{:S(2)}) collective-permute-start(bf16[4,2,2176]{2,1,0:T(2,128)(2,1)S(1)} %get-tuple-element.24._), channel_id=1, source_target_pairs={{0,12},{2,14},{1,13},{3,15},{16,28},{18,30},{17,29},{19,31}} | collective-permute-start | bytes 104456 | tf_op jit(solution)/shard_map/ppermute | solution.py:227
  11.9 0.7 %collective-permute-start.1 = (bf16[4,2,2176]{2,1,0:T(2,128)(2,1)S(1)}, bf16[4,2,2176]{2,1,0:T(2,128)(2,1)S(1)}, u32[]{:S(2)}, u32[]{:S(2)}) collective-permute-start(bf16[4,2,2176]{2,1,0:T(2,128)(2,1)S(1)} %get-tuple-element.24._), channel_id=1, source_target_pairs={{4,12},{6,14},{5,13},{7,15},{20,28},{22,30},{21,29},{23,31}} | collective-permute-start | bytes 104456 | tf_op jit(solution)/shard_map/ppermute | solution.py:227
  12.6 0.7 %collective-permute-start.2 = (bf16[4,2,2176]{2,1,0:T(2,128)(2,1)S(1)}, bf16[4,2,2176]{2,1,0:T(2,128)(2,1)S(1)}, u32[]{:S(2)}, u32[]{:S(2)}) collective-permute-start(bf16[4,2,2176]{2,1,0:T(2,128)(2,1)S(1)} %get-tuple-element.24._), channel_id=1, source_target_pairs={{8,12},{10,14},{9,13},{11,15},{24,28},{26,30},{25,29},{27,31}} | collective-permute-start | bytes 104456 | tf_op jit(solution)/shard_map/ppermute | solution.py:227
  13.3 0.1 shard_map.105.refs_3_
  13.4 0.1 collective-permute-done.refs_0_
  13.5 0.0 collective-permute-done.1.refs_1_
  13.5 0.0 collective-permute-done.2.refs_2_
  13.5 0.1 shard_map.106
  13.6 0.7 %collective-permute-start.3 = (bf16[2,3584]{1,0:T(2,128)(2,1)S(1)}, bf16[2,3584]{1,0:T(2,128)(2,1)S(1)}, u32[]{:S(2)}, u32[]{:S(2)}) collective-permute-start(bf16[2,3584]{1,0:T(2,128)(2,1)S(1)} %get-tuple-element.16), channel_id=1, source_target_pairs={{12,10},{14,8},{13,11},{15,9},{28,26},{30,24},{29,27},{31,25}} | collective-permute-start | bytes 43016 | tf_op jit(solution)/shard_map/ppermute | solution.py:260
  14.3 0.7 %collective-permute-start.4 = (bf16[2,3584]{1,0:T(2,128)(2,1)S(1)}, bf16[2,3584]{1,0:T(2,128)(2,1)S(1)}, u32[]{:S(2)}, u32[]{:S(2)}) collective-permute-start(bf16[2,3584]{1,0:T(2,128)(2,1)S(1)} %get-tuple-element.17), channel_id=1, source_target_pairs={{12,8},{14,10},{13,9},{15,11},{28,24},{30,26},{29,25},{31,27}} | collective-permute-start | bytes 43016 | tf_op jit(solution)/shard_map/ppermute | solution.py:260
  15.0 0.7 %collective-permute-start.5 = (bf16[2,3584]{1,0:T(2,128)(2,1)S(1)}, bf16[2,3584]{1,0:T(2,128)(2,1)S(1)}, u32[]{:S(2)}, u32[]{:S(2)}) collective-permute-start(bf16[2,3584]{1,0:T(2,128)(2,1)S(1)} %get-tuple-element.18), channel_id=1, source_target_pairs={{12,6},{14,4},{13,7},{15,5},{28,22},{30,20},{29,23},{31,21}} | collective-permute-start | bytes 43016 | tf_op jit(solution)/shard_map/ppermute | solution.py:260
  15.6 0.7 %collective-permute-start.6 = (bf16[2,3584]{1,0:T(2,128)(2,1)S(1)}, bf16[2,3584]{1,0:T(2,128)(2,1)S(1)}, u32[]{:S(2)}, u32[]{:S(2)}) collective-permute-start(bf16[2,3584]{1,0:T(2,128)(2,1)S(1)} %get-tuple-element.19), channel_id=1, source_target_pairs={{12,4},{14,6},{13,5},{15,7},{28,20},{30,22},{29,21},{31,23}} | collective-permute-start | bytes 43016 | tf_op jit(solution)/shard_map/ppermute | solution.py:260
  16.3 1.3 %collective-permute-start.7 = (bf16[2,3584]{1,0:T(2,128)(2,1)S(1)}, bf16[2,3584]{1,0:T(2,128)(2,1)S(1)}, u32[]{:S(2)}, u32[]{:S(2)}) collective-permute-start(bf16[2,3584]{1,0:T(2,128)(2,1)S(1)} %get-tuple-element.20), channel_id=1, source_target_pairs={{12,2},{14,0},{13,3},{15,1},{28,18},{30,16},{29,19},{31,17}} | collective-permute-start | bytes 43016 | tf_op jit(solution)/shard_map/ppermute | solution.py:260
  17.6 0.0 collective-permute-done.3
  17.6 1.3 %collective-permute-start.8 = (bf16[2,3584]{1,0:T(2,128)(2,1)S(1)}, bf16[2,3584]{1,0:T(2,128)(2,1)S(1)}, u32[]{:S(2)}, u32[]{:S(2)}) collective-permute-start(bf16[2,3584]{1,0:T(2,128)(2,1)S(1)} %get-tuple-element.21), channel_id=1, source_target_pairs={{12,0},{14,2},{13,1},{15,3},{28,16},{30,18},{29,17},{31,19}} | collective-permute-start | bytes 43016 | tf_op jit(solution)/shard_map/ppermute | solution.py:260
  18.9 0.0 collective-permute-done.4
  18.9 0.0 collective-permute-done.5
  19.0 0.0 collective-permute-done.6
  19.0 24.5 %collective-permute-done.7 = bf16[2,3584]{1,0:T(2,128)(2,1)S(1)} collective-permute-done((bf16[2,3584]{1,0:T(2,128)(2,1)S(1)}, bf16[2,3584]{1,0:T(2,128)(2,1)S(1)}, u32[]{:S(2)}, u32[]{:S(2)}) %collective-permute-start.7) | collective-permute-done | bytes 14368 | tf_op jit(solution)/shard_map/ppermute | solution.py:260
  43.5 0.3 collective-permute-done.8
  43.8 0.1 broadcast_select_fusion.11
  43.9 0.6 %maximum_bitcast_fusion = bf16[2,1,7168]{2,0,1:T(2,128)(2,1)} fusion(bf16[2,3584]{1,0:T(2,128)(2,1)S(1)} %get-tuple-element.23, bf16[2,3584]{1,0:T(2,128)(2,1)S(1)} %get-tuple-element.22), kind=kLoop, calls=%fused_computation | loop fusion | flops 57344 | bytes 57344 | tf_op jit(solution)/shard_map/reshape | solution.py:271
Async XLA Ops:
  10.6 2.9 %collective-permute-start = (bf16[4,2,2176]{2,1,0:T(2,128)(2,1)S(1)}, bf16[4,2,2176]{2,1,0:T(2,128)(2,1)S(1)}, u32[]{:S(2)}, u32[]{:S(2)}) collective-permute-start(bf16[4,2,2176]{2,1,0:T(2,128)(2,1)S(1)} %get-tuple-element.24._), channel_id=1, source_target_pairs={{0,12},{2,14},{1,13},{3,15},{16,28},{18,30},{17,29},{19,31}} | collective-permute-start | bytes 104456 | tf_op jit(solution)/shard_map/ppermute | solution.py:227
  11.9 1.6 %collective-permute-start.1 = (bf16[4,2,2176]{2,1,0:T(2,128)(2,1)S(1)}, bf16[4,2,2176]{2,1,0:T(2,128)(2,1)S(1)}, u32[]{:S(2)}, u32[]{:S(2)}) collective-permute-start(bf16[4,2,2176]{2,1,0:T(2,128)(2,1)S(1)} %get-tuple-element.24._), channel_id=1, source_target_pairs={{4,12},{6,14},{5,13},{7,15},{20,28},{22,30},{21,29},{23,31}} | collective-permute-start | bytes 104456 | tf_op jit(solution)/shard_map/ppermute | solution.py:227
  12.6 0.9 %collective-permute-start.2 = (bf16[4,2,2176]{2,1,0:T(2,128)(2,1)S(1)}, bf16[4,2,2176]{2,1,0:T(2,128)(2,1)S(1)}, u32[]{:S(2)}, u32[]{:S(2)}) collective-permute-start(bf16[4,2,2176]{2,1,0:T(2,128)(2,1)S(1)} %get-tuple-element.24._), channel_id=1, source_target_pairs={{8,12},{10,14},{9,13},{11,15},{24,28},{26,30},{25,29},{27,31}} | collective-permute-start | bytes 104456 | tf_op jit(solution)/shard_map/ppermute | solution.py:227
  13.6 4.0 %collective-permute-start.3 = (bf16[2,3584]{1,0:T(2,128)(2,1)S(1)}, bf16[2,3584]{1,0:T(2,128)(2,1)S(1)}, u32[]{:S(2)}, u32[]{:S(2)}) collective-permute-start(bf16[2,3584]{1,0:T(2,128)(2,1)S(1)} %get-tuple-element.16), channel_id=1, source_target_pairs={{12,10},{14,8},{13,11},{15,9},{28,26},{30,24},{29,27},{31,25}} | collective-permute-start | bytes 43016 | tf_op jit(solution)/shard_map/ppermute | solution.py:260
  14.3 4.6 %collective-permute-start.4 = (bf16[2,3584]{1,0:T(2,128)(2,1)S(1)}, bf16[2,3584]{1,0:T(2,128)(2,1)S(1)}, u32[]{:S(2)}, u32[]{:S(2)}) collective-permute-start(bf16[2,3584]{1,0:T(2,128)(2,1)S(1)} %get-tuple-element.17), channel_id=1, source_target_pairs={{12,8},{14,10},{13,9},{15,11},{28,24},{30,26},{29,25},{31,27}} | collective-permute-start | bytes 43016 | tf_op jit(solution)/shard_map/ppermute | solution.py:260
  15.0 4.0 %collective-permute-start.5 = (bf16[2,3584]{1,0:T(2,128)(2,1)S(1)}, bf16[2,3584]{1,0:T(2,128)(2,1)S(1)}, u32[]{:S(2)}, u32[]{:S(2)}) collective-permute-start(bf16[2,3584]{1,0:T(2,128)(2,1)S(1)} %get-tuple-element.18), channel_id=1, source_target_pairs={{12,6},{14,4},{13,7},{15,5},{28,22},{30,20},{29,23},{31,21}} | collective-permute-start | bytes 43016 | tf_op jit(solution)/shard_map/ppermute | solution.py:260
  15.6 3.3 %collective-permute-start.6 = (bf16[2,3584]{1,0:T(2,128)(2,1)S(1)}, bf16[2,3584]{1,0:T(2,128)(2,1)S(1)}, u32[]{:S(2)}, u32[]{:S(2)}) collective-permute-start(bf16[2,3584]{1,0:T(2,128)(2,1)S(1)} %get-tuple-element.19), channel_id=1, source_target_pairs={{12,4},{14,6},{13,5},{15,7},{28,20},{30,22},{29,21},{31,23}} | collective-permute-start | bytes 43016 | tf_op jit(solution)/shard_map/ppermute | solution.py:260
  16.3 27.2 %collective-permute-start.7 = (bf16[2,3584]{1,0:T(2,128)(2,1)S(1)}, bf16[2,3584]{1,0:T(2,128)(2,1)S(1)}, u32[]{:S(2)}, u32[]{:S(2)}) collective-permute-start(bf16[2,3584]{1,0:T(2,128)(2,1)S(1)} %get-tuple-element.20), channel_id=1, source_target_pairs={{12,2},{14,0},{13,3},{15,1},{28,18},{30,16},{29,19},{31,17}} | collective-permute-start | bytes 43016 | tf_op jit(solution)/shard_map/ppermute | solution.py:260
  17.6 26.2 %collective-permute-start.8 = (bf16[2,3584]{1,0:T(2,128)(2,1)S(1)}, bf16[2,3584]{1,0:T(2,128)(2,1)S(1)}, u32[]{:S(2)}, u32[]{:S(2)}) collective-permute-start(bf16[2,3584]{1,0:T(2,128)(2,1)S(1)} %get-tuple-element.21), channel_id=1, source_target_pairs={{12,0},{14,2},{13,1},{15,3},{28,16},{30,18},{29,17},{31,19}} | collective-permute-start | bytes 43016 | tf_op jit(solution)/shard_map/ppermute | solution.py:260

commit v4 on v3

--- a/solution.py
+++ b/solution.py
@@ -13,8 +13,8 @@
 TAIL = 128
 EPS = 1e-05
 DEPTH = 256
-EARLY = 5
-SLOTS = 6
+EARLY = 7
+SLOTS = 5
 
 
 def pair(squares):
@@ -53,9 +53,9 @@
     out[...] = jnp.zeros_like(out)
 
 
-def attend_kernel(serving, lengths, *refs):
-    sources, (attended, sent), held, sems = refs[:6], refs[6:8], refs[8:14], refs[14]
-    q, kv, keys, values, residual, gain = held
+def attend_kernel(serving, *refs):
+    sources, (attended, sent), held, sems = refs[:7], refs[7:9], refs[9:16], refs[16]
+    lengths, q, kv, keys, values, residual, gain = held
     owner = lax.axis_index("wide") < serving
     heads, hist, _ = keys.shape
     width = q.shape[1]
@@ -76,7 +76,7 @@
             c.start()
         for c in copies:
             c.wait()
-        length = lengths[0]
+        length = lengths[0, 0]
         slot = lax.broadcasted_iota(jnp.int32, (hist, HEAD_SIZE), 0)
         rows = group * STEPS
         place = lax.broadcasted_iota(jnp.int32, (rows, hist), 1)
@@ -150,11 +150,10 @@
         squares = jnp.sum(jnp.concatenate(tails, 0), -1, keepdims=True)
         r = lax.rsqrt(squares / D + EPS)
         for c in range(total):
-            if c >= early:
-                for copy in stream(c):
-                    copy.wait()
             rows = x[:, c * depth : (c + 1) * depth]
             for m in range(2):
+                if c >= early:
+                    stream(c)[m].wait()
                 block = held[c, m] if c < early else slots[(c - early) % room, m]
                 product = jnp.dot(rows, block, preferred_element_type=jnp.float32)
                 sums[m] = product if c == 0 else sums[m] + product
@@ -163,8 +162,31 @@
                     copy.start()
         g, u = sums[0] * r, sums[1] * r
         hidden = (g / (1.0 + jnp.exp(-g)) * u).astype(jnp.bfloat16)
-        for i, out in enumerate(outs):
+        for i in range(count):
+            out = outs[(blocks - 1 - i // workers) * workers + i % workers]
             out[...] = hidden[i * STEPS : (i + 1) * STEPS]
+
+
+def finish_kernel(blocks, workers, attended, *refs):
+    results, (attended_out, out) = refs[:-2], refs[-2:]
+    attended_out[...] = attended[...]
+    if len(results) == 1:
+        out[...] = results[0][...]
+        return
+    me = lax.axis_index("wide")
+    columns = results[0].shape[1]
+
+    @pl.when(me >= blocks * workers)
+    def _():
+        out[...] = jnp.zeros_like(out)
+
+    for i, result in enumerate(results):
+        b, shift = divmod(i, workers)
+
+        @pl.when((me >= b * workers) & (me < (b + 1) * workers))
+        def _():
+            k = lax.rem(me - b * workers + workers - shift, workers)
+            out[:, pl.ds(pl.multiple_of(k * columns, 128), columns)] = result[...]
 
 
 def shards(queries, new_kv, keys, values, lengths, residual, gain, gate, up):
@@ -187,6 +209,7 @@
     gate = in_hbm(gate.reshape(features, columns))
     up = in_hbm(up.reshape(features, columns))
     operands = (
+        lengths.reshape(1, 1),
         queries.reshape(STEPS, half),
         new_kv.reshape(STEPS, 2, -1),
         keys.reshape(keys.shape[1:]),
@@ -197,15 +220,16 @@
     attended, sent = pl.pallas_call(
         functools.partial(attend_kernel, serving),
         out_shape=(
-            jax.ShapeDtypeStruct((STEPS, half), jnp.bfloat16),
+            pltpu.VMEM((STEPS, half), jnp.bfloat16),
             jax.ShapeDtypeStruct((STEPS, half + TAIL), jnp.bfloat16),
         ),
-        in_specs=[pl.BlockSpec(memory_space=pltpu.SMEM)] + [hbm] * 6,
+        in_specs=[hbm] * 7,
         out_specs=(vmem, vmem),
-        scratch_shapes=[pltpu.VMEM(o.shape, o.dtype) for o in operands]
-        + [pltpu.SemaphoreType.DMA((6,))],
+        scratch_shapes=[]
+        + [(pltpu.SMEM if o.dtype == jnp.int32 else pltpu.VMEM)(o.shape, o.dtype) for o in operands]
+        + [pltpu.SemaphoreType.DMA((7,))],
         compiler_params=pltpu.CompilerParams(vmem_limit_bytes=8 << 20),
-    )(lengths, *map(in_hbm, operands))
+    )(operands[0], *map(in_hbm, operands[1:]))
 
     groups = [
         [w * narrow + n for w in range(at, at + workers) for n in range(narrow)]
@@ -251,23 +275,37 @@
             pltpu.VMEM((SLOTS, 2, DEPTH, local), jnp.bfloat16),
             pltpu.SemaphoreType.DMA((SLOTS, 2)),
         ],
-        compiler_params=pltpu.CompilerParams(vmem_limit_bytes=32 << 20),
+        compiler_params=pltpu.CompilerParams(vmem_limit_bytes=20 << 20),
     )(*arrived, held, gate, up)
     back = [[None] * workers for _ in range(blocks)]
-    for b in reversed(range(blocks)):
+    for b in range(blocks):
         for s in range(workers):
             pairs = [(serving + k, b * workers + (k + s) % workers) for k in range(workers)]
-            back[b][s] = lax.ppermute(hidden[b * workers + s], "wide", pairs)
-    me = lax.axis_index("wide")
-    pieces = []
-    for k in range(workers):
-        piece = jnp.zeros((), jnp.bfloat16)
-        for b in range(blocks):
-            for s in range(workers):
-                mine = me == b * workers + (k + s) % workers
-                piece = jnp.where(mine, back[b][s], piece)
-        pieces.append(piece)
-    activated = jnp.concatenate(pieces, 1)
+            back[b][s] = lax.ppermute(hidden[(blocks - 1 - b) * workers + s], "wide", pairs)
+    aligned = columns % 128 == 0
+    if aligned:
+        results = [r for some in back for r in some]
+    else:
+        me = lax.axis_index("wide")
+        pieces = []
+        for k in range(workers):
+            piece = jnp.zeros((), jnp.bfloat16)
+            for b in range(blocks):
+                for s in range(workers):
+                    mine = me == b * workers + (k + s) % workers
+                    piece = jnp.where(mine, back[b][s], piece)
+            pieces.append(piece)
+        results = [jnp.concatenate(pieces, 1)]
+    attended, activated = pl.pallas_call(
+        functools.partial(finish_kernel, blocks, workers),
+        out_shape=(
+            jax.ShapeDtypeStruct((STEPS, half), jnp.bfloat16),
+            jax.ShapeDtypeStruct((STEPS, workers * columns), jnp.bfloat16),
+        ),
+        in_specs=[vmem] * (1 + len(results)),
+        out_specs=(vmem, vmem),
+        compiler_params=pltpu.CompilerParams(vmem_limit_bytes=8 << 20),
+    )(attended, *results)
     return attended.reshape(STEPS, 1, half), activated.reshape(STEPS, 1, -1)
 
 

time: 44.8 us -> 41.4 us (0.924)
  the two profiles are of different devices: /device:TPU:0 before, /device:TPU:16 now
where the time goes in v4:
time: 41.4 us; the launch traced here: 41.1 us
  waiting for transfers between devices  23.2 us (56%)
  starting transfers between devices  7.84 us (19%)
  blocking collectives  5.2 us (13%)
  Pallas kernels  3.42 us (8%)
  between operations  1.41 us (3%)
    ppermute x6, waiting for transfers between devices, shards(): lax.ppermute(hidden[(blocks - 1 - b) * workers + s], 'wide', pairs)  23.1 us
    ppermute x6, starting transfers between devices, shards(): lax.ppermute(hidden[(blocks - 1 - b) * workers + s], 'wide', pairs)  5.23 us
    all_gather x1, blocking collectives, shards(): lax.all_gather(s, ('wide', 'narrow'), axis=0, axis_index_groups=groups)  5.2 us
    ppermute x3, starting transfers between devices, shards(): lax.ppermute(block, 'wide', [(b * workers + j, serving + j) for j in rang...  2.61 us
    pallas_call x1, Pallas kernels, shards(): pl.pallas_call(functools.partial(attend_kernel, serving), out_shape=(pltp...  2.55 us
  transfers between devices with their start and end apart: 9, of which 3 were waited for; matrix products, arithmetic and copies ran while one was open for 0% of the time, Pallas kernels for 0%

profile of v4, /device:TPU:16, one launch (start us, length us, event | category | flops | bytes accessed | tf_op | source)
XLA Modules:
  0.0 41.1 jit_solution(8132656869428344620)
XLA Ops:
  1.3 2.5 %shard_map.104 = (bf16[2,2048]{1,0:T(2,128)(2,1)S(1)}, bf16[2,2176]{1,0:T(2,128)(2,1)S(1)}) custom-call(s32[1,1]{1,0:T(1,128)} %bitcast.12.refs_0_, bf16[2,2048]{1,0:T(2,128)(2,1)} %bitcast.20, bf16[2,2,512]{2,1,0:T(2,128)(2,1)} %bitcast.23, bf16[4,128,128]{2,1,0:T(8,128)(2,1)} %bitcast.17, bf16[4,128,128]{2,1,0:T(8,128)(2,1)} %bitcast.18, ...), custom_call_target="tpu_custom_call" | custom-call | tf_op jit(solution)/shard_map/pallas_call | solution.py:220
  3.8 5.2 %conditional.1 = (bf16[4,2,2176]{2,1,0:T(2,128)(2,1)S(1)}) conditional(s32[]{:T(128)} %convert_element_type.3, () %tuple.14, bf16[2,2176]{1,0:T(2,128)(2,1)S(1)} %get-tuple-element.17), branch_computations={%region_0.0_spmd, %region_1.0_spmd} | conditional | bytes 43528 | solution.py:244
  3.9 5.2 %all-gather.1 = bf16[4,2,2176]{2,1,0:T(2,128)(2,1)S(1)} all-gather(bf16[1,2,2176]{2,1,0:T(2,128)(2,1)S(1)} %bitcast.19), channel_id=2, replica_groups={{0,1,2,3},{4,5,6,7},{8,9,10,11},{12,13,14,15},{16,17,18,19},{20,21,22,2..., dimensions={0}, use_global_device_ids=true | all-gather | bytes 43520 | tf_op jit(solution)/shard_map/cond/branch_1_fun/all_gather | solution.py:246
  9.1 1.3 %collective-permute-start.2 = (bf16[4,2,2176]{2,1,0:T(2,128)(2,1)S(1)}, bf16[4,2,2176]{2,1,0:T(2,128)(2,1)S(1)}, u32[]{:S(2)}, u32[]{:S(2)}) collective-permute-start(bf16[4,2,2176]{2,1,0:T(2,128)(2,1)S(1)} %get-tuple-element.26._), channel_id=1, source_target_pairs={{8,12},{10,14},{9,13},{11,15},{24,28},{26,30},{25,29},{27,31}} | collective-permute-start | bytes 104456 | tf_op jit(solution)/shard_map/ppermute | solution.py:251
  10.3 0.7 %collective-permute-start.1 = (bf16[4,2,2176]{2,1,0:T(2,128)(2,1)S(1)}, bf16[4,2,2176]{2,1,0:T(2,128)(2,1)S(1)}, u32[]{:S(2)}, u32[]{:S(2)}) collective-permute-start(bf16[4,2,2176]{2,1,0:T(2,128)(2,1)S(1)} %get-tuple-element.26._), channel_id=1, source_target_pairs={{4,12},{6,14},{5,13},{7,15},{20,28},{22,30},{21,29},{23,31}} | collective-permute-start | bytes 104456 | tf_op jit(solution)/shard_map/ppermute | solution.py:251
  11.0 0.7 %collective-permute-start = (bf16[4,2,2176]{2,1,0:T(2,128)(2,1)S(1)}, bf16[4,2,2176]{2,1,0:T(2,128)(2,1)S(1)}, u32[]{:S(2)}, u32[]{:S(2)}) collective-permute-start(bf16[4,2,2176]{2,1,0:T(2,128)(2,1)S(1)} %get-tuple-element.26._), channel_id=1, source_target_pairs={{0,12},{2,14},{1,13},{3,15},{16,28},{18,30},{17,29},{19,31}} | collective-permute-start | bytes 104456 | tf_op jit(solution)/shard_map/ppermute | solution.py:251
  11.7 0.2 shard_map.105.refs_3_
  11.9 0.1 collective-permute-done.2.refs_2_
  11.9 0.0 collective-permute-done.1.refs_1_
  11.9 0.0 collective-permute-done.refs_0_
  12.0 0.1 shard_map.106
  12.1 0.7 %collective-permute-start.3 = (bf16[2,3584]{1,0:T(2,128)(2,1)S(1)}, bf16[2,3584]{1,0:T(2,128)(2,1)S(1)}, u32[]{:S(2)}, u32[]{:S(2)}) collective-permute-start(bf16[2,3584]{1,0:T(2,128)(2,1)S(1)} %get-tuple-element.18), channel_id=1, source_target_pairs={{12,0},{14,2},{13,1},{15,3},{28,16},{30,18},{29,17},{31,19}} | collective-permute-start | bytes 43016 | tf_op jit(solution)/shard_map/ppermute | solution.py:284
  12.7 0.7 %collective-permute-start.4 = (bf16[2,3584]{1,0:T(2,128)(2,1)S(1)}, bf16[2,3584]{1,0:T(2,128)(2,1)S(1)}, u32[]{:S(2)}, u32[]{:S(2)}) collective-permute-start(bf16[2,3584]{1,0:T(2,128)(2,1)S(1)} %get-tuple-element.19), channel_id=1, source_target_pairs={{12,2},{14,0},{13,3},{15,1},{28,18},{30,16},{29,19},{31,17}} | collective-permute-start | bytes 43016 | tf_op jit(solution)/shard_map/ppermute | solution.py:284
  13.4 0.7 %collective-permute-start.5 = (bf16[2,3584]{1,0:T(2,128)(2,1)S(1)}, bf16[2,3584]{1,0:T(2,128)(2,1)S(1)}, u32[]{:S(2)}, u32[]{:S(2)}) collective-permute-start(bf16[2,3584]{1,0:T(2,128)(2,1)S(1)} %get-tuple-element.20), channel_id=1, source_target_pairs={{12,4},{14,6},{13,5},{15,7},{28,20},{30,22},{29,21},{31,23}} | collective-permute-start | bytes 43016 | tf_op jit(solution)/shard_map/ppermute | solution.py:284
  14.1 0.7 %collective-permute-start.6 = (bf16[2,3584]{1,0:T(2,128)(2,1)S(1)}, bf16[2,3584]{1,0:T(2,128)(2,1)S(1)}, u32[]{:S(2)}, u32[]{:S(2)}) collective-permute-start(bf16[2,3584]{1,0:T(2,128)(2,1)S(1)} %get-tuple-element.21), channel_id=1, source_target_pairs={{12,6},{14,4},{13,7},{15,5},{28,22},{30,20},{29,23},{31,21}} | collective-permute-start | bytes 43016 | tf_op jit(solution)/shard_map/ppermute | solution.py:284
  14.7 1.3 %collective-permute-start.7 = (bf16[2,3584]{1,0:T(2,128)(2,1)S(1)}, bf16[2,3584]{1,0:T(2,128)(2,1)S(1)}, u32[]{:S(2)}, u32[]{:S(2)}) collective-permute-start(bf16[2,3584]{1,0:T(2,128)(2,1)S(1)} %get-tuple-element.22), channel_id=1, source_target_pairs={{12,8},{14,10},{13,9},{15,11},{28,24},{30,26},{29,25},{31,27}} | collective-permute-start | bytes 43016 | tf_op jit(solution)/shard_map/ppermute | solution.py:284
  16.0 0.0 collective-permute-done.3.refs_0_
  16.0 1.3 %collective-permute-start.8 = (bf16[2,3584]{1,0:T(2,128)(2,1)S(1)}, bf16[2,3584]{1,0:T(2,128)(2,1)S(1)}, u32[]{:S(2)}, u32[]{:S(2)}) collective-permute-start(bf16[2,3584]{1,0:T(2,128)(2,1)S(1)} %get-tuple-element.23), channel_id=1, source_target_pairs={{12,10},{14,8},{13,11},{15,9},{28,26},{30,24},{29,27},{31,25}} | collective-permute-start | bytes 43016 | tf_op jit(solution)/shard_map/ppermute | solution.py:284
  17.3 0.0 collective-permute-done.4.refs_1_
  17.4 0.0 collective-permute-done.5.refs_2_
  17.4 0.0 collective-permute-done.6.refs_3_
  17.4 20.9 %collective-permute-done.7.refs_4_ = bf16[2,3584]{1,0:T(2,128)(2,1)S(1)} collective-permute-done((bf16[2,3584]{1,0:T(2,128)(2,1)S(1)}, bf16[2,3584]{1,0:T(2,128)(2,1)S(1)}, u32[]{:S(2)}, u32[]{:S(2)}) %collective-permute-start.7) | collective-permute-done | bytes 14368 | tf_op jit(solution)/shard_map/ppermute | solution.py:284
  38.2 2.2 %collective-permute-done.8.refs_5_ = bf16[2,3584]{1,0:T(2,128)(2,1)S(1)} collective-permute-done((bf16[2,3584]{1,0:T(2,128)(2,1)S(1)}, bf16[2,3584]{1,0:T(2,128)(2,1)S(1)}, u32[]{:S(2)}, u32[]{:S(2)}) %collective-permute-start.8) | collective-permute-done | bytes 14368 | tf_op jit(solution)/shard_map/ppermute | solution.py:284
  40.5 0.6 %shard_map.107 = (bf16[2,2048]{1,0:T(2,128)(2,1)}, bf16[2,7168]{1,0:T(2,128)(2,1)}) custom-call(bf16[2,2048]{1,0:T(2,128)(2,1)S(1)} %get-tuple-element.16.attended, bf16[2,3584]{1,0:T(2,128)(2,1)S(1)} %collective-permute-done.3.refs_0_, bf16[2,3584]{1,0:T(2,128)(2,1)S(1)} %collective-permute-done.4.refs_1_, ...), custom_call_target="tpu_custom_call" | custom-call | tf_op jit(solution)/shard_map/pallas_call | solution.py:299
Async XLA Ops:
  9.1 2.9 %collective-permute-start.2 = (bf16[4,2,2176]{2,1,0:T(2,128)(2,1)S(1)}, bf16[4,2,2176]{2,1,0:T(2,128)(2,1)S(1)}, u32[]{:S(2)}, u32[]{:S(2)}) collective-permute-start(bf16[4,2,2176]{2,1,0:T(2,128)(2,1)S(1)} %get-tuple-element.26._), channel_id=1, source_target_pairs={{8,12},{10,14},{9,13},{11,15},{24,28},{26,30},{25,29},{27,31}} | collective-permute-start | bytes 104456 | tf_op jit(solution)/shard_map/ppermute | solution.py:251
  10.3 1.6 %collective-permute-start.1 = (bf16[4,2,2176]{2,1,0:T(2,128)(2,1)S(1)}, bf16[4,2,2176]{2,1,0:T(2,128)(2,1)S(1)}, u32[]{:S(2)}, u32[]{:S(2)}) collective-permute-start(bf16[4,2,2176]{2,1,0:T(2,128)(2,1)S(1)} %get-tuple-element.26._), channel_id=1, source_target_pairs={{4,12},{6,14},{5,13},{7,15},{20,28},{22,30},{21,29},{23,31}} | collective-permute-start | bytes 104456 | tf_op jit(solution)/shard_map/ppermute | solution.py:251
  11.0 0.9 %collective-permute-start = (bf16[4,2,2176]{2,1,0:T(2,128)(2,1)S(1)}, bf16[4,2,2176]{2,1,0:T(2,128)(2,1)S(1)}, u32[]{:S(2)}, u32[]{:S(2)}) collective-permute-start(bf16[4,2,2176]{2,1,0:T(2,128)(2,1)S(1)} %get-tuple-element.26._), channel_id=1, source_target_pairs={{0,12},{2,14},{1,13},{3,15},{16,28},{18,30},{17,29},{19,31}} | collective-permute-start | bytes 104456 | tf_op jit(solution)/shard_map/ppermute | solution.py:251
  12.1 4.0 %collective-permute-start.3 = (bf16[2,3584]{1,0:T(2,128)(2,1)S(1)}, bf16[2,3584]{1,0:T(2,128)(2,1)S(1)}, u32[]{:S(2)}, u32[]{:S(2)}) collective-permute-start(bf16[2,3584]{1,0:T(2,128)(2,1)S(1)} %get-tuple-element.18), channel_id=1, source_target_pairs={{12,0},{14,2},{13,1},{15,3},{28,16},{30,18},{29,17},{31,19}} | collective-permute-start | bytes 43016 | tf_op jit(solution)/shard_map/ppermute | solution.py:284
  12.7 4.6 %collective-permute-start.4 = (bf16[2,3584]{1,0:T(2,128)(2,1)S(1)}, bf16[2,3584]{1,0:T(2,128)(2,1)S(1)}, u32[]{:S(2)}, u32[]{:S(2)}) collective-permute-start(bf16[2,3584]{1,0:T(2,128)(2,1)S(1)} %get-tuple-element.19), channel_id=1, source_target_pairs={{12,2},{14,0},{13,3},{15,1},{28,18},{30,16},{29,19},{31,17}} | collective-permute-start | bytes 43016 | tf_op jit(solution)/shard_map/ppermute | solution.py:284
  13.4 4.0 %collective-permute-start.5 = (bf16[2,3584]{1,0:T(2,128)(2,1)S(1)}, bf16[2,3584]{1,0:T(2,128)(2,1)S(1)}, u32[]{:S(2)}, u32[]{:S(2)}) collective-permute-start(bf16[2,3584]{1,0:T(2,128)(2,1)S(1)} %get-tuple-element.20), channel_id=1, source_target_pairs={{12,4},{14,6},{13,5},{15,7},{28,20},{30,22},{29,21},{31,23}} | collective-permute-start | bytes 43016 | tf_op jit(solution)/shard_map/ppermute | solution.py:284
  14.1 3.3 %collective-permute-start.6 = (bf16[2,3584]{1,0:T(2,128)(2,1)S(1)}, bf16[2,3584]{1,0:T(2,128)(2,1)S(1)}, u32[]{:S(2)}, u32[]{:S(2)}) collective-permute-start(bf16[2,3584]{1,0:T(2,128)(2,1)S(1)} %get-tuple-element.21), channel_id=1, source_target_pairs={{12,6},{14,4},{13,7},{15,5},{28,22},{30,20},{29,23},{31,21}} | collective-permute-start | bytes 43016 | tf_op jit(solution)/shard_map/ppermute | solution.py:284
  14.7 23.5 %collective-permute-start.7 = (bf16[2,3584]{1,0:T(2,128)(2,1)S(1)}, bf16[2,3584]{1,0:T(2,128)(2,1)S(1)}, u32[]{:S(2)}, u32[]{:S(2)}) collective-permute-start(bf16[2,3584]{1,0:T(2,128)(2,1)S(1)} %get-tuple-element.22), channel_id=1, source_target_pairs={{12,8},{14,10},{13,9},{15,11},{28,24},{30,26},{29,25},{31,27}} | collective-permute-start | bytes 43016 | tf_op jit(solution)/shard_map/ppermute | solution.py:284
  16.0 24.4 %collective-permute-start.8 = (bf16[2,3584]{1,0:T(2,128)(2,1)S(1)}, bf16[2,3584]{1,0:T(2,128)(2,1)S(1)}, u32[]{:S(2)}, u32[]{:S(2)}) collective-permute-start(bf16[2,3584]{1,0:T(2,128)(2,1)S(1)} %get-tuple-element.23), channel_id=1, source_target_pairs={{12,10},{14,8},{13,11},{15,9},{28,26},{30,24},{29,27},{31,25}} | collective-permute-start | bytes 43016 | tf_op jit(solution)/shard_map/ppermute | solution.py:284

commit v5 on v4

--- a/solution.py
+++ b/solution.py
@@ -12,8 +12,8 @@
 STEPS = 2
 TAIL = 128
 EPS = 1e-05
-DEPTH = 256
-EARLY = 7
+EARLY = 2048
+TILE = 256
 SLOTS = 5
 
 
@@ -24,29 +24,18 @@
     return both.astype(jnp.bfloat16)
 
 
-def fetches(share, c, slot, gate, up, held, sems):
-    depth, local = held.shape[2:]
-    here = pl.ds(c * depth, depth)
-    copies = []
-    for m, matrix in enumerate((gate, up)):
-        source = matrix.at[here]
-        if share > 1:
-            base = pl.multiple_of(lax.axis_index("parts") * local, 128)
-            source = matrix.at[here, pl.ds(base, local)]
-        copies.append(pltpu.make_async_copy(source, held.at[slot, m], sems.at[slot, m]))
-    return copies
-
-
-def fetch_kernel(serving, share, _, gate, up, held, sems):
+def fetch_kernel(serving, _, gate, up, gate_held, up_held, sems):
     @pl.when(lax.axis_index("wide") >= serving)
     def _():
-        copies = [fetches(share, c, c, gate, up, held, sems) for c in range(held.shape[0])]
-        for some in copies:
-            for c in some:
-                c.start()
-        for some in copies:
-            for c in some:
-                c.wait()
+        here = pl.ds(0, gate_held.shape[0])
+        copies = [
+            pltpu.make_async_copy(gate.at[here], gate_held, sems.at[0]),
+            pltpu.make_async_copy(up.at[here], up_held, sems.at[1]),
+        ]
+        for c in copies:
+            c.start()
+        for c in copies:
+            c.wait()
 
 
 def blank_kernel(out):
@@ -112,59 +101,65 @@
         sent[:, width:] = pair(squares)
 
 
-def forward_kernel(blocks, workers, narrow, share, *refs):
+def forward_kernel(blocks, workers, narrow, *refs):
     count = blocks * workers
-    arrived, (held, gate, up), rest = refs[:blocks], refs[blocks : blocks + 3], refs[blocks + 3 :]
-    outs, (x, sums, slots, sems) = rest[: -4], rest[-4:]
+    arrived, (gate_held, up_held, gate, up), rest = refs[:blocks], refs[blocks:][:4], refs[blocks + 4 :]
+    outs, (x, slots, sems) = rest[:-3], rest[-3:]
     me = lax.axis_index("wide") - count
-    features = gate.shape[0]
-    depth = held.shape[2]
-    early, room = held.shape[0], slots.shape[0]
-    total = features // depth
+    features, columns = gate.shape
     half = features // narrow
-
-    def stream(c):
-        return fetches(share, c, (c - early) % room, gate, up, slots, sems)
+    early = gate_held.shape[0]
+    room, _, late, tile = slots.shape
+    total = columns // tile
+
+    def stream(j):
+        s = j % room
+        here = (pl.ds(early, late), pl.ds(j * tile, tile))
+        return [
+            pltpu.make_async_copy(m.at[here], slots.at[s, i], sems.at[s, i])
+            for i, m in enumerate((gate, up))
+        ]
 
     @pl.when(me >= 0)
     def _():
-        for c in range(early, min(early + room, total)):
-            for copy in stream(c):
+        for j in range(min(room, total)):
+            for copy in stream(j):
                 copy.start()
         lines, tails = [], []
-        for d in range(share):
-            part = lax.rem(lax.axis_index("parts") + d, share) if share > 1 else 0
-            for block in arrived:
-                for shift in range(workers):
-                    owner = part * workers + lax.rem(me + shift, workers)
-                    halves = [block[owner * narrow + n] for n in range(narrow)]
-                    lines.append(
-                        jnp.concatenate([h[:, :half] for h in halves], 1).astype(jnp.float32)
-                    )
-                    tails.append(sum(h[:, half:].astype(jnp.float32) for h in halves))
-        pad = x.shape[0] - STEPS * count * share
+        for block in arrived:
+            for shift in range(workers):
+                owner = lax.rem(me + shift, workers)
+                halves = [block[owner * narrow + n] for n in range(narrow)]
+                lines.append(
+                    jnp.concatenate([h[:, :half] for h in halves], 1).astype(jnp.float32)
+                )
+                tails.append(sum(h[:, half:].astype(jnp.float32) for h in halves))
+        pad = x.shape[0] - STEPS * count
         if pad:
             lines.append(jnp.zeros((pad, features), jnp.float32))
             tails.append(jnp.zeros((pad, TAIL), jnp.float32))
         x[...] = jnp.concatenate(lines, 0).astype(jnp.bfloat16)
         squares = jnp.sum(jnp.concatenate(tails, 0), -1, keepdims=True)
         r = lax.rsqrt(squares / D + EPS)
-        for c in range(total):
-            rows = x[:, c * depth : (c + 1) * depth]
-            for m in range(2):
-                if c >= early:
-                    stream(c)[m].wait()
-                block = held[c, m] if c < early else slots[(c - early) % room, m]
-                product = jnp.dot(rows, block, preferred_element_type=jnp.float32)
-                sums[m] = product if c == 0 else sums[m] + product
-            if c >= early and c + room < total:
-                for copy in stream(c + room):
+        for j in range(total):
+            here = slice(j * tile, (j + 1) * tile)
+            sums = [
+                jnp.dot(x[:, :early], held[:, here], preferred_element_type=jnp.float32)
+                for held in (gate_held, up_held)
+            ]
+            for i, copy in enumerate(stream(j)):
+                copy.wait()
+                sums[i] += jnp.dot(
+                    x[:, early:], slots[j % room, i], preferred_element_type=jnp.float32
+                )
+            if j + room < total:
+                for copy in stream(j + room):
                     copy.start()
-        g, u = sums[0] * r, sums[1] * r
-        hidden = (g / (1.0 + jnp.exp(-g)) * u).astype(jnp.bfloat16)
-        for i in range(count):
-            out = outs[(blocks - 1 - i // workers) * workers + i % workers]
-            out[...] = hidden[i * STEPS : (i + 1) * STEPS]
+            g, u = sums[0] * r, sums[1] * r
+            hidden = (g / (1.0 + jnp.exp(-g)) * u).astype(jnp.bfloat16)
+            for i in range(count):
+                out = outs[(blocks - 1 - i // workers) * workers + i % workers]
+                out[:, here] = hidden[i * STEPS : (i + 1) * STEPS]
 
 
 def finish_kernel(blocks, workers, attended, *refs):
@@ -197,8 +192,6 @@
     blocks = serving // workers
     half = queries.shape[2]
     features, _, columns = gate.shape
-    share = 1
-    local = columns // share
     vmem = pl.BlockSpec(memory_space=pltpu.VMEM)
     hbm = pl.BlockSpec(memory_space=pltpu.HBM)
     owner = lax.axis_index("wide") < serving
@@ -251,32 +244,33 @@
         lax.ppermute(block, "wide", [(b * workers + j, serving + j) for j in range(workers)])
         for b in range(blocks)
     ]
-    early = min(EARLY, features // DEPTH - 1)
+    early = min(EARLY, features // 2)
     held = pl.pallas_call(
-        functools.partial(fetch_kernel, serving, share),
-        out_shape=pltpu.VMEM((early, 2, DEPTH, local), jnp.bfloat16),
+        functools.partial(fetch_kernel, serving),
+        out_shape=[pltpu.VMEM((early, columns), jnp.bfloat16)] * 2,
         in_specs=[pl.BlockSpec(memory_space=pl.ANY), hbm, hbm],
-        out_specs=vmem,
-        scratch_shapes=[pltpu.SemaphoreType.DMA((early, 2))],
+        out_specs=[vmem] * 2,
+        scratch_shapes=[pltpu.SemaphoreType.DMA((2,))],
         compiler_params=pltpu.CompilerParams(vmem_limit_bytes=4 << 20),
         cost_estimate=pl.CostEstimate(
-            flops=0, bytes_accessed=early * 4 * DEPTH * local, transcendentals=0
+            flops=0, bytes_accessed=early * 4 * columns, transcendentals=0
         ),
     )(block, gate, up)
-    padded = -(-STEPS * serving * share // 16) * 16
+    padded = -(-STEPS * serving // 16) * 16
+    tile = TILE if columns % TILE == 0 else columns
+    slots = min(SLOTS, columns // tile)
     hidden = pl.pallas_call(
-        functools.partial(forward_kernel, blocks, workers, narrow, share),
-        out_shape=[jax.ShapeDtypeStruct((STEPS, local), jnp.bfloat16)] * (serving * share),
-        in_specs=[vmem] * (blocks + 1) + [hbm, hbm],
-        out_specs=[vmem] * (serving * share),
+        functools.partial(forward_kernel, blocks, workers, narrow),
+        out_shape=[jax.ShapeDtypeStruct((STEPS, columns), jnp.bfloat16)] * serving,
+        in_specs=[vmem] * (blocks + 2) + [hbm, hbm],
+        out_specs=[vmem] * serving,
         scratch_shapes=[
             pltpu.VMEM((padded, features), jnp.bfloat16),
-            pltpu.VMEM((2, padded, local), jnp.float32),
-            pltpu.VMEM((SLOTS, 2, DEPTH, local), jnp.bfloat16),
-            pltpu.SemaphoreType.DMA((SLOTS, 2)),
+            pltpu.VMEM((slots, 2, features - early, tile), jnp.bfloat16),
+            pltpu.SemaphoreType.DMA((slots, 2)),
         ],
         compiler_params=pltpu.CompilerParams(vmem_limit_bytes=20 << 20),
-    )(*arrived, held, gate, up)
+    )(*arrived, *held, gate, up)
     back = [[None] * workers for _ in range(blocks)]
     for b in range(blocks):
         for s in range(workers):

time: 41.4 us -> 49.2 us (1.19)
  waiting for transfers between devices: 23.2 us -> 31.1 us
    ppermute x6, waiting for transfers between devices: 23.1 us -> 30.9 us  [shards(): lax.ppermute(hidden[(blocks - 1 - b) * workers + s], 'wide', pairs)]
where the time goes in v5:
time: 49.2 us; the launch traced here: 48.9 us
  waiting for transfers between devices  31.1 us (63%)
  starting transfers between devices  7.84 us (16%)
  blocking collectives  5.2 us (11%)
  Pallas kernels  3.29 us (7%)
  between operations  1.41 us (3%)
    ppermute x6, waiting for transfers between devices, shards(): lax.ppermute(hidden[(blocks - 1 - b) * workers + s], 'wide', pairs)  30.9 us
    ppermute x6, starting transfers between devices, shards(): lax.ppermute(hidden[(blocks - 1 - b) * workers + s], 'wide', pairs)  5.23 us
    all_gather x1, blocking collectives, shards(): lax.all_gather(s, ('wide', 'narrow'), axis=0, axis_index_groups=groups)  5.2 us
    ppermute x3, starting transfers between devices, shards(): lax.ppermute(block, 'wide', [(b * workers + j, serving + j) for j in rang...  2.61 us
    pallas_call x1, Pallas kernels, shards(): pl.pallas_call(functools.partial(attend_kernel, serving), out_shape=(pltp...  2.55 us
  transfers between devices with their start and end apart: 9, of which 3 were waited for; matrix products, arithmetic and copies ran while one was open for 0% of the time, Pallas kernels for 0%

profile of v5, /device:TPU:16, one launch (start us, length us, event | category | flops | bytes accessed | tf_op | source)
XLA Modules:
  0.0 48.9 jit_solution(5094769577994587555)
XLA Ops:
  1.3 2.5 %shard_map.104 = (bf16[2,2048]{1,0:T(2,128)(2,1)S(1)}, bf16[2,2176]{1,0:T(2,128)(2,1)S(1)}) custom-call(s32[1,1]{1,0:T(1,128)} %bitcast.12.refs_0_, bf16[2,2048]{1,0:T(2,128)(2,1)} %bitcast.20, bf16[2,2,512]{2,1,0:T(2,128)(2,1)} %bitcast.23, bf16[4,128,128]{2,1,0:T(8,128)(2,1)} %bitcast.17, bf16[4,128,128]{2,1,0:T(8,128)(2,1)} %bitcast.18, ...), custom_call_target="tpu_custom_call" | custom-call | tf_op jit(solution)/shard_map/pallas_call | solution.py:213
  3.8 5.2 %conditional.1 = (bf16[4,2,2176]{2,1,0:T(2,128)(2,1)S(1)}) conditional(s32[]{:T(128)} %convert_element_type.3, () %tuple.14, bf16[2,2176]{1,0:T(2,128)(2,1)S(1)} %get-tuple-element.19), branch_computations={%region_0.0_spmd, %region_1.0_spmd} | conditional | bytes 43528 | solution.py:237
  3.9 5.2 %all-gather.1 = bf16[4,2,2176]{2,1,0:T(2,128)(2,1)S(1)} all-gather(bf16[1,2,2176]{2,1,0:T(2,128)(2,1)S(1)} %bitcast.19), channel_id=2, replica_groups={{0,1,2,3},{4,5,6,7},{8,9,10,11},{12,13,14,15},{16,17,18,19},{20,21,22,2..., dimensions={0}, use_global_device_ids=true | all-gather | bytes 43520 | tf_op jit(solution)/shard_map/cond/branch_1_fun/all_gather | solution.py:239
  9.1 1.3 %collective-permute-start.2 = (bf16[4,2,2176]{2,1,0:T(2,128)(2,1)S(1)}, bf16[4,2,2176]{2,1,0:T(2,128)(2,1)S(1)}, u32[]{:S(2)}, u32[]{:S(2)}) collective-permute-start(bf16[4,2,2176]{2,1,0:T(2,128)(2,1)S(1)} %get-tuple-element.30._), channel_id=1, source_target_pairs={{8,12},{10,14},{9,13},{11,15},{24,28},{26,30},{25,29},{27,31}} | collective-permute-start | bytes 104456 | tf_op jit(solution)/shard_map/ppermute | solution.py:244
  10.3 0.7 %collective-permute-start.1 = (bf16[4,2,2176]{2,1,0:T(2,128)(2,1)S(1)}, bf16[4,2,2176]{2,1,0:T(2,128)(2,1)S(1)}, u32[]{:S(2)}, u32[]{:S(2)}) collective-permute-start(bf16[4,2,2176]{2,1,0:T(2,128)(2,1)S(1)} %get-tuple-element.30._), channel_id=1, source_target_pairs={{4,12},{6,14},{5,13},{7,15},{20,28},{22,30},{21,29},{23,31}} | collective-permute-start | bytes 104456 | tf_op jit(solution)/shard_map/ppermute | solution.py:244
  11.0 0.7 %collective-permute-start = (bf16[4,2,2176]{2,1,0:T(2,128)(2,1)S(1)}, bf16[4,2,2176]{2,1,0:T(2,128)(2,1)S(1)}, u32[]{:S(2)}, u32[]{:S(2)}) collective-permute-start(bf16[4,2,2176]{2,1,0:T(2,128)(2,1)S(1)} %get-tuple-element.30._), channel_id=1, source_target_pairs={{0,12},{2,14},{1,13},{3,15},{16,28},{18,30},{17,29},{19,31}} | collective-permute-start | bytes 104456 | tf_op jit(solution)/shard_map/ppermute | solution.py:244
  11.7 0.2 collective-permute-done.2.refs_2_
  11.9 0.0 collective-permute-done.1.refs_1_
  11.9 0.0 collective-permute-done.refs_0_
  12.0 0.1 shard_map.106
  12.1 0.7 %collective-permute-start.3 = (bf16[2,3584]{1,0:T(2,128)(2,1)S(1)}, bf16[2,3584]{1,0:T(2,128)(2,1)S(1)}, u32[]{:S(2)}, u32[]{:S(2)}) collective-permute-start(bf16[2,3584]{1,0:T(2,128)(2,1)S(1)} %get-tuple-element.22), channel_id=1, source_target_pairs={{12,0},{14,2},{13,1},{15,3},{28,16},{30,18},{29,17},{31,19}} | collective-permute-start | bytes 43016 | tf_op jit(solution)/shard_map/ppermute | solution.py:278
  12.7 0.7 %collective-permute-start.4 = (bf16[2,3584]{1,0:T(2,128)(2,1)S(1)}, bf16[2,3584]{1,0:T(2,128)(2,1)S(1)}, u32[]{:S(2)}, u32[]{:S(2)}) collective-permute-start(bf16[2,3584]{1,0:T(2,128)(2,1)S(1)} %get-tuple-element.23), channel_id=1, source_target_pairs={{12,2},{14,0},{13,3},{15,1},{28,18},{30,16},{29,19},{31,17}} | collective-permute-start | bytes 43016 | tf_op jit(solution)/shard_map/ppermute | solution.py:278
  13.4 0.7 %collective-permute-start.5 = (bf16[2,3584]{1,0:T(2,128)(2,1)S(1)}, bf16[2,3584]{1,0:T(2,128)(2,1)S(1)}, u32[]{:S(2)}, u32[]{:S(2)}) collective-permute-start(bf16[2,3584]{1,0:T(2,128)(2,1)S(1)} %get-tuple-element.24), channel_id=1, source_target_pairs={{12,4},{14,6},{13,5},{15,7},{28,20},{30,22},{29,21},{31,23}} | collective-permute-start | bytes 43016 | tf_op jit(solution)/shard_map/ppermute | solution.py:278
  14.1 0.7 %collective-permute-start.6 = (bf16[2,3584]{1,0:T(2,128)(2,1)S(1)}, bf16[2,3584]{1,0:T(2,128)(2,1)S(1)}, u32[]{:S(2)}, u32[]{:S(2)}) collective-permute-start(bf16[2,3584]{1,0:T(2,128)(2,1)S(1)} %get-tuple-element.25), channel_id=1, source_target_pairs={{12,6},{14,4},{13,7},{15,5},{28,22},{30,20},{29,23},{31,21}} | collective-permute-start | bytes 43016 | tf_op jit(solution)/shard_map/ppermute | solution.py:278
  14.7 1.3 %collective-permute-start.7 = (bf16[2,3584]{1,0:T(2,128)(2,1)S(1)}, bf16[2,3584]{1,0:T(2,128)(2,1)S(1)}, u32[]{:S(2)}, u32[]{:S(2)}) collective-permute-start(bf16[2,3584]{1,0:T(2,128)(2,1)S(1)} %get-tuple-element.26), channel_id=1, source_target_pairs={{12,8},{14,10},{13,9},{15,11},{28,24},{30,26},{29,25},{31,27}} | collective-permute-start | bytes 43016 | tf_op jit(solution)/shard_map/ppermute | solution.py:278
  16.0 0.0 collective-permute-done.3.refs_0_
  16.0 1.3 %collective-permute-start.8 = (bf16[2,3584]{1,0:T(2,128)(2,1)S(1)}, bf16[2,3584]{1,0:T(2,128)(2,1)S(1)}, u32[]{:S(2)}, u32[]{:S(2)}) collective-permute-start(bf16[2,3584]{1,0:T(2,128)(2,1)S(1)} %get-tuple-element.27), channel_id=1, source_target_pairs={{12,10},{14,8},{13,11},{15,9},{28,26},{30,24},{29,27},{31,25}} | collective-permute-start | bytes 43016 | tf_op jit(solution)/shard_map/ppermute | solution.py:278
  17.3 0.0 collective-permute-done.4.refs_1_
  17.4 0.0 collective-permute-done.5.refs_2_
  17.4 0.0 collective-permute-done.6.refs_3_
  17.4 28.6 %collective-permute-done.7.refs_4_ = bf16[2,3584]{1,0:T(2,128)(2,1)S(1)} collective-permute-done((bf16[2,3584]{1,0:T(2,128)(2,1)S(1)}, bf16[2,3584]{1,0:T(2,128)(2,1)S(1)}, u32[]{:S(2)}, u32[]{:S(2)}) %collective-permute-start.7) | collective-permute-done | bytes 14368 | tf_op jit(solution)/shard_map/ppermute | solution.py:278
  46.0 2.2 %collective-permute-done.8.refs_5_ = bf16[2,3584]{1,0:T(2,128)(2,1)S(1)} collective-permute-done((bf16[2,3584]{1,0:T(2,128)(2,1)S(1)}, bf16[2,3584]{1,0:T(2,128)(2,1)S(1)}, u32[]{:S(2)}, u32[]{:S(2)}) %collective-permute-start.8) | collective-permute-done | bytes 14368 | tf_op jit(solution)/shard_map/ppermute | solution.py:278
  48.3 0.6 %shard_map.107 = (bf16[2,2048]{1,0:T(2,128)(2,1)}, bf16[2,7168]{1,0:T(2,128)(2,1)}) custom-call(bf16[2,2048]{1,0:T(2,128)(2,1)S(1)} %get-tuple-element.18.attended, bf16[2,3584]{1,0:T(2,128)(2,1)S(1)} %collective-permute-done.3.refs_0_, bf16[2,3584]{1,0:T(2,128)(2,1)S(1)} %collective-permute-done.4.refs_1_, ...), custom_call_target="tpu_custom_call" | custom-call | tf_op jit(solution)/shard_map/pallas_call | solution.py:293
  (1 shorter events, 0.0 us)
Async XLA Ops:
  9.1 2.9 %collective-permute-start.2 = (bf16[4,2,2176]{2,1,0:T(2,128)(2,1)S(1)}, bf16[4,2,2176]{2,1,0:T(2,128)(2,1)S(1)}, u32[]{:S(2)}, u32[]{:S(2)}) collective-permute-start(bf16[4,2,2176]{2,1,0:T(2,128)(2,1)S(1)} %get-tuple-element.30._), channel_id=1, source_target_pairs={{8,12},{10,14},{9,13},{11,15},{24,28},{26,30},{25,29},{27,31}} | collective-permute-start | bytes 104456 | tf_op jit(solution)/shard_map/ppermute | solution.py:244
  10.3 1.6 %collective-permute-start.1 = (bf16[4,2,2176]{2,1,0:T(2,128)(2,1)S(1)}, bf16[4,2,2176]{2,1,0:T(2,128)(2,1)S(1)}, u32[]{:S(2)}, u32[]{:S(2)}) collective-permute-start(bf16[4,2,2176]{2,1,0:T(2,128)(2,1)S(1)} %get-tuple-element.30._), channel_id=1, source_target_pairs={{4,12},{6,14},{5,13},{7,15},{20,28},{22,30},{21,29},{23,31}} | collective-permute-start | bytes 104456 | tf_op jit(solution)/shard_map/ppermute | solution.py:244
  11.0 0.9 %collective-permute-start = (bf16[4,2,2176]{2,1,0:T(2,128)(2,1)S(1)}, bf16[4,2,2176]{2,1,0:T(2,128)(2,1)S(1)}, u32[]{:S(2)}, u32[]{:S(2)}) collective-permute-start(bf16[4,2,2176]{2,1,0:T(2,128)(2,1)S(1)} %get-tuple-element.30._), channel_id=1, source_target_pairs={{0,12},{2,14},{1,13},{3,15},{16,28},{18,30},{17,29},{19,31}} | collective-permute-start | bytes 104456 | tf_op jit(solution)/shard_map/ppermute | solution.py:244
  12.1 4.0 %collective-permute-start.3 = (bf16[2,3584]{1,0:T(2,128)(2,1)S(1)}, bf16[2,3584]{1,0:T(2,128)(2,1)S(1)}, u32[]{:S(2)}, u32[]{:S(2)}) collective-permute-start(bf16[2,3584]{1,0:T(2,128)(2,1)S(1)} %get-tuple-element.22), channel_id=1, source_target_pairs={{12,0},{14,2},{13,1},{15,3},{28,16},{30,18},{29,17},{31,19}} | collective-permute-start | bytes 43016 | tf_op jit(solution)/shard_map/ppermute | solution.py:278
  12.7 4.6 %collective-permute-start.4 = (bf16[2,3584]{1,0:T(2,128)(2,1)S(1)}, bf16[2,3584]{1,0:T(2,128)(2,1)S(1)}, u32[]{:S(2)}, u32[]{:S(2)}) collective-permute-start(bf16[2,3584]{1,0:T(2,128)(2,1)S(1)} %get-tuple-element.23), channel_id=1, source_target_pairs={{12,2},{14,0},{13,3},{15,1},{28,18},{30,16},{29,19},{31,17}} | collective-permute-start | bytes 43016 | tf_op jit(solution)/shard_map/ppermute | solution.py:278
  13.4 4.0 %collective-permute-start.5 = (bf16[2,3584]{1,0:T(2,128)(2,1)S(1)}, bf16[2,3584]{1,0:T(2,128)(2,1)S(1)}, u32[]{:S(2)}, u32[]{:S(2)}) collective-permute-start(bf16[2,3584]{1,0:T(2,128)(2,1)S(1)} %get-tuple-element.24), channel_id=1, source_target_pairs={{12,4},{14,6},{13,5},{15,7},{28,20},{30,22},{29,21},{31,23}} | collective-permute-start | bytes 43016 | tf_op jit(solution)/shard_map/ppermute | solution.py:278
  14.1 3.3 %collective-permute-start.6 = (bf16[2,3584]{1,0:T(2,128)(2,1)S(1)}, bf16[2,3584]{1,0:T(2,128)(2,1)S(1)}, u32[]{:S(2)}, u32[]{:S(2)}) collective-permute-start(bf16[2,3584]{1,0:T(2,128)(2,1)S(1)} %get-tuple-element.25), channel_id=1, source_target_pairs={{12,6},{14,4},{13,7},{15,5},{28,22},{30,20},{29,23},{31,21}} | collective-permute-start | bytes 43016 | tf_op jit(solution)/shard_map/ppermute | solution.py:278
  14.7 31.3 %collective-permute-start.7 = (bf16[2,3584]{1,0:T(2,128)(2,1)S(1)}, bf16[2,3584]{1,0:T(2,128)(2,1)S(1)}, u32[]{:S(2)}, u32[]{:S(2)}) collective-permute-start(bf16[2,3584]{1,0:T(2,128)(2,1)S(1)} %get-tuple-element.26), channel_id=1, source_target_pairs={{12,8},{14,10},{13,9},{15,11},{28,24},{30,26},{29,25},{31,27}} | collective-permute-start | bytes 43016 | tf_op jit(solution)/shard_map/ppermute | solution.py:278
  16.0 32.2 %collective-permute-start.8 = (bf16[2,3584]{1,0:T(2,128)(2,1)S(1)}, bf16[2,3584]{1,0:T(2,128)(2,1)S(1)}, u32[]{:S(2)}, u32[]{:S(2)}) collective-permute-start(bf16[2,3584]{1,0:T(2,128)(2,1)S(1)} %get-tuple-element.27), channel_id=1, source_target_pairs={{12,10},{14,8},{13,11},{15,9},{28,26},{30,24},{29,27},{31,25}} | collective-permute-start | bytes 43016 | tf_op jit(solution)/shard_map/ppermute | solution.py:278

commit v6 on v5

--- a/solution.py
+++ b/solution.py
@@ -13,8 +13,10 @@
 TAIL = 128
 EPS = 1e-05
 EARLY = 2048
-TILE = 256
-SLOTS = 5
+DEPTH = 512
+SLOTS = 2
+WIDTH = 512
+SHARES = (4, 2, 1, 0)
 
 
 def pair(squares):
@@ -104,17 +106,19 @@
 def forward_kernel(blocks, workers, narrow, *refs):
     count = blocks * workers
     arrived, (gate_held, up_held, gate, up), rest = refs[:blocks], refs[blocks:][:4], refs[blocks + 4 :]
-    outs, (x, slots, sems) = rest[:-3], rest[-3:]
+    outs, (x, sums, slots, sems) = rest[:-4], rest[-4:]
     me = lax.axis_index("wide") - count
     features, columns = gate.shape
     half = features // narrow
     early = gate_held.shape[0]
-    room, _, late, tile = slots.shape
-    total = columns // tile
+    room, _, depth, _ = slots.shape
+    total = (features - early) // depth
+    width = WIDTH if columns % WIDTH == 0 else columns
+    spans = [slice(at, at + width) for at in range(0, columns, width)]
 
     def stream(j):
         s = j % room
-        here = (pl.ds(early, late), pl.ds(j * tile, tile))
+        here = pl.ds(early + j * depth, depth)
         return [
             pltpu.make_async_copy(m.at[here], slots.at[s, i], sems.at[s, i])
             for i, m in enumerate((gate, up))
@@ -141,25 +145,39 @@
         x[...] = jnp.concatenate(lines, 0).astype(jnp.bfloat16)
         squares = jnp.sum(jnp.concatenate(tails, 0), -1, keepdims=True)
         r = lax.rsqrt(squares / D + EPS)
+        taken = set()
+
+        def add(i, here, rows, block):
+            product = jnp.dot(rows, block, preferred_element_type=jnp.float32)
+            first = (i, here.start) not in taken
+            taken.add((i, here.start))
+            sums[i, :, here] = product if first else sums[i, :, here] + product
+
+        waiting = list(spans)
         for j in range(total):
-            here = slice(j * tile, (j + 1) * tile)
-            sums = [
-                jnp.dot(x[:, :early], held[:, here], preferred_element_type=jnp.float32)
-                for held in (gate_held, up_held)
-            ]
-            for i, copy in enumerate(stream(j)):
+            for _ in range(-(-len(spans) * SHARES[min(j, len(SHARES) - 1)] // sum(SHARES))):
+                if waiting:
+                    here = waiting.pop(0)
+                    for i, held in enumerate((gate_held, up_held)):
+                        add(i, here, x[:, :early], held[:, here])
+            if j == total - 1:
+                for here in waiting:
+                    for i, held in enumerate((gate_held, up_held)):
+                        add(i, here, x[:, :early], held[:, here])
+            for copy in stream(j):
                 copy.wait()
-                sums[i] += jnp.dot(
-                    x[:, early:], slots[j % room, i], preferred_element_type=jnp.float32
-                )
+            at = early + j * depth
+            for here in spans:
+                for i in range(2):
+                    add(i, here, x[:, at : at + depth], slots[j % room, i, :, here])
             if j + room < total:
                 for copy in stream(j + room):
                     copy.start()
-            g, u = sums[0] * r, sums[1] * r
-            hidden = (g / (1.0 + jnp.exp(-g)) * u).astype(jnp.bfloat16)
-            for i in range(count):
-                out = outs[(blocks - 1 - i // workers) * workers + i % workers]
-                out[:, here] = hidden[i * STEPS : (i + 1) * STEPS]
+        g, u = sums[0] * r, sums[1] * r
+        hidden = (g / (1.0 + jnp.exp(-g)) * u).astype(jnp.bfloat16)
+        for i in range(count):
+            out = outs[(blocks - 1 - i // workers) * workers + i % workers]
+            out[...] = hidden[i * STEPS : (i + 1) * STEPS]
 
 
 def finish_kernel(blocks, workers, attended, *refs):
@@ -257,8 +275,7 @@
         ),
     )(block, gate, up)
     padded = -(-STEPS * serving // 16) * 16
-    tile = TILE if columns % TILE == 0 else columns
-    slots = min(SLOTS, columns // tile)
+    depth = min(DEPTH, features - early)
     hidden = pl.pallas_call(
         functools.partial(forward_kernel, blocks, workers, narrow),
         out_shape=[jax.ShapeDtypeStruct((STEPS, columns), jnp.bfloat16)] * serving,
@@ -266,10 +283,11 @@
         out_specs=[vmem] * serving,
         scratch_shapes=[
             pltpu.VMEM((padded, features), jnp.bfloat16),
-            pltpu.VMEM((slots, 2, features - early, tile), jnp.bfloat16),
-            pltpu.SemaphoreType.DMA((slots, 2)),
+            pltpu.VMEM((2, padded, columns), jnp.float32),
+            pltpu.VMEM((SLOTS, 2, depth, columns), jnp.bfloat16),
+            pltpu.SemaphoreType.DMA((SLOTS, 2)),
         ],
-        compiler_params=pltpu.CompilerParams(vmem_limit_bytes=20 << 20),
+        compiler_params=pltpu.CompilerParams(vmem_limit_bytes=16 << 20),
     )(*arrived, *held, gate, up)
     back = [[None] * workers for _ in range(blocks)]
     for b in range(blocks):

time: 49.2 us -> 39.3 us (0.80)
  waiting for transfers between devices: 31.1 us -> 21.3 us
    ppermute x6, waiting for transfers between devices: 30.9 us -> 21.1 us  [shards(): lax.ppermute(hidden[(blocks - 1 - b) * workers + s], 'wide', pairs)]
where the time goes in v6:
time: 39.3 us; the launch traced here: 39 us
  waiting for transfers between devices  21.3 us (54%)
  starting transfers between devices  7.84 us (20%)
  blocking collectives  5.2 us (13%)
  Pallas kernels  3.24 us (8%)
  between operations  1.41 us (4%)
    ppermute x6, waiting for transfers between devices, shards(): lax.ppermute(hidden[(blocks - 1 - b) * workers + s], 'wide', pairs)  21.1 us
    ppermute x6, starting transfers between devices, shards(): lax.ppermute(hidden[(blocks - 1 - b) * workers + s], 'wide', pairs)  5.23 us
    all_gather x1, blocking collectives, shards(): lax.all_gather(s, ('wide', 'narrow'), axis=0, axis_index_groups=groups)  5.2 us
    ppermute x3, starting transfers between devices, shards(): lax.ppermute(block, 'wide', [(b * workers + j, serving + j) for j in rang...  2.61 us
    pallas_call x1, Pallas kernels, shards(): pl.pallas_call(functools.partial(attend_kernel, serving), out_shape=(pltp...  2.55 us
  transfers between devices with their start and end apart: 9, of which 3 were waited for; matrix products, arithmetic and copies ran while one was open for 0% of the time, Pallas kernels for 0%

profile of v6, /device:TPU:16, one launch (start us, length us, event | category | flops | bytes accessed | tf_op | source)
XLA Modules:
  0.0 39.0 jit_solution(13345297929556946795)
XLA Ops:
  1.3 2.5 %shard_map.104 = (bf16[2,2048]{1,0:T(2,128)(2,1)S(1)}, bf16[2,2176]{1,0:T(2,128)(2,1)S(1)}) custom-call(s32[1,1]{1,0:T(1,128)} %bitcast.12.refs_0_, bf16[2,2048]{1,0:T(2,128)(2,1)} %bitcast.20, bf16[2,2,512]{2,1,0:T(2,128)(2,1)} %bitcast.23, bf16[4,128,128]{2,1,0:T(8,128)(2,1)} %bitcast.17, bf16[4,128,128]{2,1,0:T(8,128)(2,1)} %bitcast.18, ...), custom_call_target="tpu_custom_call" | custom-call | tf_op jit(solution)/shard_map/pallas_call | solution.py:231
  3.8 5.2 %conditional.1 = (bf16[4,2,2176]{2,1,0:T(2,128)(2,1)S(1)}) conditional(s32[]{:T(128)} %convert_element_type.3, () %tuple.14, bf16[2,2176]{1,0:T(2,128)(2,1)S(1)} %get-tuple-element.19), branch_computations={%region_0.0_spmd, %region_1.0_spmd} | conditional | bytes 43528 | solution.py:255
  3.9 5.2 %all-gather.1 = bf16[4,2,2176]{2,1,0:T(2,128)(2,1)S(1)} all-gather(bf16[1,2,2176]{2,1,0:T(2,128)(2,1)S(1)} %bitcast.19), channel_id=2, replica_groups={{0,1,2,3},{4,5,6,7},{8,9,10,11},{12,13,14,15},{16,17,18,19},{20,21,22,2..., dimensions={0}, use_global_device_ids=true | all-gather | bytes 43520 | tf_op jit(solution)/shard_map/cond/branch_1_fun/all_gather | solution.py:257
  9.1 1.3 %collective-permute-start.2 = (bf16[4,2,2176]{2,1,0:T(2,128)(2,1)S(1)}, bf16[4,2,2176]{2,1,0:T(2,128)(2,1)S(1)}, u32[]{:S(2)}, u32[]{:S(2)}) collective-permute-start(bf16[4,2,2176]{2,1,0:T(2,128)(2,1)S(1)} %get-tuple-element.30._), channel_id=1, source_target_pairs={{8,12},{10,14},{9,13},{11,15},{24,28},{26,30},{25,29},{27,31}} | collective-permute-start | bytes 104456 | tf_op jit(solution)/shard_map/ppermute | solution.py:262
  10.3 0.7 %collective-permute-start.1 = (bf16[4,2,2176]{2,1,0:T(2,128)(2,1)S(1)}, bf16[4,2,2176]{2,1,0:T(2,128)(2,1)S(1)}, u32[]{:S(2)}, u32[]{:S(2)}) collective-permute-start(bf16[4,2,2176]{2,1,0:T(2,128)(2,1)S(1)} %get-tuple-element.30._), channel_id=1, source_target_pairs={{4,12},{6,14},{5,13},{7,15},{20,28},{22,30},{21,29},{23,31}} | collective-permute-start | bytes 104456 | tf_op jit(solution)/shard_map/ppermute | solution.py:262
  11.0 0.7 %collective-permute-start = (bf16[4,2,2176]{2,1,0:T(2,128)(2,1)S(1)}, bf16[4,2,2176]{2,1,0:T(2,128)(2,1)S(1)}, u32[]{:S(2)}, u32[]{:S(2)}) collective-permute-start(bf16[4,2,2176]{2,1,0:T(2,128)(2,1)S(1)} %get-tuple-element.30._), channel_id=1, source_target_pairs={{0,12},{2,14},{1,13},{3,15},{16,28},{18,30},{17,29},{19,31}} | collective-permute-start | bytes 104456 | tf_op jit(solution)/shard_map/ppermute | solution.py:262
  11.7 0.2 collective-permute-done.2.refs_2_
  11.9 0.0 collective-permute-done.1.refs_1_
  11.9 0.0 collective-permute-done.refs_0_
  12.0 0.7 %collective-permute-start.3 = (bf16[2,3584]{1,0:T(2,128)(2,1)S(1)}, bf16[2,3584]{1,0:T(2,128)(2,1)S(1)}, u32[]{:S(2)}, u32[]{:S(2)}) collective-permute-start(bf16[2,3584]{1,0:T(2,128)(2,1)S(1)} %get-tuple-element.22), channel_id=1, source_target_pairs={{12,0},{14,2},{13,1},{15,3},{28,16},{30,18},{29,17},{31,19}} | collective-permute-start | bytes 43016 | tf_op jit(solution)/shard_map/ppermute | solution.py:296
  12.7 0.7 %collective-permute-start.4 = (bf16[2,3584]{1,0:T(2,128)(2,1)S(1)}, bf16[2,3584]{1,0:T(2,128)(2,1)S(1)}, u32[]{:S(2)}, u32[]{:S(2)}) collective-permute-start(bf16[2,3584]{1,0:T(2,128)(2,1)S(1)} %get-tuple-element.23), channel_id=1, source_target_pairs={{12,2},{14,0},{13,3},{15,1},{28,18},{30,16},{29,19},{31,17}} | collective-permute-start | bytes 43016 | tf_op jit(solution)/shard_map/ppermute | solution.py:296
  13.3 0.7 %collective-permute-start.5 = (bf16[2,3584]{1,0:T(2,128)(2,1)S(1)}, bf16[2,3584]{1,0:T(2,128)(2,1)S(1)}, u32[]{:S(2)}, u32[]{:S(2)}) collective-permute-start(bf16[2,3584]{1,0:T(2,128)(2,1)S(1)} %get-tuple-element.24), channel_id=1, source_target_pairs={{12,4},{14,6},{13,5},{15,7},{28,20},{30,22},{29,21},{31,23}} | collective-permute-start | bytes 43016 | tf_op jit(solution)/shard_map/ppermute | solution.py:296
  14.0 0.7 %collective-permute-start.6 = (bf16[2,3584]{1,0:T(2,128)(2,1)S(1)}, bf16[2,3584]{1,0:T(2,128)(2,1)S(1)}, u32[]{:S(2)}, u32[]{:S(2)}) collective-permute-start(bf16[2,3584]{1,0:T(2,128)(2,1)S(1)} %get-tuple-element.25), channel_id=1, source_target_pairs={{12,6},{14,4},{13,7},{15,5},{28,22},{30,20},{29,23},{31,21}} | collective-permute-start | bytes 43016 | tf_op jit(solution)/shard_map/ppermute | solution.py:296
  14.7 1.3 %collective-permute-start.7 = (bf16[2,3584]{1,0:T(2,128)(2,1)S(1)}, bf16[2,3584]{1,0:T(2,128)(2,1)S(1)}, u32[]{:S(2)}, u32[]{:S(2)}) collective-permute-start(bf16[2,3584]{1,0:T(2,128)(2,1)S(1)} %get-tuple-element.26), channel_id=1, source_target_pairs={{12,8},{14,10},{13,9},{15,11},{28,24},{30,26},{29,25},{31,27}} | collective-permute-start | bytes 43016 | tf_op jit(solution)/shard_map/ppermute | solution.py:296
  16.0 0.0 collective-permute-done.3.refs_0_
  16.0 1.3 %collective-permute-start.8 = (bf16[2,3584]{1,0:T(2,128)(2,1)S(1)}, bf16[2,3584]{1,0:T(2,128)(2,1)S(1)}, u32[]{:S(2)}, u32[]{:S(2)}) collective-permute-start(bf16[2,3584]{1,0:T(2,128)(2,1)S(1)} %get-tuple-element.27), channel_id=1, source_target_pairs={{12,10},{14,8},{13,11},{15,9},{28,26},{30,24},{29,27},{31,25}} | collective-permute-start | bytes 43016 | tf_op jit(solution)/shard_map/ppermute | solution.py:296
  17.3 0.0 collective-permute-done.4.refs_1_
  17.3 0.0 collective-permute-done.5.refs_2_
  17.3 0.0 collective-permute-done.6.refs_3_
  17.3 18.9 %collective-permute-done.7.refs_4_ = bf16[2,3584]{1,0:T(2,128)(2,1)S(1)} collective-permute-done((bf16[2,3584]{1,0:T(2,128)(2,1)S(1)}, bf16[2,3584]{1,0:T(2,128)(2,1)S(1)}, u32[]{:S(2)}, u32[]{:S(2)}) %collective-permute-start.7) | collective-permute-done | bytes 14368 | tf_op jit(solution)/shard_map/ppermute | solution.py:296
  36.2 2.2 %collective-permute-done.8.refs_5_ = bf16[2,3584]{1,0:T(2,128)(2,1)S(1)} collective-permute-done((bf16[2,3584]{1,0:T(2,128)(2,1)S(1)}, bf16[2,3584]{1,0:T(2,128)(2,1)S(1)}, u32[]{:S(2)}, u32[]{:S(2)}) %collective-permute-start.8) | collective-permute-done | bytes 14368 | tf_op jit(solution)/shard_map/ppermute | solution.py:296
  38.4 0.6 %shard_map.107 = (bf16[2,2048]{1,0:T(2,128)(2,1)}, bf16[2,7168]{1,0:T(2,128)(2,1)}) custom-call(bf16[2,2048]{1,0:T(2,128)(2,1)S(1)} %get-tuple-element.18.attended, bf16[2,3584]{1,0:T(2,128)(2,1)S(1)} %collective-permute-done.3.refs_0_, bf16[2,3584]{1,0:T(2,128)(2,1)S(1)} %collective-permute-done.4.refs_1_, ...), custom_call_target="tpu_custom_call" | custom-call | tf_op jit(solution)/shard_map/pallas_call | solution.py:311
  (2 shorter events, 0.1 us)
Async XLA Ops:
  9.1 2.9 %collective-permute-start.2 = (bf16[4,2,2176]{2,1,0:T(2,128)(2,1)S(1)}, bf16[4,2,2176]{2,1,0:T(2,128)(2,1)S(1)}, u32[]{:S(2)}, u32[]{:S(2)}) collective-permute-start(bf16[4,2,2176]{2,1,0:T(2,128)(2,1)S(1)} %get-tuple-element.30._), channel_id=1, source_target_pairs={{8,12},{10,14},{9,13},{11,15},{24,28},{26,30},{25,29},{27,31}} | collective-permute-start | bytes 104456 | tf_op jit(solution)/shard_map/ppermute | solution.py:262
  10.3 1.6 %collective-permute-start.1 = (bf16[4,2,2176]{2,1,0:T(2,128)(2,1)S(1)}, bf16[4,2,2176]{2,1,0:T(2,128)(2,1)S(1)}, u32[]{:S(2)}, u32[]{:S(2)}) collective-permute-start(bf16[4,2,2176]{2,1,0:T(2,128)(2,1)S(1)} %get-tuple-element.30._), channel_id=1, source_target_pairs={{4,12},{6,14},{5,13},{7,15},{20,28},{22,30},{21,29},{23,31}} | collective-permute-start | bytes 104456 | tf_op jit(solution)/shard_map/ppermute | solution.py:262
  11.0 0.9 %collective-permute-start = (bf16[4,2,2176]{2,1,0:T(2,128)(2,1)S(1)}, bf16[4,2,2176]{2,1,0:T(2,128)(2,1)S(1)}, u32[]{:S(2)}, u32[]{:S(2)}) collective-permute-start(bf16[4,2,2176]{2,1,0:T(2,128)(2,1)S(1)} %get-tuple-element.30._), channel_id=1, source_target_pairs={{0,12},{2,14},{1,13},{3,15},{16,28},{18,30},{17,29},{19,31}} | collective-permute-start | bytes 104456 | tf_op jit(solution)/shard_map/ppermute | solution.py:262
  12.0 4.0 %collective-permute-start.3 = (bf16[2,3584]{1,0:T(2,128)(2,1)S(1)}, bf16[2,3584]{1,0:T(2,128)(2,1)S(1)}, u32[]{:S(2)}, u32[]{:S(2)}) collective-permute-start(bf16[2,3584]{1,0:T(2,128)(2,1)S(1)} %get-tuple-element.22), channel_id=1, source_target_pairs={{12,0},{14,2},{13,1},{15,3},{28,16},{30,18},{29,17},{31,19}} | collective-permute-start | bytes 43016 | tf_op jit(solution)/shard_map/ppermute | solution.py:296
  12.7 4.6 %collective-permute-start.4 = (bf16[2,3584]{1,0:T(2,128)(2,1)S(1)}, bf16[2,3584]{1,0:T(2,128)(2,1)S(1)}, u32[]{:S(2)}, u32[]{:S(2)}) collective-permute-start(bf16[2,3584]{1,0:T(2,128)(2,1)S(1)} %get-tuple-element.23), channel_id=1, source_target_pairs={{12,2},{14,0},{13,3},{15,1},{28,18},{30,16},{29,19},{31,17}} | collective-permute-start | bytes 43016 | tf_op jit(solution)/shard_map/ppermute | solution.py:296
  13.3 4.0 %collective-permute-start.5 = (bf16[2,3584]{1,0:T(2,128)(2,1)S(1)}, bf16[2,3584]{1,0:T(2,128)(2,1)S(1)}, u32[]{:S(2)}, u32[]{:S(2)}) collective-permute-start(bf16[2,3584]{1,0:T(2,128)(2,1)S(1)} %get-tuple-element.24), channel_id=1, source_target_pairs={{12,4},{14,6},{13,5},{15,7},{28,20},{30,22},{29,21},{31,23}} | collective-permute-start | bytes 43016 | tf_op jit(solution)/shard_map/ppermute | solution.py:296
  14.0 3.3 %collective-permute-start.6 = (bf16[2,3584]{1,0:T(2,128)(2,1)S(1)}, bf16[2,3584]{1,0:T(2,128)(2,1)S(1)}, u32[]{:S(2)}, u32[]{:S(2)}) collective-permute-start(bf16[2,3584]{1,0:T(2,128)(2,1)S(1)} %get-tuple-element.25), channel_id=1, source_target_pairs={{12,6},{14,4},{13,7},{15,5},{28,22},{30,20},{29,23},{31,21}} | collective-permute-start | bytes 43016 | tf_op jit(solution)/shard_map/ppermute | solution.py:296
  14.7 21.5 %collective-permute-start.7 = (bf16[2,3584]{1,0:T(2,128)(2,1)S(1)}, bf16[2,3584]{1,0:T(2,128)(2,1)S(1)}, u32[]{:S(2)}, u32[]{:S(2)}) collective-permute-start(bf16[2,3584]{1,0:T(2,128)(2,1)S(1)} %get-tuple-element.26), channel_id=1, source_target_pairs={{12,8},{14,10},{13,9},{15,11},{28,24},{30,26},{29,25},{31,27}} | collective-permute-start | bytes 43016 | tf_op jit(solution)/shard_map/ppermute | solution.py:296
  16.0 22.4 %collective-permute-start.8 = (bf16[2,3584]{1,0:T(2,128)(2,1)S(1)}, bf16[2,3584]{1,0:T(2,128)(2,1)S(1)}, u32[]{:S(2)}, u32[]{:S(2)}) collective-permute-start(bf16[2,3584]{1,0:T(2,128)(2,1)S(1)} %get-tuple-element.27), channel_id=1, source_target_pairs={{12,10},{14,8},{13,11},{15,9},{28,26},{30,24},{29,27},{31,25}} | collective-permute-start | bytes 43016 | tf_op jit(solution)/shard_map/ppermute | solution.py:296

commit v7 on v6

--- a/solution.py
+++ b/solution.py
@@ -12,11 +12,12 @@
 STEPS = 2
 TAIL = 128
 EPS = 1e-05
-EARLY = 2048
+EARLY = 1792
 DEPTH = 512
-SLOTS = 2
+SHORT = 256
+SLOTS = 3
 WIDTH = 512
-SHARES = (4, 2, 1, 0)
+SHARES = (3, 2, 1, 1)
 
 
 def pair(squares):
@@ -40,67 +41,59 @@
             c.wait()
 
 
-def blank_kernel(out):
-    out[...] = jnp.zeros_like(out)
-
-
-def attend_kernel(serving, *refs):
+def blank_kernel(*outs):
+    for out in outs:
+        out[...] = jnp.zeros_like(out)
+
+
+def attend_kernel(*refs):
     sources, (attended, sent), held, sems = refs[:7], refs[7:9], refs[9:16], refs[16]
     lengths, q, kv, keys, values, residual, gain = held
-    owner = lax.axis_index("wide") < serving
     heads, hist, _ = keys.shape
     width = q.shape[1]
     group = width // (heads * HEAD_SIZE)
-
-    @pl.when(jnp.logical_not(owner))
-    def _():
-        attended[...] = jnp.zeros_like(attended)
-        sent[...] = jnp.zeros_like(sent)
-
-    @pl.when(owner)
-    def _():
-        copies = [
-            pltpu.make_async_copy(source, place, sems.at[i])
-            for i, (source, place) in enumerate(zip(sources, held))
-        ]
-        for c in copies:
-            c.start()
-        for c in copies:
-            c.wait()
-        length = lengths[0, 0]
-        slot = lax.broadcasted_iota(jnp.int32, (hist, HEAD_SIZE), 0)
-        rows = group * STEPS
-        place = lax.broadcasted_iota(jnp.int32, (rows, hist), 1)
-        step = lax.broadcasted_iota(jnp.int32, (rows, hist), 0) % STEPS
-        first = hist - STEPS
-        seen = (place < length) | ((place >= first) & (place - first <= step))
-        squares = jnp.zeros((STEPS, 1), jnp.float32)
-        for h in range(heads):
-            lanes = slice(h * HEAD_SIZE, (h + 1) * HEAD_SIZE)
-            k, v = keys[h], values[h]
-            for t in range(STEPS):
-                k = jnp.where(slot == first + t, kv[t, 0:1, lanes], k)
-                v = jnp.where(slot == first + t, kv[t, 1:2, lanes], v)
-            cols = [(h * group + g) * HEAD_SIZE for g in range(group)]
-            query = jnp.concatenate(
-                [q[:, c : c + HEAD_SIZE].astype(jnp.float32) for c in cols], 0
-            ).astype(jnp.bfloat16)
-            scores = lax.dot_general(
-                query, k, (((1,), (1,)), ((), ())), preferred_element_type=jnp.float32
-            ) * (1.0 / HEAD_SIZE**0.5)
-            scores = jnp.where(seen, scores, -1e30)
-            top = jnp.max(scores, -1, keepdims=True)
-            e = jnp.where(seen, jnp.exp(scores - top), 0.0)
-            weights = (e / jnp.sum(e, -1, keepdims=True)).astype(jnp.bfloat16)
-            out = jnp.dot(weights, v, preferred_element_type=jnp.float32)
-            for g, c in enumerate(cols):
-                here = slice(c, c + HEAD_SIZE)
-                got = out[g * STEPS : (g + 1) * STEPS].astype(jnp.bfloat16)
-                attended[:, here] = got
-                mixed = residual[:, here].astype(jnp.float32) + got.astype(jnp.float32)
-                squares += jnp.sum(mixed * mixed, -1, keepdims=True)
-                sent[:, here] = (mixed * gain[:, here]).astype(jnp.bfloat16)
-        sent[:, width:] = pair(squares)
+    copies = [
+        pltpu.make_async_copy(source, place, sems.at[i])
+        for i, (source, place) in enumerate(zip(sources, held))
+    ]
+    for c in copies:
+        c.start()
+    for c in copies:
+        c.wait()
+    length = lengths[0, 0]
+    slot = lax.broadcasted_iota(jnp.int32, (hist, HEAD_SIZE), 0)
+    rows = group * STEPS
+    place = lax.broadcasted_iota(jnp.int32, (rows, hist), 1)
+    step = lax.broadcasted_iota(jnp.int32, (rows, hist), 0) % STEPS
+    first = hist - STEPS
+    seen = (place < length) | ((place >= first) & (place - first <= step))
+    squares = jnp.zeros((STEPS, 1), jnp.float32)
+    for h in range(heads):
+        lanes = slice(h * HEAD_SIZE, (h + 1) * HEAD_SIZE)
+        k, v = keys[h], values[h]
+        for t in range(STEPS):
+            k = jnp.where(slot == first + t, kv[t, 0:1, lanes], k)
+            v = jnp.where(slot == first + t, kv[t, 1:2, lanes], v)
+        cols = [(h * group + g) * HEAD_SIZE for g in range(group)]
+        query = jnp.concatenate(
+            [q[:, c : c + HEAD_SIZE].astype(jnp.float32) for c in cols], 0
+        ).astype(jnp.bfloat16)
+        scores = lax.dot_general(
+            query, k, (((1,), (1,)), ((), ())), preferred_element_type=jnp.float32
+        ) * (1.0 / HEAD_SIZE**0.5)
+        scores = jnp.where(seen, scores, -1e30)
+        top = jnp.max(scores, -1, keepdims=True)
+        e = jnp.where(seen, jnp.exp(scores - top), 0.0)
+        weights = (e / jnp.sum(e, -1, keepdims=True)).astype(jnp.bfloat16)
+        out = jnp.dot(weights, v, preferred_element_type=jnp.float32)
+        for g, c in enumerate(cols):
+            here = slice(c, c + HEAD_SIZE)
+            got = out[g * STEPS : (g + 1) * STEPS].astype(jnp.bfloat16)
+            attended[:, here] = got
+            mixed = residual[:, here].astype(jnp.float32) + got.astype(jnp.float32)
+            squares += jnp.sum(mixed * mixed, -1, keepdims=True)
+            sent[:, here] = (mixed * gain[:, here]).astype(jnp.bfloat16)
+    sent[:, width:] = pair(squares)
 
 
 def forward_kernel(blocks, workers, narrow, *refs):
@@ -112,15 +105,20 @@
     half = features // narrow
     early = gate_held.shape[0]
     room, _, depth, _ = slots.shape
-    total = (features - early) // depth
+    blocks_at = [early]
+    while features - blocks_at[-1] > 2 * depth:
+        blocks_at.append(blocks_at[-1] + depth)
+    blocks_at += range(blocks_at[-1] + SHORT, features + 1, SHORT)
+    total = len(blocks_at) - 1
     width = WIDTH if columns % WIDTH == 0 else columns
     spans = [slice(at, at + width) for at in range(0, columns, width)]
 
     def stream(j):
         s = j % room
-        here = pl.ds(early + j * depth, depth)
+        at, size = blocks_at[j], blocks_at[j + 1] - blocks_at[j]
+        here, there = pl.ds(at, size), pl.ds(0, size)
         return [
-            pltpu.make_async_copy(m.at[here], slots.at[s, i], sems.at[s, i])
+            pltpu.make_async_copy(m.at[here], slots.at[s, i, there], sems.at[s, i])
             for i, m in enumerate((gate, up))
         ]
 
@@ -155,7 +153,8 @@
 
         waiting = list(spans)
         for j in range(total):
-            for _ in range(-(-len(spans) * SHARES[min(j, len(SHARES) - 1)] // sum(SHARES))):
+            share = SHARES[j] if j < len(SHARES) else 0
+            for _ in range(-(-len(spans) * share // sum(SHARES))):
                 if waiting:
                     here = waiting.pop(0)
                     for i, held in enumerate((gate_held, up_held)):
@@ -166,10 +165,10 @@
                         add(i, here, x[:, :early], held[:, here])
             for copy in stream(j):
                 copy.wait()
-            at = early + j * depth
+            at, end = blocks_at[j], blocks_at[j + 1]
             for here in spans:
                 for i in range(2):
-                    add(i, here, x[:, at : at + depth], slots[j % room, i, :, here])
+                    add(i, here, x[:, at:end], slots[j % room, i, : end - at, here])
             if j + room < total:
                 for copy in stream(j + room):
                     copy.start()
@@ -228,36 +227,40 @@
         residual.reshape(STEPS, half),
         gain.reshape(1, half),
     )
-    attended, sent = pl.pallas_call(
-        functools.partial(attend_kernel, serving),
-        out_shape=(
-            pltpu.VMEM((STEPS, half), jnp.bfloat16),
-            jax.ShapeDtypeStruct((STEPS, half + TAIL), jnp.bfloat16),
-        ),
-        in_specs=[hbm] * 7,
-        out_specs=(vmem, vmem),
-        scratch_shapes=[]
-        + [(pltpu.SMEM if o.dtype == jnp.int32 else pltpu.VMEM)(o.shape, o.dtype) for o in operands]
-        + [pltpu.SemaphoreType.DMA((7,))],
-        compiler_params=pltpu.CompilerParams(vmem_limit_bytes=8 << 20),
-    )(operands[0], *map(in_hbm, operands[1:]))
-
     groups = [
         [w * narrow + n for w in range(at, at + workers) for n in range(narrow)]
         for at in range(0, wide, workers)
     ]
-    blank = pl.pallas_call(
-        blank_kernel,
-        out_shape=jax.ShapeDtypeStruct((workers * narrow, *sent.shape), jnp.bfloat16),
-        out_specs=vmem,
-        compiler_params=pltpu.CompilerParams(vmem_limit_bytes=8 << 20),
+    shapes = (
+        jax.ShapeDtypeStruct((STEPS, half), jnp.bfloat16),
+        jax.ShapeDtypeStruct((workers * narrow, STEPS, half + TAIL), jnp.bfloat16),
     )
-    block = lax.cond(
-        owner,
-        lambda s: lax.all_gather(s, ("wide", "narrow"), axis=0, axis_index_groups=groups),
-        lambda s: blank(),
-        sent,
-    )
+
+    def serve(*operands):
+        attended, sent = pl.pallas_call(
+            attend_kernel,
+            out_shape=(shapes[0], jax.ShapeDtypeStruct(shapes[1].shape[1:], jnp.bfloat16)),
+            in_specs=[hbm] * 7,
+            out_specs=(vmem, vmem),
+            scratch_shapes=[
+                (pltpu.SMEM if o.dtype == jnp.int32 else pltpu.VMEM)(o.shape, o.dtype)
+                for o in operands
+            ]
+            + [pltpu.SemaphoreType.DMA((7,))],
+            compiler_params=pltpu.CompilerParams(vmem_limit_bytes=8 << 20),
+        )(operands[0], *map(in_hbm, operands[1:]))
+        gathered = lax.all_gather(sent, ("wide", "narrow"), axis=0, axis_index_groups=groups)
+        return attended, gathered
+
+    def rest(*operands):
+        return pl.pallas_call(
+            blank_kernel,
+            out_shape=shapes,
+            out_specs=(vmem, vmem),
+            compiler_params=pltpu.CompilerParams(vmem_limit_bytes=8 << 20),
+        )()
+
+    attended, block = lax.cond(owner, serve, rest, *operands)
     arrived = [
         lax.ppermute(block, "wide", [(b * workers + j, serving + j) for j in range(workers)])
         for b in range(blocks)
@@ -287,7 +290,7 @@
             pltpu.VMEM((SLOTS, 2, depth, columns), jnp.bfloat16),
             pltpu.SemaphoreType.DMA((SLOTS, 2)),
         ],
-        compiler_params=pltpu.CompilerParams(vmem_limit_bytes=16 << 20),
+        compiler_params=pltpu.CompilerParams(vmem_limit_bytes=22 << 20),
     )(*arrived, *held, gate, up)
     back = [[None] * workers for _ in range(blocks)]
     for b in range(blocks):

time: 39.3 us -> 39.7 us (1.010)
  between operations: 1.41 us -> 0.76 us
  Pallas kernels: 3.24 us -> 3.88 us
  waiting for transfers between devices: 21.3 us -> 21.7 us
    pallas_call x1, Pallas kernels: 2.55 us -> 3.18 us  [serve(): pl.pallas_call(attend_kernel, out_shape=(shapes[0], jax.ShapeDtypeStruct(...]
where the time goes in v7:
time: 39.7 us; the launch traced here: 39.4 us
  waiting for transfers between devices  21.7 us (55%)
  starting transfers between devices  7.84 us (20%)
  blocking collectives  5.2 us (13%)
  Pallas kernels  3.88 us (10%)
  between operations  0.76 us (2%)
    ppermute x6, waiting for transfers between devices, shards(): lax.ppermute(hidden[(blocks - 1 - b) * workers + s], 'wide', pairs)  21.5 us
    ppermute x6, starting transfers between devices, shards(): lax.ppermute(hidden[(blocks - 1 - b) * workers + s], 'wide', pairs)  5.23 us
    all_gather x1, blocking collectives, serve(): lax.all_gather(sent, ('wide', 'narrow'), axis=0, axis_index_groups=groups)  5.2 us
    pallas_call x1, Pallas kernels, serve(): pl.pallas_call(attend_kernel, out_shape=(shapes[0], jax.ShapeDtypeStruct(...  3.18 us
    ppermute x3, starting transfers between devices, shards(): lax.ppermute(block, 'wide', [(b * workers + j, serving + j) for j in rang...  2.61 us
  transfers between devices with their start and end apart: 9, of which 3 were waited for; matrix products, arithmetic and copies ran while one was open for 0% of the time, Pallas kernels for 0%

profile of v7, /device:TPU:16, one launch (start us, length us, event | category | flops | bytes accessed | tf_op | source)
XLA Modules:
  0.0 39.4 jit_solution(13885451815065852472)
XLA Ops:
  0.6 8.4 %conditional.1 = ((bf16[2,2048]{1,0:T(2,128)(2,1)S(1)}, bf16[4,2,2176]{2,1,0:T(2,128)(2,1)S(1)})) conditional(s32[]{:T(128)} %convert_element_type.3, () %tuple.15, (s32[1]{0:T(128)}, bf16[2,1,2048]{2,0,1:T(2,128)(2,1)}, bf16[2,1,2,512]{3,2,1,0:T(2,128)(2,1)}, bf16[1,4,128,128]{3,2,1,0:T(8,128)(2,1)}, bf16[1,4,128,128]{3,2,1,0:T(8,128)(2,1)}, ...), branch_computations={%region_0.0_spmd, %region_1.0_spmd} | conditional | bytes 43544 | solution.py:263
  0.7 3.2 %branch_1_fun.1 = (bf16[2,2048]{1,0:T(2,128)(2,1)S(1)}, bf16[2,2176]{1,0:T(2,128)(2,1)S(1)}) custom-call(s32[1,1]{1,0:T(1,128)} %bitcast.refs_0_, bf16[2,2048]{1,0:T(2,128)(2,1)} %bitcast.20, bf16[2,2,512]{2,1,0:T(2,128)(2,1)} %bitcast.23, bf16[4,128,128]{2,1,0:T(8,128)(2,1)} %bitcast.18, bf16[4,128,128]{2,1,0:T(8,128)(2,1)} %bitcast.19, ...), custom_call_target="tpu_custom_call" | custom-call | tf_op jit(solution)/shard_map/cond/branch_1_fun/pallas_call | solution.py:240
  3.8 5.2 %all-gather.1 = bf16[4,2,2176]{2,1,0:T(2,128)(2,1)S(1)} all-gather(bf16[1,2,2176]{2,1,0:T(2,128)(2,1)S(1)} %bitcast.13), channel_id=2, replica_groups={{0,1,2,3},{4,5,6,7},{8,9,10,11},{12,13,14,15},{16,17,18,19},{20,21,22,2..., dimensions={0}, use_global_device_ids=true | all-gather | bytes 43520 | tf_op jit(solution)/shard_map/cond/branch_1_fun/all_gather | solution.py:252
  9.0 1.3 %collective-permute-start.2 = (bf16[4,2,2176]{2,1,0:T(2,128)(2,1)S(1)}, bf16[4,2,2176]{2,1,0:T(2,128)(2,1)S(1)}, u32[]{:S(2)}, u32[]{:S(2)}) collective-permute-start(bf16[4,2,2176]{2,1,0:T(2,128)(2,1)S(1)} %get-tuple-element.45._), channel_id=1, source_target_pairs={{8,12},{10,14},{9,13},{11,15},{24,28},{26,30},{25,29},{27,31}} | collective-permute-start | bytes 104456 | tf_op jit(solution)/shard_map/ppermute | solution.py:265
  10.3 0.7 %collective-permute-start.1 = (bf16[4,2,2176]{2,1,0:T(2,128)(2,1)S(1)}, bf16[4,2,2176]{2,1,0:T(2,128)(2,1)S(1)}, u32[]{:S(2)}, u32[]{:S(2)}) collective-permute-start(bf16[4,2,2176]{2,1,0:T(2,128)(2,1)S(1)} %get-tuple-element.45._), channel_id=1, source_target_pairs={{4,12},{6,14},{5,13},{7,15},{20,28},{22,30},{21,29},{23,31}} | collective-permute-start | bytes 104456 | tf_op jit(solution)/shard_map/ppermute | solution.py:265
  11.0 0.7 %collective-permute-start = (bf16[4,2,2176]{2,1,0:T(2,128)(2,1)S(1)}, bf16[4,2,2176]{2,1,0:T(2,128)(2,1)S(1)}, u32[]{:S(2)}, u32[]{:S(2)}) collective-permute-start(bf16[4,2,2176]{2,1,0:T(2,128)(2,1)S(1)} %get-tuple-element.45._), channel_id=1, source_target_pairs={{0,12},{2,14},{1,13},{3,15},{16,28},{18,30},{17,29},{19,31}} | collective-permute-start | bytes 104456 | tf_op jit(solution)/shard_map/ppermute | solution.py:265
  11.7 0.2 collective-permute-done.2.refs_2_
  11.9 0.0 collective-permute-done.1.refs_1_
  11.9 0.0 collective-permute-done.refs_0_
  11.9 0.1 shard_map.112
  12.0 0.7 %collective-permute-start.3 = (bf16[2,3584]{1,0:T(2,128)(2,1)S(1)}, bf16[2,3584]{1,0:T(2,128)(2,1)S(1)}, u32[]{:S(2)}, u32[]{:S(2)}) collective-permute-start(bf16[2,3584]{1,0:T(2,128)(2,1)S(1)} %get-tuple-element.48), channel_id=1, source_target_pairs={{12,0},{14,2},{13,1},{15,3},{28,16},{30,18},{29,17},{31,19}} | collective-permute-start | bytes 43016 | tf_op jit(solution)/shard_map/ppermute | solution.py:299
  12.7 0.7 %collective-permute-start.4 = (bf16[2,3584]{1,0:T(2,128)(2,1)S(1)}, bf16[2,3584]{1,0:T(2,128)(2,1)S(1)}, u32[]{:S(2)}, u32[]{:S(2)}) collective-permute-start(bf16[2,3584]{1,0:T(2,128)(2,1)S(1)} %get-tuple-element.49), channel_id=1, source_target_pairs={{12,2},{14,0},{13,3},{15,1},{28,18},{30,16},{29,19},{31,17}} | collective-permute-start | bytes 43016 | tf_op jit(solution)/shard_map/ppermute | solution.py:299
  13.3 0.7 %collective-permute-start.5 = (bf16[2,3584]{1,0:T(2,128)(2,1)S(1)}, bf16[2,3584]{1,0:T(2,128)(2,1)S(1)}, u32[]{:S(2)}, u32[]{:S(2)}) collective-permute-start(bf16[2,3584]{1,0:T(2,128)(2,1)S(1)} %get-tuple-element.50), channel_id=1, source_target_pairs={{12,4},{14,6},{13,5},{15,7},{28,20},{30,22},{29,21},{31,23}} | collective-permute-start | bytes 43016 | tf_op jit(solution)/shard_map/ppermute | solution.py:299
  14.0 0.7 %collective-permute-start.6 = (bf16[2,3584]{1,0:T(2,128)(2,1)S(1)}, bf16[2,3584]{1,0:T(2,128)(2,1)S(1)}, u32[]{:S(2)}, u32[]{:S(2)}) collective-permute-start(bf16[2,3584]{1,0:T(2,128)(2,1)S(1)} %get-tuple-element.51), channel_id=1, source_target_pairs={{12,6},{14,4},{13,7},{15,5},{28,22},{30,20},{29,23},{31,21}} | collective-permute-start | bytes 43016 | tf_op jit(solution)/shard_map/ppermute | solution.py:299
  14.7 1.3 %collective-permute-start.7 = (bf16[2,3584]{1,0:T(2,128)(2,1)S(1)}, bf16[2,3584]{1,0:T(2,128)(2,1)S(1)}, u32[]{:S(2)}, u32[]{:S(2)}) collective-permute-start(bf16[2,3584]{1,0:T(2,128)(2,1)S(1)} %get-tuple-element.52), channel_id=1, source_target_pairs={{12,8},{14,10},{13,9},{15,11},{28,24},{30,26},{29,25},{31,27}} | collective-permute-start | bytes 43016 | tf_op jit(solution)/shard_map/ppermute | solution.py:299
  16.0 0.0 collective-permute-done.3.refs_0_
  16.0 1.3 %collective-permute-start.8 = (bf16[2,3584]{1,0:T(2,128)(2,1)S(1)}, bf16[2,3584]{1,0:T(2,128)(2,1)S(1)}, u32[]{:S(2)}, u32[]{:S(2)}) collective-permute-start(bf16[2,3584]{1,0:T(2,128)(2,1)S(1)} %get-tuple-element.53), channel_id=1, source_target_pairs={{12,10},{14,8},{13,11},{15,9},{28,26},{30,24},{29,27},{31,25}} | collective-permute-start | bytes 43016 | tf_op jit(solution)/shard_map/ppermute | solution.py:299
  17.3 0.0 collective-permute-done.4.refs_1_
  17.3 0.0 collective-permute-done.5.refs_2_
  17.3 0.0 collective-permute-done.6.refs_3_
  17.3 19.2 %collective-permute-done.7.refs_4_ = bf16[2,3584]{1,0:T(2,128)(2,1)S(1)} collective-permute-done((bf16[2,3584]{1,0:T(2,128)(2,1)S(1)}, bf16[2,3584]{1,0:T(2,128)(2,1)S(1)}, u32[]{:S(2)}, u32[]{:S(2)}) %collective-permute-start.7) | collective-permute-done | bytes 14368 | tf_op jit(solution)/shard_map/ppermute | solution.py:299
  36.5 2.2 %collective-permute-done.8.refs_5_ = bf16[2,3584]{1,0:T(2,128)(2,1)S(1)} collective-permute-done((bf16[2,3584]{1,0:T(2,128)(2,1)S(1)}, bf16[2,3584]{1,0:T(2,128)(2,1)S(1)}, u32[]{:S(2)}, u32[]{:S(2)}) %collective-permute-start.8) | collective-permute-done | bytes 14368 | tf_op jit(solution)/shard_map/ppermute | solution.py:299
  38.8 0.6 %shard_map.113 = (bf16[2,2048]{1,0:T(2,128)(2,1)}, bf16[2,7168]{1,0:T(2,128)(2,1)}) custom-call(bf16[2,2048]{1,0:T(2,128)(2,1)S(1)} %get-tuple-element.44.attended, bf16[2,3584]{1,0:T(2,128)(2,1)S(1)} %collective-permute-done.3.refs_0_, bf16[2,3584]{1,0:T(2,128)(2,1)S(1)} %collective-permute-done.4.refs_1_, ...), custom_call_target="tpu_custom_call" | custom-call | tf_op jit(solution)/shard_map/pallas_call | solution.py:314
  (1 shorter events, 0.0 us)
Async XLA Ops:
  9.0 2.9 %collective-permute-start.2 = (bf16[4,2,2176]{2,1,0:T(2,128)(2,1)S(1)}, bf16[4,2,2176]{2,1,0:T(2,128)(2,1)S(1)}, u32[]{:S(2)}, u32[]{:S(2)}) collective-permute-start(bf16[4,2,2176]{2,1,0:T(2,128)(2,1)S(1)} %get-tuple-element.45._), channel_id=1, source_target_pairs={{8,12},{10,14},{9,13},{11,15},{24,28},{26,30},{25,29},{27,31}} | collective-permute-start | bytes 104456 | tf_op jit(solution)/shard_map/ppermute | solution.py:265
  10.3 1.6 %collective-permute-start.1 = (bf16[4,2,2176]{2,1,0:T(2,128)(2,1)S(1)}, bf16[4,2,2176]{2,1,0:T(2,128)(2,1)S(1)}, u32[]{:S(2)}, u32[]{:S(2)}) collective-permute-start(bf16[4,2,2176]{2,1,0:T(2,128)(2,1)S(1)} %get-tuple-element.45._), channel_id=1, source_target_pairs={{4,12},{6,14},{5,13},{7,15},{20,28},{22,30},{21,29},{23,31}} | collective-permute-start | bytes 104456 | tf_op jit(solution)/shard_map/ppermute | solution.py:265
  11.0 0.9 %collective-permute-start = (bf16[4,2,2176]{2,1,0:T(2,128)(2,1)S(1)}, bf16[4,2,2176]{2,1,0:T(2,128)(2,1)S(1)}, u32[]{:S(2)}, u32[]{:S(2)}) collective-permute-start(bf16[4,2,2176]{2,1,0:T(2,128)(2,1)S(1)} %get-tuple-element.45._), channel_id=1, source_target_pairs={{0,12},{2,14},{1,13},{3,15},{16,28},{18,30},{17,29},{19,31}} | collective-permute-start | bytes 104456 | tf_op jit(solution)/shard_map/ppermute | solution.py:265
  12.0 4.0 %collective-permute-start.3 = (bf16[2,3584]{1,0:T(2,128)(2,1)S(1)}, bf16[2,3584]{1,0:T(2,128)(2,1)S(1)}, u32[]{:S(2)}, u32[]{:S(2)}) collective-permute-start(bf16[2,3584]{1,0:T(2,128)(2,1)S(1)} %get-tuple-element.48), channel_id=1, source_target_pairs={{12,0},{14,2},{13,1},{15,3},{28,16},{30,18},{29,17},{31,19}} | collective-permute-start | bytes 43016 | tf_op jit(solution)/shard_map/ppermute | solution.py:299
  12.7 4.6 %collective-permute-start.4 = (bf16[2,3584]{1,0:T(2,128)(2,1)S(1)}, bf16[2,3584]{1,0:T(2,128)(2,1)S(1)}, u32[]{:S(2)}, u32[]{:S(2)}) collective-permute-start(bf16[2,3584]{1,0:T(2,128)(2,1)S(1)} %get-tuple-element.49), channel_id=1, source_target_pairs={{12,2},{14,0},{13,3},{15,1},{28,18},{30,16},{29,19},{31,17}} | collective-permute-start | bytes 43016 | tf_op jit(solution)/shard_map/ppermute | solution.py:299
  13.3 4.0 %collective-permute-start.5 = (bf16[2,3584]{1,0:T(2,128)(2,1)S(1)}, bf16[2,3584]{1,0:T(2,128)(2,1)S(1)}, u32[]{:S(2)}, u32[]{:S(2)}) collective-permute-start(bf16[2,3584]{1,0:T(2,128)(2,1)S(1)} %get-tuple-element.50), channel_id=1, source_target_pairs={{12,4},{14,6},{13,5},{15,7},{28,20},{30,22},{29,21},{31,23}} | collective-permute-start | bytes 43016 | tf_op jit(solution)/shard_map/ppermute | solution.py:299
  14.0 3.3 %collective-permute-start.6 = (bf16[2,3584]{1,0:T(2,128)(2,1)S(1)}, bf16[2,3584]{1,0:T(2,128)(2,1)S(1)}, u32[]{:S(2)}, u32[]{:S(2)}) collective-permute-start(bf16[2,3584]{1,0:T(2,128)(2,1)S(1)} %get-tuple-element.51), channel_id=1, source_target_pairs={{12,6},{14,4},{13,7},{15,5},{28,22},{30,20},{29,23},{31,21}} | collective-permute-start | bytes 43016 | tf_op jit(solution)/shard_map/ppermute | solution.py:299
  14.7 21.9 %collective-permute-start.7 = (bf16[2,3584]{1,0:T(2,128)(2,1)S(1)}, bf16[2,3584]{1,0:T(2,128)(2,1)S(1)}, u32[]{:S(2)}, u32[]{:S(2)}) collective-permute-start(bf16[2,3584]{1,0:T(2,128)(2,1)S(1)} %get-tuple-element.52), channel_id=1, source_target_pairs={{12,8},{14,10},{13,9},{15,11},{28,24},{30,26},{29,25},{31,27}} | collective-permute-start | bytes 43016 | tf_op jit(solution)/shard_map/ppermute | solution.py:299
  16.0 22.8 %collective-permute-start.8 = (bf16[2,3584]{1,0:T(2,128)(2,1)S(1)}, bf16[2,3584]{1,0:T(2,128)(2,1)S(1)}, u32[]{:S(2)}, u32[]{:S(2)}) collective-permute-start(bf16[2,3584]{1,0:T(2,128)(2,1)S(1)} %get-tuple-element.53), channel_id=1, source_target_pairs={{12,10},{14,8},{13,11},{15,9},{28,26},{30,24},{29,27},{31,25}} | collective-permute-start | bytes 43016 | tf_op jit(solution)/shard_map/ppermute | solution.py:299

commit v8 on v7

--- a/solution.py
+++ b/solution.py
@@ -12,12 +12,10 @@
 STEPS = 2
 TAIL = 128
 EPS = 1e-05
-EARLY = 1792
+EARLY = 2048
 DEPTH = 512
-SHORT = 256
-SLOTS = 3
-WIDTH = 512
-SHARES = (3, 2, 1, 1)
+SLOTS = 4
+AHEAD = (2, 0, 1, 0, 1)
 
 
 def pair(squares):
@@ -104,27 +102,25 @@
     features, columns = gate.shape
     half = features // narrow
     early = gate_held.shape[0]
-    room, _, depth, _ = slots.shape
-    blocks_at = [early]
-    while features - blocks_at[-1] > 2 * depth:
-        blocks_at.append(blocks_at[-1] + depth)
-    blocks_at += range(blocks_at[-1] + SHORT, features + 1, SHORT)
-    total = len(blocks_at) - 1
-    width = WIDTH if columns % WIDTH == 0 else columns
-    spans = [slice(at, at + width) for at in range(0, columns, width)]
+    room, _, depth, across = slots.shape
+    units = [(at, c) for at in range(early, features, depth) for c in range(0, columns, across)]
+    cut = across // 512 * 256
+    spans = {
+        c: [slice(p, q) for p, q in ((c, c + cut), (c + cut, c + across)) if p < q]
+        for c in range(0, columns, across)
+    }
 
     def stream(j):
         s = j % room
-        at, size = blocks_at[j], blocks_at[j + 1] - blocks_at[j]
-        here, there = pl.ds(at, size), pl.ds(0, size)
+        here = (pl.ds(units[j][0], depth), pl.ds(units[j][1], across))
         return [
-            pltpu.make_async_copy(m.at[here], slots.at[s, i, there], sems.at[s, i])
+            pltpu.make_async_copy(m.at[here], slots.at[s, i], sems.at[s, i])
             for i, m in enumerate((gate, up))
         ]
 
     @pl.when(me >= 0)
     def _():
-        for j in range(min(room, total)):
+        for j in range(min(room, len(units))):
             for copy in stream(j):
                 copy.start()
         lines, tails = [], []
@@ -151,25 +147,25 @@
             taken.add((i, here.start))
             sums[i, :, here] = product if first else sums[i, :, here] + product
 
-        waiting = list(spans)
-        for j in range(total):
-            share = SHARES[j] if j < len(SHARES) else 0
-            for _ in range(-(-len(spans) * share // sum(SHARES))):
-                if waiting:
-                    here = waiting.pop(0)
-                    for i, held in enumerate((gate_held, up_held)):
-                        add(i, here, x[:, :early], held[:, here])
-            if j == total - 1:
-                for here in waiting:
-                    for i, held in enumerate((gate_held, up_held)):
-                        add(i, here, x[:, :early], held[:, here])
+        waiting = [here for some in spans.values() for here in some]
+
+        def resident(count):
+            for here in waiting[:count]:
+                for i, held in enumerate((gate_held, up_held)):
+                    add(i, here, x[:, :early], held[:, here])
+            del waiting[:count]
+
+        for j, (at, c) in enumerate(units):
+            resident(AHEAD[j] if j < len(AHEAD) else 0)
+            if j == len(units) - 1:
+                resident(len(waiting))
             for copy in stream(j):
                 copy.wait()
-            at, end = blocks_at[j], blocks_at[j + 1]
-            for here in spans:
+            for here in spans[c]:
+                there = slice(here.start - c, here.stop - c)
                 for i in range(2):
-                    add(i, here, x[:, at:end], slots[j % room, i, : end - at, here])
-            if j + room < total:
+                    add(i, here, x[:, at : at + depth], slots[j % room, i, :, there])
+            if j + room < len(units):
                 for copy in stream(j + room):
                     copy.start()
         g, u = sums[0] * r, sums[1] * r
@@ -239,7 +235,10 @@
     def serve(*operands):
         attended, sent = pl.pallas_call(
             attend_kernel,
-            out_shape=(shapes[0], jax.ShapeDtypeStruct(shapes[1].shape[1:], jnp.bfloat16)),
+            out_shape=(
+                pltpu.VMEM(shapes[0].shape, jnp.bfloat16),
+                jax.ShapeDtypeStruct(shapes[1].shape[1:], jnp.bfloat16),
+            ),
             in_specs=[hbm] * 7,
             out_specs=(vmem, vmem),
             scratch_shapes=[
@@ -255,7 +254,7 @@
     def rest(*operands):
         return pl.pallas_call(
             blank_kernel,
-            out_shape=shapes,
+            out_shape=(pltpu.VMEM(shapes[0].shape, jnp.bfloat16), shapes[1]),
             out_specs=(vmem, vmem),
             compiler_params=pltpu.CompilerParams(vmem_limit_bytes=8 << 20),
         )()
@@ -279,6 +278,7 @@
     )(block, gate, up)
     padded = -(-STEPS * serving // 16) * 16
     depth = min(DEPTH, features - early)
+    across = columns // 2 if columns % 512 == 0 else columns
     hidden = pl.pallas_call(
         functools.partial(forward_kernel, blocks, workers, narrow),
         out_shape=[jax.ShapeDtypeStruct((STEPS, columns), jnp.bfloat16)] * serving,
@@ -287,10 +287,10 @@
         scratch_shapes=[
             pltpu.VMEM((padded, features), jnp.bfloat16),
             pltpu.VMEM((2, padded, columns), jnp.float32),
-            pltpu.VMEM((SLOTS, 2, depth, columns), jnp.bfloat16),
+            pltpu.VMEM((SLOTS, 2, depth, across), jnp.bfloat16),
             pltpu.SemaphoreType.DMA((SLOTS, 2)),
         ],
-        compiler_params=pltpu.CompilerParams(vmem_limit_bytes=22 << 20),
+        compiler_params=pltpu.CompilerParams(vmem_limit_bytes=16 << 20),
     )(*arrived, *held, gate, up)
     back = [[None] * workers for _ in range(blocks)]
     for b in range(blocks):

time: 39.7 us -> 39.2 us (0.987)
  waiting for transfers between devices: 21.7 us -> 21.1 us
    ppermute x6, waiting for transfers between devices: 21.5 us -> 20.9 us  [shards(): lax.ppermute(hidden[(blocks - 1 - b) * workers + s], 'wide', pairs)]
where the time goes in v8:
time: 39.2 us; the launch traced here: 38.9 us
  waiting for transfers between devices  21.1 us (54%)
  starting transfers between devices  7.84 us (20%)
  blocking collectives  5.2 us (13%)
  Pallas kernels  3.9 us (10%)
  between operations  0.76 us (2%)
    ppermute x6, waiting for transfers between devices, shards(): lax.ppermute(hidden[(blocks - 1 - b) * workers + s], 'wide', pairs)  20.9 us
    ppermute x6, starting transfers between devices, shards(): lax.ppermute(hidden[(blocks - 1 - b) * workers + s], 'wide', pairs)  5.23 us
    all_gather x1, blocking collectives, serve(): lax.all_gather(sent, ('wide', 'narrow'), axis=0, axis_index_groups=groups)  5.2 us
    pallas_call x1, Pallas kernels, serve(): pl.pallas_call(attend_kernel, out_shape=(pltpu.VMEM(shapes[0].shape, jnp....  3.18 us
    ppermute x3, starting transfers between devices, shards(): lax.ppermute(block, 'wide', [(b * workers + j, serving + j) for j in rang...  2.61 us
  transfers between devices with their start and end apart: 9, of which 3 were waited for; matrix products, arithmetic and copies ran while one was open for 0% of the time, Pallas kernels for 0%

profile of v8, /device:TPU:16, one launch (start us, length us, event | category | flops | bytes accessed | tf_op | source)
XLA Modules:
  0.0 38.9 jit_solution(3964709950651259896)
XLA Ops:
  0.6 8.4 %conditional.1 = ((bf16[2,2048]{1,0:T(2,128)(2,1)S(1)}, bf16[4,2,2176]{2,1,0:T(2,128)(2,1)S(1)})) conditional(s32[]{:T(128)} %convert_element_type.3, () %tuple.15, (s32[1]{0:T(128)}, bf16[2,1,2048]{2,0,1:T(2,128)(2,1)}, bf16[2,1,2,512]{3,2,1,0:T(2,128)(2,1)}, bf16[1,4,128,128]{3,2,1,0:T(8,128)(2,1)}, bf16[1,4,128,128]{3,2,1,0:T(8,128)(2,1)}, ...), branch_computations={%region_0.0_spmd, %region_1.0_spmd} | conditional | bytes 43544 | solution.py:262
  0.7 3.2 %branch_1_fun.1 = (bf16[2,2048]{1,0:T(2,128)(2,1)S(1)}, bf16[2,2176]{1,0:T(2,128)(2,1)S(1)}) custom-call(s32[1,1]{1,0:T(1,128)} %bitcast.refs_0_, bf16[2,2048]{1,0:T(2,128)(2,1)} %bitcast.20, bf16[2,2,512]{2,1,0:T(2,128)(2,1)} %bitcast.23, bf16[4,128,128]{2,1,0:T(8,128)(2,1)} %bitcast.18, bf16[4,128,128]{2,1,0:T(8,128)(2,1)} %bitcast.19, ...), custom_call_target="tpu_custom_call" | custom-call | tf_op jit(solution)/shard_map/cond/branch_1_fun/pallas_call | solution.py:236
  3.8 5.2 %all-gather.1 = bf16[4,2,2176]{2,1,0:T(2,128)(2,1)S(1)} all-gather(bf16[1,2,2176]{2,1,0:T(2,128)(2,1)S(1)} %bitcast.13), channel_id=2, replica_groups={{0,1,2,3},{4,5,6,7},{8,9,10,11},{12,13,14,15},{16,17,18,19},{20,21,22,2..., dimensions={0}, use_global_device_ids=true | all-gather | bytes 43520 | tf_op jit(solution)/shard_map/cond/branch_1_fun/all_gather | solution.py:251
  9.0 1.3 %collective-permute-start.2 = (bf16[4,2,2176]{2,1,0:T(2,128)(2,1)S(1)}, bf16[4,2,2176]{2,1,0:T(2,128)(2,1)S(1)}, u32[]{:S(2)}, u32[]{:S(2)}) collective-permute-start(bf16[4,2,2176]{2,1,0:T(2,128)(2,1)S(1)} %get-tuple-element.45._), channel_id=1, source_target_pairs={{8,12},{10,14},{9,13},{11,15},{24,28},{26,30},{25,29},{27,31}} | collective-permute-start | bytes 104456 | tf_op jit(solution)/shard_map/ppermute | solution.py:264
  10.3 0.7 %collective-permute-start.1 = (bf16[4,2,2176]{2,1,0:T(2,128)(2,1)S(1)}, bf16[4,2,2176]{2,1,0:T(2,128)(2,1)S(1)}, u32[]{:S(2)}, u32[]{:S(2)}) collective-permute-start(bf16[4,2,2176]{2,1,0:T(2,128)(2,1)S(1)} %get-tuple-element.45._), channel_id=1, source_target_pairs={{4,12},{6,14},{5,13},{7,15},{20,28},{22,30},{21,29},{23,31}} | collective-permute-start | bytes 104456 | tf_op jit(solution)/shard_map/ppermute | solution.py:264
  11.0 0.7 %collective-permute-start = (bf16[4,2,2176]{2,1,0:T(2,128)(2,1)S(1)}, bf16[4,2,2176]{2,1,0:T(2,128)(2,1)S(1)}, u32[]{:S(2)}, u32[]{:S(2)}) collective-permute-start(bf16[4,2,2176]{2,1,0:T(2,128)(2,1)S(1)} %get-tuple-element.45._), channel_id=1, source_target_pairs={{0,12},{2,14},{1,13},{3,15},{16,28},{18,30},{17,29},{19,31}} | collective-permute-start | bytes 104456 | tf_op jit(solution)/shard_map/ppermute | solution.py:264
  11.7 0.2 collective-permute-done.2.refs_2_
  11.9 0.0 collective-permute-done.1.refs_1_
  11.9 0.0 collective-permute-done.refs_0_
  11.9 0.1 shard_map.112
  12.0 0.7 %collective-permute-start.3 = (bf16[2,3584]{1,0:T(2,128)(2,1)S(1)}, bf16[2,3584]{1,0:T(2,128)(2,1)S(1)}, u32[]{:S(2)}, u32[]{:S(2)}) collective-permute-start(bf16[2,3584]{1,0:T(2,128)(2,1)S(1)} %get-tuple-element.48), channel_id=1, source_target_pairs={{12,0},{14,2},{13,1},{15,3},{28,16},{30,18},{29,17},{31,19}} | collective-permute-start | bytes 43016 | tf_op jit(solution)/shard_map/ppermute | solution.py:299
  12.7 0.7 %collective-permute-start.4 = (bf16[2,3584]{1,0:T(2,128)(2,1)S(1)}, bf16[2,3584]{1,0:T(2,128)(2,1)S(1)}, u32[]{:S(2)}, u32[]{:S(2)}) collective-permute-start(bf16[2,3584]{1,0:T(2,128)(2,1)S(1)} %get-tuple-element.49), channel_id=1, source_target_pairs={{12,2},{14,0},{13,3},{15,1},{28,18},{30,16},{29,19},{31,17}} | collective-permute-start | bytes 43016 | tf_op jit(solution)/shard_map/ppermute | solution.py:299
  13.4 0.7 %collective-permute-start.5 = (bf16[2,3584]{1,0:T(2,128)(2,1)S(1)}, bf16[2,3584]{1,0:T(2,128)(2,1)S(1)}, u32[]{:S(2)}, u32[]{:S(2)}) collective-permute-start(bf16[2,3584]{1,0:T(2,128)(2,1)S(1)} %get-tuple-element.50), channel_id=1, source_target_pairs={{12,4},{14,6},{13,5},{15,7},{28,20},{30,22},{29,21},{31,23}} | collective-permute-start | bytes 43016 | tf_op jit(solution)/shard_map/ppermute | solution.py:299
  14.0 0.7 %collective-permute-start.6 = (bf16[2,3584]{1,0:T(2,128)(2,1)S(1)}, bf16[2,3584]{1,0:T(2,128)(2,1)S(1)}, u32[]{:S(2)}, u32[]{:S(2)}) collective-permute-start(bf16[2,3584]{1,0:T(2,128)(2,1)S(1)} %get-tuple-element.51), channel_id=1, source_target_pairs={{12,6},{14,4},{13,7},{15,5},{28,22},{30,20},{29,23},{31,21}} | collective-permute-start | bytes 43016 | tf_op jit(solution)/shard_map/ppermute | solution.py:299
  14.7 1.3 %collective-permute-start.7 = (bf16[2,3584]{1,0:T(2,128)(2,1)S(1)}, bf16[2,3584]{1,0:T(2,128)(2,1)S(1)}, u32[]{:S(2)}, u32[]{:S(2)}) collective-permute-start(bf16[2,3584]{1,0:T(2,128)(2,1)S(1)} %get-tuple-element.52), channel_id=1, source_target_pairs={{12,8},{14,10},{13,9},{15,11},{28,24},{30,26},{29,25},{31,27}} | collective-permute-start | bytes 43016 | tf_op jit(solution)/shard_map/ppermute | solution.py:299
  16.0 0.0 collective-permute-done.3.refs_0_
  16.0 1.3 %collective-permute-start.8 = (bf16[2,3584]{1,0:T(2,128)(2,1)S(1)}, bf16[2,3584]{1,0:T(2,128)(2,1)S(1)}, u32[]{:S(2)}, u32[]{:S(2)}) collective-permute-start(bf16[2,3584]{1,0:T(2,128)(2,1)S(1)} %get-tuple-element.53), channel_id=1, source_target_pairs={{12,10},{14,8},{13,11},{15,9},{28,26},{30,24},{29,27},{31,25}} | collective-permute-start | bytes 43016 | tf_op jit(solution)/shard_map/ppermute | solution.py:299
  17.3 0.0 collective-permute-done.4.refs_1_
  17.3 0.0 collective-permute-done.5.refs_2_
  17.3 0.0 collective-permute-done.6.refs_3_
  17.3 18.7 %collective-permute-done.7.refs_4_ = bf16[2,3584]{1,0:T(2,128)(2,1)S(1)} collective-permute-done((bf16[2,3584]{1,0:T(2,128)(2,1)S(1)}, bf16[2,3584]{1,0:T(2,128)(2,1)S(1)}, u32[]{:S(2)}, u32[]{:S(2)}) %collective-permute-start.7) | collective-permute-done | bytes 14368 | tf_op jit(solution)/shard_map/ppermute | solution.py:299
  36.0 2.2 %collective-permute-done.8.refs_5_ = bf16[2,3584]{1,0:T(2,128)(2,1)S(1)} collective-permute-done((bf16[2,3584]{1,0:T(2,128)(2,1)S(1)}, bf16[2,3584]{1,0:T(2,128)(2,1)S(1)}, u32[]{:S(2)}, u32[]{:S(2)}) %collective-permute-start.8) | collective-permute-done | bytes 14368 | tf_op jit(solution)/shard_map/ppermute | solution.py:299
  38.2 0.6 %shard_map.113 = (bf16[2,2048]{1,0:T(2,128)(2,1)}, bf16[2,7168]{1,0:T(2,128)(2,1)}) custom-call(bf16[2,2048]{1,0:T(2,128)(2,1)S(1)} %get-tuple-element.44.attended, bf16[2,3584]{1,0:T(2,128)(2,1)S(1)} %collective-permute-done.3.refs_0_, bf16[2,3584]{1,0:T(2,128)(2,1)S(1)} %collective-permute-done.4.refs_1_, ...), custom_call_target="tpu_custom_call" | custom-call | tf_op jit(solution)/shard_map/pallas_call | solution.py:314
  (1 shorter events, 0.0 us)
Async XLA Ops:
  9.0 2.9 %collective-permute-start.2 = (bf16[4,2,2176]{2,1,0:T(2,128)(2,1)S(1)}, bf16[4,2,2176]{2,1,0:T(2,128)(2,1)S(1)}, u32[]{:S(2)}, u32[]{:S(2)}) collective-permute-start(bf16[4,2,2176]{2,1,0:T(2,128)(2,1)S(1)} %get-tuple-element.45._), channel_id=1, source_target_pairs={{8,12},{10,14},{9,13},{11,15},{24,28},{26,30},{25,29},{27,31}} | collective-permute-start | bytes 104456 | tf_op jit(solution)/shard_map/ppermute | solution.py:264
  10.3 1.6 %collective-permute-start.1 = (bf16[4,2,2176]{2,1,0:T(2,128)(2,1)S(1)}, bf16[4,2,2176]{2,1,0:T(2,128)(2,1)S(1)}, u32[]{:S(2)}, u32[]{:S(2)}) collective-permute-start(bf16[4,2,2176]{2,1,0:T(2,128)(2,1)S(1)} %get-tuple-element.45._), channel_id=1, source_target_pairs={{4,12},{6,14},{5,13},{7,15},{20,28},{22,30},{21,29},{23,31}} | collective-permute-start | bytes 104456 | tf_op jit(solution)/shard_map/ppermute | solution.py:264
  11.0 0.9 %collective-permute-start = (bf16[4,2,2176]{2,1,0:T(2,128)(2,1)S(1)}, bf16[4,2,2176]{2,1,0:T(2,128)(2,1)S(1)}, u32[]{:S(2)}, u32[]{:S(2)}) collective-permute-start(bf16[4,2,2176]{2,1,0:T(2,128)(2,1)S(1)} %get-tuple-element.45._), channel_id=1, source_target_pairs={{0,12},{2,14},{1,13},{3,15},{16,28},{18,30},{17,29},{19,31}} | collective-permute-start | bytes 104456 | tf_op jit(solution)/shard_map/ppermute | solution.py:264
  12.0 4.0 %collective-permute-start.3 = (bf16[2,3584]{1,0:T(2,128)(2,1)S(1)}, bf16[2,3584]{1,0:T(2,128)(2,1)S(1)}, u32[]{:S(2)}, u32[]{:S(2)}) collective-permute-start(bf16[2,3584]{1,0:T(2,128)(2,1)S(1)} %get-tuple-element.48), channel_id=1, source_target_pairs={{12,0},{14,2},{13,1},{15,3},{28,16},{30,18},{29,17},{31,19}} | collective-permute-start | bytes 43016 | tf_op jit(solution)/shard_map/ppermute | solution.py:299
  12.7 4.6 %collective-permute-start.4 = (bf16[2,3584]{1,0:T(2,128)(2,1)S(1)}, bf16[2,3584]{1,0:T(2,128)(2,1)S(1)}, u32[]{:S(2)}, u32[]{:S(2)}) collective-permute-start(bf16[2,3584]{1,0:T(2,128)(2,1)S(1)} %get-tuple-element.49), channel_id=1, source_target_pairs={{12,2},{14,0},{13,3},{15,1},{28,18},{30,16},{29,19},{31,17}} | collective-permute-start | bytes 43016 | tf_op jit(solution)/shard_map/ppermute | solution.py:299
  13.4 4.0 %collective-permute-start.5 = (bf16[2,3584]{1,0:T(2,128)(2,1)S(1)}, bf16[2,3584]{1,0:T(2,128)(2,1)S(1)}, u32[]{:S(2)}, u32[]{:S(2)}) collective-permute-start(bf16[2,3584]{1,0:T(2,128)(2,1)S(1)} %get-tuple-element.50), channel_id=1, source_target_pairs={{12,4},{14,6},{13,5},{15,7},{28,20},{30,22},{29,21},{31,23}} | collective-permute-start | bytes 43016 | tf_op jit(solution)/shard_map/ppermute | solution.py:299
  14.0 3.3 %collective-permute-start.6 = (bf16[2,3584]{1,0:T(2,128)(2,1)S(1)}, bf16[2,3584]{1,0:T(2,128)(2,1)S(1)}, u32[]{:S(2)}, u32[]{:S(2)}) collective-permute-start(bf16[2,3584]{1,0:T(2,128)(2,1)S(1)} %get-tuple-element.51), channel_id=1, source_target_pairs={{12,6},{14,4},{13,7},{15,5},{28,22},{30,20},{29,23},{31,21}} | collective-permute-start | bytes 43016 | tf_op jit(solution)/shard_map/ppermute | solution.py:299
  14.7 21.3 %collective-permute-start.7 = (bf16[2,3584]{1,0:T(2,128)(2,1)S(1)}, bf16[2,3584]{1,0:T(2,128)(2,1)S(1)}, u32[]{:S(2)}, u32[]{:S(2)}) collective-permute-start(bf16[2,3584]{1,0:T(2,128)(2,1)S(1)} %get-tuple-element.52), channel_id=1, source_target_pairs={{12,8},{14,10},{13,9},{15,11},{28,24},{30,26},{29,25},{31,27}} | collective-permute-start | bytes 43016 | tf_op jit(solution)/shard_map/ppermute | solution.py:299
  16.0 22.2 %collective-permute-start.8 = (bf16[2,3584]{1,0:T(2,128)(2,1)S(1)}, bf16[2,3584]{1,0:T(2,128)(2,1)S(1)}, u32[]{:S(2)}, u32[]{:S(2)}) collective-permute-start(bf16[2,3584]{1,0:T(2,128)(2,1)S(1)} %get-tuple-element.53), channel_id=1, source_target_pairs={{12,10},{14,8},{13,11},{15,9},{28,26},{30,24},{29,27},{31,25}} | collective-permute-start | bytes 43016 | tf_op jit(solution)/shard_map/ppermute | solution.py:299

commit v9 on v8

--- a/solution.py
+++ b/solution.py
@@ -12,10 +12,9 @@
 STEPS = 2
 TAIL = 128
 EPS = 1e-05
-EARLY = 2048
-DEPTH = 512
+TILE = 256
 SLOTS = 4
-AHEAD = (2, 0, 1, 0, 1)
+AHEAD = (3, 1, 1, 1, 1)
 
 
 def pair(squares):
@@ -28,10 +27,10 @@
 def fetch_kernel(serving, _, gate, up, gate_held, up_held, sems):
     @pl.when(lax.axis_index("wide") >= serving)
     def _():
-        here = pl.ds(0, gate_held.shape[0])
+        here = pl.ds(0, gate_held.shape[1])
         copies = [
-            pltpu.make_async_copy(gate.at[here], gate_held, sems.at[0]),
-            pltpu.make_async_copy(up.at[here], up_held, sems.at[1]),
+            pltpu.make_async_copy(gate.at[:, here], gate_held, sems.at[0]),
+            pltpu.make_async_copy(up.at[:, here], up_held, sems.at[1]),
         ]
         for c in copies:
             c.start()
@@ -97,24 +96,19 @@
 def forward_kernel(blocks, workers, narrow, *refs):
     count = blocks * workers
     arrived, (gate_held, up_held, gate, up), rest = refs[:blocks], refs[blocks:][:4], refs[blocks + 4 :]
-    outs, (x, sums, slots, sems) = rest[:-4], rest[-4:]
+    outs, (x, slots, sems) = rest[:-3], rest[-3:]
     me = lax.axis_index("wide") - count
     features, columns = gate.shape
     half = features // narrow
-    early = gate_held.shape[0]
-    room, _, depth, across = slots.shape
-    units = [(at, c) for at in range(early, features, depth) for c in range(0, columns, across)]
-    cut = across // 512 * 256
-    spans = {
-        c: [slice(p, q) for p, q in ((c, c + cut), (c + cut, c + across)) if p < q]
-        for c in range(0, columns, across)
-    }
+    early = gate_held.shape[1]
+    room, _, _, tile = slots.shape
+    units = list(range(early, columns, tile))
 
     def stream(j):
         s = j % room
-        here = (pl.ds(units[j][0], depth), pl.ds(units[j][1], across))
+        here = pl.ds(units[j], tile)
         return [
-            pltpu.make_async_copy(m.at[here], slots.at[s, i], sems.at[s, i])
+            pltpu.make_async_copy(m.at[:, here], slots.at[s, i], sems.at[s, i])
             for i, m in enumerate((gate, up))
         ]
 
@@ -139,40 +133,34 @@
         x[...] = jnp.concatenate(lines, 0).astype(jnp.bfloat16)
         squares = jnp.sum(jnp.concatenate(tails, 0), -1, keepdims=True)
         r = lax.rsqrt(squares / D + EPS)
-        taken = set()
-
-        def add(i, here, rows, block):
-            product = jnp.dot(rows, block, preferred_element_type=jnp.float32)
-            first = (i, here.start) not in taken
-            taken.add((i, here.start))
-            sums[i, :, here] = product if first else sums[i, :, here] + product
-
-        waiting = [here for some in spans.values() for here in some]
-
-        def resident(count):
-            for here in waiting[:count]:
-                for i, held in enumerate((gate_held, up_held)):
-                    add(i, here, x[:, :early], held[:, here])
-            del waiting[:count]
-
-        for j, (at, c) in enumerate(units):
+
+        def produce(at, gate_tile, up_tile):
+            g = jnp.dot(x[...], gate_tile, preferred_element_type=jnp.float32) * r
+            u = jnp.dot(x[...], up_tile, preferred_element_type=jnp.float32) * r
+            hidden = (g / (1.0 + jnp.exp(-g)) * u).astype(jnp.bfloat16)
+            for i in range(count):
+                out = outs[(blocks - 1 - i // workers) * workers + i % workers]
+                out[:, at : at + tile] = hidden[i * STEPS : (i + 1) * STEPS]
+
+        waiting = list(range(0, early, tile))
+
+        def resident(some):
+            for at in waiting[:some]:
+                produce(at, gate_held[:, at : at + tile], up_held[:, at : at + tile])
+            del waiting[:some]
+
+        for j, at in enumerate(units):
             resident(AHEAD[j] if j < len(AHEAD) else 0)
             if j == len(units) - 1:
                 resident(len(waiting))
             for copy in stream(j):
                 copy.wait()
-            for here in spans[c]:
-                there = slice(here.start - c, here.stop - c)
-                for i in range(2):
-                    add(i, here, x[:, at : at + depth], slots[j % room, i, :, there])
+            produce(at, slots[j % room, 0], slots[j % room, 1])
             if j + room < len(units):
                 for copy in stream(j + room):
                     copy.start()
-        g, u = sums[0] * r, sums[1] * r
-        hidden = (g / (1.0 + jnp.exp(-g)) * u).astype(jnp.bfloat16)
-        for i in range(count):
-            out = outs[(blocks - 1 - i // workers) * workers + i % workers]
-            out[...] = hidden[i * STEPS : (i + 1) * STEPS]
+        if not units:
+            resident(len(waiting))
 
 
 def finish_kernel(blocks, workers, attended, *refs):
@@ -264,21 +252,20 @@
         lax.ppermute(block, "wide", [(b * workers + j, serving + j) for j in range(workers)])
         for b in range(blocks)
     ]
-    early = min(EARLY, features // 2)
+    tile = TILE if columns % (2 * TILE) == 0 else columns
+    early = columns // 2 // tile * tile or columns
     held = pl.pallas_call(
         functools.partial(fetch_kernel, serving),
-        out_shape=[pltpu.VMEM((early, columns), jnp.bfloat16)] * 2,
+        out_shape=[pltpu.VMEM((features, early), jnp.bfloat16)] * 2,
         in_specs=[pl.BlockSpec(memory_space=pl.ANY), hbm, hbm],
         out_specs=[vmem] * 2,
         scratch_shapes=[pltpu.SemaphoreType.DMA((2,))],
         compiler_params=pltpu.CompilerParams(vmem_limit_bytes=4 << 20),
         cost_estimate=pl.CostEstimate(
-            flops=0, bytes_accessed=early * 4 * columns, transcendentals=0
+            flops=0, bytes_accessed=early * 4 * features, transcendentals=0
         ),
     )(block, gate, up)
     padded = -(-STEPS * serving // 16) * 16
-    depth = min(DEPTH, features - early)
-    across = columns // 2 if columns % 512 == 0 else columns
     hidden = pl.pallas_call(
         functools.partial(forward_kernel, blocks, workers, narrow),
         out_shape=[jax.ShapeDtypeStruct((STEPS, columns), jnp.bfloat16)] * serving,
@@ -286,11 +273,10 @@
         out_specs=[vmem] * serving,
         scratch_shapes=[
             pltpu.VMEM((padded, features), jnp.bfloat16),
-            pltpu.VMEM((2, padded, columns), jnp.float32),
-            pltpu.VMEM((SLOTS, 2, depth, across), jnp.bfloat16),
+            pltpu.VMEM((SLOTS, 2, features, tile), jnp.bfloat16),
             pltpu.SemaphoreType.DMA((SLOTS, 2)),
         ],
-        compiler_params=pltpu.CompilerParams(vmem_limit_bytes=16 << 20),
+        compiler_params=pltpu.CompilerParams(vmem_limit_bytes=18 << 20),
     )(*arrived, *held, gate, up)
     back = [[None] * workers for _ in range(blocks)]
     for b in range(blocks):

time: 39.2 us -> 38.2 us (0.974)
  waiting for transfers between devices: 21.1 us -> 20.2 us
    ppermute x6, waiting for transfers between devices: 20.9 us -> 19.9 us  [shards(): lax.ppermute(hidden[(blocks - 1 - b) * workers + s], 'wide', pairs)]
where the time goes in v9:
time: 38.2 us; the launch traced here: 37.9 us
  waiting for transfers between devices  20.2 us (53%)
  starting transfers between devices  7.84 us (21%)
  blocking collectives  5.2 us (14%)
  Pallas kernels  3.9 us (10%)
  between operations  0.76 us (2%)
    ppermute x6, waiting for transfers between devices, shards(): lax.ppermute(hidden[(blocks - 1 - b) * workers + s], 'wide', pairs)  19.9 us
    ppermute x6, starting transfers between devices, shards(): lax.ppermute(hidden[(blocks - 1 - b) * workers + s], 'wide', pairs)  5.23 us
    all_gather x1, blocking collectives, serve(): lax.all_gather(sent, ('wide', 'narrow'), axis=0, axis_index_groups=groups)  5.2 us
    pallas_call x1, Pallas kernels, serve(): pl.pallas_call(attend_kernel, out_shape=(pltpu.VMEM(shapes[0].shape, jnp....  3.18 us
    ppermute x3, starting transfers between devices, shards(): lax.ppermute(block, 'wide', [(b * workers + j, serving + j) for j in rang...  2.61 us
  transfers between devices with their start and end apart: 9, of which 3 were waited for; matrix products, arithmetic and copies ran while one was open for 0% of the time, Pallas kernels for 0%

profile of v9, /device:TPU:16, one launch (start us, length us, event | category | flops | bytes accessed | tf_op | source)
XLA Modules:
  0.0 37.9 jit_solution(915748075750565839)
XLA Ops:
  0.6 8.4 %conditional.1 = ((bf16[2,2048]{1,0:T(2,128)(2,1)S(1)}, bf16[4,2,2176]{2,1,0:T(2,128)(2,1)S(1)})) conditional(s32[]{:T(128)} %convert_element_type.3, () %tuple.15, (s32[1]{0:T(128)}, bf16[2,1,2048]{2,0,1:T(2,128)(2,1)}, bf16[2,1,2,512]{3,2,1,0:T(2,128)(2,1)}, bf16[1,4,128,128]{3,2,1,0:T(8,128)(2,1)}, bf16[1,4,128,128]{3,2,1,0:T(8,128)(2,1)}, ...), branch_computations={%region_0.0_spmd, %region_1.0_spmd} | conditional | bytes 43544 | solution.py:250
  0.7 3.2 %branch_1_fun.1 = (bf16[2,2048]{1,0:T(2,128)(2,1)S(1)}, bf16[2,2176]{1,0:T(2,128)(2,1)S(1)}) custom-call(s32[1,1]{1,0:T(1,128)} %bitcast.refs_0_, bf16[2,2048]{1,0:T(2,128)(2,1)} %bitcast.20, bf16[2,2,512]{2,1,0:T(2,128)(2,1)} %bitcast.23, bf16[4,128,128]{2,1,0:T(8,128)(2,1)} %bitcast.18, bf16[4,128,128]{2,1,0:T(8,128)(2,1)} %bitcast.19, ...), custom_call_target="tpu_custom_call" | custom-call | tf_op jit(solution)/shard_map/cond/branch_1_fun/pallas_call | solution.py:224
  3.8 5.2 %all-gather.1 = bf16[4,2,2176]{2,1,0:T(2,128)(2,1)S(1)} all-gather(bf16[1,2,2176]{2,1,0:T(2,128)(2,1)S(1)} %bitcast.13), channel_id=2, replica_groups={{0,1,2,3},{4,5,6,7},{8,9,10,11},{12,13,14,15},{16,17,18,19},{20,21,22,2..., dimensions={0}, use_global_device_ids=true | all-gather | bytes 43520 | tf_op jit(solution)/shard_map/cond/branch_1_fun/all_gather | solution.py:239
  9.0 1.3 %collective-permute-start.2 = (bf16[4,2,2176]{2,1,0:T(2,128)(2,1)S(1)}, bf16[4,2,2176]{2,1,0:T(2,128)(2,1)S(1)}, u32[]{:S(2)}, u32[]{:S(2)}) collective-permute-start(bf16[4,2,2176]{2,1,0:T(2,128)(2,1)S(1)} %get-tuple-element.45._), channel_id=1, source_target_pairs={{8,12},{10,14},{9,13},{11,15},{24,28},{26,30},{25,29},{27,31}} | collective-permute-start | bytes 104456 | tf_op jit(solution)/shard_map/ppermute | solution.py:252
  10.3 0.7 %collective-permute-start.1 = (bf16[4,2,2176]{2,1,0:T(2,128)(2,1)S(1)}, bf16[4,2,2176]{2,1,0:T(2,128)(2,1)S(1)}, u32[]{:S(2)}, u32[]{:S(2)}) collective-permute-start(bf16[4,2,2176]{2,1,0:T(2,128)(2,1)S(1)} %get-tuple-element.45._), channel_id=1, source_target_pairs={{4,12},{6,14},{5,13},{7,15},{20,28},{22,30},{21,29},{23,31}} | collective-permute-start | bytes 104456 | tf_op jit(solution)/shard_map/ppermute | solution.py:252
  11.0 0.7 %collective-permute-start = (bf16[4,2,2176]{2,1,0:T(2,128)(2,1)S(1)}, bf16[4,2,2176]{2,1,0:T(2,128)(2,1)S(1)}, u32[]{:S(2)}, u32[]{:S(2)}) collective-permute-start(bf16[4,2,2176]{2,1,0:T(2,128)(2,1)S(1)} %get-tuple-element.45._), channel_id=1, source_target_pairs={{0,12},{2,14},{1,13},{3,15},{16,28},{18,30},{17,29},{19,31}} | collective-permute-start | bytes 104456 | tf_op jit(solution)/shard_map/ppermute | solution.py:252
  11.7 0.2 collective-permute-done.2.refs_2_
  11.9 0.0 collective-permute-done.1.refs_1_
  11.9 0.0 collective-permute-done.refs_0_
  11.9 0.1 shard_map.112
  12.0 0.7 %collective-permute-start.3 = (bf16[2,3584]{1,0:T(2,128)(2,1)S(1)}, bf16[2,3584]{1,0:T(2,128)(2,1)S(1)}, u32[]{:S(2)}, u32[]{:S(2)}) collective-permute-start(bf16[2,3584]{1,0:T(2,128)(2,1)S(1)} %get-tuple-element.48), channel_id=1, source_target_pairs={{12,0},{14,2},{13,1},{15,3},{28,16},{30,18},{29,17},{31,19}} | collective-permute-start | bytes 43016 | tf_op jit(solution)/shard_map/ppermute | solution.py:285
  12.7 0.7 %collective-permute-start.4 = (bf16[2,3584]{1,0:T(2,128)(2,1)S(1)}, bf16[2,3584]{1,0:T(2,128)(2,1)S(1)}, u32[]{:S(2)}, u32[]{:S(2)}) collective-permute-start(bf16[2,3584]{1,0:T(2,128)(2,1)S(1)} %get-tuple-element.49), channel_id=1, source_target_pairs={{12,2},{14,0},{13,3},{15,1},{28,18},{30,16},{29,19},{31,17}} | collective-permute-start | bytes 43016 | tf_op jit(solution)/shard_map/ppermute | solution.py:285
  13.4 0.7 %collective-permute-start.5 = (bf16[2,3584]{1,0:T(2,128)(2,1)S(1)}, bf16[2,3584]{1,0:T(2,128)(2,1)S(1)}, u32[]{:S(2)}, u32[]{:S(2)}) collective-permute-start(bf16[2,3584]{1,0:T(2,128)(2,1)S(1)} %get-tuple-element.50), channel_id=1, source_target_pairs={{12,4},{14,6},{13,5},{15,7},{28,20},{30,22},{29,21},{31,23}} | collective-permute-start | bytes 43016 | tf_op jit(solution)/shard_map/ppermute | solution.py:285
  14.0 0.7 %collective-permute-start.6 = (bf16[2,3584]{1,0:T(2,128)(2,1)S(1)}, bf16[2,3584]{1,0:T(2,128)(2,1)S(1)}, u32[]{:S(2)}, u32[]{:S(2)}) collective-permute-start(bf16[2,3584]{1,0:T(2,128)(2,1)S(1)} %get-tuple-element.51), channel_id=1, source_target_pairs={{12,6},{14,4},{13,7},{15,5},{28,22},{30,20},{29,23},{31,21}} | collective-permute-start | bytes 43016 | tf_op jit(solution)/shard_map/ppermute | solution.py:285
  14.7 1.3 %collective-permute-start.7 = (bf16[2,3584]{1,0:T(2,128)(2,1)S(1)}, bf16[2,3584]{1,0:T(2,128)(2,1)S(1)}, u32[]{:S(2)}, u32[]{:S(2)}) collective-permute-start(bf16[2,3584]{1,0:T(2,128)(2,1)S(1)} %get-tuple-element.52), channel_id=1, source_target_pairs={{12,8},{14,10},{13,9},{15,11},{28,24},{30,26},{29,25},{31,27}} | collective-permute-start | bytes 43016 | tf_op jit(solution)/shard_map/ppermute | solution.py:285
  16.0 0.0 collective-permute-done.3.refs_0_
  16.0 1.3 %collective-permute-start.8 = (bf16[2,3584]{1,0:T(2,128)(2,1)S(1)}, bf16[2,3584]{1,0:T(2,128)(2,1)S(1)}, u32[]{:S(2)}, u32[]{:S(2)}) collective-permute-start(bf16[2,3584]{1,0:T(2,128)(2,1)S(1)} %get-tuple-element.53), channel_id=1, source_target_pairs={{12,10},{14,8},{13,11},{15,9},{28,26},{30,24},{29,27},{31,25}} | collective-permute-start | bytes 43016 | tf_op jit(solution)/shard_map/ppermute | solution.py:285
  17.3 0.0 collective-permute-done.4.refs_1_
  17.3 0.0 collective-permute-done.5.refs_2_
  17.3 0.0 collective-permute-done.6.refs_3_
  17.3 17.7 %collective-permute-done.7.refs_4_ = bf16[2,3584]{1,0:T(2,128)(2,1)S(1)} collective-permute-done((bf16[2,3584]{1,0:T(2,128)(2,1)S(1)}, bf16[2,3584]{1,0:T(2,128)(2,1)S(1)}, u32[]{:S(2)}, u32[]{:S(2)}) %collective-permute-start.7) | collective-permute-done | bytes 14368 | tf_op jit(solution)/shard_map/ppermute | solution.py:285
  35.0 2.2 %collective-permute-done.8.refs_5_ = bf16[2,3584]{1,0:T(2,128)(2,1)S(1)} collective-permute-done((bf16[2,3584]{1,0:T(2,128)(2,1)S(1)}, bf16[2,3584]{1,0:T(2,128)(2,1)S(1)}, u32[]{:S(2)}, u32[]{:S(2)}) %collective-permute-start.8) | collective-permute-done | bytes 14368 | tf_op jit(solution)/shard_map/ppermute | solution.py:285
  37.3 0.6 %shard_map.113 = (bf16[2,2048]{1,0:T(2,128)(2,1)}, bf16[2,7168]{1,0:T(2,128)(2,1)}) custom-call(bf16[2,2048]{1,0:T(2,128)(2,1)S(1)} %get-tuple-element.44.attended, bf16[2,3584]{1,0:T(2,128)(2,1)S(1)} %collective-permute-done.3.refs_0_, bf16[2,3584]{1,0:T(2,128)(2,1)S(1)} %collective-permute-done.4.refs_1_, ...), custom_call_target="tpu_custom_call" | custom-call | tf_op jit(solution)/shard_map/pallas_call | solution.py:300
  (1 shorter events, 0.0 us)
Async XLA Ops:
  9.0 2.9 %collective-permute-start.2 = (bf16[4,2,2176]{2,1,0:T(2,128)(2,1)S(1)}, bf16[4,2,2176]{2,1,0:T(2,128)(2,1)S(1)}, u32[]{:S(2)}, u32[]{:S(2)}) collective-permute-start(bf16[4,2,2176]{2,1,0:T(2,128)(2,1)S(1)} %get-tuple-element.45._), channel_id=1, source_target_pairs={{8,12},{10,14},{9,13},{11,15},{24,28},{26,30},{25,29},{27,31}} | collective-permute-start | bytes 104456 | tf_op jit(solution)/shard_map/ppermute | solution.py:252
  10.3 1.6 %collective-permute-start.1 = (bf16[4,2,2176]{2,1,0:T(2,128)(2,1)S(1)}, bf16[4,2,2176]{2,1,0:T(2,128)(2,1)S(1)}, u32[]{:S(2)}, u32[]{:S(2)}) collective-permute-start(bf16[4,2,2176]{2,1,0:T(2,128)(2,1)S(1)} %get-tuple-element.45._), channel_id=1, source_target_pairs={{4,12},{6,14},{5,13},{7,15},{20,28},{22,30},{21,29},{23,31}} | collective-permute-start | bytes 104456 | tf_op jit(solution)/shard_map/ppermute | solution.py:252
  11.0 0.9 %collective-permute-start = (bf16[4,2,2176]{2,1,0:T(2,128)(2,1)S(1)}, bf16[4,2,2176]{2,1,0:T(2,128)(2,1)S(1)}, u32[]{:S(2)}, u32[]{:S(2)}) collective-permute-start(bf16[4,2,2176]{2,1,0:T(2,128)(2,1)S(1)} %get-tuple-element.45._), channel_id=1, source_target_pairs={{0,12},{2,14},{1,13},{3,15},{16,28},{18,30},{17,29},{19,31}} | collective-permute-start | bytes 104456 | tf_op jit(solution)/shard_map/ppermute | solution.py:252
  12.0 4.0 %collective-permute-start.3 = (bf16[2,3584]{1,0:T(2,128)(2,1)S(1)}, bf16[2,3584]{1,0:T(2,128)(2,1)S(1)}, u32[]{:S(2)}, u32[]{:S(2)}) collective-permute-start(bf16[2,3584]{1,0:T(2,128)(2,1)S(1)} %get-tuple-element.48), channel_id=1, source_target_pairs={{12,0},{14,2},{13,1},{15,3},{28,16},{30,18},{29,17},{31,19}} | collective-permute-start | bytes 43016 | tf_op jit(solution)/shard_map/ppermute | solution.py:285
  12.7 4.6 %collective-permute-start.4 = (bf16[2,3584]{1,0:T(2,128)(2,1)S(1)}, bf16[2,3584]{1,0:T(2,128)(2,1)S(1)}, u32[]{:S(2)}, u32[]{:S(2)}) collective-permute-start(bf16[2,3584]{1,0:T(2,128)(2,1)S(1)} %get-tuple-element.49), channel_id=1, source_target_pairs={{12,2},{14,0},{13,3},{15,1},{28,18},{30,16},{29,19},{31,17}} | collective-permute-start | bytes 43016 | tf_op jit(solution)/shard_map/ppermute | solution.py:285
  13.4 4.0 %collective-permute-start.5 = (bf16[2,3584]{1,0:T(2,128)(2,1)S(1)}, bf16[2,3584]{1,0:T(2,128)(2,1)S(1)}, u32[]{:S(2)}, u32[]{:S(2)}) collective-permute-start(bf16[2,3584]{1,0:T(2,128)(2,1)S(1)} %get-tuple-element.50), channel_id=1, source_target_pairs={{12,4},{14,6},{13,5},{15,7},{28,20},{30,22},{29,21},{31,23}} | collective-permute-start | bytes 43016 | tf_op jit(solution)/shard_map/ppermute | solution.py:285
  14.0 3.3 %collective-permute-start.6 = (bf16[2,3584]{1,0:T(2,128)(2,1)S(1)}, bf16[2,3584]{1,0:T(2,128)(2,1)S(1)}, u32[]{:S(2)}, u32[]{:S(2)}) collective-permute-start(bf16[2,3584]{1,0:T(2,128)(2,1)S(1)} %get-tuple-element.51), channel_id=1, source_target_pairs={{12,6},{14,4},{13,7},{15,5},{28,22},{30,20},{29,23},{31,21}} | collective-permute-start | bytes 43016 | tf_op jit(solution)/shard_map/ppermute | solution.py:285
  14.7 20.3 %collective-permute-start.7 = (bf16[2,3584]{1,0:T(2,128)(2,1)S(1)}, bf16[2,3584]{1,0:T(2,128)(2,1)S(1)}, u32[]{:S(2)}, u32[]{:S(2)}) collective-permute-start(bf16[2,3584]{1,0:T(2,128)(2,1)S(1)} %get-tuple-element.52), channel_id=1, source_target_pairs={{12,8},{14,10},{13,9},{15,11},{28,24},{30,26},{29,25},{31,27}} | collective-permute-start | bytes 43016 | tf_op jit(solution)/shard_map/ppermute | solution.py:285
  16.0 21.3 %collective-permute-start.8 = (bf16[2,3584]{1,0:T(2,128)(2,1)S(1)}, bf16[2,3584]{1,0:T(2,128)(2,1)S(1)}, u32[]{:S(2)}, u32[]{:S(2)}) collective-permute-start(bf16[2,3584]{1,0:T(2,128)(2,1)S(1)} %get-tuple-element.53), channel_id=1, source_target_pairs={{12,10},{14,8},{13,11},{15,9},{28,26},{30,24},{29,27},{31,25}} | collective-permute-start | bytes 43016 | tf_op jit(solution)/shard_map/ppermute | solution.py:285

commit v10 on v9

--- a/solution.py
+++ b/solution.py
@@ -139,8 +139,8 @@
             u = jnp.dot(x[...], up_tile, preferred_element_type=jnp.float32) * r
             hidden = (g / (1.0 + jnp.exp(-g)) * u).astype(jnp.bfloat16)
             for i in range(count):
-                out = outs[(blocks - 1 - i // workers) * workers + i % workers]
-                out[:, at : at + tile] = hidden[i * STEPS : (i + 1) * STEPS]
+                out = outs[blocks - 1 - i // workers]
+                out[i % workers, :, at : at + tile] = hidden[i * STEPS : (i + 1) * STEPS]
 
         waiting = list(range(0, early, tile))
 
@@ -163,26 +163,22 @@
             resident(len(waiting))
 
 
-def finish_kernel(blocks, workers, attended, *refs):
-    results, (attended_out, out) = refs[:-2], refs[-2:]
+def choose_kernel(workers, *refs):
+    results, out = refs[:-1], refs[-1]
+    for b, result in enumerate(results):
+
+        @pl.when(lax.axis_index("wide") // workers == b)
+        def _():
+            out[...] = result[...]
+
+
+def finish_kernel(workers, attended, gathered, attended_out, out):
+    me = lax.axis_index("wide")
+    columns = gathered.shape[3]
     attended_out[...] = attended[...]
-    if len(results) == 1:
-        out[...] = results[0][...]
-        return
-    me = lax.axis_index("wide")
-    columns = results[0].shape[1]
-
-    @pl.when(me >= blocks * workers)
-    def _():
-        out[...] = jnp.zeros_like(out)
-
-    for i, result in enumerate(results):
-        b, shift = divmod(i, workers)
-
-        @pl.when((me >= b * workers) & (me < (b + 1) * workers))
-        def _():
-            k = lax.rem(me - b * workers + workers - shift, workers)
-            out[:, pl.ds(pl.multiple_of(k * columns, 128), columns)] = result[...]
+    for k in range(workers):
+        shift = lax.rem(lax.rem(me, workers) + workers - k, workers)
+        out[:, k * columns : (k + 1) * columns] = gathered[k, shift]
 
 
 def shards(queries, new_kv, keys, values, lengths, residual, gain, gate, up):
@@ -268,9 +264,9 @@
     padded = -(-STEPS * serving // 16) * 16
     hidden = pl.pallas_call(
         functools.partial(forward_kernel, blocks, workers, narrow),
-        out_shape=[jax.ShapeDtypeStruct((STEPS, columns), jnp.bfloat16)] * serving,
+        out_shape=[jax.ShapeDtypeStruct((workers, STEPS, columns), jnp.bfloat16)] * blocks,
         in_specs=[vmem] * (blocks + 2) + [hbm, hbm],
-        out_specs=[vmem] * serving,
+        out_specs=[vmem] * blocks,
         scratch_shapes=[
             pltpu.VMEM((padded, features), jnp.bfloat16),
             pltpu.VMEM((SLOTS, 2, features, tile), jnp.bfloat16),
@@ -278,35 +274,44 @@
         ],
         compiler_params=pltpu.CompilerParams(vmem_limit_bytes=18 << 20),
     )(*arrived, *held, gate, up)
-    back = [[None] * workers for _ in range(blocks)]
-    for b in range(blocks):
-        for s in range(workers):
-            pairs = [(serving + k, b * workers + (k + s) % workers) for k in range(workers)]
-            back[b][s] = lax.ppermute(hidden[(blocks - 1 - b) * workers + s], "wide", pairs)
-    aligned = columns % 128 == 0
-    if aligned:
-        results = [r for some in back for r in some]
-    else:
-        me = lax.axis_index("wide")
-        pieces = []
-        for k in range(workers):
-            piece = jnp.zeros((), jnp.bfloat16)
-            for b in range(blocks):
-                for s in range(workers):
-                    mine = me == b * workers + (k + s) % workers
-                    piece = jnp.where(mine, back[b][s], piece)
-            pieces.append(piece)
-        results = [jnp.concatenate(pieces, 1)]
+    back = [
+        lax.ppermute(
+            hidden[blocks - 1 - b], "wide", [(serving + k, b * workers + k) for k in range(workers)]
+        )
+        for b in range(blocks)
+    ]
+    peers = [list(range(at, at + workers)) for at in range(0, wide, workers)]
+    shape = jax.ShapeDtypeStruct((workers, STEPS, columns), jnp.bfloat16)
+
+    def collect(*back):
+        mine = pl.pallas_call(
+            functools.partial(choose_kernel, workers),
+            out_shape=shape,
+            in_specs=[vmem] * blocks,
+            out_specs=vmem,
+            compiler_params=pltpu.CompilerParams(vmem_limit_bytes=8 << 20),
+        )(*back)
+        return lax.all_gather(mine, "wide", axis=0, axis_index_groups=peers)
+
+    def skip(*back):
+        return pl.pallas_call(
+            blank_kernel,
+            out_shape=jax.ShapeDtypeStruct((workers, *shape.shape), jnp.bfloat16),
+            out_specs=vmem,
+            compiler_params=pltpu.CompilerParams(vmem_limit_bytes=8 << 20),
+        )()
+
+    gathered = lax.cond(owner, collect, skip, *back)
     attended, activated = pl.pallas_call(
-        functools.partial(finish_kernel, blocks, workers),
+        functools.partial(finish_kernel, workers),
         out_shape=(
             jax.ShapeDtypeStruct((STEPS, half), jnp.bfloat16),
             jax.ShapeDtypeStruct((STEPS, workers * columns), jnp.bfloat16),
         ),
-        in_specs=[vmem] * (1 + len(results)),
+        in_specs=[vmem] * 2,
         out_specs=(vmem, vmem),
         compiler_params=pltpu.CompilerParams(vmem_limit_bytes=8 << 20),
-    )(attended, *results)
+    )(attended, gathered)
     return attended.reshape(STEPS, 1, half), activated.reshape(STEPS, 1, -1)
 
 

time: 38.2 us -> 38.9 us (1.018)
  the two profiles are of different devices: /device:TPU:16 before, /device:TPU:0 now
where the time goes in v10:
time: 38.9 us; the launch traced here: 38.6 us
  waiting for transfers between devices  18 us (46%)
  blocking collectives  10.7 us (28%)
  starting transfers between devices  5.23 us (13%)
  Pallas kernels  3.91 us (10%)
  between operations  0.72 us (2%)
    ppermute x3, waiting for transfers between devices, shards(): lax.ppermute(hidden[blocks - 1 - b], 'wide', [(serving + k, b * workers +...  16.5 us
    all_gather x1, blocking collectives, serve(): lax.all_gather(sent, ('wide', 'narrow'), axis=0, axis_index_groups=groups)  6.18 us
    all_gather x1, blocking collectives, collect(): return lax.all_gather(mine, 'wide', axis=0, axis_index_groups=peers)  4.55 us
    pallas_call x1, Pallas kernels, serve(): pl.pallas_call(attend_kernel, out_shape=(pltpu.VMEM(shapes[0].shape, jnp....  3.18 us
    ppermute x3, starting transfers between devices, shards(): lax.ppermute(hidden[blocks - 1 - b], 'wide', [(serving + k, b * workers +...  2.62 us
    ppermute x3, starting transfers between devices, shards(): lax.ppermute(block, 'wide', [(b * workers + j, serving + j) for j in rang...  2.61 us
    ppermute x3, waiting for transfers between devices, shards(): lax.ppermute(block, 'wide', [(b * workers + j, serving + j) for j in rang...  1.54 us
  transfers between devices with their start and end apart: 6, of which 2 were waited for; matrix products, arithmetic and copies ran while one was open for 0% of the time, Pallas kernels for 0%

profile of v10, /device:TPU:0, one launch (start us, length us, event | category | flops | bytes accessed | tf_op | source)
XLA Modules:
  0.0 38.6 jit_solution(2299244514304163687)
XLA Ops:
  0.6 9.4 %conditional.2 = ((bf16[2,2048]{1,0:T(2,128)(2,1)S(1)}, bf16[4,2,2176]{2,1,0:T(2,128)(2,1)S(1)})) conditional(s32[]{:T(128)} %convert_element_type.4, () %tuple.21, (s32[1]{0:T(128)}, bf16[2,1,2048]{2,0,1:T(2,128)(2,1)}, bf16[2,1,2,512]{3,2,1,0:T(2,128)(2,1)}, bf16[1,4,128,128]{3,2,1,0:T(8,128)(2,1)}, bf16[1,4,128,128]{3,2,1,0:T(8,128)(2,1)}, ...), branch_computations={%region_0.0_spmd, %region_1.0_spmd} | conditional | bytes 43544 | solution.py:246
  0.7 3.2 %branch_1_fun.2 = (bf16[2,2048]{1,0:T(2,128)(2,1)S(1)}, bf16[2,2176]{1,0:T(2,128)(2,1)S(1)}) custom-call(s32[1,1]{1,0:T(1,128)} %bitcast.refs_0_, bf16[2,2048]{1,0:T(2,128)(2,1)} %bitcast.22, bf16[2,2,512]{2,1,0:T(2,128)(2,1)} %bitcast.25, bf16[4,128,128]{2,1,0:T(8,128)(2,1)} %bitcast.20, bf16[4,128,128]{2,1,0:T(8,128)(2,1)} %bitcast.21, ...), custom_call_target="tpu_custom_call" | custom-call | tf_op jit(solution)/shard_map/cond/branch_1_fun/pallas_call | solution.py:220
  3.8 6.2 %all-gather.2 = bf16[4,2,2176]{2,1,0:T(2,128)(2,1)S(1)} all-gather(bf16[1,2,2176]{2,1,0:T(2,128)(2,1)S(1)} %bitcast.14), channel_id=2, replica_groups={{0,1,2,3},{4,5,6,7},{8,9,10,11},{12,13,14,15},{16,17,18,19},{20,21,22,2..., dimensions={0}, use_global_device_ids=true | all-gather | bytes 43520 | tf_op jit(solution)/shard_map/cond/branch_1_fun/all_gather | solution.py:235
  10.0 0.7 %collective-permute-start.2 = (bf16[4,2,2176]{2,1,0:T(2,128)(2,1)S(1)}, bf16[4,2,2176]{2,1,0:T(2,128)(2,1)S(1)}, u32[]{:S(2)}, u32[]{:S(2)}) collective-permute-start(bf16[4,2,2176]{2,1,0:T(2,128)(2,1)S(1)} %get-tuple-element.54._), channel_id=1, source_target_pairs={{8,12},{10,14},{9,13},{11,15},{24,28},{26,30},{25,29},{27,31}} | collective-permute-start | bytes 104456 | tf_op jit(solution)/shard_map/ppermute | solution.py:248
  10.7 0.7 %collective-permute-start.1 = (bf16[4,2,2176]{2,1,0:T(2,128)(2,1)S(1)}, bf16[4,2,2176]{2,1,0:T(2,128)(2,1)S(1)}, u32[]{:S(2)}, u32[]{:S(2)}) collective-permute-start(bf16[4,2,2176]{2,1,0:T(2,128)(2,1)S(1)} %get-tuple-element.54._), channel_id=1, source_target_pairs={{4,12},{6,14},{5,13},{7,15},{20,28},{22,30},{21,29},{23,31}} | collective-permute-start | bytes 104456 | tf_op jit(solution)/shard_map/ppermute | solution.py:248
  11.4 1.3 %collective-permute-start = (bf16[4,2,2176]{2,1,0:T(2,128)(2,1)S(1)}, bf16[4,2,2176]{2,1,0:T(2,128)(2,1)S(1)}, u32[]{:S(2)}, u32[]{:S(2)}) collective-permute-start(bf16[4,2,2176]{2,1,0:T(2,128)(2,1)S(1)} %get-tuple-element.54._), channel_id=1, source_target_pairs={{0,12},{2,14},{1,13},{3,15},{16,28},{18,30},{17,29},{19,31}} | collective-permute-start | bytes 104456 | tf_op jit(solution)/shard_map/ppermute | solution.py:248
  12.7 0.0 collective-permute-done.2.refs_2_
  12.7 0.0 collective-permute-done.1.refs_1_
  12.7 1.5 %collective-permute-done.refs_0_ = bf16[4,2,2176]{2,1,0:T(2,128)(2,1)S(1)} collective-permute-done((bf16[4,2,2176]{2,1,0:T(2,128)(2,1)S(1)}, bf16[4,2,2176]{2,1,0:T(2,128)(2,1)S(1)}, u32[]{:S(2)}, u32[]{:S(2)}) %collective-permute-start) | collective-permute-done | bytes 34848 | tf_op jit(solution)/shard_map/ppermute | solution.py:248
  14.2 0.1 shard_map.112
  14.3 1.3 %collective-permute-start.3 = (bf16[2,2,3584]{2,1,0:T(2,128)(2,1)S(1)}, bf16[2,2,3584]{2,1,0:T(2,128)(2,1)S(1)}, u32[]{:S(2)}, u32[]{:S(2)}) collective-permute-start(bf16[2,2,3584]{2,1,0:T(2,128)(2,1)S(1)} %get-tuple-element.57), channel_id=1, source_target_pairs={{12,0},{14,2},{13,1},{15,3},{28,16},{30,18},{29,17},{31,19}} | collective-permute-start | bytes 86024 | tf_op jit(solution)/shard_map/ppermute | solution.py:278
  15.6 0.7 %collective-permute-start.4 = (bf16[2,2,3584]{2,1,0:T(2,128)(2,1)S(1)}, bf16[2,2,3584]{2,1,0:T(2,128)(2,1)S(1)}, u32[]{:S(2)}, u32[]{:S(2)}) collective-permute-start(bf16[2,2,3584]{2,1,0:T(2,128)(2,1)S(1)} %get-tuple-element.58), channel_id=1, source_target_pairs={{12,4},{14,6},{13,5},{15,7},{28,20},{30,22},{29,21},{31,23}} | collective-permute-start | bytes 86024 | tf_op jit(solution)/shard_map/ppermute | solution.py:278
  16.3 0.7 %collective-permute-start.5 = (bf16[2,2,3584]{2,1,0:T(2,128)(2,1)S(1)}, bf16[2,2,3584]{2,1,0:T(2,128)(2,1)S(1)}, u32[]{:S(2)}, u32[]{:S(2)}) collective-permute-start(bf16[2,2,3584]{2,1,0:T(2,128)(2,1)S(1)} %get-tuple-element.59), channel_id=1, source_target_pairs={{12,8},{14,10},{13,9},{15,11},{28,24},{30,26},{29,25},{31,27}} | collective-permute-start | bytes 86024 | tf_op jit(solution)/shard_map/ppermute | solution.py:278
  17.0 16.5 %collective-permute-done.3 = bf16[2,2,3584]{2,1,0:T(2,128)(2,1)S(1)} collective-permute-done((bf16[2,2,3584]{2,1,0:T(2,128)(2,1)S(1)}, bf16[2,2,3584]{2,1,0:T(2,128)(2,1)S(1)}, u32[]{:S(2)}, u32[]{:S(2)}) %collective-permute-start.3) | collective-permute-done | bytes 28704 | tf_op jit(solution)/shard_map/ppermute | solution.py:278
  33.4 0.0 collective-permute-done.4
  33.4 0.0 collective-permute-done.5
  33.4 4.6 %conditional.3 = (bf16[2,2,2,3584]{3,2,1,0:T(2,128)(2,1)S(1)}) conditional(s32[]{:T(128)} %convert_element_type.4, () %tuple.23, (bf16[2,2,3584]{2,1,0:T(2,128)(2,1)S(1)}, bf16[2,2,3584]{2,1,0:T(2,128)(2,1)S(1)}, bf16[2,2,3584]{2,1,0:T(2,128)(2,1)S(1)}) %tuple.24), branch_computations={%region_2.0_spmd, %region_3.0_spmd} | conditional | bytes 86024 | solution.py:304
  33.5 4.5 %all-gather.1 = bf16[4,2,3584]{2,1,0:T(2,128)(2,1)S(1)} all-gather(bf16[2,2,3584]{2,1,0:T(2,128)(2,1)S(1)} %branch_1_fun.3), channel_id=3, replica_groups={{0,2},{4,6},{8,10},{12,14},{1,3},{5,7},{9,11},{13,15},{16,18},{20,22},{..., dimensions={0}, use_global_device_ids=true | all-gather | bytes 86016 | tf_op jit(solution)/shard_map/cond/branch_1_fun/all_gather | solution.py:294
  38.0 0.6 %shard_map.113 = (bf16[2,2048]{1,0:T(2,128)(2,1)}, bf16[2,7168]{1,0:T(2,128)(2,1)}) custom-call(bf16[2,2048]{1,0:T(2,128)(2,1)S(1)} %get-tuple-element.53.attended, bf16[2,2,2,3584]{3,2,1,0:T(2,128)(2,1)S(1)} %get-tuple-element.95.gathered), custom_call_target="tpu_custom_call" | custom-call | tf_op jit(solution)/shard_map/pallas_call | solution.py:305
  (2 shorter events, 0.0 us)
Async XLA Ops:
  10.0 2.7 %collective-permute-start.2 = (bf16[4,2,2176]{2,1,0:T(2,128)(2,1)S(1)}, bf16[4,2,2176]{2,1,0:T(2,128)(2,1)S(1)}, u32[]{:S(2)}, u32[]{:S(2)}) collective-permute-start(bf16[4,2,2176]{2,1,0:T(2,128)(2,1)S(1)} %get-tuple-element.54._), channel_id=1, source_target_pairs={{8,12},{10,14},{9,13},{11,15},{24,28},{26,30},{25,29},{27,31}} | collective-permute-start | bytes 104456 | tf_op jit(solution)/shard_map/ppermute | solution.py:248
  10.7 2.0 %collective-permute-start.1 = (bf16[4,2,2176]{2,1,0:T(2,128)(2,1)S(1)}, bf16[4,2,2176]{2,1,0:T(2,128)(2,1)S(1)}, u32[]{:S(2)}, u32[]{:S(2)}) collective-permute-start(bf16[4,2,2176]{2,1,0:T(2,128)(2,1)S(1)} %get-tuple-element.54._), channel_id=1, source_target_pairs={{4,12},{6,14},{5,13},{7,15},{20,28},{22,30},{21,29},{23,31}} | collective-permute-start | bytes 104456 | tf_op jit(solution)/shard_map/ppermute | solution.py:248
  11.4 2.9 %collective-permute-start = (bf16[4,2,2176]{2,1,0:T(2,128)(2,1)S(1)}, bf16[4,2,2176]{2,1,0:T(2,128)(2,1)S(1)}, u32[]{:S(2)}, u32[]{:S(2)}) collective-permute-start(bf16[4,2,2176]{2,1,0:T(2,128)(2,1)S(1)} %get-tuple-element.54._), channel_id=1, source_target_pairs={{0,12},{2,14},{1,13},{3,15},{16,28},{18,30},{17,29},{19,31}} | collective-permute-start | bytes 104456 | tf_op jit(solution)/shard_map/ppermute | solution.py:248
  14.3 19.1 %collective-permute-start.3 = (bf16[2,2,3584]{2,1,0:T(2,128)(2,1)S(1)}, bf16[2,2,3584]{2,1,0:T(2,128)(2,1)S(1)}, u32[]{:S(2)}, u32[]{:S(2)}) collective-permute-start(bf16[2,2,3584]{2,1,0:T(2,128)(2,1)S(1)} %get-tuple-element.57), channel_id=1, source_target_pairs={{12,0},{14,2},{13,1},{15,3},{28,16},{30,18},{29,17},{31,19}} | collective-permute-start | bytes 86024 | tf_op jit(solution)/shard_map/ppermute | solution.py:278
  15.6 17.8 %collective-permute-start.4 = (bf16[2,2,3584]{2,1,0:T(2,128)(2,1)S(1)}, bf16[2,2,3584]{2,1,0:T(2,128)(2,1)S(1)}, u32[]{:S(2)}, u32[]{:S(2)}) collective-permute-start(bf16[2,2,3584]{2,1,0:T(2,128)(2,1)S(1)} %get-tuple-element.58), channel_id=1, source_target_pairs={{12,4},{14,6},{13,5},{15,7},{28,20},{30,22},{29,21},{31,23}} | collective-permute-start | bytes 86024 | tf_op jit(solution)/shard_map/ppermute | solution.py:278
  16.3 17.1 %collective-permute-start.5 = (bf16[2,2,3584]{2,1,0:T(2,128)(2,1)S(1)}, bf16[2,2,3584]{2,1,0:T(2,128)(2,1)S(1)}, u32[]{:S(2)}, u32[]{:S(2)}) collective-permute-start(bf16[2,2,3584]{2,1,0:T(2,128)(2,1)S(1)} %get-tuple-element.59), channel_id=1, source_target_pairs={{12,8},{14,10},{13,9},{15,11},{28,24},{30,26},{29,25},{31,27}} | collective-permute-start | bytes 86024 | tf_op jit(solution)/shard_map/ppermute | solution.py:278

commit v11 on v9

--- a/solution.py
+++ b/solution.py
@@ -22,20 +22,6 @@
     lane = lax.broadcasted_iota(jnp.int32, (squares.shape[0], TAIL), 1)
     both = jnp.where(lane == 0, high, jnp.where(lane == 1, squares - high, 0.0))
     return both.astype(jnp.bfloat16)
-
-
-def fetch_kernel(serving, _, gate, up, gate_held, up_held, sems):
-    @pl.when(lax.axis_index("wide") >= serving)
-    def _():
-        here = pl.ds(0, gate_held.shape[1])
-        copies = [
-            pltpu.make_async_copy(gate.at[:, here], gate_held, sems.at[0]),
-            pltpu.make_async_copy(up.at[:, here], up_held, sems.at[1]),
-        ]
-        for c in copies:
-            c.start()
-        for c in copies:
-            c.wait()
 
 
 def blank_kernel(*outs):
@@ -200,8 +186,8 @@
     def in_hbm(a):
         return pltpu.with_memory_space_constraint(a, pltpu.HBM)
 
-    gate = in_hbm(gate.reshape(features, columns))
-    up = in_hbm(up.reshape(features, columns))
+    gate = gate.reshape(features, columns)
+    up = up.reshape(features, columns)
     operands = (
         lengths.reshape(1, 1),
         queries.reshape(STEPS, half),
@@ -254,17 +240,7 @@
     ]
     tile = TILE if columns % (2 * TILE) == 0 else columns
     early = columns // 2 // tile * tile or columns
-    held = pl.pallas_call(
-        functools.partial(fetch_kernel, serving),
-        out_shape=[pltpu.VMEM((features, early), jnp.bfloat16)] * 2,
-        in_specs=[pl.BlockSpec(memory_space=pl.ANY), hbm, hbm],
-        out_specs=[vmem] * 2,
-        scratch_shapes=[pltpu.SemaphoreType.DMA((2,))],
-        compiler_params=pltpu.CompilerParams(vmem_limit_bytes=4 << 20),
-        cost_estimate=pl.CostEstimate(
-            flops=0, bytes_accessed=early * 4 * features, transcendentals=0
-        ),
-    )(block, gate, up)
+    held = [m[:, :early] for m in (gate, up)]
     padded = -(-STEPS * serving // 16) * 16
     hidden = pl.pallas_call(
         functools.partial(forward_kernel, blocks, workers, narrow),
@@ -277,7 +253,7 @@
             pltpu.SemaphoreType.DMA((SLOTS, 2)),
         ],
         compiler_params=pltpu.CompilerParams(vmem_limit_bytes=18 << 20),
-    )(*arrived, *held, gate, up)
+    )(*arrived, *held, in_hbm(gate), in_hbm(up))
     back = [[None] * workers for _ in range(blocks)]
     for b in range(blocks):
         for s in range(workers):

time: 38.2 us -> 43.3 us (1.13)
  local copies, waits for them, and re-layouts: 0 us -> 14.7 us
  waiting for transfers between devices: 20.2 us -> 10.6 us
    slice x0 -> x2, local copies, waits for them, and re-layouts: none -> 14.7 us  [shards(): held = [m[:, :early] for m in (gate, up)]]
    ppermute x6, waiting for transfers between devices: 19.9 us -> 10.6 us  [shards(): lax.ppermute(hidden[(blocks - 1 - b) * workers + s], 'wide', pairs)]
  transfers between devices with their start and end apart: 9 -> 9, of which waited for: 3 -> 2; matrix products, arithmetic and copies ran while one was open for 0% -> 34% of each run, Pallas kernels for 0% -> 0%
where the time goes in v11:
time: 43.3 us; the launch traced here: 43 us
  local copies, waits for them, and re-layouts  14.7 us (34%)
  waiting for transfers between devices  10.6 us (24%)
  starting transfers between devices  7.84 us (18%)
  blocking collectives  5.2 us (12%)
  Pallas kernels  3.89 us (9%)
  between operations  0.79 us (2%)
    slice x2, local copies, waits for them, and re-layouts, shards(): held = [m[:, :early] for m in (gate, up)]  14.7 us
    ppermute x6, waiting for transfers between devices, shards(): lax.ppermute(hidden[(blocks - 1 - b) * workers + s], 'wide', pairs)  10.6 us
    ppermute x6, starting transfers between devices, shards(): lax.ppermute(hidden[(blocks - 1 - b) * workers + s], 'wide', pairs)  5.23 us
    all_gather x1, blocking collectives, serve(): lax.all_gather(sent, ('wide', 'narrow'), axis=0, axis_index_groups=groups)  5.2 us
    pallas_call x1, Pallas kernels, serve(): pl.pallas_call(attend_kernel, out_shape=(pltpu.VMEM(shapes[0].shape, jnp....  3.18 us
    ppermute x3, starting transfers between devices, shards(): lax.ppermute(block, 'wide', [(b * workers + j, serving + j) for j in rang...  2.61 us
  transfers between devices with their start and end apart: 9, of which 2 were waited for; matrix products, arithmetic and copies ran while one was open for 34% of the time, Pallas kernels for 0%

profile of v11, /device:TPU:16, one launch (start us, length us, event | category | flops | bytes accessed | tf_op | source)
XLA Modules:
  0.0 43.0 jit_solution(17963121057322493979)
XLA Ops:
  0.6 8.4 %conditional.1 = ((bf16[2,2048]{1,0:T(2,128)(2,1)S(1)}, bf16[4,2,2176]{2,1,0:T(2,128)(2,1)S(1)})) conditional(s32[]{:T(128)} %convert_element_type.3, () %tuple.15, (s32[1]{0:T(128)}, bf16[2,1,2048]{2,0,1:T(2,128)(2,1)}, bf16[2,1,2,512]{3,2,1,0:T(2,128)(2,1)}, bf16[1,4,128,128]{3,2,1,0:T(8,128)(2,1)}, bf16[1,4,128,128]{3,2,1,0:T(8,128)(2,1)}, ...), branch_computations={%region_0.0_spmd, %region_1.0_spmd} | conditional | bytes 43544 | solution.py:236
  0.7 3.2 %branch_1_fun.1 = (bf16[2,2048]{1,0:T(2,128)(2,1)S(1)}, bf16[2,2176]{1,0:T(2,128)(2,1)S(1)}) custom-call(s32[1,1]{1,0:T(1,128)} %bitcast.refs_0_, bf16[2,2048]{1,0:T(2,128)(2,1)} %bitcast.20, bf16[2,2,512]{2,1,0:T(2,128)(2,1)} %bitcast.23, bf16[4,128,128]{2,1,0:T(8,128)(2,1)} %bitcast.18, bf16[4,128,128]{2,1,0:T(8,128)(2,1)} %bitcast.19, ...), custom_call_target="tpu_custom_call" | custom-call | tf_op jit(solution)/shard_map/cond/branch_1_fun/pallas_call | solution.py:210
  3.8 5.2 %all-gather.1 = bf16[4,2,2176]{2,1,0:T(2,128)(2,1)S(1)} all-gather(bf16[1,2,2176]{2,1,0:T(2,128)(2,1)S(1)} %bitcast.13), channel_id=2, replica_groups={{0,1,2,3},{4,5,6,7},{8,9,10,11},{12,13,14,15},{16,17,18,19},{20,21,22,2..., dimensions={0}, use_global_device_ids=true | all-gather | bytes 43520 | tf_op jit(solution)/shard_map/cond/branch_1_fun/all_gather | solution.py:225
  9.0 1.3 %collective-permute-start.2 = (bf16[4,2,2176]{2,1,0:T(2,128)(2,1)S(1)}, bf16[4,2,2176]{2,1,0:T(2,128)(2,1)S(1)}, u32[]{:S(2)}, u32[]{:S(2)}) collective-permute-start(bf16[4,2,2176]{2,1,0:T(2,128)(2,1)S(1)} %get-tuple-element.43), channel_id=1, source_target_pairs={{8,12},{10,14},{9,13},{11,15},{24,28},{26,30},{25,29},{27,31}} | collective-permute-start | bytes 104456 | tf_op jit(solution)/shard_map/ppermute | solution.py:238
  10.3 0.7 %collective-permute-start.1 = (bf16[4,2,2176]{2,1,0:T(2,128)(2,1)S(1)}, bf16[4,2,2176]{2,1,0:T(2,128)(2,1)S(1)}, u32[]{:S(2)}, u32[]{:S(2)}) collective-permute-start(bf16[4,2,2176]{2,1,0:T(2,128)(2,1)S(1)} %get-tuple-element.43), channel_id=1, source_target_pairs={{4,12},{6,14},{5,13},{7,15},{20,28},{22,30},{21,29},{23,31}} | collective-permute-start | bytes 104456 | tf_op jit(solution)/shard_map/ppermute | solution.py:238
  11.0 0.7 %collective-permute-start = (bf16[4,2,2176]{2,1,0:T(2,128)(2,1)S(1)}, bf16[4,2,2176]{2,1,0:T(2,128)(2,1)S(1)}, u32[]{:S(2)}, u32[]{:S(2)}) collective-permute-start(bf16[4,2,2176]{2,1,0:T(2,128)(2,1)S(1)} %get-tuple-element.43), channel_id=1, source_target_pairs={{0,12},{2,14},{1,13},{3,15},{16,28},{18,30},{17,29},{19,31}} | collective-permute-start | bytes 104456 | tf_op jit(solution)/shard_map/ppermute | solution.py:238
  11.7 7.3 %slice.8.refs_3_ = bf16[4096,1792]{1,0:T(8,128)(2,1)S(1)} slice(bf16[4096,3584]{1,0:T(8,128)(2,1)} %bitcast.14), slice={[0:4096], [0:1792]} | slice | bytes 29360128 | tf_op jit(solution)/shard_map/slice | solution.py:243
  19.0 7.3 %slice.9.refs_4_ = bf16[4096,1792]{1,0:T(8,128)(2,1)S(1)} slice(bf16[4096,3584]{1,0:T(8,128)(2,1)} %bitcast.16), slice={[0:4096], [0:1792]} | slice | bytes 29360128 | tf_op jit(solution)/shard_map/slice | solution.py:243
  26.3 0.0 collective-permute-done.2.refs_2_
  26.3 0.0 collective-permute-done.1.refs_1_
  26.4 0.0 collective-permute-done.refs_0_
  26.4 0.1 shard_map.111
  26.5 0.7 %collective-permute-start.3 = (bf16[2,3584]{1,0:T(2,128)(2,1)S(1)}, bf16[2,3584]{1,0:T(2,128)(2,1)S(1)}, u32[]{:S(2)}, u32[]{:S(2)}) collective-permute-start(bf16[2,3584]{1,0:T(2,128)(2,1)S(1)} %get-tuple-element.44), channel_id=1, source_target_pairs={{12,0},{14,2},{13,1},{15,3},{28,16},{30,18},{29,17},{31,19}} | collective-permute-start | bytes 43016 | tf_op jit(solution)/shard_map/ppermute | solution.py:261
  27.1 0.7 %collective-permute-start.4 = (bf16[2,3584]{1,0:T(2,128)(2,1)S(1)}, bf16[2,3584]{1,0:T(2,128)(2,1)S(1)}, u32[]{:S(2)}, u32[]{:S(2)}) collective-permute-start(bf16[2,3584]{1,0:T(2,128)(2,1)S(1)} %get-tuple-element.45), channel_id=1, source_target_pairs={{12,2},{14,0},{13,3},{15,1},{28,18},{30,16},{29,19},{31,17}} | collective-permute-start | bytes 43016 | tf_op jit(solution)/shard_map/ppermute | solution.py:261
  27.8 0.7 %collective-permute-start.5 = (bf16[2,3584]{1,0:T(2,128)(2,1)S(1)}, bf16[2,3584]{1,0:T(2,128)(2,1)S(1)}, u32[]{:S(2)}, u32[]{:S(2)}) collective-permute-start(bf16[2,3584]{1,0:T(2,128)(2,1)S(1)} %get-tuple-element.46), channel_id=1, source_target_pairs={{12,4},{14,6},{13,5},{15,7},{28,20},{30,22},{29,21},{31,23}} | collective-permute-start | bytes 43016 | tf_op jit(solution)/shard_map/ppermute | solution.py:261
  28.5 0.7 %collective-permute-start.6 = (bf16[2,3584]{1,0:T(2,128)(2,1)S(1)}, bf16[2,3584]{1,0:T(2,128)(2,1)S(1)}, u32[]{:S(2)}, u32[]{:S(2)}) collective-permute-start(bf16[2,3584]{1,0:T(2,128)(2,1)S(1)} %get-tuple-element.47), channel_id=1, source_target_pairs={{12,6},{14,4},{13,7},{15,5},{28,22},{30,20},{29,23},{31,21}} | collective-permute-start | bytes 43016 | tf_op jit(solution)/shard_map/ppermute | solution.py:261
  29.1 1.3 %collective-permute-start.7 = (bf16[2,3584]{1,0:T(2,128)(2,1)S(1)}, bf16[2,3584]{1,0:T(2,128)(2,1)S(1)}, u32[]{:S(2)}, u32[]{:S(2)}) collective-permute-start(bf16[2,3584]{1,0:T(2,128)(2,1)S(1)} %get-tuple-element.48), channel_id=1, source_target_pairs={{12,8},{14,10},{13,9},{15,11},{28,24},{30,26},{29,25},{31,27}} | collective-permute-start | bytes 43016 | tf_op jit(solution)/shard_map/ppermute | solution.py:261
  30.4 0.0 collective-permute-done.3.refs_0_
  30.5 1.3 %collective-permute-start.8 = (bf16[2,3584]{1,0:T(2,128)(2,1)S(1)}, bf16[2,3584]{1,0:T(2,128)(2,1)S(1)}, u32[]{:S(2)}, u32[]{:S(2)}) collective-permute-start(bf16[2,3584]{1,0:T(2,128)(2,1)S(1)} %get-tuple-element.49), channel_id=1, source_target_pairs={{12,10},{14,8},{13,11},{15,9},{28,26},{30,24},{29,27},{31,25}} | collective-permute-start | bytes 43016 | tf_op jit(solution)/shard_map/ppermute | solution.py:261
  31.8 0.0 collective-permute-done.4.refs_1_
  31.8 0.0 collective-permute-done.5.refs_2_
  31.8 0.0 collective-permute-done.6.refs_3_
  31.8 8.3 %collective-permute-done.7.refs_4_ = bf16[2,3584]{1,0:T(2,128)(2,1)S(1)} collective-permute-done((bf16[2,3584]{1,0:T(2,128)(2,1)S(1)}, bf16[2,3584]{1,0:T(2,128)(2,1)S(1)}, u32[]{:S(2)}, u32[]{:S(2)}) %collective-permute-start.7) | collective-permute-done | bytes 14368 | tf_op jit(solution)/shard_map/ppermute | solution.py:261
  40.1 2.2 %collective-permute-done.8.refs_5_ = bf16[2,3584]{1,0:T(2,128)(2,1)S(1)} collective-permute-done((bf16[2,3584]{1,0:T(2,128)(2,1)S(1)}, bf16[2,3584]{1,0:T(2,128)(2,1)S(1)}, u32[]{:S(2)}, u32[]{:S(2)}) %collective-permute-start.8) | collective-permute-done | bytes 14368 | tf_op jit(solution)/shard_map/ppermute | solution.py:261
  42.3 0.6 %shard_map.112 = (bf16[2,2048]{1,0:T(2,128)(2,1)}, bf16[2,7168]{1,0:T(2,128)(2,1)}) custom-call(bf16[2,2048]{1,0:T(2,128)(2,1)S(1)} %get-tuple-element.42.attended, bf16[2,3584]{1,0:T(2,128)(2,1)S(1)} %collective-permute-done.3.refs_0_, bf16[2,3584]{1,0:T(2,128)(2,1)S(1)} %collective-permute-done.4.refs_1_, ...), custom_call_target="tpu_custom_call" | custom-call | tf_op jit(solution)/shard_map/pallas_call | solution.py:276
Async XLA Ops:
  9.0 17.3 %collective-permute-start.2 = (bf16[4,2,2176]{2,1,0:T(2,128)(2,1)S(1)}, bf16[4,2,2176]{2,1,0:T(2,128)(2,1)S(1)}, u32[]{:S(2)}, u32[]{:S(2)}) collective-permute-start(bf16[4,2,2176]{2,1,0:T(2,128)(2,1)S(1)} %get-tuple-element.43), channel_id=1, source_target_pairs={{8,12},{10,14},{9,13},{11,15},{24,28},{26,30},{25,29},{27,31}} | collective-permute-start | bytes 104456 | tf_op jit(solution)/shard_map/ppermute | solution.py:238
  10.3 16.0 %collective-permute-start.1 = (bf16[4,2,2176]{2,1,0:T(2,128)(2,1)S(1)}, bf16[4,2,2176]{2,1,0:T(2,128)(2,1)S(1)}, u32[]{:S(2)}, u32[]{:S(2)}) collective-permute-start(bf16[4,2,2176]{2,1,0:T(2,128)(2,1)S(1)} %get-tuple-element.43), channel_id=1, source_target_pairs={{4,12},{6,14},{5,13},{7,15},{20,28},{22,30},{21,29},{23,31}} | collective-permute-start | bytes 104456 | tf_op jit(solution)/shard_map/ppermute | solution.py:238
  11.0 15.4 %collective-permute-start = (bf16[4,2,2176]{2,1,0:T(2,128)(2,1)S(1)}, bf16[4,2,2176]{2,1,0:T(2,128)(2,1)S(1)}, u32[]{:S(2)}, u32[]{:S(2)}) collective-permute-start(bf16[4,2,2176]{2,1,0:T(2,128)(2,1)S(1)} %get-tuple-element.43), channel_id=1, source_target_pairs={{0,12},{2,14},{1,13},{3,15},{16,28},{18,30},{17,29},{19,31}} | collective-permute-start | bytes 104456 | tf_op jit(solution)/shard_map/ppermute | solution.py:238
  26.5 4.0 %collective-permute-start.3 = (bf16[2,3584]{1,0:T(2,128)(2,1)S(1)}, bf16[2,3584]{1,0:T(2,128)(2,1)S(1)}, u32[]{:S(2)}, u32[]{:S(2)}) collective-permute-start(bf16[2,3584]{1,0:T(2,128)(2,1)S(1)} %get-tuple-element.44), channel_id=1, source_target_pairs={{12,0},{14,2},{13,1},{15,3},{28,16},{30,18},{29,17},{31,19}} | collective-permute-start | bytes 43016 | tf_op jit(solution)/shard_map/ppermute | solution.py:261
  27.1 4.6 %collective-permute-start.4 = (bf16[2,3584]{1,0:T(2,128)(2,1)S(1)}, bf16[2,3584]{1,0:T(2,128)(2,1)S(1)}, u32[]{:S(2)}, u32[]{:S(2)}) collective-permute-start(bf16[2,3584]{1,0:T(2,128)(2,1)S(1)} %get-tuple-element.45), channel_id=1, source_target_pairs={{12,2},{14,0},{13,3},{15,1},{28,18},{30,16},{29,19},{31,17}} | collective-permute-start | bytes 43016 | tf_op jit(solution)/shard_map/ppermute | solution.py:261
  27.8 4.0 %collective-permute-start.5 = (bf16[2,3584]{1,0:T(2,128)(2,1)S(1)}, bf16[2,3584]{1,0:T(2,128)(2,1)S(1)}, u32[]{:S(2)}, u32[]{:S(2)}) collective-permute-start(bf16[2,3584]{1,0:T(2,128)(2,1)S(1)} %get-tuple-element.46), channel_id=1, source_target_pairs={{12,4},{14,6},{13,5},{15,7},{28,20},{30,22},{29,21},{31,23}} | collective-permute-start | bytes 43016 | tf_op jit(solution)/shard_map/ppermute | solution.py:261
  28.5 3.3 %collective-permute-start.6 = (bf16[2,3584]{1,0:T(2,128)(2,1)S(1)}, bf16[2,3584]{1,0:T(2,128)(2,1)S(1)}, u32[]{:S(2)}, u32[]{:S(2)}) collective-permute-start(bf16[2,3584]{1,0:T(2,128)(2,1)S(1)} %get-tuple-element.47), channel_id=1, source_target_pairs={{12,6},{14,4},{13,7},{15,5},{28,22},{30,20},{29,23},{31,21}} | collective-permute-start | bytes 43016 | tf_op jit(solution)/shard_map/ppermute | solution.py:261
  29.1 11.0 %collective-permute-start.7 = (bf16[2,3584]{1,0:T(2,128)(2,1)S(1)}, bf16[2,3584]{1,0:T(2,128)(2,1)S(1)}, u32[]{:S(2)}, u32[]{:S(2)}) collective-permute-start(bf16[2,3584]{1,0:T(2,128)(2,1)S(1)} %get-tuple-element.48), channel_id=1, source_target_pairs={{12,8},{14,10},{13,9},{15,11},{28,24},{30,26},{29,25},{31,27}} | collective-permute-start | bytes 43016 | tf_op jit(solution)/shard_map/ppermute | solution.py:261
  30.5 11.9 %collective-permute-start.8 = (bf16[2,3584]{1,0:T(2,128)(2,1)S(1)}, bf16[2,3584]{1,0:T(2,128)(2,1)S(1)}, u32[]{:S(2)}, u32[]{:S(2)}) collective-permute-start(bf16[2,3584]{1,0:T(2,128)(2,1)S(1)} %get-tuple-element.49), channel_id=1, source_target_pairs={{12,10},{14,8},{13,11},{15,9},{28,26},{30,24},{29,27},{31,25}} | collective-permute-start | bytes 43016 | tf_op jit(solution)/shard_map/ppermute | solution.py:261

commit v12 on v10

--- a/solution.py
+++ b/solution.py
@@ -93,6 +93,17 @@
     sent[:, width:] = pair(squares)
 
 
+def places(blocks, workers):
+    middle = blocks // 2
+    leaving = [b for b in range(blocks) if b != middle]
+    found = []
+    for b in range(blocks):
+        for shift in range(workers):
+            nth = leaving.index(b) * workers + shift if b != middle else None
+            found.append(nth)
+    return found
+
+
 def forward_kernel(blocks, workers, narrow, *refs):
     count = blocks * workers
     arrived, (gate_held, up_held, gate, up), rest = refs[:blocks], refs[blocks:][:4], refs[blocks + 4 :]
@@ -138,9 +149,12 @@
             g = jnp.dot(x[...], gate_tile, preferred_element_type=jnp.float32) * r
             u = jnp.dot(x[...], up_tile, preferred_element_type=jnp.float32) * r
             hidden = (g / (1.0 + jnp.exp(-g)) * u).astype(jnp.bfloat16)
-            for i in range(count):
-                out = outs[blocks - 1 - i // workers]
-                out[i % workers, :, at : at + tile] = hidden[i * STEPS : (i + 1) * STEPS]
+            for i, place in enumerate(places(blocks, workers)):
+                rows = hidden[i * STEPS : (i + 1) * STEPS]
+                if place is None:
+                    outs[-1][i % workers, :, at : at + tile] = rows
+                else:
+                    outs[place][:, at : at + tile] = rows
 
         waiting = list(range(0, early, tile))
 
@@ -163,22 +177,33 @@
             resident(len(waiting))
 
 
-def choose_kernel(workers, *refs):
-    results, out = refs[:-1], refs[-1]
-    for b, result in enumerate(results):
-
-        @pl.when(lax.axis_index("wide") // workers == b)
-        def _():
-            out[...] = result[...]
-
-
-def finish_kernel(workers, attended, gathered, attended_out, out):
+def finish_kernel(blocks, workers, attended, gathered, *refs):
+    results, (attended_out, out) = refs[:-2], refs[-2:]
     me = lax.axis_index("wide")
+    block, place = me // workers, lax.rem(me, workers)
     columns = gathered.shape[3]
     attended_out[...] = attended[...]
-    for k in range(workers):
-        shift = lax.rem(lax.rem(me, workers) + workers - k, workers)
-        out[:, k * columns : (k + 1) * columns] = gathered[k, shift]
+
+    @pl.when(block >= blocks)
+    def _():
+        out[...] = jnp.zeros_like(out)
+
+    @pl.when(block == blocks // 2)
+    def _():
+        for k in range(workers):
+            shift = lax.rem(place + workers - k, workers)
+            out[:, k * columns : (k + 1) * columns] = gathered[k, shift]
+
+    if not results:
+        return
+
+    for i, nth in enumerate(places(blocks, workers)):
+        if nth is not None:
+
+            @pl.when(block == i // workers)
+            def _(i=i, nth=nth):
+                k = lax.rem(place + workers - i % workers, workers)
+                out[:, pl.ds(pl.multiple_of(k * columns, 128), columns)] = results[nth][...]
 
 
 def shards(queries, new_kv, keys, values, lengths, residual, gain, gate, up):
@@ -262,11 +287,13 @@
         ),
     )(block, gate, up)
     padded = -(-STEPS * serving // 16) * 16
-    hidden = pl.pallas_call(
+    together = jax.ShapeDtypeStruct((workers, STEPS, columns), jnp.bfloat16)
+    *hidden, shared = pl.pallas_call(
         functools.partial(forward_kernel, blocks, workers, narrow),
-        out_shape=[jax.ShapeDtypeStruct((workers, STEPS, columns), jnp.bfloat16)] * blocks,
+        out_shape=[jax.ShapeDtypeStruct((STEPS, columns), jnp.bfloat16)] * (serving - workers)
+        + [together],
         in_specs=[vmem] * (blocks + 2) + [hbm, hbm],
-        out_specs=[vmem] * blocks,
+        out_specs=[vmem] * (serving - workers + 1),
         scratch_shapes=[
             pltpu.VMEM((padded, features), jnp.bfloat16),
             pltpu.VMEM((SLOTS, 2, features, tile), jnp.bfloat16),
@@ -274,44 +301,54 @@
         ],
         compiler_params=pltpu.CompilerParams(vmem_limit_bytes=18 << 20),
     )(*arrived, *held, gate, up)
-    back = [
-        lax.ppermute(
-            hidden[blocks - 1 - b], "wide", [(serving + k, b * workers + k) for k in range(workers)]
-        )
-        for b in range(blocks)
-    ]
+    middle = blocks // 2
+    shared = lax.ppermute(
+        shared, "wide", [(serving + k, middle * workers + k) for k in range(workers)]
+    )
     peers = [list(range(at, at + workers)) for at in range(0, wide, workers)]
-    shape = jax.ShapeDtypeStruct((workers, STEPS, columns), jnp.bfloat16)
-
-    def collect(*back):
-        mine = pl.pallas_call(
-            functools.partial(choose_kernel, workers),
-            out_shape=shape,
-            in_specs=[vmem] * blocks,
-            out_specs=vmem,
-            compiler_params=pltpu.CompilerParams(vmem_limit_bytes=8 << 20),
-        )(*back)
-        return lax.all_gather(mine, "wide", axis=0, axis_index_groups=peers)
-
-    def skip(*back):
+
+    def skip(shared):
         return pl.pallas_call(
             blank_kernel,
-            out_shape=jax.ShapeDtypeStruct((workers, *shape.shape), jnp.bfloat16),
+            out_shape=jax.ShapeDtypeStruct((workers, *shared.shape), jnp.bfloat16),
             out_specs=vmem,
             compiler_params=pltpu.CompilerParams(vmem_limit_bytes=8 << 20),
         )()
 
-    gathered = lax.cond(owner, collect, skip, *back)
+    gathered = lax.cond(
+        lax.axis_index("wide") // workers == middle,
+        lambda shared: lax.all_gather(shared, "wide", axis=0, axis_index_groups=peers),
+        skip,
+        shared,
+    )
+    results = list(hidden)
+    for i, nth in enumerate(places(blocks, workers)):
+        if nth is not None:
+            b, s = divmod(i, workers)
+            pairs = [(serving + k, b * workers + (k + s) % workers) for k in range(workers)]
+            results[nth] = lax.ppermute(hidden[nth], "wide", pairs)
+    aligned = columns % 128 == 0
     attended, activated = pl.pallas_call(
-        functools.partial(finish_kernel, workers),
+        functools.partial(finish_kernel, blocks, workers),
         out_shape=(
             jax.ShapeDtypeStruct((STEPS, half), jnp.bfloat16),
             jax.ShapeDtypeStruct((STEPS, workers * columns), jnp.bfloat16),
         ),
-        in_specs=[vmem] * 2,
+        in_specs=[vmem] * (2 + (len(results) if aligned else 0)),
         out_specs=(vmem, vmem),
         compiler_params=pltpu.CompilerParams(vmem_limit_bytes=8 << 20),
-    )(attended, gathered)
+    )(attended, gathered, *(results if aligned else []))
+    if not aligned:
+        me = lax.axis_index("wide")
+        pieces = []
+        for k in range(workers):
+            piece = activated[:, k * columns : (k + 1) * columns]
+            for i, nth in enumerate(places(blocks, workers)):
+                if nth is not None:
+                    mine = me == i // workers * workers + (k + i) % workers
+                    piece = jnp.where(mine, results[nth], piece)
+            pieces.append(piece)
+        activated = jnp.concatenate(pieces, 1)
     return attended.reshape(STEPS, 1, half), activated.reshape(STEPS, 1, -1)
 
 

time: 38.9 us -> 37.3 us (0.959)
  blocking collectives: 10.7 us -> 6.18 us
  starting transfers between devices: 5.23 us -> 7.18 us
  waiting for transfers between devices: 18 us -> 18.9 us
    all_gather x1 -> x0, blocking collectives: 4.55 us -> none  [collect(): return lax.all_gather(mine, 'wide', axis=0, axis_index_groups=peers)]
    ppermute x3 -> x5, starting transfers between devices: 2.62 us -> 4.57 us  [the longest x4 3.91 us: shards(): results[nth] = lax.ppermute(hidden[nth], 'wide', pairs)]
    ppermute x3 -> x5, waiting for transfers between devices: 16.5 us -> 17.4 us  [the longest x4 17.3 us: shards(): results[nth] = lax.ppermute(hidden[nth], 'wide', pairs)]
  transfers between devices with their start and end apart: 6 -> 8, of which waited for: 2 -> 3; matrix products, arithmetic and copies ran while one was open for 0% -> 0% of each run, Pallas kernels for 0% -> 0%
where the time goes in v12:
time: 37.3 us; the launch traced here: 37 us
  waiting for transfers between devices  18.9 us (51%)
  starting transfers between devices  7.18 us (19%)
  blocking collectives  6.18 us (17%)
  Pallas kernels  3.94 us (11%)
  between operations  0.76 us (2%)
    ppermute x4, waiting for transfers between devices, shards(): results[nth] = lax.ppermute(hidden[nth], 'wide', pairs)  17.3 us
    all_gather x1, blocking collectives, serve(): lax.all_gather(sent, ('wide', 'narrow'), axis=0, axis_index_groups=groups)  6.18 us
    ppermute x4, starting transfers between devices, shards(): results[nth] = lax.ppermute(hidden[nth], 'wide', pairs)  3.91 us
    pallas_call x1, Pallas kernels, serve(): pl.pallas_call(attend_kernel, out_shape=(pltpu.VMEM(shapes[0].shape, jnp....  3.18 us
    ppermute x3, starting transfers between devices, shards(): lax.ppermute(block, 'wide', [(b * workers + j, serving + j) for j in rang...  2.61 us
    ppermute x3, waiting for transfers between devices, shards(): lax.ppermute(block, 'wide', [(b * workers + j, serving + j) for j in rang...  1.54 us
  transfers between devices with their start and end apart: 8, of which 3 were waited for; matrix products, arithmetic and copies ran while one was open for 0% of the time, Pallas kernels for 0%

profile of v12, /device:TPU:0, one launch (start us, length us, event | category | flops | bytes accessed | tf_op | source)
XLA Modules:
  0.0 37.0 jit_solution(5426804684368750759)
XLA Ops:
  0.6 9.4 %conditional.2 = ((bf16[2,2048]{1,0:T(2,128)(2,1)S(1)}, bf16[4,2,2176]{2,1,0:T(2,128)(2,1)S(1)})) conditional(s32[]{:T(128)} %convert_element_type.6, () %tuple.21, (s32[1]{0:T(128)}, bf16[2,1,2048]{2,0,1:T(2,128)(2,1)}, bf16[2,1,2,512]{3,2,1,0:T(2,128)(2,1)}, bf16[1,4,128,128]{3,2,1,0:T(8,128)(2,1)}, bf16[1,4,128,128]{3,2,1,0:T(8,128)(2,1)}, ...), branch_computations={%region_0.0_spmd, %region_1.0_spmd} | conditional | bytes 43544 | solution.py:271
  0.7 3.2 %branch_1_fun.1 = (bf16[2,2048]{1,0:T(2,128)(2,1)S(1)}, bf16[2,2176]{1,0:T(2,128)(2,1)S(1)}) custom-call(s32[1,1]{1,0:T(1,128)} %bitcast.refs_0_, bf16[2,2048]{1,0:T(2,128)(2,1)} %bitcast.22, bf16[2,2,512]{2,1,0:T(2,128)(2,1)} %bitcast.25, bf16[4,128,128]{2,1,0:T(8,128)(2,1)} %bitcast.20, bf16[4,128,128]{2,1,0:T(8,128)(2,1)} %bitcast.21, ...), custom_call_target="tpu_custom_call" | custom-call | tf_op jit(solution)/shard_map/cond/branch_1_fun/pallas_call | solution.py:245
  3.8 6.2 %all-gather.2 = bf16[4,2,2176]{2,1,0:T(2,128)(2,1)S(1)} all-gather(bf16[1,2,2176]{2,1,0:T(2,128)(2,1)S(1)} %bitcast.14), channel_id=2, replica_groups={{0,1,2,3},{4,5,6,7},{8,9,10,11},{12,13,14,15},{16,17,18,19},{20,21,22,2..., dimensions={0}, use_global_device_ids=true | all-gather | bytes 43520 | tf_op jit(solution)/shard_map/cond/branch_1_fun/all_gather | solution.py:260
  10.0 0.7 %collective-permute-start.2 = (bf16[4,2,2176]{2,1,0:T(2,128)(2,1)S(1)}, bf16[4,2,2176]{2,1,0:T(2,128)(2,1)S(1)}, u32[]{:S(2)}, u32[]{:S(2)}) collective-permute-start(bf16[4,2,2176]{2,1,0:T(2,128)(2,1)S(1)} %get-tuple-element.48._), channel_id=1, source_target_pairs={{8,12},{10,14},{9,13},{11,15},{24,28},{26,30},{25,29},{27,31}} | collective-permute-start | bytes 104456 | tf_op jit(solution)/shard_map/ppermute | solution.py:273
  10.7 0.7 %collective-permute-start.1 = (bf16[4,2,2176]{2,1,0:T(2,128)(2,1)S(1)}, bf16[4,2,2176]{2,1,0:T(2,128)(2,1)S(1)}, u32[]{:S(2)}, u32[]{:S(2)}) collective-permute-start(bf16[4,2,2176]{2,1,0:T(2,128)(2,1)S(1)} %get-tuple-element.48._), channel_id=1, source_target_pairs={{4,12},{6,14},{5,13},{7,15},{20,28},{22,30},{21,29},{23,31}} | collective-permute-start | bytes 104456 | tf_op jit(solution)/shard_map/ppermute | solution.py:273
  11.4 1.3 %collective-permute-start = (bf16[4,2,2176]{2,1,0:T(2,128)(2,1)S(1)}, bf16[4,2,2176]{2,1,0:T(2,128)(2,1)S(1)}, u32[]{:S(2)}, u32[]{:S(2)}) collective-permute-start(bf16[4,2,2176]{2,1,0:T(2,128)(2,1)S(1)} %get-tuple-element.48._), channel_id=1, source_target_pairs={{0,12},{2,14},{1,13},{3,15},{16,28},{18,30},{17,29},{19,31}} | collective-permute-start | bytes 104456 | tf_op jit(solution)/shard_map/ppermute | solution.py:273
  12.7 0.0 collective-permute-done.2.refs_2_
  12.7 0.0 collective-permute-done.1.refs_1_
  12.7 1.5 %collective-permute-done.refs_0_ = bf16[4,2,2176]{2,1,0:T(2,128)(2,1)S(1)} collective-permute-done((bf16[4,2,2176]{2,1,0:T(2,128)(2,1)S(1)}, bf16[4,2,2176]{2,1,0:T(2,128)(2,1)S(1)}, u32[]{:S(2)}, u32[]{:S(2)}) %collective-permute-start) | collective-permute-done | bytes 34848 | tf_op jit(solution)/shard_map/ppermute | solution.py:273
  14.2 0.1 shard_map.112
  14.3 0.7 %collective-permute-start.3 = (bf16[2,2,3584]{2,1,0:T(2,128)(2,1)S(1)}, bf16[2,2,3584]{2,1,0:T(2,128)(2,1)S(1)}, u32[]{:S(2)}, u32[]{:S(2)}) collective-permute-start(bf16[2,2,3584]{2,1,0:T(2,128)(2,1)S(1)} %get-tuple-element.51), channel_id=1, source_target_pairs={{12,4},{14,6},{13,5},{15,7},{28,20},{30,22},{29,21},{31,23}} | collective-permute-start | bytes 86024 | tf_op jit(solution)/shard_map/ppermute | solution.py:305
  15.0 1.3 %collective-permute-start.4 = (bf16[2,3584]{1,0:T(2,128)(2,1)S(1)}, bf16[2,3584]{1,0:T(2,128)(2,1)S(1)}, u32[]{:S(2)}, u32[]{:S(2)}) collective-permute-start(bf16[2,3584]{1,0:T(2,128)(2,1)S(1)} %get-tuple-element.52), channel_id=1, source_target_pairs={{12,0},{14,2},{13,1},{15,3},{28,16},{30,18},{29,17},{31,19}} | collective-permute-start | bytes 43016 | tf_op jit(solution)/shard_map/ppermute | solution.py:329
  16.3 1.3 %collective-permute-start.5 = (bf16[2,3584]{1,0:T(2,128)(2,1)S(1)}, bf16[2,3584]{1,0:T(2,128)(2,1)S(1)}, u32[]{:S(2)}, u32[]{:S(2)}) collective-permute-start(bf16[2,3584]{1,0:T(2,128)(2,1)S(1)} %get-tuple-element.53), channel_id=1, source_target_pairs={{12,2},{14,0},{13,3},{15,1},{28,18},{30,16},{29,19},{31,17}} | collective-permute-start | bytes 43016 | tf_op jit(solution)/shard_map/ppermute | solution.py:329
  17.6 0.7 %collective-permute-start.6 = (bf16[2,3584]{1,0:T(2,128)(2,1)S(1)}, bf16[2,3584]{1,0:T(2,128)(2,1)S(1)}, u32[]{:S(2)}, u32[]{:S(2)}) collective-permute-start(bf16[2,3584]{1,0:T(2,128)(2,1)S(1)} %get-tuple-element.54), channel_id=1, source_target_pairs={{12,8},{14,10},{13,9},{15,11},{28,24},{30,26},{29,25},{31,27}} | collective-permute-start | bytes 43016 | tf_op jit(solution)/shard_map/ppermute | solution.py:329
  18.3 0.7 %collective-permute-start.7 = (bf16[2,3584]{1,0:T(2,128)(2,1)S(1)}, bf16[2,3584]{1,0:T(2,128)(2,1)S(1)}, u32[]{:S(2)}, u32[]{:S(2)}) collective-permute-start(bf16[2,3584]{1,0:T(2,128)(2,1)S(1)} %get-tuple-element.55), channel_id=1, source_target_pairs={{12,10},{14,8},{13,11},{15,9},{28,26},{30,24},{29,27},{31,25}} | collective-permute-start | bytes 43016 | tf_op jit(solution)/shard_map/ppermute | solution.py:329
  19.0 0.0 collective-permute-done.3
  19.0 15.1 %collective-permute-done.4.refs_0_ = bf16[2,3584]{1,0:T(2,128)(2,1)S(1)} collective-permute-done((bf16[2,3584]{1,0:T(2,128)(2,1)S(1)}, bf16[2,3584]{1,0:T(2,128)(2,1)S(1)}, u32[]{:S(2)}, u32[]{:S(2)}) %collective-permute-start.4) | collective-permute-done | bytes 14368 | tf_op jit(solution)/shard_map/ppermute | solution.py:329
  34.1 2.2 %collective-permute-done.5.refs_1_ = bf16[2,3584]{1,0:T(2,128)(2,1)S(1)} collective-permute-done((bf16[2,3584]{1,0:T(2,128)(2,1)S(1)}, bf16[2,3584]{1,0:T(2,128)(2,1)S(1)}, u32[]{:S(2)}, u32[]{:S(2)}) %collective-permute-start.5) | collective-permute-done | bytes 14368 | tf_op jit(solution)/shard_map/ppermute | solution.py:329
  36.3 0.0 collective-permute-done.6.refs_2_
  36.3 0.0 collective-permute-done.7.refs_3_
  36.3 0.6 %shard_map.113 = (bf16[2,2048]{1,0:T(2,128)(2,1)}, bf16[2,7168]{1,0:T(2,128)(2,1)}) custom-call(bf16[2,2048]{1,0:T(2,128)(2,1)S(1)} %get-tuple-element.47.attended, bf16[2,2,2,3584]{3,2,1,0:T(2,128)(2,1)S(1)} %get-tuple-element.91.gathered, bf16[2,3584]{1,0:T(2,128)(2,1)S(1)} %collective-permute-done.4.refs_0_, ...), custom_call_target="tpu_custom_call" | custom-call | tf_op jit(solution)/shard_map/pallas_call | solution.py:331
  (3 shorter events, 0.1 us)
Async XLA Ops:
  10.0 2.7 %collective-permute-start.2 = (bf16[4,2,2176]{2,1,0:T(2,128)(2,1)S(1)}, bf16[4,2,2176]{2,1,0:T(2,128)(2,1)S(1)}, u32[]{:S(2)}, u32[]{:S(2)}) collective-permute-start(bf16[4,2,2176]{2,1,0:T(2,128)(2,1)S(1)} %get-tuple-element.48._), channel_id=1, source_target_pairs={{8,12},{10,14},{9,13},{11,15},{24,28},{26,30},{25,29},{27,31}} | collective-permute-start | bytes 104456 | tf_op jit(solution)/shard_map/ppermute | solution.py:273
  10.7 2.0 %collective-permute-start.1 = (bf16[4,2,2176]{2,1,0:T(2,128)(2,1)S(1)}, bf16[4,2,2176]{2,1,0:T(2,128)(2,1)S(1)}, u32[]{:S(2)}, u32[]{:S(2)}) collective-permute-start(bf16[4,2,2176]{2,1,0:T(2,128)(2,1)S(1)} %get-tuple-element.48._), channel_id=1, source_target_pairs={{4,12},{6,14},{5,13},{7,15},{20,28},{22,30},{21,29},{23,31}} | collective-permute-start | bytes 104456 | tf_op jit(solution)/shard_map/ppermute | solution.py:273
  11.4 2.9 %collective-permute-start = (bf16[4,2,2176]{2,1,0:T(2,128)(2,1)S(1)}, bf16[4,2,2176]{2,1,0:T(2,128)(2,1)S(1)}, u32[]{:S(2)}, u32[]{:S(2)}) collective-permute-start(bf16[4,2,2176]{2,1,0:T(2,128)(2,1)S(1)} %get-tuple-element.48._), channel_id=1, source_target_pairs={{0,12},{2,14},{1,13},{3,15},{16,28},{18,30},{17,29},{19,31}} | collective-permute-start | bytes 104456 | tf_op jit(solution)/shard_map/ppermute | solution.py:273
  14.3 4.6 %collective-permute-start.3 = (bf16[2,2,3584]{2,1,0:T(2,128)(2,1)S(1)}, bf16[2,2,3584]{2,1,0:T(2,128)(2,1)S(1)}, u32[]{:S(2)}, u32[]{:S(2)}) collective-permute-start(bf16[2,2,3584]{2,1,0:T(2,128)(2,1)S(1)} %get-tuple-element.51), channel_id=1, source_target_pairs={{12,4},{14,6},{13,5},{15,7},{28,20},{30,22},{29,21},{31,23}} | collective-permute-start | bytes 86024 | tf_op jit(solution)/shard_map/ppermute | solution.py:305
  15.0 19.1 %collective-permute-start.4 = (bf16[2,3584]{1,0:T(2,128)(2,1)S(1)}, bf16[2,3584]{1,0:T(2,128)(2,1)S(1)}, u32[]{:S(2)}, u32[]{:S(2)}) collective-permute-start(bf16[2,3584]{1,0:T(2,128)(2,1)S(1)} %get-tuple-element.52), channel_id=1, source_target_pairs={{12,0},{14,2},{13,1},{15,3},{28,16},{30,18},{29,17},{31,19}} | collective-permute-start | bytes 43016 | tf_op jit(solution)/shard_map/ppermute | solution.py:329
  16.3 20.0 %collective-permute-start.5 = (bf16[2,3584]{1,0:T(2,128)(2,1)S(1)}, bf16[2,3584]{1,0:T(2,128)(2,1)S(1)}, u32[]{:S(2)}, u32[]{:S(2)}) collective-permute-start(bf16[2,3584]{1,0:T(2,128)(2,1)S(1)} %get-tuple-element.53), channel_id=1, source_target_pairs={{12,2},{14,0},{13,3},{15,1},{28,18},{30,16},{29,19},{31,17}} | collective-permute-start | bytes 43016 | tf_op jit(solution)/shard_map/ppermute | solution.py:329
  17.6 18.7 %collective-permute-start.6 = (bf16[2,3584]{1,0:T(2,128)(2,1)S(1)}, bf16[2,3584]{1,0:T(2,128)(2,1)S(1)}, u32[]{:S(2)}, u32[]{:S(2)}) collective-permute-start(bf16[2,3584]{1,0:T(2,128)(2,1)S(1)} %get-tuple-element.54), channel_id=1, source_target_pairs={{12,8},{14,10},{13,9},{15,11},{28,24},{30,26},{29,25},{31,27}} | collective-permute-start | bytes 43016 | tf_op jit(solution)/shard_map/ppermute | solution.py:329
  18.3 18.1 %collective-permute-start.7 = (bf16[2,3584]{1,0:T(2,128)(2,1)S(1)}, bf16[2,3584]{1,0:T(2,128)(2,1)S(1)}, u32[]{:S(2)}, u32[]{:S(2)}) collective-permute-start(bf16[2,3584]{1,0:T(2,128)(2,1)S(1)} %get-tuple-element.55), channel_id=1, source_target_pairs={{12,10},{14,8},{13,11},{15,9},{28,26},{30,24},{29,27},{31,25}} | collective-permute-start | bytes 43016 | tf_op jit(solution)/shard_map/ppermute | solution.py:329

commit v13 on v12

--- a/solution.py
+++ b/solution.py
@@ -14,7 +14,8 @@
 EPS = 1e-05
 TILE = 256
 SLOTS = 4
-AHEAD = (3, 1, 1, 1, 1)
+SPAN = 512
+AHEAD = (1, 1, 1, 1)
 
 
 def pair(squares):
@@ -58,38 +59,46 @@
     for c in copies:
         c.wait()
     length = lengths[0, 0]
-    slot = lax.broadcasted_iota(jnp.int32, (hist, HEAD_SIZE), 0)
-    rows = group * STEPS
+    first = hist - STEPS
+    for h in range(heads):
+        lanes = slice(h * HEAD_SIZE, (h + 1) * HEAD_SIZE)
+        for t in range(STEPS):
+            keys[h, first + t : first + t + 1, :] = kv[t, 0:1, lanes]
+            values[h, first + t : first + t + 1, :] = kv[t, 1:2, lanes]
+    rows = heads * group * STEPS
     place = lax.broadcasted_iota(jnp.int32, (rows, hist), 1)
     step = lax.broadcasted_iota(jnp.int32, (rows, hist), 0) % STEPS
-    first = hist - STEPS
     seen = (place < length) | ((place >= first) & (place - first <= step))
-    squares = jnp.zeros((STEPS, 1), jnp.float32)
-    for h in range(heads):
-        lanes = slice(h * HEAD_SIZE, (h + 1) * HEAD_SIZE)
-        k, v = keys[h], values[h]
-        for t in range(STEPS):
-            k = jnp.where(slot == first + t, kv[t, 0:1, lanes], k)
-            v = jnp.where(slot == first + t, kv[t, 1:2, lanes], v)
-        cols = [(h * group + g) * HEAD_SIZE for g in range(group)]
-        query = jnp.concatenate(
-            [q[:, c : c + HEAD_SIZE].astype(jnp.float32) for c in cols], 0
-        ).astype(jnp.bfloat16)
-        scores = lax.dot_general(
-            query, k, (((1,), (1,)), ((), ())), preferred_element_type=jnp.float32
-        ) * (1.0 / HEAD_SIZE**0.5)
-        scores = jnp.where(seen, scores, -1e30)
-        top = jnp.max(scores, -1, keepdims=True)
-        e = jnp.where(seen, jnp.exp(scores - top), 0.0)
-        weights = (e / jnp.sum(e, -1, keepdims=True)).astype(jnp.bfloat16)
-        out = jnp.dot(weights, v, preferred_element_type=jnp.float32)
-        for g, c in enumerate(cols):
-            here = slice(c, c + HEAD_SIZE)
-            got = out[g * STEPS : (g + 1) * STEPS].astype(jnp.bfloat16)
-            attended[:, here] = got
-            mixed = residual[:, here].astype(jnp.float32) + got.astype(jnp.float32)
-            squares += jnp.sum(mixed * mixed, -1, keepdims=True)
-            sent[:, here] = (mixed * gain[:, here]).astype(jnp.bfloat16)
+    cols = [c * HEAD_SIZE for c in range(heads * group)]
+    query = jnp.concatenate([q[:, c : c + HEAD_SIZE].astype(jnp.float32) for c in cols], 0)
+    query = query.astype(jnp.bfloat16).reshape(heads, group * STEPS, HEAD_SIZE)
+    scores = jnp.concatenate(
+        [
+            lax.dot_general(
+                query[h], keys[h], (((1,), (1,)), ((), ())), preferred_element_type=jnp.float32
+            )
+            for h in range(heads)
+        ],
+        0,
+    ) * (1.0 / HEAD_SIZE**0.5)
+    scores = jnp.where(seen, scores, -1e30)
+    top = jnp.max(scores, -1, keepdims=True)
+    e = jnp.where(seen, jnp.exp(scores - top), 0.0)
+    weights = (e / jnp.sum(e, -1, keepdims=True)).astype(jnp.bfloat16)
+    weights = weights.reshape(heads, group * STEPS, hist)
+    outs = [
+        jnp.dot(weights[h], values[h], preferred_element_type=jnp.float32) for h in range(heads)
+    ]
+    squares = jnp.zeros((STEPS, HEAD_SIZE), jnp.float32)
+    for i, c in enumerate(cols):
+        here = slice(c, c + HEAD_SIZE)
+        g = i % group * STEPS
+        got = outs[i // group][g : g + STEPS].astype(jnp.bfloat16)
+        attended[:, here] = got
+        mixed = residual[:, here].astype(jnp.float32) + got.astype(jnp.float32)
+        squares += mixed * mixed
+        sent[:, here] = (mixed * gain[:, here]).astype(jnp.bfloat16)
+    squares = jnp.sum(squares, -1, keepdims=True)
     sent[:, width:] = pair(squares)
 
 
@@ -152,15 +161,16 @@
             for i, place in enumerate(places(blocks, workers)):
                 rows = hidden[i * STEPS : (i + 1) * STEPS]
                 if place is None:
-                    outs[-1][i % workers, :, at : at + tile] = rows
+                    outs[-1][i % workers, :, at : at + rows.shape[1]] = rows
                 else:
-                    outs[place][:, at : at + tile] = rows
-
-        waiting = list(range(0, early, tile))
+                    outs[place][:, at : at + rows.shape[1]] = rows
+
+        waiting = list(range(0, early, SPAN))
 
         def resident(some):
             for at in waiting[:some]:
-                produce(at, gate_held[:, at : at + tile], up_held[:, at : at + tile])
+                end = min(at + SPAN, early)
+                produce(at, gate_held[:, at:end], up_held[:, at:end])
             del waiting[:some]
 
         for j, at in enumerate(units):

time: 37.3 us -> 37.7 us (1.011)
  waiting for transfers between devices: 18.9 us -> 20.2 us
  Pallas kernels: 3.94 us -> 3.03 us
    ppermute x4, waiting for transfers between devices: 17.3 us -> 18.7 us  [shards(): results[nth] = lax.ppermute(hidden[nth], 'wide', pairs)]
    pallas_call x1, Pallas kernels: 3.18 us -> 2.28 us  [serve(): pl.pallas_call(attend_kernel, out_shape=(pltpu.VMEM(shapes[0].shape, jnp....]
where the time goes in v13:
time: 37.7 us; the launch traced here: 37.4 us
  waiting for transfers between devices  20.2 us (54%)
  starting transfers between devices  7.18 us (19%)
  blocking collectives  6.18 us (16%)
  Pallas kernels  3.03 us (8%)
  between operations  0.76 us (2%)
    ppermute x4, waiting for transfers between devices, shards(): results[nth] = lax.ppermute(hidden[nth], 'wide', pairs)  18.7 us
    all_gather x1, blocking collectives, serve(): lax.all_gather(sent, ('wide', 'narrow'), axis=0, axis_index_groups=groups)  6.18 us
    ppermute x4, starting transfers between devices, shards(): results[nth] = lax.ppermute(hidden[nth], 'wide', pairs)  3.91 us
    ppermute x3, starting transfers between devices, shards(): lax.ppermute(block, 'wide', [(b * workers + j, serving + j) for j in rang...  2.61 us
    pallas_call x1, Pallas kernels, serve(): pl.pallas_call(attend_kernel, out_shape=(pltpu.VMEM(shapes[0].shape, jnp....  2.28 us
    ppermute x3, waiting for transfers between devices, shards(): lax.ppermute(block, 'wide', [(b * workers + j, serving + j) for j in rang...  1.54 us
  transfers between devices with their start and end apart: 8, of which 3 were waited for; matrix products, arithmetic and copies ran while one was open for 0% of the time, Pallas kernels for 0%

profile of v13, /device:TPU:0, one launch (start us, length us, event | category | flops | bytes accessed | tf_op | source)
XLA Modules:
  0.0 37.4 jit_solution(9311404658870199100)
XLA Ops:
  0.6 8.5 %conditional.2 = ((bf16[2,2048]{1,0:T(2,128)(2,1)S(1)}, bf16[4,2,2176]{2,1,0:T(2,128)(2,1)S(1)})) conditional(s32[]{:T(128)} %convert_element_type.6, () %tuple.21, (s32[1]{0:T(128)}, bf16[2,1,2048]{2,0,1:T(2,128)(2,1)}, bf16[2,1,2,512]{3,2,1,0:T(2,128)(2,1)}, bf16[1,4,128,128]{3,2,1,0:T(8,128)(2,1)}, bf16[1,4,128,128]{3,2,1,0:T(8,128)(2,1)}, ...), branch_computations={%region_0.0_spmd, %region_1.0_spmd} | conditional | bytes 43544 | solution.py:281
  0.7 2.3 %branch_1_fun.1 = (bf16[2,2048]{1,0:T(2,128)(2,1)S(1)}, bf16[2,2176]{1,0:T(2,128)(2,1)S(1)}) custom-call(s32[1,1]{1,0:T(1,128)} %bitcast.refs_0_, bf16[2,2048]{1,0:T(2,128)(2,1)} %bitcast.22, bf16[2,2,512]{2,1,0:T(2,128)(2,1)} %bitcast.25, bf16[4,128,128]{2,1,0:T(8,128)(2,1)} %bitcast.20, bf16[4,128,128]{2,1,0:T(8,128)(2,1)} %bitcast.21, ...), custom_call_target="tpu_custom_call" | custom-call | tf_op jit(solution)/shard_map/cond/branch_1_fun/pallas_call | solution.py:255
  2.9 6.2 %all-gather.2 = bf16[4,2,2176]{2,1,0:T(2,128)(2,1)S(1)} all-gather(bf16[1,2,2176]{2,1,0:T(2,128)(2,1)S(1)} %bitcast.14), channel_id=2, replica_groups={{0,1,2,3},{4,5,6,7},{8,9,10,11},{12,13,14,15},{16,17,18,19},{20,21,22,2..., dimensions={0}, use_global_device_ids=true | all-gather | bytes 43520 | tf_op jit(solution)/shard_map/cond/branch_1_fun/all_gather | solution.py:270
  9.1 0.7 %collective-permute-start.2 = (bf16[4,2,2176]{2,1,0:T(2,128)(2,1)S(1)}, bf16[4,2,2176]{2,1,0:T(2,128)(2,1)S(1)}, u32[]{:S(2)}, u32[]{:S(2)}) collective-permute-start(bf16[4,2,2176]{2,1,0:T(2,128)(2,1)S(1)} %get-tuple-element.48._), channel_id=1, source_target_pairs={{8,12},{10,14},{9,13},{11,15},{24,28},{26,30},{25,29},{27,31}} | collective-permute-start | bytes 104456 | tf_op jit(solution)/shard_map/ppermute | solution.py:283
  9.8 0.7 %collective-permute-start.1 = (bf16[4,2,2176]{2,1,0:T(2,128)(2,1)S(1)}, bf16[4,2,2176]{2,1,0:T(2,128)(2,1)S(1)}, u32[]{:S(2)}, u32[]{:S(2)}) collective-permute-start(bf16[4,2,2176]{2,1,0:T(2,128)(2,1)S(1)} %get-tuple-element.48._), channel_id=1, source_target_pairs={{4,12},{6,14},{5,13},{7,15},{20,28},{22,30},{21,29},{23,31}} | collective-permute-start | bytes 104456 | tf_op jit(solution)/shard_map/ppermute | solution.py:283
  10.5 1.3 %collective-permute-start = (bf16[4,2,2176]{2,1,0:T(2,128)(2,1)S(1)}, bf16[4,2,2176]{2,1,0:T(2,128)(2,1)S(1)}, u32[]{:S(2)}, u32[]{:S(2)}) collective-permute-start(bf16[4,2,2176]{2,1,0:T(2,128)(2,1)S(1)} %get-tuple-element.48._), channel_id=1, source_target_pairs={{0,12},{2,14},{1,13},{3,15},{16,28},{18,30},{17,29},{19,31}} | collective-permute-start | bytes 104456 | tf_op jit(solution)/shard_map/ppermute | solution.py:283
  11.8 0.0 collective-permute-done.2.refs_2_
  11.8 0.0 collective-permute-done.1.refs_1_
  11.8 1.5 %collective-permute-done.refs_0_ = bf16[4,2,2176]{2,1,0:T(2,128)(2,1)S(1)} collective-permute-done((bf16[4,2,2176]{2,1,0:T(2,128)(2,1)S(1)}, bf16[4,2,2176]{2,1,0:T(2,128)(2,1)S(1)}, u32[]{:S(2)}, u32[]{:S(2)}) %collective-permute-start) | collective-permute-done | bytes 34848 | tf_op jit(solution)/shard_map/ppermute | solution.py:283
  13.3 0.1 shard_map.112
  13.4 0.7 %collective-permute-start.3 = (bf16[2,2,3584]{2,1,0:T(2,128)(2,1)S(1)}, bf16[2,2,3584]{2,1,0:T(2,128)(2,1)S(1)}, u32[]{:S(2)}, u32[]{:S(2)}) collective-permute-start(bf16[2,2,3584]{2,1,0:T(2,128)(2,1)S(1)} %get-tuple-element.51), channel_id=1, source_target_pairs={{12,4},{14,6},{13,5},{15,7},{28,20},{30,22},{29,21},{31,23}} | collective-permute-start | bytes 86024 | tf_op jit(solution)/shard_map/ppermute | solution.py:315
  14.1 1.3 %collective-permute-start.4 = (bf16[2,3584]{1,0:T(2,128)(2,1)S(1)}, bf16[2,3584]{1,0:T(2,128)(2,1)S(1)}, u32[]{:S(2)}, u32[]{:S(2)}) collective-permute-start(bf16[2,3584]{1,0:T(2,128)(2,1)S(1)} %get-tuple-element.52), channel_id=1, source_target_pairs={{12,0},{14,2},{13,1},{15,3},{28,16},{30,18},{29,17},{31,19}} | collective-permute-start | bytes 43016 | tf_op jit(solution)/shard_map/ppermute | solution.py:339
  15.4 1.3 %collective-permute-start.5 = (bf16[2,3584]{1,0:T(2,128)(2,1)S(1)}, bf16[2,3584]{1,0:T(2,128)(2,1)S(1)}, u32[]{:S(2)}, u32[]{:S(2)}) collective-permute-start(bf16[2,3584]{1,0:T(2,128)(2,1)S(1)} %get-tuple-element.53), channel_id=1, source_target_pairs={{12,2},{14,0},{13,3},{15,1},{28,18},{30,16},{29,19},{31,17}} | collective-permute-start | bytes 43016 | tf_op jit(solution)/shard_map/ppermute | solution.py:339
  16.7 0.7 %collective-permute-start.6 = (bf16[2,3584]{1,0:T(2,128)(2,1)S(1)}, bf16[2,3584]{1,0:T(2,128)(2,1)S(1)}, u32[]{:S(2)}, u32[]{:S(2)}) collective-permute-start(bf16[2,3584]{1,0:T(2,128)(2,1)S(1)} %get-tuple-element.54), channel_id=1, source_target_pairs={{12,8},{14,10},{13,9},{15,11},{28,24},{30,26},{29,25},{31,27}} | collective-permute-start | bytes 43016 | tf_op jit(solution)/shard_map/ppermute | solution.py:339
  17.4 0.7 %collective-permute-start.7 = (bf16[2,3584]{1,0:T(2,128)(2,1)S(1)}, bf16[2,3584]{1,0:T(2,128)(2,1)S(1)}, u32[]{:S(2)}, u32[]{:S(2)}) collective-permute-start(bf16[2,3584]{1,0:T(2,128)(2,1)S(1)} %get-tuple-element.55), channel_id=1, source_target_pairs={{12,10},{14,8},{13,11},{15,9},{28,26},{30,24},{29,27},{31,25}} | collective-permute-start | bytes 43016 | tf_op jit(solution)/shard_map/ppermute | solution.py:339
  18.1 0.0 collective-permute-done.3
  18.1 16.4 %collective-permute-done.4.refs_0_ = bf16[2,3584]{1,0:T(2,128)(2,1)S(1)} collective-permute-done((bf16[2,3584]{1,0:T(2,128)(2,1)S(1)}, bf16[2,3584]{1,0:T(2,128)(2,1)S(1)}, u32[]{:S(2)}, u32[]{:S(2)}) %collective-permute-start.4) | collective-permute-done | bytes 14368 | tf_op jit(solution)/shard_map/ppermute | solution.py:339
  34.5 2.2 %collective-permute-done.5.refs_1_ = bf16[2,3584]{1,0:T(2,128)(2,1)S(1)} collective-permute-done((bf16[2,3584]{1,0:T(2,128)(2,1)S(1)}, bf16[2,3584]{1,0:T(2,128)(2,1)S(1)}, u32[]{:S(2)}, u32[]{:S(2)}) %collective-permute-start.5) | collective-permute-done | bytes 14368 | tf_op jit(solution)/shard_map/ppermute | solution.py:339
  36.8 0.0 collective-permute-done.6.refs_2_
  36.8 0.0 collective-permute-done.7.refs_3_
  36.8 0.6 %shard_map.113 = (bf16[2,2048]{1,0:T(2,128)(2,1)}, bf16[2,7168]{1,0:T(2,128)(2,1)}) custom-call(bf16[2,2048]{1,0:T(2,128)(2,1)S(1)} %get-tuple-element.47.attended, bf16[2,2,2,3584]{3,2,1,0:T(2,128)(2,1)S(1)} %get-tuple-element.91.gathered, bf16[2,3584]{1,0:T(2,128)(2,1)S(1)} %collective-permute-done.4.refs_0_, ...), custom_call_target="tpu_custom_call" | custom-call | tf_op jit(solution)/shard_map/pallas_call | solution.py:341
  (3 shorter events, 0.1 us)
Async XLA Ops:
  9.1 2.7 %collective-permute-start.2 = (bf16[4,2,2176]{2,1,0:T(2,128)(2,1)S(1)}, bf16[4,2,2176]{2,1,0:T(2,128)(2,1)S(1)}, u32[]{:S(2)}, u32[]{:S(2)}) collective-permute-start(bf16[4,2,2176]{2,1,0:T(2,128)(2,1)S(1)} %get-tuple-element.48._), channel_id=1, source_target_pairs={{8,12},{10,14},{9,13},{11,15},{24,28},{26,30},{25,29},{27,31}} | collective-permute-start | bytes 104456 | tf_op jit(solution)/shard_map/ppermute | solution.py:283
  9.8 2.0 %collective-permute-start.1 = (bf16[4,2,2176]{2,1,0:T(2,128)(2,1)S(1)}, bf16[4,2,2176]{2,1,0:T(2,128)(2,1)S(1)}, u32[]{:S(2)}, u32[]{:S(2)}) collective-permute-start(bf16[4,2,2176]{2,1,0:T(2,128)(2,1)S(1)} %get-tuple-element.48._), channel_id=1, source_target_pairs={{4,12},{6,14},{5,13},{7,15},{20,28},{22,30},{21,29},{23,31}} | collective-permute-start | bytes 104456 | tf_op jit(solution)/shard_map/ppermute | solution.py:283
  10.5 2.9 %collective-permute-start = (bf16[4,2,2176]{2,1,0:T(2,128)(2,1)S(1)}, bf16[4,2,2176]{2,1,0:T(2,128)(2,1)S(1)}, u32[]{:S(2)}, u32[]{:S(2)}) collective-permute-start(bf16[4,2,2176]{2,1,0:T(2,128)(2,1)S(1)} %get-tuple-element.48._), channel_id=1, source_target_pairs={{0,12},{2,14},{1,13},{3,15},{16,28},{18,30},{17,29},{19,31}} | collective-permute-start | bytes 104456 | tf_op jit(solution)/shard_map/ppermute | solution.py:283
  13.4 4.6 %collective-permute-start.3 = (bf16[2,2,3584]{2,1,0:T(2,128)(2,1)S(1)}, bf16[2,2,3584]{2,1,0:T(2,128)(2,1)S(1)}, u32[]{:S(2)}, u32[]{:S(2)}) collective-permute-start(bf16[2,2,3584]{2,1,0:T(2,128)(2,1)S(1)} %get-tuple-element.51), channel_id=1, source_target_pairs={{12,4},{14,6},{13,5},{15,7},{28,20},{30,22},{29,21},{31,23}} | collective-permute-start | bytes 86024 | tf_op jit(solution)/shard_map/ppermute | solution.py:315
  14.1 20.4 %collective-permute-start.4 = (bf16[2,3584]{1,0:T(2,128)(2,1)S(1)}, bf16[2,3584]{1,0:T(2,128)(2,1)S(1)}, u32[]{:S(2)}, u32[]{:S(2)}) collective-permute-start(bf16[2,3584]{1,0:T(2,128)(2,1)S(1)} %get-tuple-element.52), channel_id=1, source_target_pairs={{12,0},{14,2},{13,1},{15,3},{28,16},{30,18},{29,17},{31,19}} | collective-permute-start | bytes 43016 | tf_op jit(solution)/shard_map/ppermute | solution.py:339
  15.4 21.4 %collective-permute-start.5 = (bf16[2,3584]{1,0:T(2,128)(2,1)S(1)}, bf16[2,3584]{1,0:T(2,128)(2,1)S(1)}, u32[]{:S(2)}, u32[]{:S(2)}) collective-permute-start(bf16[2,3584]{1,0:T(2,128)(2,1)S(1)} %get-tuple-element.53), channel_id=1, source_target_pairs={{12,2},{14,0},{13,3},{15,1},{28,18},{30,16},{29,19},{31,17}} | collective-permute-start | bytes 43016 | tf_op jit(solution)/shard_map/ppermute | solution.py:339
  16.7 20.1 %collective-permute-start.6 = (bf16[2,3584]{1,0:T(2,128)(2,1)S(1)}, bf16[2,3584]{1,0:T(2,128)(2,1)S(1)}, u32[]{:S(2)}, u32[]{:S(2)}) collective-permute-start(bf16[2,3584]{1,0:T(2,128)(2,1)S(1)} %get-tuple-element.54), channel_id=1, source_target_pairs={{12,8},{14,10},{13,9},{15,11},{28,24},{30,26},{29,25},{31,27}} | collective-permute-start | bytes 43016 | tf_op jit(solution)/shard_map/ppermute | solution.py:339
  17.4 19.4 %collective-permute-start.7 = (bf16[2,3584]{1,0:T(2,128)(2,1)S(1)}, bf16[2,3584]{1,0:T(2,128)(2,1)S(1)}, u32[]{:S(2)}, u32[]{:S(2)}) collective-permute-start(bf16[2,3584]{1,0:T(2,128)(2,1)S(1)} %get-tuple-element.55), channel_id=1, source_target_pairs={{12,10},{14,8},{13,11},{15,9},{28,26},{30,24},{29,27},{31,25}} | collective-permute-start | bytes 43016 | tf_op jit(solution)/shard_map/ppermute | solution.py:339

commit v14 on v13

--- a/solution.py
+++ b/solution.py
@@ -14,8 +14,7 @@
 EPS = 1e-05
 TILE = 256
 SLOTS = 4
-SPAN = 512
-AHEAD = (1, 1, 1, 1)
+AHEAD = (3, 1, 1, 1, 1)
 
 
 def pair(squares):
@@ -123,12 +122,14 @@
     early = gate_held.shape[1]
     room, _, _, tile = slots.shape
     units = list(range(early, columns, tile))
+    depths = [pl.ds(0, features // 2), pl.ds(features // 2, features // 2)]
 
     def stream(j):
         s = j % room
         here = pl.ds(units[j], tile)
         return [
-            pltpu.make_async_copy(m.at[:, here], slots.at[s, i], sems.at[s, i])
+            pltpu.make_async_copy(m.at[k, here], slots.at[s, i, k], sems.at[s, i, part])
+            for part, k in enumerate(depths)
             for i, m in enumerate((gate, up))
         ]
 
@@ -137,26 +138,29 @@
         for j in range(min(room, len(units))):
             for copy in stream(j):
                 copy.start()
-        lines, tails = [], []
-        for block in arrived:
+        tails = []
+        for b, block in enumerate(arrived):
             for shift in range(workers):
                 owner = lax.rem(me + shift, workers)
-                halves = [block[owner * narrow + n] for n in range(narrow)]
-                lines.append(
-                    jnp.concatenate([h[:, :half] for h in halves], 1).astype(jnp.float32)
-                )
-                tails.append(sum(h[:, half:].astype(jnp.float32) for h in halves))
+                at = (b * workers + shift) * STEPS
+                tail = jnp.zeros((STEPS, TAIL), jnp.float32)
+                for n in range(narrow):
+                    piece = block[owner * narrow + n]
+                    x[at : at + STEPS, n * half : (n + 1) * half] = piece[:, :half]
+                    tail += piece[:, half:].astype(jnp.float32)
+                tails.append(tail)
         pad = x.shape[0] - STEPS * count
         if pad:
-            lines.append(jnp.zeros((pad, features), jnp.float32))
+            x[STEPS * count :, :] = jnp.zeros((pad, features), jnp.bfloat16)
             tails.append(jnp.zeros((pad, TAIL), jnp.float32))
-        x[...] = jnp.concatenate(lines, 0).astype(jnp.bfloat16)
         squares = jnp.sum(jnp.concatenate(tails, 0), -1, keepdims=True)
         r = lax.rsqrt(squares / D + EPS)
 
-        def produce(at, gate_tile, up_tile):
-            g = jnp.dot(x[...], gate_tile, preferred_element_type=jnp.float32) * r
-            u = jnp.dot(x[...], up_tile, preferred_element_type=jnp.float32) * r
+        def product(rows, block):
+            return jnp.dot(rows, block, preferred_element_type=jnp.float32)
+
+        def produce(at, g, u):
+            g, u = g * r, u * r
             hidden = (g / (1.0 + jnp.exp(-g)) * u).astype(jnp.bfloat16)
             for i, place in enumerate(places(blocks, workers)):
                 rows = hidden[i * STEPS : (i + 1) * STEPS]
@@ -165,21 +169,32 @@
                 else:
                     outs[place][:, at : at + rows.shape[1]] = rows
 
-        waiting = list(range(0, early, SPAN))
+        waiting = list(range(0, early, tile))
 
         def resident(some):
             for at in waiting[:some]:
-                end = min(at + SPAN, early)
-                produce(at, gate_held[:, at:end], up_held[:, at:end])
+                here = slice(at, at + tile)
+                produce(at, *[product(x[...], held[:, here]) for held in (gate_held, up_held)])
             del waiting[:some]
 
         for j, at in enumerate(units):
             resident(AHEAD[j] if j < len(AHEAD) else 0)
             if j == len(units) - 1:
                 resident(len(waiting))
-            for copy in stream(j):
-                copy.wait()
-            produce(at, slots[j % room, 0], slots[j % room, 1])
+            s = j % room
+            if j < len(units) - 1:
+                for copy in stream(j):
+                    copy.wait()
+                produce(at, *[product(x[...], slots[s, i]) for i in range(2)])
+            else:
+                sums = [0.0, 0.0]
+                for part in range(2):
+                    k = slice(part * features // 2, (part + 1) * features // 2)
+                    for copy in stream(j)[part * 2 : part * 2 + 2]:
+                        copy.wait()
+                    for i in range(2):
+                        sums[i] += product(x[:, k], slots[s, i, k])
+                produce(at, *sums)
             if j + room < len(units):
                 for copy in stream(j + room):
                     copy.start()
@@ -307,9 +322,9 @@
         scratch_shapes=[
             pltpu.VMEM((padded, features), jnp.bfloat16),
             pltpu.VMEM((SLOTS, 2, features, tile), jnp.bfloat16),
-            pltpu.SemaphoreType.DMA((SLOTS, 2)),
+            pltpu.SemaphoreType.DMA((SLOTS, 2, 2)),
         ],
-        compiler_params=pltpu.CompilerParams(vmem_limit_bytes=18 << 20),
+        compiler_params=pltpu.CompilerParams(vmem_limit_bytes=19 << 20),
     )(*arrived, *held, gate, up)
     middle = blocks // 2
     shared = lax.ppermute(

time: 37.7 us -> 37.9 us (level)
  no operation moved by 1% of the time
where the time goes in v14:
time: 37.9 us; the launch traced here: 37.6 us
  waiting for transfers between devices  20.3 us (54%)
  starting transfers between devices  7.18 us (19%)
  blocking collectives  6.18 us (16%)
  Pallas kernels  3.11 us (8%)
  between operations  0.76 us (2%)
    ppermute x4, waiting for transfers between devices, shards(): results[nth] = lax.ppermute(hidden[nth], 'wide', pairs)  18.8 us
    all_gather x1, blocking collectives, serve(): lax.all_gather(sent, ('wide', 'narrow'), axis=0, axis_index_groups=groups)  6.18 us
    ppermute x4, starting transfers between devices, shards(): results[nth] = lax.ppermute(hidden[nth], 'wide', pairs)  3.91 us
    ppermute x3, starting transfers between devices, shards(): lax.ppermute(block, 'wide', [(b * workers + j, serving + j) for j in rang...  2.61 us
    pallas_call x1, Pallas kernels, serve(): pl.pallas_call(attend_kernel, out_shape=(pltpu.VMEM(shapes[0].shape, jnp....  2.28 us
    ppermute x3, waiting for transfers between devices, shards(): lax.ppermute(block, 'wide', [(b * workers + j, serving + j) for j in rang...  1.54 us
  transfers between devices with their start and end apart: 8, of which 3 were waited for; matrix products, arithmetic and copies ran while one was open for 0% of the time, Pallas kernels for 0%

profile of v14, /device:TPU:0, one launch (start us, length us, event | category | flops | bytes accessed | tf_op | source)
XLA Modules:
  0.0 37.6 jit_solution(3059505922077300785)
XLA Ops:
  0.6 8.5 %conditional.2 = ((bf16[2,2048]{1,0:T(2,128)(2,1)S(1)}, bf16[4,2,2176]{2,1,0:T(2,128)(2,1)S(1)})) conditional(s32[]{:T(128)} %convert_element_type.6, () %tuple.21, (s32[1]{0:T(128)}, bf16[2,1,2048]{2,0,1:T(2,128)(2,1)}, bf16[2,1,2,512]{3,2,1,0:T(2,128)(2,1)}, bf16[1,4,128,128]{3,2,1,0:T(8,128)(2,1)}, bf16[1,4,128,128]{3,2,1,0:T(8,128)(2,1)}, ...), branch_computations={%region_0.0_spmd, %region_1.0_spmd} | conditional | bytes 43544 | solution.py:296
  0.7 2.3 %branch_1_fun.1 = (bf16[2,2048]{1,0:T(2,128)(2,1)S(1)}, bf16[2,2176]{1,0:T(2,128)(2,1)S(1)}) custom-call(s32[1,1]{1,0:T(1,128)} %bitcast.refs_0_, bf16[2,2048]{1,0:T(2,128)(2,1)} %bitcast.22, bf16[2,2,512]{2,1,0:T(2,128)(2,1)} %bitcast.25, bf16[4,128,128]{2,1,0:T(8,128)(2,1)} %bitcast.20, bf16[4,128,128]{2,1,0:T(8,128)(2,1)} %bitcast.21, ...), custom_call_target="tpu_custom_call" | custom-call | tf_op jit(solution)/shard_map/cond/branch_1_fun/pallas_call | solution.py:270
  2.9 6.2 %all-gather.2 = bf16[4,2,2176]{2,1,0:T(2,128)(2,1)S(1)} all-gather(bf16[1,2,2176]{2,1,0:T(2,128)(2,1)S(1)} %bitcast.14), channel_id=2, replica_groups={{0,1,2,3},{4,5,6,7},{8,9,10,11},{12,13,14,15},{16,17,18,19},{20,21,22,2..., dimensions={0}, use_global_device_ids=true | all-gather | bytes 43520 | tf_op jit(solution)/shard_map/cond/branch_1_fun/all_gather | solution.py:285
  9.1 0.7 %collective-permute-start.2 = (bf16[4,2,2176]{2,1,0:T(2,128)(2,1)S(1)}, bf16[4,2,2176]{2,1,0:T(2,128)(2,1)S(1)}, u32[]{:S(2)}, u32[]{:S(2)}) collective-permute-start(bf16[4,2,2176]{2,1,0:T(2,128)(2,1)S(1)} %get-tuple-element.48._), channel_id=1, source_target_pairs={{8,12},{10,14},{9,13},{11,15},{24,28},{26,30},{25,29},{27,31}} | collective-permute-start | bytes 104456 | tf_op jit(solution)/shard_map/ppermute | solution.py:298
  9.8 0.7 %collective-permute-start.1 = (bf16[4,2,2176]{2,1,0:T(2,128)(2,1)S(1)}, bf16[4,2,2176]{2,1,0:T(2,128)(2,1)S(1)}, u32[]{:S(2)}, u32[]{:S(2)}) collective-permute-start(bf16[4,2,2176]{2,1,0:T(2,128)(2,1)S(1)} %get-tuple-element.48._), channel_id=1, source_target_pairs={{4,12},{6,14},{5,13},{7,15},{20,28},{22,30},{21,29},{23,31}} | collective-permute-start | bytes 104456 | tf_op jit(solution)/shard_map/ppermute | solution.py:298
  10.5 1.3 %collective-permute-start = (bf16[4,2,2176]{2,1,0:T(2,128)(2,1)S(1)}, bf16[4,2,2176]{2,1,0:T(2,128)(2,1)S(1)}, u32[]{:S(2)}, u32[]{:S(2)}) collective-permute-start(bf16[4,2,2176]{2,1,0:T(2,128)(2,1)S(1)} %get-tuple-element.48._), channel_id=1, source_target_pairs={{0,12},{2,14},{1,13},{3,15},{16,28},{18,30},{17,29},{19,31}} | collective-permute-start | bytes 104456 | tf_op jit(solution)/shard_map/ppermute | solution.py:298
  11.8 0.0 collective-permute-done.2.refs_2_
  11.8 0.0 collective-permute-done.1.refs_1_
  11.8 1.5 %collective-permute-done.refs_0_ = bf16[4,2,2176]{2,1,0:T(2,128)(2,1)S(1)} collective-permute-done((bf16[4,2,2176]{2,1,0:T(2,128)(2,1)S(1)}, bf16[4,2,2176]{2,1,0:T(2,128)(2,1)S(1)}, u32[]{:S(2)}, u32[]{:S(2)}) %collective-permute-start) | collective-permute-done | bytes 34848 | tf_op jit(solution)/shard_map/ppermute | solution.py:298
  13.3 0.1 shard_map.112
  13.5 0.7 %collective-permute-start.3 = (bf16[2,2,3584]{2,1,0:T(2,128)(2,1)S(1)}, bf16[2,2,3584]{2,1,0:T(2,128)(2,1)S(1)}, u32[]{:S(2)}, u32[]{:S(2)}) collective-permute-start(bf16[2,2,3584]{2,1,0:T(2,128)(2,1)S(1)} %get-tuple-element.51), channel_id=1, source_target_pairs={{12,4},{14,6},{13,5},{15,7},{28,20},{30,22},{29,21},{31,23}} | collective-permute-start | bytes 86024 | tf_op jit(solution)/shard_map/ppermute | solution.py:330
  14.2 1.3 %collective-permute-start.4 = (bf16[2,3584]{1,0:T(2,128)(2,1)S(1)}, bf16[2,3584]{1,0:T(2,128)(2,1)S(1)}, u32[]{:S(2)}, u32[]{:S(2)}) collective-permute-start(bf16[2,3584]{1,0:T(2,128)(2,1)S(1)} %get-tuple-element.52), channel_id=1, source_target_pairs={{12,0},{14,2},{13,1},{15,3},{28,16},{30,18},{29,17},{31,19}} | collective-permute-start | bytes 43016 | tf_op jit(solution)/shard_map/ppermute | solution.py:354
  15.5 1.3 %collective-permute-start.5 = (bf16[2,3584]{1,0:T(2,128)(2,1)S(1)}, bf16[2,3584]{1,0:T(2,128)(2,1)S(1)}, u32[]{:S(2)}, u32[]{:S(2)}) collective-permute-start(bf16[2,3584]{1,0:T(2,128)(2,1)S(1)} %get-tuple-element.53), channel_id=1, source_target_pairs={{12,2},{14,0},{13,3},{15,1},{28,18},{30,16},{29,19},{31,17}} | collective-permute-start | bytes 43016 | tf_op jit(solution)/shard_map/ppermute | solution.py:354
  16.8 0.7 %collective-permute-start.6 = (bf16[2,3584]{1,0:T(2,128)(2,1)S(1)}, bf16[2,3584]{1,0:T(2,128)(2,1)S(1)}, u32[]{:S(2)}, u32[]{:S(2)}) collective-permute-start(bf16[2,3584]{1,0:T(2,128)(2,1)S(1)} %get-tuple-element.54), channel_id=1, source_target_pairs={{12,8},{14,10},{13,9},{15,11},{28,24},{30,26},{29,25},{31,27}} | collective-permute-start | bytes 43016 | tf_op jit(solution)/shard_map/ppermute | solution.py:354
  17.4 0.7 %collective-permute-start.7 = (bf16[2,3584]{1,0:T(2,128)(2,1)S(1)}, bf16[2,3584]{1,0:T(2,128)(2,1)S(1)}, u32[]{:S(2)}, u32[]{:S(2)}) collective-permute-start(bf16[2,3584]{1,0:T(2,128)(2,1)S(1)} %get-tuple-element.55), channel_id=1, source_target_pairs={{12,10},{14,8},{13,11},{15,9},{28,26},{30,24},{29,27},{31,25}} | collective-permute-start | bytes 43016 | tf_op jit(solution)/shard_map/ppermute | solution.py:354
  18.1 0.0 collective-permute-done.3
  18.2 16.6 %collective-permute-done.4.refs_0_ = bf16[2,3584]{1,0:T(2,128)(2,1)S(1)} collective-permute-done((bf16[2,3584]{1,0:T(2,128)(2,1)S(1)}, bf16[2,3584]{1,0:T(2,128)(2,1)S(1)}, u32[]{:S(2)}, u32[]{:S(2)}) %collective-permute-start.4) | collective-permute-done | bytes 14368 | tf_op jit(solution)/shard_map/ppermute | solution.py:354
  34.7 2.2 %collective-permute-done.5.refs_1_ = bf16[2,3584]{1,0:T(2,128)(2,1)S(1)} collective-permute-done((bf16[2,3584]{1,0:T(2,128)(2,1)S(1)}, bf16[2,3584]{1,0:T(2,128)(2,1)S(1)}, u32[]{:S(2)}, u32[]{:S(2)}) %collective-permute-start.5) | collective-permute-done | bytes 14368 | tf_op jit(solution)/shard_map/ppermute | solution.py:354
  36.9 0.0 collective-permute-done.6.refs_2_
  37.0 0.0 collective-permute-done.7.refs_3_
  37.0 0.6 %shard_map.113 = (bf16[2,2048]{1,0:T(2,128)(2,1)}, bf16[2,7168]{1,0:T(2,128)(2,1)}) custom-call(bf16[2,2048]{1,0:T(2,128)(2,1)S(1)} %get-tuple-element.47.attended, bf16[2,2,2,3584]{3,2,1,0:T(2,128)(2,1)S(1)} %get-tuple-element.91.gathered, bf16[2,3584]{1,0:T(2,128)(2,1)S(1)} %collective-permute-done.4.refs_0_, ...), custom_call_target="tpu_custom_call" | custom-call | tf_op jit(solution)/shard_map/pallas_call | solution.py:356
  (3 shorter events, 0.1 us)
Async XLA Ops:
  9.1 2.7 %collective-permute-start.2 = (bf16[4,2,2176]{2,1,0:T(2,128)(2,1)S(1)}, bf16[4,2,2176]{2,1,0:T(2,128)(2,1)S(1)}, u32[]{:S(2)}, u32[]{:S(2)}) collective-permute-start(bf16[4,2,2176]{2,1,0:T(2,128)(2,1)S(1)} %get-tuple-element.48._), channel_id=1, source_target_pairs={{8,12},{10,14},{9,13},{11,15},{24,28},{26,30},{25,29},{27,31}} | collective-permute-start | bytes 104456 | tf_op jit(solution)/shard_map/ppermute | solution.py:298
  9.8 2.0 %collective-permute-start.1 = (bf16[4,2,2176]{2,1,0:T(2,128)(2,1)S(1)}, bf16[4,2,2176]{2,1,0:T(2,128)(2,1)S(1)}, u32[]{:S(2)}, u32[]{:S(2)}) collective-permute-start(bf16[4,2,2176]{2,1,0:T(2,128)(2,1)S(1)} %get-tuple-element.48._), channel_id=1, source_target_pairs={{4,12},{6,14},{5,13},{7,15},{20,28},{22,30},{21,29},{23,31}} | collective-permute-start | bytes 104456 | tf_op jit(solution)/shard_map/ppermute | solution.py:298
  10.5 2.9 %collective-permute-start = (bf16[4,2,2176]{2,1,0:T(2,128)(2,1)S(1)}, bf16[4,2,2176]{2,1,0:T(2,128)(2,1)S(1)}, u32[]{:S(2)}, u32[]{:S(2)}) collective-permute-start(bf16[4,2,2176]{2,1,0:T(2,128)(2,1)S(1)} %get-tuple-element.48._), channel_id=1, source_target_pairs={{0,12},{2,14},{1,13},{3,15},{16,28},{18,30},{17,29},{19,31}} | collective-permute-start | bytes 104456 | tf_op jit(solution)/shard_map/ppermute | solution.py:298
  13.5 4.6 %collective-permute-start.3 = (bf16[2,2,3584]{2,1,0:T(2,128)(2,1)S(1)}, bf16[2,2,3584]{2,1,0:T(2,128)(2,1)S(1)}, u32[]{:S(2)}, u32[]{:S(2)}) collective-permute-start(bf16[2,2,3584]{2,1,0:T(2,128)(2,1)S(1)} %get-tuple-element.51), channel_id=1, source_target_pairs={{12,4},{14,6},{13,5},{15,7},{28,20},{30,22},{29,21},{31,23}} | collective-permute-start | bytes 86024 | tf_op jit(solution)/shard_map/ppermute | solution.py:330
  14.2 20.6 %collective-permute-start.4 = (bf16[2,3584]{1,0:T(2,128)(2,1)S(1)}, bf16[2,3584]{1,0:T(2,128)(2,1)S(1)}, u32[]{:S(2)}, u32[]{:S(2)}) collective-permute-start(bf16[2,3584]{1,0:T(2,128)(2,1)S(1)} %get-tuple-element.52), channel_id=1, source_target_pairs={{12,0},{14,2},{13,1},{15,3},{28,16},{30,18},{29,17},{31,19}} | collective-permute-start | bytes 43016 | tf_op jit(solution)/shard_map/ppermute | solution.py:354
  15.5 21.5 %collective-permute-start.5 = (bf16[2,3584]{1,0:T(2,128)(2,1)S(1)}, bf16[2,3584]{1,0:T(2,128)(2,1)S(1)}, u32[]{:S(2)}, u32[]{:S(2)}) collective-permute-start(bf16[2,3584]{1,0:T(2,128)(2,1)S(1)} %get-tuple-element.53), channel_id=1, source_target_pairs={{12,2},{14,0},{13,3},{15,1},{28,18},{30,16},{29,19},{31,17}} | collective-permute-start | bytes 43016 | tf_op jit(solution)/shard_map/ppermute | solution.py:354
  16.8 20.2 %collective-permute-start.6 = (bf16[2,3584]{1,0:T(2,128)(2,1)S(1)}, bf16[2,3584]{1,0:T(2,128)(2,1)S(1)}, u32[]{:S(2)}, u32[]{:S(2)}) collective-permute-start(bf16[2,3584]{1,0:T(2,128)(2,1)S(1)} %get-tuple-element.54), channel_id=1, source_target_pairs={{12,8},{14,10},{13,9},{15,11},{28,24},{30,26},{29,25},{31,27}} | collective-permute-start | bytes 43016 | tf_op jit(solution)/shard_map/ppermute | solution.py:354
  17.4 19.5 %collective-permute-start.7 = (bf16[2,3584]{1,0:T(2,128)(2,1)S(1)}, bf16[2,3584]{1,0:T(2,128)(2,1)S(1)}, u32[]{:S(2)}, u32[]{:S(2)}) collective-permute-start(bf16[2,3584]{1,0:T(2,128)(2,1)S(1)} %get-tuple-element.55), channel_id=1, source_target_pairs={{12,10},{14,8},{13,11},{15,9},{28,26},{30,24},{29,27},{31,25}} | collective-permute-start | bytes 43016 | tf_op jit(solution)/shard_map/ppermute | solution.py:354

commit v15 on v13

--- a/solution.py
+++ b/solution.py
@@ -14,8 +14,8 @@
 EPS = 1e-05
 TILE = 256
 SLOTS = 4
-SPAN = 512
-AHEAD = (1, 1, 1, 1)
+AHEAD = (3, 1, 1, 1, 1)
+CHUNK = 1024
 
 
 def pair(squares):
@@ -127,8 +127,11 @@
     def stream(j):
         s = j % room
         here = pl.ds(units[j], tile)
+        size = features // 2 if j == len(units) - 1 else features
+        depths = [pl.ds(at, size) for at in range(0, features, size)]
         return [
-            pltpu.make_async_copy(m.at[:, here], slots.at[s, i], sems.at[s, i])
+            pltpu.make_async_copy(m.at[k, here], slots.at[s, i, k], sems.at[s, i, part])
+            for part, k in enumerate(depths)
             for i, m in enumerate((gate, up))
         ]
 
@@ -154,32 +157,45 @@
         squares = jnp.sum(jnp.concatenate(tails, 0), -1, keepdims=True)
         r = lax.rsqrt(squares / D + EPS)
 
-        def produce(at, gate_tile, up_tile):
-            g = jnp.dot(x[...], gate_tile, preferred_element_type=jnp.float32) * r
-            u = jnp.dot(x[...], up_tile, preferred_element_type=jnp.float32) * r
+        def multiply(depth, sums, tiles):
+            for at in range(depth.start, depth.stop, CHUNK):
+                k = slice(at, min(at + CHUNK, depth.stop))
+                for i, some in enumerate(tiles):
+                    more = jnp.dot(x[:, k], some(k), preferred_element_type=jnp.float32)
+                    sums[i] = more if sums[i] is None else sums[i] + more
+            return sums
+
+        def produce(at, g, u):
+            g, u = g * r, u * r
             hidden = (g / (1.0 + jnp.exp(-g)) * u).astype(jnp.bfloat16)
             for i, place in enumerate(places(blocks, workers)):
                 rows = hidden[i * STEPS : (i + 1) * STEPS]
                 if place is None:
-                    outs[-1][i % workers, :, at : at + rows.shape[1]] = rows
+                    outs[-1][i % workers, :, at : at + tile] = rows
                 else:
-                    outs[place][:, at : at + rows.shape[1]] = rows
-
-        waiting = list(range(0, early, SPAN))
+                    outs[place][:, at : at + tile] = rows
+
+        waiting = list(range(0, early, tile))
 
         def resident(some):
             for at in waiting[:some]:
-                end = min(at + SPAN, early)
-                produce(at, gate_held[:, at:end], up_held[:, at:end])
+                here = slice(at, at + tile)
+                tiles = [lambda k, m=m: m[k, here] for m in (gate_held, up_held)]
+                produce(at, *multiply(slice(0, features), [None] * 2, tiles))
             del waiting[:some]
 
         for j, at in enumerate(units):
             resident(AHEAD[j] if j < len(AHEAD) else 0)
             if j == len(units) - 1:
                 resident(len(waiting))
-            for copy in stream(j):
-                copy.wait()
-            produce(at, slots[j % room, 0], slots[j % room, 1])
+            copies, sums = stream(j), [None] * 2
+            tiles = [lambda k, i=i, s=j % room: slots[s, i, k, :] for i in range(2)]
+            size = features * 2 // len(copies)
+            for part in range(len(copies) // 2):
+                for copy in copies[part * 2 : part * 2 + 2]:
+                    copy.wait()
+                multiply(slice(part * size, (part + 1) * size), sums, tiles)
+            produce(at, *sums)
             if j + room < len(units):
                 for copy in stream(j + room):
                     copy.start()
@@ -307,9 +323,9 @@
         scratch_shapes=[
             pltpu.VMEM((padded, features), jnp.bfloat16),
             pltpu.VMEM((SLOTS, 2, features, tile), jnp.bfloat16),
-            pltpu.SemaphoreType.DMA((SLOTS, 2)),
+            pltpu.SemaphoreType.DMA((SLOTS, 2, 2)),
         ],
-        compiler_params=pltpu.CompilerParams(vmem_limit_bytes=18 << 20),
+        compiler_params=pltpu.CompilerParams(vmem_limit_bytes=19 << 20),
     )(*arrived, *held, gate, up)
     middle = blocks // 2
     shared = lax.ppermute(

time: 37.7 us -> 37 us (0.981)
  waiting for transfers between devices: 20.2 us -> 19.4 us
    ppermute x4, waiting for transfers between devices: 18.7 us -> 17.8 us  [shards(): results[nth] = lax.ppermute(hidden[nth], 'wide', pairs)]
where the time goes in v15:
time: 37 us; the launch traced here: 36.7 us
  waiting for transfers between devices  19.4 us (52%)
  starting transfers between devices  7.18 us (19%)
  blocking collectives  6.18 us (17%)
  Pallas kernels  3.11 us (8%)
  between operations  0.76 us (2%)
    ppermute x4, waiting for transfers between devices, shards(): results[nth] = lax.ppermute(hidden[nth], 'wide', pairs)  17.8 us
    all_gather x1, blocking collectives, serve(): lax.all_gather(sent, ('wide', 'narrow'), axis=0, axis_index_groups=groups)  6.18 us
    ppermute x4, starting transfers between devices, shards(): results[nth] = lax.ppermute(hidden[nth], 'wide', pairs)  3.91 us
    ppermute x3, starting transfers between devices, shards(): lax.ppermute(block, 'wide', [(b * workers + j, serving + j) for j in rang...  2.61 us
    pallas_call x1, Pallas kernels, serve(): pl.pallas_call(attend_kernel, out_shape=(pltpu.VMEM(shapes[0].shape, jnp....  2.28 us
    ppermute x3, waiting for transfers between devices, shards(): lax.ppermute(block, 'wide', [(b * workers + j, serving + j) for j in rang...  1.54 us
  transfers between devices with their start and end apart: 8, of which 3 were waited for; matrix products, arithmetic and copies ran while one was open for 0% of the time, Pallas kernels for 0%

profile of v15, /device:TPU:0, one launch (start us, length us, event | category | flops | bytes accessed | tf_op | source)
XLA Modules:
  0.0 36.7 jit_solution(15775923640955712554)
XLA Ops:
  0.6 8.5 %conditional.2 = ((bf16[2,2048]{1,0:T(2,128)(2,1)S(1)}, bf16[4,2,2176]{2,1,0:T(2,128)(2,1)S(1)})) conditional(s32[]{:T(128)} %convert_element_type.6, () %tuple.21, (s32[1]{0:T(128)}, bf16[2,1,2048]{2,0,1:T(2,128)(2,1)}, bf16[2,1,2,512]{3,2,1,0:T(2,128)(2,1)}, bf16[1,4,128,128]{3,2,1,0:T(8,128)(2,1)}, bf16[1,4,128,128]{3,2,1,0:T(8,128)(2,1)}, ...), branch_computations={%region_0.0_spmd, %region_1.0_spmd} | conditional | bytes 43544 | solution.py:297
  0.7 2.3 %branch_1_fun.1 = (bf16[2,2048]{1,0:T(2,128)(2,1)S(1)}, bf16[2,2176]{1,0:T(2,128)(2,1)S(1)}) custom-call(s32[1,1]{1,0:T(1,128)} %bitcast.refs_0_, bf16[2,2048]{1,0:T(2,128)(2,1)} %bitcast.22, bf16[2,2,512]{2,1,0:T(2,128)(2,1)} %bitcast.25, bf16[4,128,128]{2,1,0:T(8,128)(2,1)} %bitcast.20, bf16[4,128,128]{2,1,0:T(8,128)(2,1)} %bitcast.21, ...), custom_call_target="tpu_custom_call" | custom-call | tf_op jit(solution)/shard_map/cond/branch_1_fun/pallas_call | solution.py:271
  2.9 6.2 %all-gather.2 = bf16[4,2,2176]{2,1,0:T(2,128)(2,1)S(1)} all-gather(bf16[1,2,2176]{2,1,0:T(2,128)(2,1)S(1)} %bitcast.14), channel_id=2, replica_groups={{0,1,2,3},{4,5,6,7},{8,9,10,11},{12,13,14,15},{16,17,18,19},{20,21,22,2..., dimensions={0}, use_global_device_ids=true | all-gather | bytes 43520 | tf_op jit(solution)/shard_map/cond/branch_1_fun/all_gather | solution.py:286
  9.1 0.7 %collective-permute-start.2 = (bf16[4,2,2176]{2,1,0:T(2,128)(2,1)S(1)}, bf16[4,2,2176]{2,1,0:T(2,128)(2,1)S(1)}, u32[]{:S(2)}, u32[]{:S(2)}) collective-permute-start(bf16[4,2,2176]{2,1,0:T(2,128)(2,1)S(1)} %get-tuple-element.48._), channel_id=1, source_target_pairs={{8,12},{10,14},{9,13},{11,15},{24,28},{26,30},{25,29},{27,31}} | collective-permute-start | bytes 104456 | tf_op jit(solution)/shard_map/ppermute | solution.py:299
  9.8 0.7 %collective-permute-start.1 = (bf16[4,2,2176]{2,1,0:T(2,128)(2,1)S(1)}, bf16[4,2,2176]{2,1,0:T(2,128)(2,1)S(1)}, u32[]{:S(2)}, u32[]{:S(2)}) collective-permute-start(bf16[4,2,2176]{2,1,0:T(2,128)(2,1)S(1)} %get-tuple-element.48._), channel_id=1, source_target_pairs={{4,12},{6,14},{5,13},{7,15},{20,28},{22,30},{21,29},{23,31}} | collective-permute-start | bytes 104456 | tf_op jit(solution)/shard_map/ppermute | solution.py:299
  10.5 1.3 %collective-permute-start = (bf16[4,2,2176]{2,1,0:T(2,128)(2,1)S(1)}, bf16[4,2,2176]{2,1,0:T(2,128)(2,1)S(1)}, u32[]{:S(2)}, u32[]{:S(2)}) collective-permute-start(bf16[4,2,2176]{2,1,0:T(2,128)(2,1)S(1)} %get-tuple-element.48._), channel_id=1, source_target_pairs={{0,12},{2,14},{1,13},{3,15},{16,28},{18,30},{17,29},{19,31}} | collective-permute-start | bytes 104456 | tf_op jit(solution)/shard_map/ppermute | solution.py:299
  11.8 0.0 collective-permute-done.2.refs_2_
  11.8 0.0 collective-permute-done.1.refs_1_
  11.8 1.5 %collective-permute-done.refs_0_ = bf16[4,2,2176]{2,1,0:T(2,128)(2,1)S(1)} collective-permute-done((bf16[4,2,2176]{2,1,0:T(2,128)(2,1)S(1)}, bf16[4,2,2176]{2,1,0:T(2,128)(2,1)S(1)}, u32[]{:S(2)}, u32[]{:S(2)}) %collective-permute-start) | collective-permute-done | bytes 34848 | tf_op jit(solution)/shard_map/ppermute | solution.py:299
  13.3 0.1 shard_map.112
  13.5 0.7 %collective-permute-start.3 = (bf16[2,2,3584]{2,1,0:T(2,128)(2,1)S(1)}, bf16[2,2,3584]{2,1,0:T(2,128)(2,1)S(1)}, u32[]{:S(2)}, u32[]{:S(2)}) collective-permute-start(bf16[2,2,3584]{2,1,0:T(2,128)(2,1)S(1)} %get-tuple-element.51), channel_id=1, source_target_pairs={{12,4},{14,6},{13,5},{15,7},{28,20},{30,22},{29,21},{31,23}} | collective-permute-start | bytes 86024 | tf_op jit(solution)/shard_map/ppermute | solution.py:331
  14.2 1.3 %collective-permute-start.4 = (bf16[2,3584]{1,0:T(2,128)(2,1)S(1)}, bf16[2,3584]{1,0:T(2,128)(2,1)S(1)}, u32[]{:S(2)}, u32[]{:S(2)}) collective-permute-start(bf16[2,3584]{1,0:T(2,128)(2,1)S(1)} %get-tuple-element.52), channel_id=1, source_target_pairs={{12,0},{14,2},{13,1},{15,3},{28,16},{30,18},{29,17},{31,19}} | collective-permute-start | bytes 43016 | tf_op jit(solution)/shard_map/ppermute | solution.py:355
  15.5 1.3 %collective-permute-start.5 = (bf16[2,3584]{1,0:T(2,128)(2,1)S(1)}, bf16[2,3584]{1,0:T(2,128)(2,1)S(1)}, u32[]{:S(2)}, u32[]{:S(2)}) collective-permute-start(bf16[2,3584]{1,0:T(2,128)(2,1)S(1)} %get-tuple-element.53), channel_id=1, source_target_pairs={{12,2},{14,0},{13,3},{15,1},{28,18},{30,16},{29,19},{31,17}} | collective-permute-start | bytes 43016 | tf_op jit(solution)/shard_map/ppermute | solution.py:355
  16.8 0.7 %collective-permute-start.6 = (bf16[2,3584]{1,0:T(2,128)(2,1)S(1)}, bf16[2,3584]{1,0:T(2,128)(2,1)S(1)}, u32[]{:S(2)}, u32[]{:S(2)}) collective-permute-start(bf16[2,3584]{1,0:T(2,128)(2,1)S(1)} %get-tuple-element.54), channel_id=1, source_target_pairs={{12,8},{14,10},{13,9},{15,11},{28,24},{30,26},{29,25},{31,27}} | collective-permute-start | bytes 43016 | tf_op jit(solution)/shard_map/ppermute | solution.py:355
  17.4 0.7 %collective-permute-start.7 = (bf16[2,3584]{1,0:T(2,128)(2,1)S(1)}, bf16[2,3584]{1,0:T(2,128)(2,1)S(1)}, u32[]{:S(2)}, u32[]{:S(2)}) collective-permute-start(bf16[2,3584]{1,0:T(2,128)(2,1)S(1)} %get-tuple-element.55), channel_id=1, source_target_pairs={{12,10},{14,8},{13,11},{15,9},{28,26},{30,24},{29,27},{31,25}} | collective-permute-start | bytes 43016 | tf_op jit(solution)/shard_map/ppermute | solution.py:355
  18.1 0.0 collective-permute-done.3
  18.2 15.6 %collective-permute-done.4.refs_0_ = bf16[2,3584]{1,0:T(2,128)(2,1)S(1)} collective-permute-done((bf16[2,3584]{1,0:T(2,128)(2,1)S(1)}, bf16[2,3584]{1,0:T(2,128)(2,1)S(1)}, u32[]{:S(2)}, u32[]{:S(2)}) %collective-permute-start.4) | collective-permute-done | bytes 14368 | tf_op jit(solution)/shard_map/ppermute | solution.py:355
  33.8 2.2 %collective-permute-done.5.refs_1_ = bf16[2,3584]{1,0:T(2,128)(2,1)S(1)} collective-permute-done((bf16[2,3584]{1,0:T(2,128)(2,1)S(1)}, bf16[2,3584]{1,0:T(2,128)(2,1)S(1)}, u32[]{:S(2)}, u32[]{:S(2)}) %collective-permute-start.5) | collective-permute-done | bytes 14368 | tf_op jit(solution)/shard_map/ppermute | solution.py:355
  36.0 0.0 collective-permute-done.6.refs_2_
  36.0 0.0 collective-permute-done.7.refs_3_
  36.0 0.6 %shard_map.113 = (bf16[2,2048]{1,0:T(2,128)(2,1)}, bf16[2,7168]{1,0:T(2,128)(2,1)}) custom-call(bf16[2,2048]{1,0:T(2,128)(2,1)S(1)} %get-tuple-element.47.attended, bf16[2,2,2,3584]{3,2,1,0:T(2,128)(2,1)S(1)} %get-tuple-element.91.gathered, bf16[2,3584]{1,0:T(2,128)(2,1)S(1)} %collective-permute-done.4.refs_0_, ...), custom_call_target="tpu_custom_call" | custom-call | tf_op jit(solution)/shard_map/pallas_call | solution.py:357
  (3 shorter events, 0.1 us)
Async XLA Ops:
  9.1 2.7 %collective-permute-start.2 = (bf16[4,2,2176]{2,1,0:T(2,128)(2,1)S(1)}, bf16[4,2,2176]{2,1,0:T(2,128)(2,1)S(1)}, u32[]{:S(2)}, u32[]{:S(2)}) collective-permute-start(bf16[4,2,2176]{2,1,0:T(2,128)(2,1)S(1)} %get-tuple-element.48._), channel_id=1, source_target_pairs={{8,12},{10,14},{9,13},{11,15},{24,28},{26,30},{25,29},{27,31}} | collective-permute-start | bytes 104456 | tf_op jit(solution)/shard_map/ppermute | solution.py:299
  9.8 2.0 %collective-permute-start.1 = (bf16[4,2,2176]{2,1,0:T(2,128)(2,1)S(1)}, bf16[4,2,2176]{2,1,0:T(2,128)(2,1)S(1)}, u32[]{:S(2)}, u32[]{:S(2)}) collective-permute-start(bf16[4,2,2176]{2,1,0:T(2,128)(2,1)S(1)} %get-tuple-element.48._), channel_id=1, source_target_pairs={{4,12},{6,14},{5,13},{7,15},{20,28},{22,30},{21,29},{23,31}} | collective-permute-start | bytes 104456 | tf_op jit(solution)/shard_map/ppermute | solution.py:299
  10.5 2.9 %collective-permute-start = (bf16[4,2,2176]{2,1,0:T(2,128)(2,1)S(1)}, bf16[4,2,2176]{2,1,0:T(2,128)(2,1)S(1)}, u32[]{:S(2)}, u32[]{:S(2)}) collective-permute-start(bf16[4,2,2176]{2,1,0:T(2,128)(2,1)S(1)} %get-tuple-element.48._), channel_id=1, source_target_pairs={{0,12},{2,14},{1,13},{3,15},{16,28},{18,30},{17,29},{19,31}} | collective-permute-start | bytes 104456 | tf_op jit(solution)/shard_map/ppermute | solution.py:299
  13.5 4.6 %collective-permute-start.3 = (bf16[2,2,3584]{2,1,0:T(2,128)(2,1)S(1)}, bf16[2,2,3584]{2,1,0:T(2,128)(2,1)S(1)}, u32[]{:S(2)}, u32[]{:S(2)}) collective-permute-start(bf16[2,2,3584]{2,1,0:T(2,128)(2,1)S(1)} %get-tuple-element.51), channel_id=1, source_target_pairs={{12,4},{14,6},{13,5},{15,7},{28,20},{30,22},{29,21},{31,23}} | collective-permute-start | bytes 86024 | tf_op jit(solution)/shard_map/ppermute | solution.py:331
  14.2 19.6 %collective-permute-start.4 = (bf16[2,3584]{1,0:T(2,128)(2,1)S(1)}, bf16[2,3584]{1,0:T(2,128)(2,1)S(1)}, u32[]{:S(2)}, u32[]{:S(2)}) collective-permute-start(bf16[2,3584]{1,0:T(2,128)(2,1)S(1)} %get-tuple-element.52), channel_id=1, source_target_pairs={{12,0},{14,2},{13,1},{15,3},{28,16},{30,18},{29,17},{31,19}} | collective-permute-start | bytes 43016 | tf_op jit(solution)/shard_map/ppermute | solution.py:355
  15.5 20.5 %collective-permute-start.5 = (bf16[2,3584]{1,0:T(2,128)(2,1)S(1)}, bf16[2,3584]{1,0:T(2,128)(2,1)S(1)}, u32[]{:S(2)}, u32[]{:S(2)}) collective-permute-start(bf16[2,3584]{1,0:T(2,128)(2,1)S(1)} %get-tuple-element.53), channel_id=1, source_target_pairs={{12,2},{14,0},{13,3},{15,1},{28,18},{30,16},{29,19},{31,17}} | collective-permute-start | bytes 43016 | tf_op jit(solution)/shard_map/ppermute | solution.py:355
  16.8 19.2 %collective-permute-start.6 = (bf16[2,3584]{1,0:T(2,128)(2,1)S(1)}, bf16[2,3584]{1,0:T(2,128)(2,1)S(1)}, u32[]{:S(2)}, u32[]{:S(2)}) collective-permute-start(bf16[2,3584]{1,0:T(2,128)(2,1)S(1)} %get-tuple-element.54), channel_id=1, source_target_pairs={{12,8},{14,10},{13,9},{15,11},{28,24},{30,26},{29,25},{31,27}} | collective-permute-start | bytes 43016 | tf_op jit(solution)/shard_map/ppermute | solution.py:355
  17.4 18.6 %collective-permute-start.7 = (bf16[2,3584]{1,0:T(2,128)(2,1)S(1)}, bf16[2,3584]{1,0:T(2,128)(2,1)S(1)}, u32[]{:S(2)}, u32[]{:S(2)}) collective-permute-start(bf16[2,3584]{1,0:T(2,128)(2,1)S(1)} %get-tuple-element.55), channel_id=1, source_target_pairs={{12,10},{14,8},{13,11},{15,9},{28,26},{30,24},{29,27},{31,25}} | collective-permute-start | bytes 43016 | tf_op jit(solution)/shard_map/ppermute | solution.py:355

commit v16 on v15

--- a/solution.py
+++ b/solution.py
@@ -16,6 +16,7 @@
 SLOTS = 4
 AHEAD = (3, 1, 1, 1, 1)
 CHUNK = 1024
+PARTS = 4
 
 
 def pair(squares):
@@ -28,11 +29,14 @@
 def fetch_kernel(serving, _, gate, up, gate_held, up_held, sems):
     @pl.when(lax.axis_index("wide") >= serving)
     def _():
-        here = pl.ds(0, gate_held.shape[1])
-        copies = [
-            pltpu.make_async_copy(gate.at[:, here], gate_held, sems.at[0]),
-            pltpu.make_async_copy(up.at[:, here], up_held, sems.at[1]),
-        ]
+        features, early = gate_held.shape
+        copies = []
+        for part in range(PARTS):
+            k = pl.ds(part * features // PARTS, features // PARTS)
+            for i, (m, held) in enumerate(((gate, gate_held), (up, up_held))):
+                copies.append(
+                    pltpu.make_async_copy(m.at[k, pl.ds(0, early)], held.at[k], sems.at[i, part])
+                )
         for c in copies:
             c.start()
         for c in copies:
@@ -127,7 +131,7 @@
     def stream(j):
         s = j % room
         here = pl.ds(units[j], tile)
-        size = features // 2 if j == len(units) - 1 else features
+        size = features // PARTS if j == len(units) - 1 else features
         depths = [pl.ds(at, size) for at in range(0, features, size)]
         return [
             pltpu.make_async_copy(m.at[k, here], slots.at[s, i, k], sems.at[s, i, part])
@@ -306,7 +310,7 @@
         out_shape=[pltpu.VMEM((features, early), jnp.bfloat16)] * 2,
         in_specs=[pl.BlockSpec(memory_space=pl.ANY), hbm, hbm],
         out_specs=[vmem] * 2,
-        scratch_shapes=[pltpu.SemaphoreType.DMA((2,))],
+        scratch_shapes=[pltpu.SemaphoreType.DMA((2, PARTS))],
         compiler_params=pltpu.CompilerParams(vmem_limit_bytes=4 << 20),
         cost_estimate=pl.CostEstimate(
             flops=0, bytes_accessed=early * 4 * features, transcendentals=0
@@ -323,7 +327,7 @@
         scratch_shapes=[
             pltpu.VMEM((padded, features), jnp.bfloat16),
             pltpu.VMEM((SLOTS, 2, features, tile), jnp.bfloat16),
-            pltpu.SemaphoreType.DMA((SLOTS, 2, 2)),
+            pltpu.SemaphoreType.DMA((SLOTS, 2, PARTS)),
         ],
         compiler_params=pltpu.CompilerParams(vmem_limit_bytes=19 << 20),
     )(*arrived, *held, gate, up)

time: 37 us -> 37 us (level)
  no operation moved by 1% of the time
where the time goes in v16:
time: 37 us; the launch traced here: 36.7 us
  waiting for transfers between devices  19.3 us (52%)
  starting transfers between devices  7.18 us (19%)
  blocking collectives  6.18 us (17%)
  Pallas kernels  3.32 us (9%)
  between operations  0.76 us (2%)
    ppermute x4, waiting for transfers between devices, shards(): results[nth] = lax.ppermute(hidden[nth], 'wide', pairs)  17.8 us
    all_gather x1, blocking collectives, serve(): lax.all_gather(sent, ('wide', 'narrow'), axis=0, axis_index_groups=groups)  6.18 us
    ppermute x4, starting transfers between devices, shards(): results[nth] = lax.ppermute(hidden[nth], 'wide', pairs)  3.91 us
    ppermute x3, starting transfers between devices, shards(): lax.ppermute(block, 'wide', [(b * workers + j, serving + j) for j in rang...  2.61 us
    pallas_call x1, Pallas kernels, serve(): pl.pallas_call(attend_kernel, out_shape=(pltpu.VMEM(shapes[0].shape, jnp....  2.28 us
    ppermute x3, waiting for transfers between devices, shards(): lax.ppermute(block, 'wide', [(b * workers + j, serving + j) for j in rang...  1.47 us
  transfers between devices with their start and end apart: 8, of which 3 were waited for; matrix products, arithmetic and copies ran while one was open for 0% of the time, Pallas kernels for 0%

profile of v16, /device:TPU:0, one launch (start us, length us, event | category | flops | bytes accessed | tf_op | source)
XLA Modules:
  0.0 36.7 jit_solution(814300547858211462)
XLA Ops:
  0.6 8.5 %conditional.2 = ((bf16[2,2048]{1,0:T(2,128)(2,1)S(1)}, bf16[4,2,2176]{2,1,0:T(2,128)(2,1)S(1)})) conditional(s32[]{:T(128)} %convert_element_type.6, () %tuple.21, (s32[1]{0:T(128)}, bf16[2,1,2048]{2,0,1:T(2,128)(2,1)}, bf16[2,1,2,512]{3,2,1,0:T(2,128)(2,1)}, bf16[1,4,128,128]{3,2,1,0:T(8,128)(2,1)}, bf16[1,4,128,128]{3,2,1,0:T(8,128)(2,1)}, ...), branch_computations={%region_0.0_spmd, %region_1.0_spmd} | conditional | bytes 43544 | solution.py:301
  0.7 2.3 %branch_1_fun.1 = (bf16[2,2048]{1,0:T(2,128)(2,1)S(1)}, bf16[2,2176]{1,0:T(2,128)(2,1)S(1)}) custom-call(s32[1,1]{1,0:T(1,128)} %bitcast.refs_0_, bf16[2,2048]{1,0:T(2,128)(2,1)} %bitcast.22, bf16[2,2,512]{2,1,0:T(2,128)(2,1)} %bitcast.25, bf16[4,128,128]{2,1,0:T(8,128)(2,1)} %bitcast.20, bf16[4,128,128]{2,1,0:T(8,128)(2,1)} %bitcast.21, ...), custom_call_target="tpu_custom_call" | custom-call | tf_op jit(solution)/shard_map/cond/branch_1_fun/pallas_call | solution.py:275
  2.9 6.2 %all-gather.2 = bf16[4,2,2176]{2,1,0:T(2,128)(2,1)S(1)} all-gather(bf16[1,2,2176]{2,1,0:T(2,128)(2,1)S(1)} %bitcast.14), channel_id=2, replica_groups={{0,1,2,3},{4,5,6,7},{8,9,10,11},{12,13,14,15},{16,17,18,19},{20,21,22,2..., dimensions={0}, use_global_device_ids=true | all-gather | bytes 43520 | tf_op jit(solution)/shard_map/cond/branch_1_fun/all_gather | solution.py:290
  9.1 0.7 %collective-permute-start.2 = (bf16[4,2,2176]{2,1,0:T(2,128)(2,1)S(1)}, bf16[4,2,2176]{2,1,0:T(2,128)(2,1)S(1)}, u32[]{:S(2)}, u32[]{:S(2)}) collective-permute-start(bf16[4,2,2176]{2,1,0:T(2,128)(2,1)S(1)} %get-tuple-element.48._), channel_id=1, source_target_pairs={{8,12},{10,14},{9,13},{11,15},{24,28},{26,30},{25,29},{27,31}} | collective-permute-start | bytes 104456 | tf_op jit(solution)/shard_map/ppermute | solution.py:303
  9.8 0.7 %collective-permute-start.1 = (bf16[4,2,2176]{2,1,0:T(2,128)(2,1)S(1)}, bf16[4,2,2176]{2,1,0:T(2,128)(2,1)S(1)}, u32[]{:S(2)}, u32[]{:S(2)}) collective-permute-start(bf16[4,2,2176]{2,1,0:T(2,128)(2,1)S(1)} %get-tuple-element.48._), channel_id=1, source_target_pairs={{4,12},{6,14},{5,13},{7,15},{20,28},{22,30},{21,29},{23,31}} | collective-permute-start | bytes 104456 | tf_op jit(solution)/shard_map/ppermute | solution.py:303
  10.5 1.3 %collective-permute-start = (bf16[4,2,2176]{2,1,0:T(2,128)(2,1)S(1)}, bf16[4,2,2176]{2,1,0:T(2,128)(2,1)S(1)}, u32[]{:S(2)}, u32[]{:S(2)}) collective-permute-start(bf16[4,2,2176]{2,1,0:T(2,128)(2,1)S(1)} %get-tuple-element.48._), channel_id=1, source_target_pairs={{0,12},{2,14},{1,13},{3,15},{16,28},{18,30},{17,29},{19,31}} | collective-permute-start | bytes 104456 | tf_op jit(solution)/shard_map/ppermute | solution.py:303
  11.8 0.1 shard_map.111
  11.9 0.0 collective-permute-done.2.refs_2_
  11.9 0.0 collective-permute-done.1.refs_1_
  11.9 1.5 %collective-permute-done.refs_0_ = bf16[4,2,2176]{2,1,0:T(2,128)(2,1)S(1)} collective-permute-done((bf16[4,2,2176]{2,1,0:T(2,128)(2,1)S(1)}, bf16[4,2,2176]{2,1,0:T(2,128)(2,1)S(1)}, u32[]{:S(2)}, u32[]{:S(2)}) %collective-permute-start) | collective-permute-done | bytes 34848 | tf_op jit(solution)/shard_map/ppermute | solution.py:303
  13.3 0.3 shard_map.112
  13.6 0.7 %collective-permute-start.3 = (bf16[2,2,3584]{2,1,0:T(2,128)(2,1)S(1)}, bf16[2,2,3584]{2,1,0:T(2,128)(2,1)S(1)}, u32[]{:S(2)}, u32[]{:S(2)}) collective-permute-start(bf16[2,2,3584]{2,1,0:T(2,128)(2,1)S(1)} %get-tuple-element.51), channel_id=1, source_target_pairs={{12,4},{14,6},{13,5},{15,7},{28,20},{30,22},{29,21},{31,23}} | collective-permute-start | bytes 86024 | tf_op jit(solution)/shard_map/ppermute | solution.py:335
  14.3 1.3 %collective-permute-start.4 = (bf16[2,3584]{1,0:T(2,128)(2,1)S(1)}, bf16[2,3584]{1,0:T(2,128)(2,1)S(1)}, u32[]{:S(2)}, u32[]{:S(2)}) collective-permute-start(bf16[2,3584]{1,0:T(2,128)(2,1)S(1)} %get-tuple-element.52), channel_id=1, source_target_pairs={{12,0},{14,2},{13,1},{15,3},{28,16},{30,18},{29,17},{31,19}} | collective-permute-start | bytes 43016 | tf_op jit(solution)/shard_map/ppermute | solution.py:359
  15.6 1.3 %collective-permute-start.5 = (bf16[2,3584]{1,0:T(2,128)(2,1)S(1)}, bf16[2,3584]{1,0:T(2,128)(2,1)S(1)}, u32[]{:S(2)}, u32[]{:S(2)}) collective-permute-start(bf16[2,3584]{1,0:T(2,128)(2,1)S(1)} %get-tuple-element.53), channel_id=1, source_target_pairs={{12,2},{14,0},{13,3},{15,1},{28,18},{30,16},{29,19},{31,17}} | collective-permute-start | bytes 43016 | tf_op jit(solution)/shard_map/ppermute | solution.py:359
  16.9 0.7 %collective-permute-start.6 = (bf16[2,3584]{1,0:T(2,128)(2,1)S(1)}, bf16[2,3584]{1,0:T(2,128)(2,1)S(1)}, u32[]{:S(2)}, u32[]{:S(2)}) collective-permute-start(bf16[2,3584]{1,0:T(2,128)(2,1)S(1)} %get-tuple-element.54), channel_id=1, source_target_pairs={{12,8},{14,10},{13,9},{15,11},{28,24},{30,26},{29,25},{31,27}} | collective-permute-start | bytes 43016 | tf_op jit(solution)/shard_map/ppermute | solution.py:359
  17.6 0.7 %collective-permute-start.7 = (bf16[2,3584]{1,0:T(2,128)(2,1)S(1)}, bf16[2,3584]{1,0:T(2,128)(2,1)S(1)}, u32[]{:S(2)}, u32[]{:S(2)}) collective-permute-start(bf16[2,3584]{1,0:T(2,128)(2,1)S(1)} %get-tuple-element.55), channel_id=1, source_target_pairs={{12,10},{14,8},{13,11},{15,9},{28,26},{30,24},{29,27},{31,25}} | collective-permute-start | bytes 43016 | tf_op jit(solution)/shard_map/ppermute | solution.py:359
  18.3 0.0 collective-permute-done.3
  18.3 15.5 %collective-permute-done.4.refs_0_ = bf16[2,3584]{1,0:T(2,128)(2,1)S(1)} collective-permute-done((bf16[2,3584]{1,0:T(2,128)(2,1)S(1)}, bf16[2,3584]{1,0:T(2,128)(2,1)S(1)}, u32[]{:S(2)}, u32[]{:S(2)}) %collective-permute-start.4) | collective-permute-done | bytes 14368 | tf_op jit(solution)/shard_map/ppermute | solution.py:359
  33.9 2.2 %collective-permute-done.5.refs_1_ = bf16[2,3584]{1,0:T(2,128)(2,1)S(1)} collective-permute-done((bf16[2,3584]{1,0:T(2,128)(2,1)S(1)}, bf16[2,3584]{1,0:T(2,128)(2,1)S(1)}, u32[]{:S(2)}, u32[]{:S(2)}) %collective-permute-start.5) | collective-permute-done | bytes 14368 | tf_op jit(solution)/shard_map/ppermute | solution.py:359
  36.1 0.0 collective-permute-done.6.refs_2_
  36.1 0.0 collective-permute-done.7.refs_3_
  36.1 0.6 %shard_map.113 = (bf16[2,2048]{1,0:T(2,128)(2,1)}, bf16[2,7168]{1,0:T(2,128)(2,1)}) custom-call(bf16[2,2048]{1,0:T(2,128)(2,1)S(1)} %get-tuple-element.47.attended, bf16[2,2,2,3584]{3,2,1,0:T(2,128)(2,1)S(1)} %get-tuple-element.91.gathered, bf16[2,3584]{1,0:T(2,128)(2,1)S(1)} %collective-permute-done.4.refs_0_, ...), custom_call_target="tpu_custom_call" | custom-call | tf_op jit(solution)/shard_map/pallas_call | solution.py:361
  (2 shorter events, 0.0 us)
Async XLA Ops:
  9.1 2.7 %collective-permute-start.2 = (bf16[4,2,2176]{2,1,0:T(2,128)(2,1)S(1)}, bf16[4,2,2176]{2,1,0:T(2,128)(2,1)S(1)}, u32[]{:S(2)}, u32[]{:S(2)}) collective-permute-start(bf16[4,2,2176]{2,1,0:T(2,128)(2,1)S(1)} %get-tuple-element.48._), channel_id=1, source_target_pairs={{8,12},{10,14},{9,13},{11,15},{24,28},{26,30},{25,29},{27,31}} | collective-permute-start | bytes 104456 | tf_op jit(solution)/shard_map/ppermute | solution.py:303
  9.8 2.1 %collective-permute-start.1 = (bf16[4,2,2176]{2,1,0:T(2,128)(2,1)S(1)}, bf16[4,2,2176]{2,1,0:T(2,128)(2,1)S(1)}, u32[]{:S(2)}, u32[]{:S(2)}) collective-permute-start(bf16[4,2,2176]{2,1,0:T(2,128)(2,1)S(1)} %get-tuple-element.48._), channel_id=1, source_target_pairs={{4,12},{6,14},{5,13},{7,15},{20,28},{22,30},{21,29},{23,31}} | collective-permute-start | bytes 104456 | tf_op jit(solution)/shard_map/ppermute | solution.py:303
  10.5 2.9 %collective-permute-start = (bf16[4,2,2176]{2,1,0:T(2,128)(2,1)S(1)}, bf16[4,2,2176]{2,1,0:T(2,128)(2,1)S(1)}, u32[]{:S(2)}, u32[]{:S(2)}) collective-permute-start(bf16[4,2,2176]{2,1,0:T(2,128)(2,1)S(1)} %get-tuple-element.48._), channel_id=1, source_target_pairs={{0,12},{2,14},{1,13},{3,15},{16,28},{18,30},{17,29},{19,31}} | collective-permute-start | bytes 104456 | tf_op jit(solution)/shard_map/ppermute | solution.py:303
  13.6 4.6 %collective-permute-start.3 = (bf16[2,2,3584]{2,1,0:T(2,128)(2,1)S(1)}, bf16[2,2,3584]{2,1,0:T(2,128)(2,1)S(1)}, u32[]{:S(2)}, u32[]{:S(2)}) collective-permute-start(bf16[2,2,3584]{2,1,0:T(2,128)(2,1)S(1)} %get-tuple-element.51), channel_id=1, source_target_pairs={{12,4},{14,6},{13,5},{15,7},{28,20},{30,22},{29,21},{31,23}} | collective-permute-start | bytes 86024 | tf_op jit(solution)/shard_map/ppermute | solution.py:335
  14.3 19.5 %collective-permute-start.4 = (bf16[2,3584]{1,0:T(2,128)(2,1)S(1)}, bf16[2,3584]{1,0:T(2,128)(2,1)S(1)}, u32[]{:S(2)}, u32[]{:S(2)}) collective-permute-start(bf16[2,3584]{1,0:T(2,128)(2,1)S(1)} %get-tuple-element.52), channel_id=1, source_target_pairs={{12,0},{14,2},{13,1},{15,3},{28,16},{30,18},{29,17},{31,19}} | collective-permute-start | bytes 43016 | tf_op jit(solution)/shard_map/ppermute | solution.py:359
  15.6 20.5 %collective-permute-start.5 = (bf16[2,3584]{1,0:T(2,128)(2,1)S(1)}, bf16[2,3584]{1,0:T(2,128)(2,1)S(1)}, u32[]{:S(2)}, u32[]{:S(2)}) collective-permute-start(bf16[2,3584]{1,0:T(2,128)(2,1)S(1)} %get-tuple-element.53), channel_id=1, source_target_pairs={{12,2},{14,0},{13,3},{15,1},{28,18},{30,16},{29,19},{31,17}} | collective-permute-start | bytes 43016 | tf_op jit(solution)/shard_map/ppermute | solution.py:359
  16.9 19.2 %collective-permute-start.6 = (bf16[2,3584]{1,0:T(2,128)(2,1)S(1)}, bf16[2,3584]{1,0:T(2,128)(2,1)S(1)}, u32[]{:S(2)}, u32[]{:S(2)}) collective-permute-start(bf16[2,3584]{1,0:T(2,128)(2,1)S(1)} %get-tuple-element.54), channel_id=1, source_target_pairs={{12,8},{14,10},{13,9},{15,11},{28,24},{30,26},{29,25},{31,27}} | collective-permute-start | bytes 43016 | tf_op jit(solution)/shard_map/ppermute | solution.py:359
  17.6 18.5 %collective-permute-start.7 = (bf16[2,3584]{1,0:T(2,128)(2,1)S(1)}, bf16[2,3584]{1,0:T(2,128)(2,1)S(1)}, u32[]{:S(2)}, u32[]{:S(2)}) collective-permute-start(bf16[2,3584]{1,0:T(2,128)(2,1)S(1)} %get-tuple-element.55), channel_id=1, source_target_pairs={{12,10},{14,8},{13,11},{15,9},{28,26},{30,24},{29,27},{31,25}} | collective-permute-start | bytes 43016 | tf_op jit(solution)/shard_map/ppermute | solution.py:359

commit v17 on v15

--- a/solution.py
+++ b/solution.py
@@ -15,7 +15,7 @@
 TILE = 256
 SLOTS = 4
 AHEAD = (3, 1, 1, 1, 1)
-CHUNK = 1024
+CHUNK = 512
 
 
 def pair(squares):

time: 37 us -> 37 us (level)
  no operation moved by 1% of the time
where the time goes in v17:
time: 37 us; the launch traced here: 36.7 us
  waiting for transfers between devices  19.4 us (52%)
  starting transfers between devices  7.18 us (19%)
  blocking collectives  6.18 us (17%)
  Pallas kernels  3.11 us (8%)
  between operations  0.76 us (2%)
    ppermute x4, waiting for transfers between devices, shards(): results[nth] = lax.ppermute(hidden[nth], 'wide', pairs)  17.8 us
    all_gather x1, blocking collectives, serve(): lax.all_gather(sent, ('wide', 'narrow'), axis=0, axis_index_groups=groups)  6.18 us
    ppermute x4, starting transfers between devices, shards(): results[nth] = lax.ppermute(hidden[nth], 'wide', pairs)  3.91 us
    ppermute x3, starting transfers between devices, shards(): lax.ppermute(block, 'wide', [(b * workers + j, serving + j) for j in rang...  2.61 us
    pallas_call x1, Pallas kernels, serve(): pl.pallas_call(attend_kernel, out_shape=(pltpu.VMEM(shapes[0].shape, jnp....  2.28 us
    ppermute x3, waiting for transfers between devices, shards(): lax.ppermute(block, 'wide', [(b * workers + j, serving + j) for j in rang...  1.54 us
  transfers between devices with their start and end apart: 8, of which 3 were waited for; matrix products, arithmetic and copies ran while one was open for 0% of the time, Pallas kernels for 0%

profile of v17, /device:TPU:0, one launch (start us, length us, event | category | flops | bytes accessed | tf_op | source)
XLA Modules:
  0.0 36.7 jit_solution(6489283312119075222)
XLA Ops:
  0.6 8.5 %conditional.2 = ((bf16[2,2048]{1,0:T(2,128)(2,1)S(1)}, bf16[4,2,2176]{2,1,0:T(2,128)(2,1)S(1)})) conditional(s32[]{:T(128)} %convert_element_type.6, () %tuple.21, (s32[1]{0:T(128)}, bf16[2,1,2048]{2,0,1:T(2,128)(2,1)}, bf16[2,1,2,512]{3,2,1,0:T(2,128)(2,1)}, bf16[1,4,128,128]{3,2,1,0:T(8,128)(2,1)}, bf16[1,4,128,128]{3,2,1,0:T(8,128)(2,1)}, ...), branch_computations={%region_0.0_spmd, %region_1.0_spmd} | conditional | bytes 43544 | solution.py:297
  0.7 2.3 %branch_1_fun.1 = (bf16[2,2048]{1,0:T(2,128)(2,1)S(1)}, bf16[2,2176]{1,0:T(2,128)(2,1)S(1)}) custom-call(s32[1,1]{1,0:T(1,128)} %bitcast.refs_0_, bf16[2,2048]{1,0:T(2,128)(2,1)} %bitcast.22, bf16[2,2,512]{2,1,0:T(2,128)(2,1)} %bitcast.25, bf16[4,128,128]{2,1,0:T(8,128)(2,1)} %bitcast.20, bf16[4,128,128]{2,1,0:T(8,128)(2,1)} %bitcast.21, ...), custom_call_target="tpu_custom_call" | custom-call | tf_op jit(solution)/shard_map/cond/branch_1_fun/pallas_call | solution.py:271
  2.9 6.2 %all-gather.2 = bf16[4,2,2176]{2,1,0:T(2,128)(2,1)S(1)} all-gather(bf16[1,2,2176]{2,1,0:T(2,128)(2,1)S(1)} %bitcast.14), channel_id=2, replica_groups={{0,1,2,3},{4,5,6,7},{8,9,10,11},{12,13,14,15},{16,17,18,19},{20,21,22,2..., dimensions={0}, use_global_device_ids=true | all-gather | bytes 43520 | tf_op jit(solution)/shard_map/cond/branch_1_fun/all_gather | solution.py:286
  9.1 0.7 %collective-permute-start.2 = (bf16[4,2,2176]{2,1,0:T(2,128)(2,1)S(1)}, bf16[4,2,2176]{2,1,0:T(2,128)(2,1)S(1)}, u32[]{:S(2)}, u32[]{:S(2)}) collective-permute-start(bf16[4,2,2176]{2,1,0:T(2,128)(2,1)S(1)} %get-tuple-element.48._), channel_id=1, source_target_pairs={{8,12},{10,14},{9,13},{11,15},{24,28},{26,30},{25,29},{27,31}} | collective-permute-start | bytes 104456 | tf_op jit(solution)/shard_map/ppermute | solution.py:299
  9.8 0.7 %collective-permute-start.1 = (bf16[4,2,2176]{2,1,0:T(2,128)(2,1)S(1)}, bf16[4,2,2176]{2,1,0:T(2,128)(2,1)S(1)}, u32[]{:S(2)}, u32[]{:S(2)}) collective-permute-start(bf16[4,2,2176]{2,1,0:T(2,128)(2,1)S(1)} %get-tuple-element.48._), channel_id=1, source_target_pairs={{4,12},{6,14},{5,13},{7,15},{20,28},{22,30},{21,29},{23,31}} | collective-permute-start | bytes 104456 | tf_op jit(solution)/shard_map/ppermute | solution.py:299
  10.5 1.3 %collective-permute-start = (bf16[4,2,2176]{2,1,0:T(2,128)(2,1)S(1)}, bf16[4,2,2176]{2,1,0:T(2,128)(2,1)S(1)}, u32[]{:S(2)}, u32[]{:S(2)}) collective-permute-start(bf16[4,2,2176]{2,1,0:T(2,128)(2,1)S(1)} %get-tuple-element.48._), channel_id=1, source_target_pairs={{0,12},{2,14},{1,13},{3,15},{16,28},{18,30},{17,29},{19,31}} | collective-permute-start | bytes 104456 | tf_op jit(solution)/shard_map/ppermute | solution.py:299
  11.8 0.0 collective-permute-done.2.refs_2_
  11.8 0.0 collective-permute-done.1.refs_1_
  11.8 1.5 %collective-permute-done.refs_0_ = bf16[4,2,2176]{2,1,0:T(2,128)(2,1)S(1)} collective-permute-done((bf16[4,2,2176]{2,1,0:T(2,128)(2,1)S(1)}, bf16[4,2,2176]{2,1,0:T(2,128)(2,1)S(1)}, u32[]{:S(2)}, u32[]{:S(2)}) %collective-permute-start) | collective-permute-done | bytes 34848 | tf_op jit(solution)/shard_map/ppermute | solution.py:299
  13.3 0.1 shard_map.112
  13.5 0.7 %collective-permute-start.3 = (bf16[2,2,3584]{2,1,0:T(2,128)(2,1)S(1)}, bf16[2,2,3584]{2,1,0:T(2,128)(2,1)S(1)}, u32[]{:S(2)}, u32[]{:S(2)}) collective-permute-start(bf16[2,2,3584]{2,1,0:T(2,128)(2,1)S(1)} %get-tuple-element.51), channel_id=1, source_target_pairs={{12,4},{14,6},{13,5},{15,7},{28,20},{30,22},{29,21},{31,23}} | collective-permute-start | bytes 86024 | tf_op jit(solution)/shard_map/ppermute | solution.py:331
  14.2 1.3 %collective-permute-start.4 = (bf16[2,3584]{1,0:T(2,128)(2,1)S(1)}, bf16[2,3584]{1,0:T(2,128)(2,1)S(1)}, u32[]{:S(2)}, u32[]{:S(2)}) collective-permute-start(bf16[2,3584]{1,0:T(2,128)(2,1)S(1)} %get-tuple-element.52), channel_id=1, source_target_pairs={{12,0},{14,2},{13,1},{15,3},{28,16},{30,18},{29,17},{31,19}} | collective-permute-start | bytes 43016 | tf_op jit(solution)/shard_map/ppermute | solution.py:355
  15.5 1.3 %collective-permute-start.5 = (bf16[2,3584]{1,0:T(2,128)(2,1)S(1)}, bf16[2,3584]{1,0:T(2,128)(2,1)S(1)}, u32[]{:S(2)}, u32[]{:S(2)}) collective-permute-start(bf16[2,3584]{1,0:T(2,128)(2,1)S(1)} %get-tuple-element.53), channel_id=1, source_target_pairs={{12,2},{14,0},{13,3},{15,1},{28,18},{30,16},{29,19},{31,17}} | collective-permute-start | bytes 43016 | tf_op jit(solution)/shard_map/ppermute | solution.py:355
  16.8 0.7 %collective-permute-start.6 = (bf16[2,3584]{1,0:T(2,128)(2,1)S(1)}, bf16[2,3584]{1,0:T(2,128)(2,1)S(1)}, u32[]{:S(2)}, u32[]{:S(2)}) collective-permute-start(bf16[2,3584]{1,0:T(2,128)(2,1)S(1)} %get-tuple-element.54), channel_id=1, source_target_pairs={{12,8},{14,10},{13,9},{15,11},{28,24},{30,26},{29,25},{31,27}} | collective-permute-start | bytes 43016 | tf_op jit(solution)/shard_map/ppermute | solution.py:355
  17.4 0.7 %collective-permute-start.7 = (bf16[2,3584]{1,0:T(2,128)(2,1)S(1)}, bf16[2,3584]{1,0:T(2,128)(2,1)S(1)}, u32[]{:S(2)}, u32[]{:S(2)}) collective-permute-start(bf16[2,3584]{1,0:T(2,128)(2,1)S(1)} %get-tuple-element.55), channel_id=1, source_target_pairs={{12,10},{14,8},{13,11},{15,9},{28,26},{30,24},{29,27},{31,25}} | collective-permute-start | bytes 43016 | tf_op jit(solution)/shard_map/ppermute | solution.py:355
  18.1 0.0 collective-permute-done.3
  18.2 15.6 %collective-permute-done.4.refs_0_ = bf16[2,3584]{1,0:T(2,128)(2,1)S(1)} collective-permute-done((bf16[2,3584]{1,0:T(2,128)(2,1)S(1)}, bf16[2,3584]{1,0:T(2,128)(2,1)S(1)}, u32[]{:S(2)}, u32[]{:S(2)}) %collective-permute-start.4) | collective-permute-done | bytes 14368 | tf_op jit(solution)/shard_map/ppermute | solution.py:355
  33.8 2.2 %collective-permute-done.5.refs_1_ = bf16[2,3584]{1,0:T(2,128)(2,1)S(1)} collective-permute-done((bf16[2,3584]{1,0:T(2,128)(2,1)S(1)}, bf16[2,3584]{1,0:T(2,128)(2,1)S(1)}, u32[]{:S(2)}, u32[]{:S(2)}) %collective-permute-start.5) | collective-permute-done | bytes 14368 | tf_op jit(solution)/shard_map/ppermute | solution.py:355
  36.0 0.0 collective-permute-done.6.refs_2_
  36.0 0.0 collective-permute-done.7.refs_3_
  36.0 0.6 %shard_map.113 = (bf16[2,2048]{1,0:T(2,128)(2,1)}, bf16[2,7168]{1,0:T(2,128)(2,1)}) custom-call(bf16[2,2048]{1,0:T(2,128)(2,1)S(1)} %get-tuple-element.47.attended, bf16[2,2,2,3584]{3,2,1,0:T(2,128)(2,1)S(1)} %get-tuple-element.91.gathered, bf16[2,3584]{1,0:T(2,128)(2,1)S(1)} %collective-permute-done.4.refs_0_, ...), custom_call_target="tpu_custom_call" | custom-call | tf_op jit(solution)/shard_map/pallas_call | solution.py:357
  (3 shorter events, 0.1 us)
Async XLA Ops:
  9.1 2.7 %collective-permute-start.2 = (bf16[4,2,2176]{2,1,0:T(2,128)(2,1)S(1)}, bf16[4,2,2176]{2,1,0:T(2,128)(2,1)S(1)}, u32[]{:S(2)}, u32[]{:S(2)}) collective-permute-start(bf16[4,2,2176]{2,1,0:T(2,128)(2,1)S(1)} %get-tuple-element.48._), channel_id=1, source_target_pairs={{8,12},{10,14},{9,13},{11,15},{24,28},{26,30},{25,29},{27,31}} | collective-permute-start | bytes 104456 | tf_op jit(solution)/shard_map/ppermute | solution.py:299
  9.8 2.0 %collective-permute-start.1 = (bf16[4,2,2176]{2,1,0:T(2,128)(2,1)S(1)}, bf16[4,2,2176]{2,1,0:T(2,128)(2,1)S(1)}, u32[]{:S(2)}, u32[]{:S(2)}) collective-permute-start(bf16[4,2,2176]{2,1,0:T(2,128)(2,1)S(1)} %get-tuple-element.48._), channel_id=1, source_target_pairs={{4,12},{6,14},{5,13},{7,15},{20,28},{22,30},{21,29},{23,31}} | collective-permute-start | bytes 104456 | tf_op jit(solution)/shard_map/ppermute | solution.py:299
  10.5 2.9 %collective-permute-start = (bf16[4,2,2176]{2,1,0:T(2,128)(2,1)S(1)}, bf16[4,2,2176]{2,1,0:T(2,128)(2,1)S(1)}, u32[]{:S(2)}, u32[]{:S(2)}) collective-permute-start(bf16[4,2,2176]{2,1,0:T(2,128)(2,1)S(1)} %get-tuple-element.48._), channel_id=1, source_target_pairs={{0,12},{2,14},{1,13},{3,15},{16,28},{18,30},{17,29},{19,31}} | collective-permute-start | bytes 104456 | tf_op jit(solution)/shard_map/ppermute | solution.py:299
  13.5 4.6 %collective-permute-start.3 = (bf16[2,2,3584]{2,1,0:T(2,128)(2,1)S(1)}, bf16[2,2,3584]{2,1,0:T(2,128)(2,1)S(1)}, u32[]{:S(2)}, u32[]{:S(2)}) collective-permute-start(bf16[2,2,3584]{2,1,0:T(2,128)(2,1)S(1)} %get-tuple-element.51), channel_id=1, source_target_pairs={{12,4},{14,6},{13,5},{15,7},{28,20},{30,22},{29,21},{31,23}} | collective-permute-start | bytes 86024 | tf_op jit(solution)/shard_map/ppermute | solution.py:331
  14.2 19.6 %collective-permute-start.4 = (bf16[2,3584]{1,0:T(2,128)(2,1)S(1)}, bf16[2,3584]{1,0:T(2,128)(2,1)S(1)}, u32[]{:S(2)}, u32[]{:S(2)}) collective-permute-start(bf16[2,3584]{1,0:T(2,128)(2,1)S(1)} %get-tuple-element.52), channel_id=1, source_target_pairs={{12,0},{14,2},{13,1},{15,3},{28,16},{30,18},{29,17},{31,19}} | collective-permute-start | bytes 43016 | tf_op jit(solution)/shard_map/ppermute | solution.py:355
  15.5 20.5 %collective-permute-start.5 = (bf16[2,3584]{1,0:T(2,128)(2,1)S(1)}, bf16[2,3584]{1,0:T(2,128)(2,1)S(1)}, u32[]{:S(2)}, u32[]{:S(2)}) collective-permute-start(bf16[2,3584]{1,0:T(2,128)(2,1)S(1)} %get-tuple-element.53), channel_id=1, source_target_pairs={{12,2},{14,0},{13,3},{15,1},{28,18},{30,16},{29,19},{31,17}} | collective-permute-start | bytes 43016 | tf_op jit(solution)/shard_map/ppermute | solution.py:355
  16.8 19.2 %collective-permute-start.6 = (bf16[2,3584]{1,0:T(2,128)(2,1)S(1)}, bf16[2,3584]{1,0:T(2,128)(2,1)S(1)}, u32[]{:S(2)}, u32[]{:S(2)}) collective-permute-start(bf16[2,3584]{1,0:T(2,128)(2,1)S(1)} %get-tuple-element.54), channel_id=1, source_target_pairs={{12,8},{14,10},{13,9},{15,11},{28,24},{30,26},{29,25},{31,27}} | collective-permute-start | bytes 43016 | tf_op jit(solution)/shard_map/ppermute | solution.py:355
  17.4 18.6 %collective-permute-start.7 = (bf16[2,3584]{1,0:T(2,128)(2,1)S(1)}, bf16[2,3584]{1,0:T(2,128)(2,1)S(1)}, u32[]{:S(2)}, u32[]{:S(2)}) collective-permute-start(bf16[2,3584]{1,0:T(2,128)(2,1)S(1)} %get-tuple-element.55), channel_id=1, source_target_pairs={{12,10},{14,8},{13,11},{15,9},{28,26},{30,24},{29,27},{31,25}} | collective-permute-start | bytes 43016 | tf_op jit(solution)/shard_map/ppermute | solution.py:355

commit v18 on v15

--- a/solution.py
+++ b/solution.py
@@ -113,11 +113,22 @@
     return found
 
 
+PAIRED = (
+    ((1, 0), (0, 0)),
+    ((1, 1), (1, 0)),
+    ((0, 0), (1, 1)),
+    ((0, 1), (2, 1)),
+    ((2, 0), (0, 1)),
+    ((2, 1), (2, 0)),
+)
+
+
 def forward_kernel(blocks, workers, narrow, *refs):
     count = blocks * workers
     arrived, (gate_held, up_held, gate, up), rest = refs[:blocks], refs[blocks:][:4], refs[blocks + 4 :]
     outs, (x, slots, sems) = rest[:-3], rest[-3:]
     me = lax.axis_index("wide") - count
+    paired = (blocks, workers) == (3, 2)
     features, columns = gate.shape
     half = features // narrow
     early = gate_held.shape[1]
@@ -141,14 +152,19 @@
             for copy in stream(j):
                 copy.start()
         lines, tails = [], []
-        for block in arrived:
-            for shift in range(workers):
-                owner = lax.rem(me + shift, workers)
-                halves = [block[owner * narrow + n] for n in range(narrow)]
-                lines.append(
-                    jnp.concatenate([h[:, :half] for h in halves], 1).astype(jnp.float32)
-                )
-                tails.append(sum(h[:, half:].astype(jnp.float32) for h in halves))
+        for i in range(count):
+            b, shift = divmod(i, workers)
+            parts = [arrived[b][lax.rem(me + shift, workers) * narrow + n] for n in range(narrow)]
+            parts = [p.astype(jnp.float32) for p in parts]
+            if paired:
+                parts = []
+                for n in range(narrow):
+                    first, second = [
+                        arrived[b][o * narrow + n].astype(jnp.float32) for b, o in PAIRED[i]
+                    ]
+                    parts.append(jnp.where(me == 0, first, second))
+            lines.append(jnp.concatenate([p[:, :half] for p in parts], 1))
+            tails.append(sum(p[:, half:] for p in parts))
         pad = x.shape[0] - STEPS * count
         if pad:
             lines.append(jnp.zeros((pad, features), jnp.float32))
@@ -168,6 +184,14 @@
         def produce(at, g, u):
             g, u = g * r, u * r
             hidden = (g / (1.0 + jnp.exp(-g)) * u).astype(jnp.bfloat16)
+            here = slice(at, at + tile)
+            if paired:
+                rows = [hidden[i * STEPS : (i + 1) * STEPS] for i in range(count)]
+                outs[0][0, :, here], outs[0][1, :, here] = rows[0], rows[1]
+                outs[1][0, :, here], outs[1][1, :, here] = rows[2], rows[1]
+                for out, some in zip(outs[2:], rows[3:]):
+                    out[:, here] = some
+                return
             for i, place in enumerate(places(blocks, workers)):
                 rows = hidden[i * STEPS : (i + 1) * STEPS]
                 if place is None:
@@ -201,6 +225,41 @@
                     copy.start()
         if not units:
             resident(len(waiting))
+
+
+def other_kernel(first, second, out):
+    @pl.when(lax.rem(lax.axis_index("wide"), 2) == 0)
+    def _():
+        out[...] = first[1]
+
+    @pl.when(lax.rem(lax.axis_index("wide"), 2) == 1)
+    def _():
+        out[...] = second[1]
+
+
+def finish_paired_kernel(attended, swapped, first, second, third, fourth, fifth, attended_out, out):
+    me = lax.axis_index("wide")
+    columns = swapped.shape[1]
+    attended_out[...] = attended[...]
+    found = (
+        (second.at[0], first.at[0]),
+        (third, fourth),
+        (first.at[0], swapped),
+        (swapped, second.at[0]),
+        (fourth, fifth),
+        (fifth, third),
+    )
+
+    @pl.when(me >= len(found))
+    def _():
+        out[...] = jnp.zeros_like(out)
+
+    for i, halves in enumerate(found):
+
+        @pl.when(me == i)
+        def _(halves=halves):
+            for k, some in enumerate(halves):
+                out[:, k * columns : (k + 1) * columns] = some[...]
 
 
 def finish_kernel(blocks, workers, attended, gathered, *refs):
@@ -314,12 +373,16 @@
     )(block, gate, up)
     padded = -(-STEPS * serving // 16) * 16
     together = jax.ShapeDtypeStruct((workers, STEPS, columns), jnp.bfloat16)
+    paired = (blocks, workers) == (3, 2)
+    single = jax.ShapeDtypeStruct((STEPS, columns), jnp.bfloat16)
+    messages = [single] * (serving - workers) + [together]
+    if paired:
+        messages = [together] * 2 + [single] * 3
     *hidden, shared = pl.pallas_call(
         functools.partial(forward_kernel, blocks, workers, narrow),
-        out_shape=[jax.ShapeDtypeStruct((STEPS, columns), jnp.bfloat16)] * (serving - workers)
-        + [together],
+        out_shape=messages,
         in_specs=[vmem] * (blocks + 2) + [hbm, hbm],
-        out_specs=[vmem] * (serving - workers + 1),
+        out_specs=[vmem] * len(messages),
         scratch_shapes=[
             pltpu.VMEM((padded, features), jnp.bfloat16),
             pltpu.VMEM((SLOTS, 2, features, tile), jnp.bfloat16),
@@ -327,6 +390,44 @@
         ],
         compiler_params=pltpu.CompilerParams(vmem_limit_bytes=19 << 20),
     )(*arrived, *held, gate, up)
+    ends = (
+        jax.ShapeDtypeStruct((STEPS, half), jnp.bfloat16),
+        jax.ShapeDtypeStruct((STEPS, workers * columns), jnp.bfloat16),
+    )
+    if paired:
+        got = []
+        for message, place in zip([*hidden, shared], (0, 2, 3, 4, 5)):
+            targets = [b * workers + o for b, o in PAIRED[place]]
+            got.append(lax.ppermute(message, "wide", [(serving + k, t) for k, t in enumerate(targets)]))
+
+        def exchange(first, second):
+            other = pl.pallas_call(
+                other_kernel,
+                out_shape=single,
+                in_specs=[vmem] * 2,
+                out_specs=vmem,
+                compiler_params=pltpu.CompilerParams(vmem_limit_bytes=8 << 20),
+            )(first, second)
+            return lax.ppermute(other, "wide", [(w, w ^ 1) for w in range(wide)])
+
+        def none(first, second):
+            return pl.pallas_call(
+                blank_kernel,
+                out_shape=single,
+                out_specs=vmem,
+                compiler_params=pltpu.CompilerParams(vmem_limit_bytes=8 << 20),
+            )()
+
+        middle = lax.axis_index("wide") // workers == 1
+        swapped = lax.cond(middle, exchange, none, got[0], got[1])
+        attended, activated = pl.pallas_call(
+            finish_paired_kernel,
+            out_shape=ends,
+            in_specs=[vmem] * 7,
+            out_specs=(vmem, vmem),
+            compiler_params=pltpu.CompilerParams(vmem_limit_bytes=8 << 20),
+        )(attended, swapped, *got)
+        return attended.reshape(STEPS, 1, half), activated.reshape(STEPS, 1, -1)
     middle = blocks // 2
     shared = lax.ppermute(
         shared, "wide", [(serving + k, middle * workers + k) for k in range(workers)]

time: 37 us -> 37.5 us (1.014)
  the two profiles are of different devices: /device:TPU:0 before, /device:TPU:10 now
where the time goes in v18:
time: 37.5 us; the launch traced here: 37.1 us
  waiting for transfers between devices  20.8 us (55%)
  starting transfers between devices  6.55 us (17%)
  blocking collectives  5.2 us (14%)
  Pallas kernels  3.79 us (10%)
  between operations  0.75 us (2%)
    ppermute x5, waiting for transfers between devices, shards(): lax.ppermute(message, 'wide', [(serving + k, t) for k, t in enumerate(tar...  16.1 us
    all_gather x1, blocking collectives, serve(): lax.all_gather(sent, ('wide', 'narrow'), axis=0, axis_index_groups=groups)  5.2 us
    ppermute x5, starting transfers between devices, shards(): lax.ppermute(message, 'wide', [(serving + k, t) for k, t in enumerate(tar...  3.94 us
    ppermute x1, waiting for transfers between devices, exchange(): return lax.ppermute(other, 'wide', [(w, w ^ 1) for w in range(wide)])  3.82 us
    ppermute x3, starting transfers between devices, shards(): lax.ppermute(block, 'wide', [(b * workers + j, serving + j) for j in rang...  2.61 us
    pallas_call x1, Pallas kernels, serve(): pl.pallas_call(attend_kernel, out_shape=(pltpu.VMEM(shapes[0].shape, jnp....  2.28 us
    pallas_call x1, Pallas kernels, shards(): pl.pallas_call(finish_paired_kernel, out_shape=ends, in_specs=[vmem] * 7,...  1.33 us
    ppermute x3, waiting for transfers between devices, shards(): lax.ppermute(block, 'wide', [(b * workers + j, serving + j) for j in rang...  0.88 us
  transfers between devices with their start and end apart: 9, of which 3 were waited for; matrix products, arithmetic and copies ran while one was open for 0% of the time, Pallas kernels for 0%

profile of v18, /device:TPU:10, one launch (start us, length us, event | category | flops | bytes accessed | tf_op | source)
XLA Modules:
  0.0 37.1 jit_solution(6698512073691360549)
XLA Ops:
  0.6 7.5 %conditional.2 = ((bf16[2,2048]{1,0:T(2,128)(2,1)S(1)}, bf16[4,2,2176]{2,1,0:T(2,128)(2,1)S(1)})) conditional(s32[]{:T(128)} %convert_element_type.6, () %tuple.21, (s32[1]{0:T(128)}, bf16[2,1,2048]{2,0,1:T(2,128)(2,1)}, bf16[2,1,2,512]{3,2,1,0:T(2,128)(2,1)}, bf16[1,4,128,128]{3,2,1,0:T(8,128)(2,1)}, bf16[1,4,128,128]{3,2,1,0:T(8,128)(2,1)}, ...), branch_computations={%region_0.0_spmd, %region_1.0_spmd} | conditional | bytes 43544 | solution.py:356
  0.7 2.3 %branch_1_fun.2 = (bf16[2,2048]{1,0:T(2,128)(2,1)S(1)}, bf16[2,2176]{1,0:T(2,128)(2,1)S(1)}) custom-call(s32[1,1]{1,0:T(1,128)} %bitcast.refs_0_, bf16[2,2048]{1,0:T(2,128)(2,1)} %bitcast.20, bf16[2,2,512]{2,1,0:T(2,128)(2,1)} %bitcast.23, bf16[4,128,128]{2,1,0:T(8,128)(2,1)} %bitcast.18, bf16[4,128,128]{2,1,0:T(8,128)(2,1)} %bitcast.19, ...), custom_call_target="tpu_custom_call" | custom-call | tf_op jit(solution)/shard_map/cond/branch_1_fun/pallas_call | solution.py:330
  2.9 5.2 %all-gather.1 = bf16[4,2,2176]{2,1,0:T(2,128)(2,1)S(1)} all-gather(bf16[1,2,2176]{2,1,0:T(2,128)(2,1)S(1)} %bitcast.13), channel_id=2, replica_groups={{0,1,2,3},{4,5,6,7},{8,9,10,11},{12,13,14,15},{16,17,18,19},{20,21,22,2..., dimensions={0}, use_global_device_ids=true | all-gather | bytes 43520 | tf_op jit(solution)/shard_map/cond/branch_1_fun/all_gather | solution.py:345
  8.1 0.7 %collective-permute-start.3 = (bf16[4,2,2176]{2,1,0:T(2,128)(2,1)S(1)}, bf16[4,2,2176]{2,1,0:T(2,128)(2,1)S(1)}, u32[]{:S(2)}, u32[]{:S(2)}) collective-permute-start(bf16[4,2,2176]{2,1,0:T(2,128)(2,1)S(1)} %get-tuple-element.53._), channel_id=1, source_target_pairs={{8,12},{10,14},{9,13},{11,15},{24,28},{26,30},{25,29},{27,31}} | collective-permute-start | bytes 104456 | tf_op jit(solution)/shard_map/ppermute | solution.py:358
  8.8 1.3 %collective-permute-start.2 = (bf16[4,2,2176]{2,1,0:T(2,128)(2,1)S(1)}, bf16[4,2,2176]{2,1,0:T(2,128)(2,1)S(1)}, u32[]{:S(2)}, u32[]{:S(2)}) collective-permute-start(bf16[4,2,2176]{2,1,0:T(2,128)(2,1)S(1)} %get-tuple-element.53._), channel_id=1, source_target_pairs={{4,12},{6,14},{5,13},{7,15},{20,28},{22,30},{21,29},{23,31}} | collective-permute-start | bytes 104456 | tf_op jit(solution)/shard_map/ppermute | solution.py:358
  10.1 0.7 %collective-permute-start.1 = (bf16[4,2,2176]{2,1,0:T(2,128)(2,1)S(1)}, bf16[4,2,2176]{2,1,0:T(2,128)(2,1)S(1)}, u32[]{:S(2)}, u32[]{:S(2)}) collective-permute-start(bf16[4,2,2176]{2,1,0:T(2,128)(2,1)S(1)} %get-tuple-element.53._), channel_id=1, source_target_pairs={{0,12},{2,14},{1,13},{3,15},{16,28},{18,30},{17,29},{19,31}} | collective-permute-start | bytes 104456 | tf_op jit(solution)/shard_map/ppermute | solution.py:358
  10.8 0.0 collective-permute-done.3.refs_2_
  10.8 0.9 %collective-permute-done.2.refs_1_ = bf16[4,2,2176]{2,1,0:T(2,128)(2,1)S(1)} collective-permute-done((bf16[4,2,2176]{2,1,0:T(2,128)(2,1)S(1)}, bf16[4,2,2176]{2,1,0:T(2,128)(2,1)S(1)}, u32[]{:S(2)}, u32[]{:S(2)}) %collective-permute-start.2) | collective-permute-done | bytes 34848 | tf_op jit(solution)/shard_map/ppermute | solution.py:358
  11.7 0.0 collective-permute-done.1.refs_0_
  11.7 0.1 shard_map.112
  11.9 0.7 %collective-permute-start.4 = (bf16[2,2,3584]{2,1,0:T(2,128)(2,1)S(1)}, bf16[2,2,3584]{2,1,0:T(2,128)(2,1)S(1)}, u32[]{:S(2)}, u32[]{:S(2)}) collective-permute-start(bf16[2,2,3584]{2,1,0:T(2,128)(2,1)S(1)} %get-tuple-element.56), channel_id=1, source_target_pairs={{12,4},{14,0},{13,5},{15,1},{28,20},{30,16},{29,21},{31,17}} | collective-permute-start | bytes 86024 | tf_op jit(solution)/shard_map/ppermute | solution.py:401
  12.5 1.3 %collective-permute-start.5 = (bf16[2,2,3584]{2,1,0:T(2,128)(2,1)S(1)}, bf16[2,2,3584]{2,1,0:T(2,128)(2,1)S(1)}, u32[]{:S(2)}, u32[]{:S(2)}) collective-permute-start(bf16[2,2,3584]{2,1,0:T(2,128)(2,1)S(1)} %get-tuple-element.57), channel_id=1, source_target_pairs={{12,0},{14,6},{13,1},{15,7},{28,16},{30,22},{29,17},{31,23}} | collective-permute-start | bytes 86024 | tf_op jit(solution)/shard_map/ppermute | solution.py:401
  13.8 0.7 %collective-permute-start.6 = (bf16[2,3584]{1,0:T(2,128)(2,1)S(1)}, bf16[2,3584]{1,0:T(2,128)(2,1)S(1)}, u32[]{:S(2)}, u32[]{:S(2)}) collective-permute-start(bf16[2,3584]{1,0:T(2,128)(2,1)S(1)} %get-tuple-element.58), channel_id=1, source_target_pairs={{12,2},{14,10},{13,3},{15,11},{28,18},{30,26},{29,19},{31,27}} | collective-permute-start | bytes 43016 | tf_op jit(solution)/shard_map/ppermute | solution.py:401
  14.5 0.7 %collective-permute-start.7 = (bf16[2,3584]{1,0:T(2,128)(2,1)S(1)}, bf16[2,3584]{1,0:T(2,128)(2,1)S(1)}, u32[]{:S(2)}, u32[]{:S(2)}) collective-permute-start(bf16[2,3584]{1,0:T(2,128)(2,1)S(1)} %get-tuple-element.59), channel_id=1, source_target_pairs={{12,8},{14,2},{13,9},{15,3},{28,24},{30,18},{29,25},{31,19}} | collective-permute-start | bytes 43016 | tf_op jit(solution)/shard_map/ppermute | solution.py:401
  15.2 0.7 %collective-permute-start.8 = (bf16[2,3584]{1,0:T(2,128)(2,1)S(1)}, bf16[2,3584]{1,0:T(2,128)(2,1)S(1)}, u32[]{:S(2)}, u32[]{:S(2)}) collective-permute-start(bf16[2,3584]{1,0:T(2,128)(2,1)S(1)} %get-tuple-element.60), channel_id=1, source_target_pairs={{12,10},{14,8},{13,11},{15,9},{28,26},{30,24},{29,27},{31,25}} | collective-permute-start | bytes 43016 | tf_op jit(solution)/shard_map/ppermute | solution.py:401
  15.8 0.0 collective-permute-done.4.first
  15.9 16.1 %collective-permute-done.5.second = bf16[2,2,3584]{2,1,0:T(2,128)(2,1)S(1)} collective-permute-done((bf16[2,2,3584]{2,1,0:T(2,128)(2,1)S(1)}, bf16[2,2,3584]{2,1,0:T(2,128)(2,1)S(1)}, u32[]{:S(2)}, u32[]{:S(2)}) %collective-permute-start.5) | collective-permute-done | bytes 28704 | tf_op jit(solution)/shard_map/ppermute | solution.py:401
  32.0 3.8 %conditional.3 = (bf16[2,3584]{1,0:T(2,128)(2,1)}) conditional(s32[]{:T(128)} %convert_element_type.7, () %tuple.23, (bf16[2,2,3584]{2,1,0:T(2,128)(2,1)S(1)}, bf16[2,2,3584]{2,1,0:T(2,128)(2,1)S(1)}) %tuple.24), branch_computations={%region_2.3_spmd, %region_3.4_spmd} | conditional | bytes 57392 | solution.py:422
  32.0 0.0 collective-permute-start
  32.0 3.8 %collective-permute-done = bf16[2,3584]{1,0:T(2,128)(2,1)} collective-permute-done((bf16[2,3584]{1,0:T(2,128)(2,1)S(1)}, bf16[2,3584]{1,0:T(2,128)(2,1)}, u32[]{:S(2)}, u32[]{:S(2)}) %collective-permute-start) | collective-permute-done | bytes 14368 | tf_op jit(solution)/shard_map/cond/branch_1_fun/ppermute | solution.py:411
  35.8 0.0 collective-permute-done.6.third
  35.8 0.0 collective-permute-done.7.fourth
  35.8 0.0 collective-permute-done.8.fifth
  35.8 1.3 %shard_map.113 = (bf16[2,2048]{1,0:T(2,128)(2,1)}, bf16[2,7168]{1,0:T(2,128)(2,1)}) custom-call(bf16[2,2048]{1,0:T(2,128)(2,1)S(1)} %get-tuple-element.52.attended, bf16[2,3584]{1,0:T(2,128)(2,1)} %get-tuple-element.96.swapped, bf16[2,2,3584]{2,1,0:T(2,128)(2,1)S(1)} %collective-permute-done.4.first, bf16[2,2,3584]{2,1,0:T(2,128)(2,1)S(1)} %collective-permute-done.5.second, ...), custom_call_target="tpu_custom_call" | custom-call | tf_op jit(solution)/shard_map/pallas_call | solution.py:423
  (2 shorter events, 0.0 us)
Async XLA Ops:
  8.1 2.7 %collective-permute-start.3 = (bf16[4,2,2176]{2,1,0:T(2,128)(2,1)S(1)}, bf16[4,2,2176]{2,1,0:T(2,128)(2,1)S(1)}, u32[]{:S(2)}, u32[]{:S(2)}) collective-permute-start(bf16[4,2,2176]{2,1,0:T(2,128)(2,1)S(1)} %get-tuple-element.53._), channel_id=1, source_target_pairs={{8,12},{10,14},{9,13},{11,15},{24,28},{26,30},{25,29},{27,31}} | collective-permute-start | bytes 104456 | tf_op jit(solution)/shard_map/ppermute | solution.py:358
  8.8 2.9 %collective-permute-start.2 = (bf16[4,2,2176]{2,1,0:T(2,128)(2,1)S(1)}, bf16[4,2,2176]{2,1,0:T(2,128)(2,1)S(1)}, u32[]{:S(2)}, u32[]{:S(2)}) collective-permute-start(bf16[4,2,2176]{2,1,0:T(2,128)(2,1)S(1)} %get-tuple-element.53._), channel_id=1, source_target_pairs={{4,12},{6,14},{5,13},{7,15},{20,28},{22,30},{21,29},{23,31}} | collective-permute-start | bytes 104456 | tf_op jit(solution)/shard_map/ppermute | solution.py:358
  10.1 1.6 %collective-permute-start.1 = (bf16[4,2,2176]{2,1,0:T(2,128)(2,1)S(1)}, bf16[4,2,2176]{2,1,0:T(2,128)(2,1)S(1)}, u32[]{:S(2)}, u32[]{:S(2)}) collective-permute-start(bf16[4,2,2176]{2,1,0:T(2,128)(2,1)S(1)} %get-tuple-element.53._), channel_id=1, source_target_pairs={{0,12},{2,14},{1,13},{3,15},{16,28},{18,30},{17,29},{19,31}} | collective-permute-start | bytes 104456 | tf_op jit(solution)/shard_map/ppermute | solution.py:358
  11.9 4.0 %collective-permute-start.4 = (bf16[2,2,3584]{2,1,0:T(2,128)(2,1)S(1)}, bf16[2,2,3584]{2,1,0:T(2,128)(2,1)S(1)}, u32[]{:S(2)}, u32[]{:S(2)}) collective-permute-start(bf16[2,2,3584]{2,1,0:T(2,128)(2,1)S(1)} %get-tuple-element.56), channel_id=1, source_target_pairs={{12,4},{14,0},{13,5},{15,1},{28,20},{30,16},{29,21},{31,17}} | collective-permute-start | bytes 86024 | tf_op jit(solution)/shard_map/ppermute | solution.py:401
  12.5 19.4 %collective-permute-start.5 = (bf16[2,2,3584]{2,1,0:T(2,128)(2,1)S(1)}, bf16[2,2,3584]{2,1,0:T(2,128)(2,1)S(1)}, u32[]{:S(2)}, u32[]{:S(2)}) collective-permute-start(bf16[2,2,3584]{2,1,0:T(2,128)(2,1)S(1)} %get-tuple-element.57), channel_id=1, source_target_pairs={{12,0},{14,6},{13,1},{15,7},{28,16},{30,22},{29,17},{31,23}} | collective-permute-start | bytes 86024 | tf_op jit(solution)/shard_map/ppermute | solution.py:401
  13.8 22.0 %collective-permute-start.6 = (bf16[2,3584]{1,0:T(2,128)(2,1)S(1)}, bf16[2,3584]{1,0:T(2,128)(2,1)S(1)}, u32[]{:S(2)}, u32[]{:S(2)}) collective-permute-start(bf16[2,3584]{1,0:T(2,128)(2,1)S(1)} %get-tuple-element.58), channel_id=1, source_target_pairs={{12,2},{14,10},{13,3},{15,11},{28,18},{30,26},{29,19},{31,27}} | collective-permute-start | bytes 43016 | tf_op jit(solution)/shard_map/ppermute | solution.py:401
  14.5 21.3 %collective-permute-start.7 = (bf16[2,3584]{1,0:T(2,128)(2,1)S(1)}, bf16[2,3584]{1,0:T(2,128)(2,1)S(1)}, u32[]{:S(2)}, u32[]{:S(2)}) collective-permute-start(bf16[2,3584]{1,0:T(2,128)(2,1)S(1)} %get-tuple-element.59), channel_id=1, source_target_pairs={{12,8},{14,2},{13,9},{15,3},{28,24},{30,18},{29,25},{31,19}} | collective-permute-start | bytes 43016 | tf_op jit(solution)/shard_map/ppermute | solution.py:401
  15.2 20.6 %collective-permute-start.8 = (bf16[2,3584]{1,0:T(2,128)(2,1)S(1)}, bf16[2,3584]{1,0:T(2,128)(2,1)S(1)}, u32[]{:S(2)}, u32[]{:S(2)}) collective-permute-start(bf16[2,3584]{1,0:T(2,128)(2,1)S(1)} %get-tuple-element.60), channel_id=1, source_target_pairs={{12,10},{14,8},{13,11},{15,9},{28,26},{30,24},{29,27},{31,25}} | collective-permute-start | bytes 43016 | tf_op jit(solution)/shard_map/ppermute | solution.py:401
  32.0 3.8 %collective-permute-start = (bf16[2,3584]{1,0:T(2,128)(2,1)S(1)}, bf16[2,3584]{1,0:T(2,128)(2,1)}, u32[]{:S(2)}, u32[]{:S(2)}) collective-permute-start(bf16[2,3584]{1,0:T(2,128)(2,1)S(1)} %branch_1_fun.3), channel_id=1, source_target_pairs={{0,2},{2,0},{4,6},{6,4},{8,10},{10,8},{12,14},{14,12},{1,3},{3,1},... | collective-permute-start | bytes 43016 | tf_op jit(solution)/shard_map/cond/branch_1_fun/ppermute | solution.py:411

commit v19 on v15

--- a/solution.py
+++ b/solution.py
@@ -146,14 +146,14 @@
                 owner = lax.rem(me + shift, workers)
                 halves = [block[owner * narrow + n] for n in range(narrow)]
                 lines.append(
-                    jnp.concatenate([h[:, :half] for h in halves], 1).astype(jnp.float32)
+                    jnp.concatenate([h[:, :half] for h in halves], 1)
                 )
                 tails.append(sum(h[:, half:].astype(jnp.float32) for h in halves))
         pad = x.shape[0] - STEPS * count
         if pad:
-            lines.append(jnp.zeros((pad, features), jnp.float32))
+            lines.append(jnp.zeros((pad, features), jnp.bfloat16))
             tails.append(jnp.zeros((pad, TAIL), jnp.float32))
-        x[...] = jnp.concatenate(lines, 0).astype(jnp.bfloat16)
+        x[...] = jnp.concatenate(lines, 0)
         squares = jnp.sum(jnp.concatenate(tails, 0), -1, keepdims=True)
         r = lax.rsqrt(squares / D + EPS)
 

time: 37 us -> 37.4 us (1.011)
  waiting for transfers between devices: 19.4 us -> 19.9 us
    ppermute x4, waiting for transfers between devices: 17.8 us -> 18.3 us  [shards(): results[nth] = lax.ppermute(hidden[nth], 'wide', pairs)]
where the time goes in v19:
time: 37.4 us; the launch traced here: 37.2 us
  waiting for transfers between devices  19.9 us (53%)
  starting transfers between devices  7.18 us (19%)
  blocking collectives  6.18 us (17%)
  Pallas kernels  3.11 us (8%)
  between operations  0.76 us (2%)
    ppermute x4, waiting for transfers between devices, shards(): results[nth] = lax.ppermute(hidden[nth], 'wide', pairs)  18.3 us
    all_gather x1, blocking collectives, serve(): lax.all_gather(sent, ('wide', 'narrow'), axis=0, axis_index_groups=groups)  6.18 us
    ppermute x4, starting transfers between devices, shards(): results[nth] = lax.ppermute(hidden[nth], 'wide', pairs)  3.91 us
    ppermute x3, starting transfers between devices, shards(): lax.ppermute(block, 'wide', [(b * workers + j, serving + j) for j in rang...  2.61 us
    pallas_call x1, Pallas kernels, serve(): pl.pallas_call(attend_kernel, out_shape=(pltpu.VMEM(shapes[0].shape, jnp....  2.28 us
    ppermute x3, waiting for transfers between devices, shards(): lax.ppermute(block, 'wide', [(b * workers + j, serving + j) for j in rang...  1.54 us
  transfers between devices with their start and end apart: 8, of which 3 were waited for; matrix products, arithmetic and copies ran while one was open for 0% of the time, Pallas kernels for 0%

profile of v19, /device:TPU:0, one launch (start us, length us, event | category | flops | bytes accessed | tf_op | source)
XLA Modules:
  0.0 37.2 jit_solution(16891527306345831311)
XLA Ops:
  0.6 8.5 %conditional.2 = ((bf16[2,2048]{1,0:T(2,128)(2,1)S(1)}, bf16[4,2,2176]{2,1,0:T(2,128)(2,1)S(1)})) conditional(s32[]{:T(128)} %convert_element_type.6, () %tuple.21, (s32[1]{0:T(128)}, bf16[2,1,2048]{2,0,1:T(2,128)(2,1)}, bf16[2,1,2,512]{3,2,1,0:T(2,128)(2,1)}, bf16[1,4,128,128]{3,2,1,0:T(8,128)(2,1)}, bf16[1,4,128,128]{3,2,1,0:T(8,128)(2,1)}, ...), branch_computations={%region_0.0_spmd, %region_1.0_spmd} | conditional | bytes 43544 | solution.py:297
  0.7 2.3 %branch_1_fun.1 = (bf16[2,2048]{1,0:T(2,128)(2,1)S(1)}, bf16[2,2176]{1,0:T(2,128)(2,1)S(1)}) custom-call(s32[1,1]{1,0:T(1,128)} %bitcast.refs_0_, bf16[2,2048]{1,0:T(2,128)(2,1)} %bitcast.22, bf16[2,2,512]{2,1,0:T(2,128)(2,1)} %bitcast.25, bf16[4,128,128]{2,1,0:T(8,128)(2,1)} %bitcast.20, bf16[4,128,128]{2,1,0:T(8,128)(2,1)} %bitcast.21, ...), custom_call_target="tpu_custom_call" | custom-call | tf_op jit(solution)/shard_map/cond/branch_1_fun/pallas_call | solution.py:271
  2.9 6.2 %all-gather.2 = bf16[4,2,2176]{2,1,0:T(2,128)(2,1)S(1)} all-gather(bf16[1,2,2176]{2,1,0:T(2,128)(2,1)S(1)} %bitcast.14), channel_id=2, replica_groups={{0,1,2,3},{4,5,6,7},{8,9,10,11},{12,13,14,15},{16,17,18,19},{20,21,22,2..., dimensions={0}, use_global_device_ids=true | all-gather | bytes 43520 | tf_op jit(solution)/shard_map/cond/branch_1_fun/all_gather | solution.py:286
  9.1 0.7 %collective-permute-start.2 = (bf16[4,2,2176]{2,1,0:T(2,128)(2,1)S(1)}, bf16[4,2,2176]{2,1,0:T(2,128)(2,1)S(1)}, u32[]{:S(2)}, u32[]{:S(2)}) collective-permute-start(bf16[4,2,2176]{2,1,0:T(2,128)(2,1)S(1)} %get-tuple-element.48._), channel_id=1, source_target_pairs={{8,12},{10,14},{9,13},{11,15},{24,28},{26,30},{25,29},{27,31}} | collective-permute-start | bytes 104456 | tf_op jit(solution)/shard_map/ppermute | solution.py:299
  9.8 0.7 %collective-permute-start.1 = (bf16[4,2,2176]{2,1,0:T(2,128)(2,1)S(1)}, bf16[4,2,2176]{2,1,0:T(2,128)(2,1)S(1)}, u32[]{:S(2)}, u32[]{:S(2)}) collective-permute-start(bf16[4,2,2176]{2,1,0:T(2,128)(2,1)S(1)} %get-tuple-element.48._), channel_id=1, source_target_pairs={{4,12},{6,14},{5,13},{7,15},{20,28},{22,30},{21,29},{23,31}} | collective-permute-start | bytes 104456 | tf_op jit(solution)/shard_map/ppermute | solution.py:299
  10.5 1.3 %collective-permute-start = (bf16[4,2,2176]{2,1,0:T(2,128)(2,1)S(1)}, bf16[4,2,2176]{2,1,0:T(2,128)(2,1)S(1)}, u32[]{:S(2)}, u32[]{:S(2)}) collective-permute-start(bf16[4,2,2176]{2,1,0:T(2,128)(2,1)S(1)} %get-tuple-element.48._), channel_id=1, source_target_pairs={{0,12},{2,14},{1,13},{3,15},{16,28},{18,30},{17,29},{19,31}} | collective-permute-start | bytes 104456 | tf_op jit(solution)/shard_map/ppermute | solution.py:299
  11.8 0.0 collective-permute-done.2.refs_2_
  11.8 0.0 collective-permute-done.1.refs_1_
  11.8 1.5 %collective-permute-done.refs_0_ = bf16[4,2,2176]{2,1,0:T(2,128)(2,1)S(1)} collective-permute-done((bf16[4,2,2176]{2,1,0:T(2,128)(2,1)S(1)}, bf16[4,2,2176]{2,1,0:T(2,128)(2,1)S(1)}, u32[]{:S(2)}, u32[]{:S(2)}) %collective-permute-start) | collective-permute-done | bytes 34848 | tf_op jit(solution)/shard_map/ppermute | solution.py:299
  13.3 0.1 shard_map.112
  13.5 0.7 %collective-permute-start.3 = (bf16[2,2,3584]{2,1,0:T(2,128)(2,1)S(1)}, bf16[2,2,3584]{2,1,0:T(2,128)(2,1)S(1)}, u32[]{:S(2)}, u32[]{:S(2)}) collective-permute-start(bf16[2,2,3584]{2,1,0:T(2,128)(2,1)S(1)} %get-tuple-element.51), channel_id=1, source_target_pairs={{12,4},{14,6},{13,5},{15,7},{28,20},{30,22},{29,21},{31,23}} | collective-permute-start | bytes 86024 | tf_op jit(solution)/shard_map/ppermute | solution.py:331
  14.2 1.3 %collective-permute-start.4 = (bf16[2,3584]{1,0:T(2,128)(2,1)S(1)}, bf16[2,3584]{1,0:T(2,128)(2,1)S(1)}, u32[]{:S(2)}, u32[]{:S(2)}) collective-permute-start(bf16[2,3584]{1,0:T(2,128)(2,1)S(1)} %get-tuple-element.52), channel_id=1, source_target_pairs={{12,0},{14,2},{13,1},{15,3},{28,16},{30,18},{29,17},{31,19}} | collective-permute-start | bytes 43016 | tf_op jit(solution)/shard_map/ppermute | solution.py:355
  15.5 1.3 %collective-permute-start.5 = (bf16[2,3584]{1,0:T(2,128)(2,1)S(1)}, bf16[2,3584]{1,0:T(2,128)(2,1)S(1)}, u32[]{:S(2)}, u32[]{:S(2)}) collective-permute-start(bf16[2,3584]{1,0:T(2,128)(2,1)S(1)} %get-tuple-element.53), channel_id=1, source_target_pairs={{12,2},{14,0},{13,3},{15,1},{28,18},{30,16},{29,19},{31,17}} | collective-permute-start | bytes 43016 | tf_op jit(solution)/shard_map/ppermute | solution.py:355
  16.8 0.7 %collective-permute-start.6 = (bf16[2,3584]{1,0:T(2,128)(2,1)S(1)}, bf16[2,3584]{1,0:T(2,128)(2,1)S(1)}, u32[]{:S(2)}, u32[]{:S(2)}) collective-permute-start(bf16[2,3584]{1,0:T(2,128)(2,1)S(1)} %get-tuple-element.54), channel_id=1, source_target_pairs={{12,8},{14,10},{13,9},{15,11},{28,24},{30,26},{29,25},{31,27}} | collective-permute-start | bytes 43016 | tf_op jit(solution)/shard_map/ppermute | solution.py:355
  17.4 0.7 %collective-permute-start.7 = (bf16[2,3584]{1,0:T(2,128)(2,1)S(1)}, bf16[2,3584]{1,0:T(2,128)(2,1)S(1)}, u32[]{:S(2)}, u32[]{:S(2)}) collective-permute-start(bf16[2,3584]{1,0:T(2,128)(2,1)S(1)} %get-tuple-element.55), channel_id=1, source_target_pairs={{12,10},{14,8},{13,11},{15,9},{28,26},{30,24},{29,27},{31,25}} | collective-permute-start | bytes 43016 | tf_op jit(solution)/shard_map/ppermute | solution.py:355
  18.1 0.0 collective-permute-done.3
  18.2 16.1 %collective-permute-done.4.refs_0_ = bf16[2,3584]{1,0:T(2,128)(2,1)S(1)} collective-permute-done((bf16[2,3584]{1,0:T(2,128)(2,1)S(1)}, bf16[2,3584]{1,0:T(2,128)(2,1)S(1)}, u32[]{:S(2)}, u32[]{:S(2)}) %collective-permute-start.4) | collective-permute-done | bytes 14368 | tf_op jit(solution)/shard_map/ppermute | solution.py:355
  34.3 2.2 %collective-permute-done.5.refs_1_ = bf16[2,3584]{1,0:T(2,128)(2,1)S(1)} collective-permute-done((bf16[2,3584]{1,0:T(2,128)(2,1)S(1)}, bf16[2,3584]{1,0:T(2,128)(2,1)S(1)}, u32[]{:S(2)}, u32[]{:S(2)}) %collective-permute-start.5) | collective-permute-done | bytes 14368 | tf_op jit(solution)/shard_map/ppermute | solution.py:355
  36.5 0.0 collective-permute-done.6.refs_2_
  36.5 0.0 collective-permute-done.7.refs_3_
  36.5 0.6 %shard_map.113 = (bf16[2,2048]{1,0:T(2,128)(2,1)}, bf16[2,7168]{1,0:T(2,128)(2,1)}) custom-call(bf16[2,2048]{1,0:T(2,128)(2,1)S(1)} %get-tuple-element.47.attended, bf16[2,2,2,3584]{3,2,1,0:T(2,128)(2,1)S(1)} %get-tuple-element.91.gathered, bf16[2,3584]{1,0:T(2,128)(2,1)S(1)} %collective-permute-done.4.refs_0_, ...), custom_call_target="tpu_custom_call" | custom-call | tf_op jit(solution)/shard_map/pallas_call | solution.py:357
  (3 shorter events, 0.1 us)
Async XLA Ops:
  9.1 2.7 %collective-permute-start.2 = (bf16[4,2,2176]{2,1,0:T(2,128)(2,1)S(1)}, bf16[4,2,2176]{2,1,0:T(2,128)(2,1)S(1)}, u32[]{:S(2)}, u32[]{:S(2)}) collective-permute-start(bf16[4,2,2176]{2,1,0:T(2,128)(2,1)S(1)} %get-tuple-element.48._), channel_id=1, source_target_pairs={{8,12},{10,14},{9,13},{11,15},{24,28},{26,30},{25,29},{27,31}} | collective-permute-start | bytes 104456 | tf_op jit(solution)/shard_map/ppermute | solution.py:299
  9.8 2.0 %collective-permute-start.1 = (bf16[4,2,2176]{2,1,0:T(2,128)(2,1)S(1)}, bf16[4,2,2176]{2,1,0:T(2,128)(2,1)S(1)}, u32[]{:S(2)}, u32[]{:S(2)}) collective-permute-start(bf16[4,2,2176]{2,1,0:T(2,128)(2,1)S(1)} %get-tuple-element.48._), channel_id=1, source_target_pairs={{4,12},{6,14},{5,13},{7,15},{20,28},{22,30},{21,29},{23,31}} | collective-permute-start | bytes 104456 | tf_op jit(solution)/shard_map/ppermute | solution.py:299
  10.5 2.9 %collective-permute-start = (bf16[4,2,2176]{2,1,0:T(2,128)(2,1)S(1)}, bf16[4,2,2176]{2,1,0:T(2,128)(2,1)S(1)}, u32[]{:S(2)}, u32[]{:S(2)}) collective-permute-start(bf16[4,2,2176]{2,1,0:T(2,128)(2,1)S(1)} %get-tuple-element.48._), channel_id=1, source_target_pairs={{0,12},{2,14},{1,13},{3,15},{16,28},{18,30},{17,29},{19,31}} | collective-permute-start | bytes 104456 | tf_op jit(solution)/shard_map/ppermute | solution.py:299
  13.5 4.6 %collective-permute-start.3 = (bf16[2,2,3584]{2,1,0:T(2,128)(2,1)S(1)}, bf16[2,2,3584]{2,1,0:T(2,128)(2,1)S(1)}, u32[]{:S(2)}, u32[]{:S(2)}) collective-permute-start(bf16[2,2,3584]{2,1,0:T(2,128)(2,1)S(1)} %get-tuple-element.51), channel_id=1, source_target_pairs={{12,4},{14,6},{13,5},{15,7},{28,20},{30,22},{29,21},{31,23}} | collective-permute-start | bytes 86024 | tf_op jit(solution)/shard_map/ppermute | solution.py:331
  14.2 20.1 %collective-permute-start.4 = (bf16[2,3584]{1,0:T(2,128)(2,1)S(1)}, bf16[2,3584]{1,0:T(2,128)(2,1)S(1)}, u32[]{:S(2)}, u32[]{:S(2)}) collective-permute-start(bf16[2,3584]{1,0:T(2,128)(2,1)S(1)} %get-tuple-element.52), channel_id=1, source_target_pairs={{12,0},{14,2},{13,1},{15,3},{28,16},{30,18},{29,17},{31,19}} | collective-permute-start | bytes 43016 | tf_op jit(solution)/shard_map/ppermute | solution.py:355
  15.5 21.0 %collective-permute-start.5 = (bf16[2,3584]{1,0:T(2,128)(2,1)S(1)}, bf16[2,3584]{1,0:T(2,128)(2,1)S(1)}, u32[]{:S(2)}, u32[]{:S(2)}) collective-permute-start(bf16[2,3584]{1,0:T(2,128)(2,1)S(1)} %get-tuple-element.53), channel_id=1, source_target_pairs={{12,2},{14,0},{13,3},{15,1},{28,18},{30,16},{29,19},{31,17}} | collective-permute-start | bytes 43016 | tf_op jit(solution)/shard_map/ppermute | solution.py:355
  16.8 19.7 %collective-permute-start.6 = (bf16[2,3584]{1,0:T(2,128)(2,1)S(1)}, bf16[2,3584]{1,0:T(2,128)(2,1)S(1)}, u32[]{:S(2)}, u32[]{:S(2)}) collective-permute-start(bf16[2,3584]{1,0:T(2,128)(2,1)S(1)} %get-tuple-element.54), channel_id=1, source_target_pairs={{12,8},{14,10},{13,9},{15,11},{28,24},{30,26},{29,25},{31,27}} | collective-permute-start | bytes 43016 | tf_op jit(solution)/shard_map/ppermute | solution.py:355
  17.4 19.1 %collective-permute-start.7 = (bf16[2,3584]{1,0:T(2,128)(2,1)S(1)}, bf16[2,3584]{1,0:T(2,128)(2,1)S(1)}, u32[]{:S(2)}, u32[]{:S(2)}) collective-permute-start(bf16[2,3584]{1,0:T(2,128)(2,1)S(1)} %get-tuple-element.55), channel_id=1, source_target_pairs={{12,10},{14,8},{13,11},{15,9},{28,26},{30,24},{29,27},{31,25}} | collective-permute-start | bytes 43016 | tf_op jit(solution)/shard_map/ppermute | solution.py:355

commit v20 on v19

--- a/solution.py
+++ b/solution.py
@@ -116,7 +116,7 @@
 def forward_kernel(blocks, workers, narrow, *refs):
     count = blocks * workers
     arrived, (gate_held, up_held, gate, up), rest = refs[:blocks], refs[blocks:][:4], refs[blocks + 4 :]
-    outs, (x, slots, sems) = rest[:-3], rest[-3:]
+    outs, (x, wide_rows, slots, sems) = rest[:-4], rest[-4:]
     me = lax.axis_index("wide") - count
     features, columns = gate.shape
     half = features // narrow
@@ -140,20 +140,22 @@
         for j in range(min(room, len(units))):
             for copy in stream(j):
                 copy.start()
-        lines, tails = [], []
-        for block in arrived:
+        tails = []
+        for b, block in enumerate(arrived):
             for shift in range(workers):
                 owner = lax.rem(me + shift, workers)
-                halves = [block[owner * narrow + n] for n in range(narrow)]
-                lines.append(
-                    jnp.concatenate([h[:, :half] for h in halves], 1)
-                )
-                tails.append(sum(h[:, half:].astype(jnp.float32) for h in halves))
+                at = (b * workers + shift) * STEPS
+                tail = jnp.zeros((STEPS, TAIL), jnp.float32)
+                for n in range(narrow):
+                    piece = block[owner * narrow + n].astype(jnp.float32)
+                    wide_rows[at : at + STEPS, n * half : (n + 1) * half] = piece[:, :half]
+                    tail += piece[:, half:]
+                tails.append(tail)
         pad = x.shape[0] - STEPS * count
         if pad:
-            lines.append(jnp.zeros((pad, features), jnp.bfloat16))
+            wide_rows[STEPS * count :, :] = jnp.zeros((pad, features), jnp.float32)
             tails.append(jnp.zeros((pad, TAIL), jnp.float32))
-        x[...] = jnp.concatenate(lines, 0)
+        x[...] = wide_rows[...].astype(jnp.bfloat16)
         squares = jnp.sum(jnp.concatenate(tails, 0), -1, keepdims=True)
         r = lax.rsqrt(squares / D + EPS)
 
@@ -322,6 +324,7 @@
         out_specs=[vmem] * (serving - workers + 1),
         scratch_shapes=[
             pltpu.VMEM((padded, features), jnp.bfloat16),
+            pltpu.VMEM((padded, features), jnp.float32),
             pltpu.VMEM((SLOTS, 2, features, tile), jnp.bfloat16),
             pltpu.SemaphoreType.DMA((SLOTS, 2, 2)),
         ],

time: 37.4 us -> 37.4 us (level)
  no operation moved by 1% of the time
where the time goes in v20:
time: 37.4 us; the launch traced here: 37.2 us
  waiting for transfers between devices  19.9 us (53%)
  starting transfers between devices  7.18 us (19%)
  blocking collectives  6.18 us (17%)
  Pallas kernels  3.11 us (8%)
  between operations  0.76 us (2%)
    ppermute x4, waiting for transfers between devices, shards(): results[nth] = lax.ppermute(hidden[nth], 'wide', pairs)  18.3 us
    all_gather x1, blocking collectives, serve(): lax.all_gather(sent, ('wide', 'narrow'), axis=0, axis_index_groups=groups)  6.18 us
    ppermute x4, starting transfers between devices, shards(): results[nth] = lax.ppermute(hidden[nth], 'wide', pairs)  3.91 us
    ppermute x3, starting transfers between devices, shards(): lax.ppermute(block, 'wide', [(b * workers + j, serving + j) for j in rang...  2.61 us
    pallas_call x1, Pallas kernels, serve(): pl.pallas_call(attend_kernel, out_shape=(pltpu.VMEM(shapes[0].shape, jnp....  2.28 us
    ppermute x3, waiting for transfers between devices, shards(): lax.ppermute(block, 'wide', [(b * workers + j, serving + j) for j in rang...  1.54 us
  transfers between devices with their start and end apart: 8, of which 3 were waited for; matrix products, arithmetic and copies ran while one was open for 0% of the time, Pallas kernels for 0%

profile of v20, /device:TPU:0, one launch (start us, length us, event | category | flops | bytes accessed | tf_op | source)
XLA Modules:
  0.0 37.2 jit_solution(6176705579460789592)
XLA Ops:
  0.6 8.5 %conditional.2 = ((bf16[2,2048]{1,0:T(2,128)(2,1)S(1)}, bf16[4,2,2176]{2,1,0:T(2,128)(2,1)S(1)})) conditional(s32[]{:T(128)} %convert_element_type.6, () %tuple.21, (s32[1]{0:T(128)}, bf16[2,1,2048]{2,0,1:T(2,128)(2,1)}, bf16[2,1,2,512]{3,2,1,0:T(2,128)(2,1)}, bf16[1,4,128,128]{3,2,1,0:T(8,128)(2,1)}, bf16[1,4,128,128]{3,2,1,0:T(8,128)(2,1)}, ...), branch_computations={%region_0.0_spmd, %region_1.0_spmd} | conditional | bytes 43544 | solution.py:299
  0.7 2.3 %branch_1_fun.1 = (bf16[2,2048]{1,0:T(2,128)(2,1)S(1)}, bf16[2,2176]{1,0:T(2,128)(2,1)S(1)}) custom-call(s32[1,1]{1,0:T(1,128)} %bitcast.refs_0_, bf16[2,2048]{1,0:T(2,128)(2,1)} %bitcast.22, bf16[2,2,512]{2,1,0:T(2,128)(2,1)} %bitcast.25, bf16[4,128,128]{2,1,0:T(8,128)(2,1)} %bitcast.20, bf16[4,128,128]{2,1,0:T(8,128)(2,1)} %bitcast.21, ...), custom_call_target="tpu_custom_call" | custom-call | tf_op jit(solution)/shard_map/cond/branch_1_fun/pallas_call | solution.py:273
  2.9 6.2 %all-gather.2 = bf16[4,2,2176]{2,1,0:T(2,128)(2,1)S(1)} all-gather(bf16[1,2,2176]{2,1,0:T(2,128)(2,1)S(1)} %bitcast.14), channel_id=2, replica_groups={{0,1,2,3},{4,5,6,7},{8,9,10,11},{12,13,14,15},{16,17,18,19},{20,21,22,2..., dimensions={0}, use_global_device_ids=true | all-gather | bytes 43520 | tf_op jit(solution)/shard_map/cond/branch_1_fun/all_gather | solution.py:288
  9.1 0.7 %collective-permute-start.2 = (bf16[4,2,2176]{2,1,0:T(2,128)(2,1)S(1)}, bf16[4,2,2176]{2,1,0:T(2,128)(2,1)S(1)}, u32[]{:S(2)}, u32[]{:S(2)}) collective-permute-start(bf16[4,2,2176]{2,1,0:T(2,128)(2,1)S(1)} %get-tuple-element.48._), channel_id=1, source_target_pairs={{8,12},{10,14},{9,13},{11,15},{24,28},{26,30},{25,29},{27,31}} | collective-permute-start | bytes 104456 | tf_op jit(solution)/shard_map/ppermute | solution.py:301
  9.8 0.7 %collective-permute-start.1 = (bf16[4,2,2176]{2,1,0:T(2,128)(2,1)S(1)}, bf16[4,2,2176]{2,1,0:T(2,128)(2,1)S(1)}, u32[]{:S(2)}, u32[]{:S(2)}) collective-permute-start(bf16[4,2,2176]{2,1,0:T(2,128)(2,1)S(1)} %get-tuple-element.48._), channel_id=1, source_target_pairs={{4,12},{6,14},{5,13},{7,15},{20,28},{22,30},{21,29},{23,31}} | collective-permute-start | bytes 104456 | tf_op jit(solution)/shard_map/ppermute | solution.py:301
  10.5 1.3 %collective-permute-start = (bf16[4,2,2176]{2,1,0:T(2,128)(2,1)S(1)}, bf16[4,2,2176]{2,1,0:T(2,128)(2,1)S(1)}, u32[]{:S(2)}, u32[]{:S(2)}) collective-permute-start(bf16[4,2,2176]{2,1,0:T(2,128)(2,1)S(1)} %get-tuple-element.48._), channel_id=1, source_target_pairs={{0,12},{2,14},{1,13},{3,15},{16,28},{18,30},{17,29},{19,31}} | collective-permute-start | bytes 104456 | tf_op jit(solution)/shard_map/ppermute | solution.py:301
  11.8 0.0 collective-permute-done.2.refs_2_
  11.8 0.0 collective-permute-done.1.refs_1_
  11.8 1.5 %collective-permute-done.refs_0_ = bf16[4,2,2176]{2,1,0:T(2,128)(2,1)S(1)} collective-permute-done((bf16[4,2,2176]{2,1,0:T(2,128)(2,1)S(1)}, bf16[4,2,2176]{2,1,0:T(2,128)(2,1)S(1)}, u32[]{:S(2)}, u32[]{:S(2)}) %collective-permute-start) | collective-permute-done | bytes 34848 | tf_op jit(solution)/shard_map/ppermute | solution.py:301
  13.3 0.1 shard_map.112
  13.5 0.7 %collective-permute-start.3 = (bf16[2,2,3584]{2,1,0:T(2,128)(2,1)S(1)}, bf16[2,2,3584]{2,1,0:T(2,128)(2,1)S(1)}, u32[]{:S(2)}, u32[]{:S(2)}) collective-permute-start(bf16[2,2,3584]{2,1,0:T(2,128)(2,1)S(1)} %get-tuple-element.51), channel_id=1, source_target_pairs={{12,4},{14,6},{13,5},{15,7},{28,20},{30,22},{29,21},{31,23}} | collective-permute-start | bytes 86024 | tf_op jit(solution)/shard_map/ppermute | solution.py:334
  14.2 1.3 %collective-permute-start.4 = (bf16[2,3584]{1,0:T(2,128)(2,1)S(1)}, bf16[2,3584]{1,0:T(2,128)(2,1)S(1)}, u32[]{:S(2)}, u32[]{:S(2)}) collective-permute-start(bf16[2,3584]{1,0:T(2,128)(2,1)S(1)} %get-tuple-element.52), channel_id=1, source_target_pairs={{12,0},{14,2},{13,1},{15,3},{28,16},{30,18},{29,17},{31,19}} | collective-permute-start | bytes 43016 | tf_op jit(solution)/shard_map/ppermute | solution.py:358
  15.5 1.3 %collective-permute-start.5 = (bf16[2,3584]{1,0:T(2,128)(2,1)S(1)}, bf16[2,3584]{1,0:T(2,128)(2,1)S(1)}, u32[]{:S(2)}, u32[]{:S(2)}) collective-permute-start(bf16[2,3584]{1,0:T(2,128)(2,1)S(1)} %get-tuple-element.53), channel_id=1, source_target_pairs={{12,2},{14,0},{13,3},{15,1},{28,18},{30,16},{29,19},{31,17}} | collective-permute-start | bytes 43016 | tf_op jit(solution)/shard_map/ppermute | solution.py:358
  16.8 0.7 %collective-permute-start.6 = (bf16[2,3584]{1,0:T(2,128)(2,1)S(1)}, bf16[2,3584]{1,0:T(2,128)(2,1)S(1)}, u32[]{:S(2)}, u32[]{:S(2)}) collective-permute-start(bf16[2,3584]{1,0:T(2,128)(2,1)S(1)} %get-tuple-element.54), channel_id=1, source_target_pairs={{12,8},{14,10},{13,9},{15,11},{28,24},{30,26},{29,25},{31,27}} | collective-permute-start | bytes 43016 | tf_op jit(solution)/shard_map/ppermute | solution.py:358
  17.4 0.7 %collective-permute-start.7 = (bf16[2,3584]{1,0:T(2,128)(2,1)S(1)}, bf16[2,3584]{1,0:T(2,128)(2,1)S(1)}, u32[]{:S(2)}, u32[]{:S(2)}) collective-permute-start(bf16[2,3584]{1,0:T(2,128)(2,1)S(1)} %get-tuple-element.55), channel_id=1, source_target_pairs={{12,10},{14,8},{13,11},{15,9},{28,26},{30,24},{29,27},{31,25}} | collective-permute-start | bytes 43016 | tf_op jit(solution)/shard_map/ppermute | solution.py:358
  18.1 0.0 collective-permute-done.3
  18.2 16.1 %collective-permute-done.4.refs_0_ = bf16[2,3584]{1,0:T(2,128)(2,1)S(1)} collective-permute-done((bf16[2,3584]{1,0:T(2,128)(2,1)S(1)}, bf16[2,3584]{1,0:T(2,128)(2,1)S(1)}, u32[]{:S(2)}, u32[]{:S(2)}) %collective-permute-start.4) | collective-permute-done | bytes 14368 | tf_op jit(solution)/shard_map/ppermute | solution.py:358
  34.3 2.2 %collective-permute-done.5.refs_1_ = bf16[2,3584]{1,0:T(2,128)(2,1)S(1)} collective-permute-done((bf16[2,3584]{1,0:T(2,128)(2,1)S(1)}, bf16[2,3584]{1,0:T(2,128)(2,1)S(1)}, u32[]{:S(2)}, u32[]{:S(2)}) %collective-permute-start.5) | collective-permute-done | bytes 14368 | tf_op jit(solution)/shard_map/ppermute | solution.py:358
  36.5 0.0 collective-permute-done.6.refs_2_
  36.5 0.0 collective-permute-done.7.refs_3_
  36.5 0.6 %shard_map.113 = (bf16[2,2048]{1,0:T(2,128)(2,1)}, bf16[2,7168]{1,0:T(2,128)(2,1)}) custom-call(bf16[2,2048]{1,0:T(2,128)(2,1)S(1)} %get-tuple-element.47.attended, bf16[2,2,2,3584]{3,2,1,0:T(2,128)(2,1)S(1)} %get-tuple-element.91.gathered, bf16[2,3584]{1,0:T(2,128)(2,1)S(1)} %collective-permute-done.4.refs_0_, ...), custom_call_target="tpu_custom_call" | custom-call | tf_op jit(solution)/shard_map/pallas_call | solution.py:360
  (3 shorter events, 0.1 us)
Async XLA Ops:
  9.1 2.7 %collective-permute-start.2 = (bf16[4,2,2176]{2,1,0:T(2,128)(2,1)S(1)}, bf16[4,2,2176]{2,1,0:T(2,128)(2,1)S(1)}, u32[]{:S(2)}, u32[]{:S(2)}) collective-permute-start(bf16[4,2,2176]{2,1,0:T(2,128)(2,1)S(1)} %get-tuple-element.48._), channel_id=1, source_target_pairs={{8,12},{10,14},{9,13},{11,15},{24,28},{26,30},{25,29},{27,31}} | collective-permute-start | bytes 104456 | tf_op jit(solution)/shard_map/ppermute | solution.py:301
  9.8 2.0 %collective-permute-start.1 = (bf16[4,2,2176]{2,1,0:T(2,128)(2,1)S(1)}, bf16[4,2,2176]{2,1,0:T(2,128)(2,1)S(1)}, u32[]{:S(2)}, u32[]{:S(2)}) collective-permute-start(bf16[4,2,2176]{2,1,0:T(2,128)(2,1)S(1)} %get-tuple-element.48._), channel_id=1, source_target_pairs={{4,12},{6,14},{5,13},{7,15},{20,28},{22,30},{21,29},{23,31}} | collective-permute-start | bytes 104456 | tf_op jit(solution)/shard_map/ppermute | solution.py:301
  10.5 2.9 %collective-permute-start = (bf16[4,2,2176]{2,1,0:T(2,128)(2,1)S(1)}, bf16[4,2,2176]{2,1,0:T(2,128)(2,1)S(1)}, u32[]{:S(2)}, u32[]{:S(2)}) collective-permute-start(bf16[4,2,2176]{2,1,0:T(2,128)(2,1)S(1)} %get-tuple-element.48._), channel_id=1, source_target_pairs={{0,12},{2,14},{1,13},{3,15},{16,28},{18,30},{17,29},{19,31}} | collective-permute-start | bytes 104456 | tf_op jit(solution)/shard_map/ppermute | solution.py:301
  13.5 4.6 %collective-permute-start.3 = (bf16[2,2,3584]{2,1,0:T(2,128)(2,1)S(1)}, bf16[2,2,3584]{2,1,0:T(2,128)(2,1)S(1)}, u32[]{:S(2)}, u32[]{:S(2)}) collective-permute-start(bf16[2,2,3584]{2,1,0:T(2,128)(2,1)S(1)} %get-tuple-element.51), channel_id=1, source_target_pairs={{12,4},{14,6},{13,5},{15,7},{28,20},{30,22},{29,21},{31,23}} | collective-permute-start | bytes 86024 | tf_op jit(solution)/shard_map/ppermute | solution.py:334
  14.2 20.1 %collective-permute-start.4 = (bf16[2,3584]{1,0:T(2,128)(2,1)S(1)}, bf16[2,3584]{1,0:T(2,128)(2,1)S(1)}, u32[]{:S(2)}, u32[]{:S(2)}) collective-permute-start(bf16[2,3584]{1,0:T(2,128)(2,1)S(1)} %get-tuple-element.52), channel_id=1, source_target_pairs={{12,0},{14,2},{13,1},{15,3},{28,16},{30,18},{29,17},{31,19}} | collective-permute-start | bytes 43016 | tf_op jit(solution)/shard_map/ppermute | solution.py:358
  15.5 21.0 %collective-permute-start.5 = (bf16[2,3584]{1,0:T(2,128)(2,1)S(1)}, bf16[2,3584]{1,0:T(2,128)(2,1)S(1)}, u32[]{:S(2)}, u32[]{:S(2)}) collective-permute-start(bf16[2,3584]{1,0:T(2,128)(2,1)S(1)} %get-tuple-element.53), channel_id=1, source_target_pairs={{12,2},{14,0},{13,3},{15,1},{28,18},{30,16},{29,19},{31,17}} | collective-permute-start | bytes 43016 | tf_op jit(solution)/shard_map/ppermute | solution.py:358
  16.8 19.7 %collective-permute-start.6 = (bf16[2,3584]{1,0:T(2,128)(2,1)S(1)}, bf16[2,3584]{1,0:T(2,128)(2,1)S(1)}, u32[]{:S(2)}, u32[]{:S(2)}) collective-permute-start(bf16[2,3584]{1,0:T(2,128)(2,1)S(1)} %get-tuple-element.54), channel_id=1, source_target_pairs={{12,8},{14,10},{13,9},{15,11},{28,24},{30,26},{29,25},{31,27}} | collective-permute-start | bytes 43016 | tf_op jit(solution)/shard_map/ppermute | solution.py:358
  17.4 19.1 %collective-permute-start.7 = (bf16[2,3584]{1,0:T(2,128)(2,1)S(1)}, bf16[2,3584]{1,0:T(2,128)(2,1)S(1)}, u32[]{:S(2)}, u32[]{:S(2)}) collective-permute-start(bf16[2,3584]{1,0:T(2,128)(2,1)S(1)} %get-tuple-element.55), channel_id=1, source_target_pairs={{12,10},{14,8},{13,11},{15,9},{28,26},{30,24},{29,27},{31,25}} | collective-permute-start | bytes 43016 | tf_op jit(solution)/shard_map/ppermute | solution.py:358

commit v21 on v15

--- a/solution.py
+++ b/solution.py
@@ -14,7 +14,7 @@
 EPS = 1e-05
 TILE = 256
 SLOTS = 4
-AHEAD = (3, 1, 1, 1, 1)
+AHEAD = (2, 1, 1, 1, 1)
 CHUNK = 1024
 
 
@@ -300,7 +300,7 @@
         for b in range(blocks)
     ]
     tile = TILE if columns % (2 * TILE) == 0 else columns
-    early = columns // 2 // tile * tile or columns
+    early = columns * 3 // 7 // tile * tile or columns
     held = pl.pallas_call(
         functools.partial(fetch_kernel, serving),
         out_shape=[pltpu.VMEM((features, early), jnp.bfloat16)] * 2,

time: 37 us -> 38 us (1.027)
  waiting for transfers between devices: 19.4 us -> 20.4 us
    ppermute x4, waiting for transfers between devices: 17.8 us -> 18.9 us  [shards(): results[nth] = lax.ppermute(hidden[nth], 'wide', pairs)]
where the time goes in v21:
time: 38 us; the launch traced here: 37.7 us
  waiting for transfers between devices  20.4 us (54%)
  starting transfers between devices  7.18 us (19%)
  blocking collectives  6.18 us (16%)
  Pallas kernels  3.11 us (8%)
  between operations  0.76 us (2%)
    ppermute x4, waiting for transfers between devices, shards(): results[nth] = lax.ppermute(hidden[nth], 'wide', pairs)  18.9 us
    all_gather x1, blocking collectives, serve(): lax.all_gather(sent, ('wide', 'narrow'), axis=0, axis_index_groups=groups)  6.18 us
    ppermute x4, starting transfers between devices, shards(): results[nth] = lax.ppermute(hidden[nth], 'wide', pairs)  3.91 us
    ppermute x3, starting transfers between devices, shards(): lax.ppermute(block, 'wide', [(b * workers + j, serving + j) for j in rang...  2.61 us
    pallas_call x1, Pallas kernels, serve(): pl.pallas_call(attend_kernel, out_shape=(pltpu.VMEM(shapes[0].shape, jnp....  2.28 us
    ppermute x3, waiting for transfers between devices, shards(): lax.ppermute(block, 'wide', [(b * workers + j, serving + j) for j in rang...  1.54 us
  transfers between devices with their start and end apart: 8, of which 3 were waited for; matrix products, arithmetic and copies ran while one was open for 0% of the time, Pallas kernels for 0%

profile of v21, /device:TPU:0, one launch (start us, length us, event | category | flops | bytes accessed | tf_op | source)
XLA Modules:
  0.0 37.7 jit_solution(990757123421457879)
XLA Ops:
  0.6 8.5 %conditional.2 = ((bf16[2,2048]{1,0:T(2,128)(2,1)S(1)}, bf16[4,2,2176]{2,1,0:T(2,128)(2,1)S(1)})) conditional(s32[]{:T(128)} %convert_element_type.6, () %tuple.21, (s32[1]{0:T(128)}, bf16[2,1,2048]{2,0,1:T(2,128)(2,1)}, bf16[2,1,2,512]{3,2,1,0:T(2,128)(2,1)}, bf16[1,4,128,128]{3,2,1,0:T(8,128)(2,1)}, bf16[1,4,128,128]{3,2,1,0:T(8,128)(2,1)}, ...), branch_computations={%region_0.0_spmd, %region_1.0_spmd} | conditional | bytes 43544 | solution.py:297
  0.7 2.3 %branch_1_fun.1 = (bf16[2,2048]{1,0:T(2,128)(2,1)S(1)}, bf16[2,2176]{1,0:T(2,128)(2,1)S(1)}) custom-call(s32[1,1]{1,0:T(1,128)} %bitcast.refs_0_, bf16[2,2048]{1,0:T(2,128)(2,1)} %bitcast.22, bf16[2,2,512]{2,1,0:T(2,128)(2,1)} %bitcast.25, bf16[4,128,128]{2,1,0:T(8,128)(2,1)} %bitcast.20, bf16[4,128,128]{2,1,0:T(8,128)(2,1)} %bitcast.21, ...), custom_call_target="tpu_custom_call" | custom-call | tf_op jit(solution)/shard_map/cond/branch_1_fun/pallas_call | solution.py:271
  2.9 6.2 %all-gather.2 = bf16[4,2,2176]{2,1,0:T(2,128)(2,1)S(1)} all-gather(bf16[1,2,2176]{2,1,0:T(2,128)(2,1)S(1)} %bitcast.14), channel_id=2, replica_groups={{0,1,2,3},{4,5,6,7},{8,9,10,11},{12,13,14,15},{16,17,18,19},{20,21,22,2..., dimensions={0}, use_global_device_ids=true | all-gather | bytes 43520 | tf_op jit(solution)/shard_map/cond/branch_1_fun/all_gather | solution.py:286
  9.1 0.7 %collective-permute-start.2 = (bf16[4,2,2176]{2,1,0:T(2,128)(2,1)S(1)}, bf16[4,2,2176]{2,1,0:T(2,128)(2,1)S(1)}, u32[]{:S(2)}, u32[]{:S(2)}) collective-permute-start(bf16[4,2,2176]{2,1,0:T(2,128)(2,1)S(1)} %get-tuple-element.48._), channel_id=1, source_target_pairs={{8,12},{10,14},{9,13},{11,15},{24,28},{26,30},{25,29},{27,31}} | collective-permute-start | bytes 104456 | tf_op jit(solution)/shard_map/ppermute | solution.py:299
  9.8 0.7 %collective-permute-start.1 = (bf16[4,2,2176]{2,1,0:T(2,128)(2,1)S(1)}, bf16[4,2,2176]{2,1,0:T(2,128)(2,1)S(1)}, u32[]{:S(2)}, u32[]{:S(2)}) collective-permute-start(bf16[4,2,2176]{2,1,0:T(2,128)(2,1)S(1)} %get-tuple-element.48._), channel_id=1, source_target_pairs={{4,12},{6,14},{5,13},{7,15},{20,28},{22,30},{21,29},{23,31}} | collective-permute-start | bytes 104456 | tf_op jit(solution)/shard_map/ppermute | solution.py:299
  10.5 1.3 %collective-permute-start = (bf16[4,2,2176]{2,1,0:T(2,128)(2,1)S(1)}, bf16[4,2,2176]{2,1,0:T(2,128)(2,1)S(1)}, u32[]{:S(2)}, u32[]{:S(2)}) collective-permute-start(bf16[4,2,2176]{2,1,0:T(2,128)(2,1)S(1)} %get-tuple-element.48._), channel_id=1, source_target_pairs={{0,12},{2,14},{1,13},{3,15},{16,28},{18,30},{17,29},{19,31}} | collective-permute-start | bytes 104456 | tf_op jit(solution)/shard_map/ppermute | solution.py:299
  11.8 0.0 collective-permute-done.2.refs_2_
  11.8 0.0 collective-permute-done.1.refs_1_
  11.8 1.5 %collective-permute-done.refs_0_ = bf16[4,2,2176]{2,1,0:T(2,128)(2,1)S(1)} collective-permute-done((bf16[4,2,2176]{2,1,0:T(2,128)(2,1)S(1)}, bf16[4,2,2176]{2,1,0:T(2,128)(2,1)S(1)}, u32[]{:S(2)}, u32[]{:S(2)}) %collective-permute-start) | collective-permute-done | bytes 34848 | tf_op jit(solution)/shard_map/ppermute | solution.py:299
  13.3 0.1 shard_map.112
  13.5 0.7 %collective-permute-start.3 = (bf16[2,2,3584]{2,1,0:T(2,128)(2,1)S(1)}, bf16[2,2,3584]{2,1,0:T(2,128)(2,1)S(1)}, u32[]{:S(2)}, u32[]{:S(2)}) collective-permute-start(bf16[2,2,3584]{2,1,0:T(2,128)(2,1)S(1)} %get-tuple-element.51), channel_id=1, source_target_pairs={{12,4},{14,6},{13,5},{15,7},{28,20},{30,22},{29,21},{31,23}} | collective-permute-start | bytes 86024 | tf_op jit(solution)/shard_map/ppermute | solution.py:331
  14.2 1.3 %collective-permute-start.4 = (bf16[2,3584]{1,0:T(2,128)(2,1)S(1)}, bf16[2,3584]{1,0:T(2,128)(2,1)S(1)}, u32[]{:S(2)}, u32[]{:S(2)}) collective-permute-start(bf16[2,3584]{1,0:T(2,128)(2,1)S(1)} %get-tuple-element.52), channel_id=1, source_target_pairs={{12,0},{14,2},{13,1},{15,3},{28,16},{30,18},{29,17},{31,19}} | collective-permute-start | bytes 43016 | tf_op jit(solution)/shard_map/ppermute | solution.py:355
  15.5 1.3 %collective-permute-start.5 = (bf16[2,3584]{1,0:T(2,128)(2,1)S(1)}, bf16[2,3584]{1,0:T(2,128)(2,1)S(1)}, u32[]{:S(2)}, u32[]{:S(2)}) collective-permute-start(bf16[2,3584]{1,0:T(2,128)(2,1)S(1)} %get-tuple-element.53), channel_id=1, source_target_pairs={{12,2},{14,0},{13,3},{15,1},{28,18},{30,16},{29,19},{31,17}} | collective-permute-start | bytes 43016 | tf_op jit(solution)/shard_map/ppermute | solution.py:355
  16.8 0.7 %collective-permute-start.6 = (bf16[2,3584]{1,0:T(2,128)(2,1)S(1)}, bf16[2,3584]{1,0:T(2,128)(2,1)S(1)}, u32[]{:S(2)}, u32[]{:S(2)}) collective-permute-start(bf16[2,3584]{1,0:T(2,128)(2,1)S(1)} %get-tuple-element.54), channel_id=1, source_target_pairs={{12,8},{14,10},{13,9},{15,11},{28,24},{30,26},{29,25},{31,27}} | collective-permute-start | bytes 43016 | tf_op jit(solution)/shard_map/ppermute | solution.py:355
  17.4 0.7 %collective-permute-start.7 = (bf16[2,3584]{1,0:T(2,128)(2,1)S(1)}, bf16[2,3584]{1,0:T(2,128)(2,1)S(1)}, u32[]{:S(2)}, u32[]{:S(2)}) collective-permute-start(bf16[2,3584]{1,0:T(2,128)(2,1)S(1)} %get-tuple-element.55), channel_id=1, source_target_pairs={{12,10},{14,8},{13,11},{15,9},{28,26},{30,24},{29,27},{31,25}} | collective-permute-start | bytes 43016 | tf_op jit(solution)/shard_map/ppermute | solution.py:355
  18.1 0.0 collective-permute-done.3
  18.2 16.5 %collective-permute-done.4.refs_0_ = bf16[2,3584]{1,0:T(2,128)(2,1)S(1)} collective-permute-done((bf16[2,3584]{1,0:T(2,128)(2,1)S(1)}, bf16[2,3584]{1,0:T(2,128)(2,1)S(1)}, u32[]{:S(2)}, u32[]{:S(2)}) %collective-permute-start.4) | collective-permute-done | bytes 14368 | tf_op jit(solution)/shard_map/ppermute | solution.py:355
  34.7 2.3 %collective-permute-done.5.refs_1_ = bf16[2,3584]{1,0:T(2,128)(2,1)S(1)} collective-permute-done((bf16[2,3584]{1,0:T(2,128)(2,1)S(1)}, bf16[2,3584]{1,0:T(2,128)(2,1)S(1)}, u32[]{:S(2)}, u32[]{:S(2)}) %collective-permute-start.5) | collective-permute-done | bytes 14368 | tf_op jit(solution)/shard_map/ppermute | solution.py:355
  37.0 0.0 collective-permute-done.6.refs_2_
  37.0 0.0 collective-permute-done.7.refs_3_
  37.0 0.6 %shard_map.113 = (bf16[2,2048]{1,0:T(2,128)(2,1)}, bf16[2,7168]{1,0:T(2,128)(2,1)}) custom-call(bf16[2,2048]{1,0:T(2,128)(2,1)S(1)} %get-tuple-element.47.attended, bf16[2,2,2,3584]{3,2,1,0:T(2,128)(2,1)S(1)} %get-tuple-element.91.gathered, bf16[2,3584]{1,0:T(2,128)(2,1)S(1)} %collective-permute-done.4.refs_0_, ...), custom_call_target="tpu_custom_call" | custom-call | tf_op jit(solution)/shard_map/pallas_call | solution.py:357
  (3 shorter events, 0.1 us)
Async XLA Ops:
  9.1 2.7 %collective-permute-start.2 = (bf16[4,2,2176]{2,1,0:T(2,128)(2,1)S(1)}, bf16[4,2,2176]{2,1,0:T(2,128)(2,1)S(1)}, u32[]{:S(2)}, u32[]{:S(2)}) collective-permute-start(bf16[4,2,2176]{2,1,0:T(2,128)(2,1)S(1)} %get-tuple-element.48._), channel_id=1, source_target_pairs={{8,12},{10,14},{9,13},{11,15},{24,28},{26,30},{25,29},{27,31}} | collective-permute-start | bytes 104456 | tf_op jit(solution)/shard_map/ppermute | solution.py:299
  9.8 2.0 %collective-permute-start.1 = (bf16[4,2,2176]{2,1,0:T(2,128)(2,1)S(1)}, bf16[4,2,2176]{2,1,0:T(2,128)(2,1)S(1)}, u32[]{:S(2)}, u32[]{:S(2)}) collective-permute-start(bf16[4,2,2176]{2,1,0:T(2,128)(2,1)S(1)} %get-tuple-element.48._), channel_id=1, source_target_pairs={{4,12},{6,14},{5,13},{7,15},{20,28},{22,30},{21,29},{23,31}} | collective-permute-start | bytes 104456 | tf_op jit(solution)/shard_map/ppermute | solution.py:299
  10.5 2.9 %collective-permute-start = (bf16[4,2,2176]{2,1,0:T(2,128)(2,1)S(1)}, bf16[4,2,2176]{2,1,0:T(2,128)(2,1)S(1)}, u32[]{:S(2)}, u32[]{:S(2)}) collective-permute-start(bf16[4,2,2176]{2,1,0:T(2,128)(2,1)S(1)} %get-tuple-element.48._), channel_id=1, source_target_pairs={{0,12},{2,14},{1,13},{3,15},{16,28},{18,30},{17,29},{19,31}} | collective-permute-start | bytes 104456 | tf_op jit(solution)/shard_map/ppermute | solution.py:299
  13.5 4.6 %collective-permute-start.3 = (bf16[2,2,3584]{2,1,0:T(2,128)(2,1)S(1)}, bf16[2,2,3584]{2,1,0:T(2,128)(2,1)S(1)}, u32[]{:S(2)}, u32[]{:S(2)}) collective-permute-start(bf16[2,2,3584]{2,1,0:T(2,128)(2,1)S(1)} %get-tuple-element.51), channel_id=1, source_target_pairs={{12,4},{14,6},{13,5},{15,7},{28,20},{30,22},{29,21},{31,23}} | collective-permute-start | bytes 86024 | tf_op jit(solution)/shard_map/ppermute | solution.py:331
  14.2 20.5 %collective-permute-start.4 = (bf16[2,3584]{1,0:T(2,128)(2,1)S(1)}, bf16[2,3584]{1,0:T(2,128)(2,1)S(1)}, u32[]{:S(2)}, u32[]{:S(2)}) collective-permute-start(bf16[2,3584]{1,0:T(2,128)(2,1)S(1)} %get-tuple-element.52), channel_id=1, source_target_pairs={{12,0},{14,2},{13,1},{15,3},{28,16},{30,18},{29,17},{31,19}} | collective-permute-start | bytes 43016 | tf_op jit(solution)/shard_map/ppermute | solution.py:355
  15.5 21.6 %collective-permute-start.5 = (bf16[2,3584]{1,0:T(2,128)(2,1)S(1)}, bf16[2,3584]{1,0:T(2,128)(2,1)S(1)}, u32[]{:S(2)}, u32[]{:S(2)}) collective-permute-start(bf16[2,3584]{1,0:T(2,128)(2,1)S(1)} %get-tuple-element.53), channel_id=1, source_target_pairs={{12,2},{14,0},{13,3},{15,1},{28,18},{30,16},{29,19},{31,17}} | collective-permute-start | bytes 43016 | tf_op jit(solution)/shard_map/ppermute | solution.py:355
  16.8 20.3 %collective-permute-start.6 = (bf16[2,3584]{1,0:T(2,128)(2,1)S(1)}, bf16[2,3584]{1,0:T(2,128)(2,1)S(1)}, u32[]{:S(2)}, u32[]{:S(2)}) collective-permute-start(bf16[2,3584]{1,0:T(2,128)(2,1)S(1)} %get-tuple-element.54), channel_id=1, source_target_pairs={{12,8},{14,10},{13,9},{15,11},{28,24},{30,26},{29,25},{31,27}} | collective-permute-start | bytes 43016 | tf_op jit(solution)/shard_map/ppermute | solution.py:355
  17.4 19.6 %collective-permute-start.7 = (bf16[2,3584]{1,0:T(2,128)(2,1)S(1)}, bf16[2,3584]{1,0:T(2,128)(2,1)S(1)}, u32[]{:S(2)}, u32[]{:S(2)}) collective-permute-start(bf16[2,3584]{1,0:T(2,128)(2,1)S(1)} %get-tuple-element.55), channel_id=1, source_target_pairs={{12,10},{14,8},{13,11},{15,9},{28,26},{30,24},{29,27},{31,25}} | collective-permute-start | bytes 43016 | tf_op jit(solution)/shard_map/ppermute | solution.py:355
